TPU v7x, 32 devices: a whole 2x2x4 slice. The times are simulated.
32 devices in a mesh: blk: 4 (over z), batch: 8 (over y, x, core).
Axes of the slice: x: 2, y: 2, z: 4, core: 2. Of those that a mesh axis runs over, the one named last changes fastest.
Arguments:
- hidden_in: bfloat16 [8, 1024, 1024], P('batch', 'blk'), may hold values from -6 to 6
- key_mask: int32 [8, 1024], P('batch'), may hold values 0 or 1
- lengths: int32 [8], P('batch'), may hold values from 769 to 1024, as said below
- first_gain: bfloat16 [1024], P(('blk', 'batch')), may hold values from 0.5 to 1.5
- first_shift: bfloat16 [1024], P(('blk', 'batch')), may hold values from -1.1953125 to 1.1953125
- input_weight: bfloat16 [1024, 3072], P(('blk', 'batch')), may hold values from -0.1875 to 0.1875
- query_bias: bfloat16 [1024], P(('blk', 'batch')), may hold values from -1.1953125 to 1.1953125
- value_bias: bfloat16 [1024], P(('blk', 'batch')), may hold values from -1.1953125 to 1.1953125
- output_weight: bfloat16 [1024, 1024], P(('blk', 'batch')), may hold values from -0.75 to 0.75
- output_bias: bfloat16 [1024], P(('blk', 'batch')), may hold values from -1.1953125 to 1.1953125
- second_gain: bfloat16 [1024], P(('blk', 'batch')), may hold values from 0.5 to 1.5
- second_shift: bfloat16 [1024], P(('blk', 'batch')), may hold values from -1.1953125 to 1.1953125
- up_weight: bfloat16 [1024, 4096], P(('blk', 'batch')), may hold values from -0.1875 to 0.1875
- up_bias: bfloat16 [4096], P(('blk', 'batch')), may hold values from -1.1953125 to 1.1953125
- down_weight: bfloat16 [4096, 1024], P(('blk', 'batch')), may hold values from -0.09375 to 0.09375
- down_bias: bfloat16 [1024], P(('blk', 'batch')), may hold values from -1.1953125 to 1.1953125
- cotangent: bfloat16 [8, 1024, 1024], P('batch', 'blk'), may hold values from -6 to 6
Outputs:
- layer_out: bfloat16 [8, 1024, 1024], P('batch', 'blk')
- input_gradient: bfloat16 [8, 1024, 1024], P('batch', 'blk')
- first_gain_gradient: float32 [1024], P(('blk', 'batch'))
- first_shift_gradient: float32 [1024], P(('blk', 'batch'))
- input_weight_gradient: float32 [1024, 3072], P(('blk', 'batch'))
- query_bias_gradient: float32 [1024], P(('blk', 'batch'))
- value_bias_gradient: float32 [1024], P(('blk', 'batch'))
- output_weight_gradient: float32 [1024, 1024], P(('blk', 'batch'))
- output_bias_gradient: float32 [1024], P(('blk', 'batch'))
- second_gain_gradient: float32 [1024], P(('blk', 'batch'))
- second_shift_gradient: float32 [1024], P(('blk', 'batch'))
- up_weight_gradient: float32 [1024, 4096], P(('blk', 'batch'))
- up_bias_gradient: float32 [4096], P(('blk', 'batch'))
- down_weight_gradient: float32 [4096, 1024], P(('blk', 'batch'))
- down_bias_gradient: float32 [1024], P(('blk', 'batch'))
Inputs may be any that keep to these rules, and one draw needn't show every extreme that they name: `lengths`: every sequence ends within its last 256 positions.
All inputs are finite; a program needn't handle non-finite values. No bound on the sum of `key_mask` on one device may be relied on, other than what follows from the above.
Results may differ from a plain program's by a relative error of at most 0.03.
Values may be sent and summed in bfloat16 or wider, within the bound.
No kernel may reach another device: no remote copies, remote signals or barrier semaphores. Data moves between devices by JAX's collectives and lax.ppermute only.
A program may use at most 96 MiB of HBM per device.

v0:
```python
import jax
import jax.numpy as jnp
from jax import lax
from jax.sharding import PartitionSpec as P

HEADS = 16


EPSILON = 1e-05
SCORE_SCALE = 0.125
MASKED = -1e30


def normalize(values, gain, shift):
    average = jnp.mean(values, axis=-1, keepdims=True)
    centred = values - average
    variance = jnp.mean(centred * centred, axis=-1, keepdims=True)
    return centred * lax.rsqrt(variance + EPSILON) * gain + shift


def fetch_attention(
    first_gain, first_shift, input_weight, query_bias, value_bias, output_weight, output_bias
):
    return (
        lax.all_gather(first_gain, ("blk", "batch"), axis=0, tiled=True),
        lax.all_gather(first_shift, ("blk", "batch"), axis=0, tiled=True),
        lax.all_gather(input_weight, ("blk", "batch"), axis=0, tiled=True),
        lax.all_gather(query_bias, ("blk", "batch"), axis=0, tiled=True),
        lax.all_gather(value_bias, ("blk", "batch"), axis=0, tiled=True),
        lax.all_gather(output_weight, ("blk", "batch"), axis=0, tiled=True),
        lax.all_gather(output_bias, ("blk", "batch"), axis=0, tiled=True),
    )


def fetch_forward(second_gain, second_shift, up_weight, up_bias, down_weight, down_bias):
    return (
        lax.all_gather(second_gain, ("blk", "batch"), axis=0, tiled=True),
        lax.all_gather(second_shift, ("blk", "batch"), axis=0, tiled=True),
        lax.all_gather(up_weight, ("blk", "batch"), axis=0, tiled=True),
        lax.all_gather(up_bias, ("blk", "batch"), axis=0, tiled=True),
        lax.all_gather(down_weight, ("blk", "batch"), axis=0, tiled=True),
        lax.all_gather(down_bias, ("blk", "batch"), axis=0, tiled=True),
    )


def key_valid(key_mask, lengths, offset, span_rows):
    marks = lax.dynamic_slice_in_dim(key_mask, offset, span_rows, 1)
    places = offset + jnp.arange(span_rows, dtype=jnp.int32)
    return (marks > 0) & (places[None, :] < lengths[:, None])


def allowed(query_places, key_places, valid):
    causal = key_places[None, :] <= query_places[:, None]
    itself = key_places[None, :] == query_places[:, None]
    return (causal[None] & (itself[None] | valid[:, None, :]))[:, None]


def block_terms(query_block, slope_block, top_block, delta_block, key_block, value_block, keep):
    scores = (
        jnp.einsum("sqhe,skhe->shqk", query_block, key_block, preferred_element_type=jnp.float32)
        * SCORE_SCALE
    )
    scores = jnp.where(keep, scores, MASKED)
    chances = jnp.where(keep, jnp.exp(scores - top_block[..., None]), 0.0)
    gradient_chances = jnp.einsum(
        "sqhe,skhe->shqk", slope_block, value_block, preferred_element_type=jnp.float32
    )
    gradient_scores = (chances * (gradient_chances - delta_block[..., None])).astype(jnp.bfloat16)
    return (chances.astype(jnp.bfloat16), gradient_scores)


def local(
    hidden_in,
    key_mask,
    lengths,
    first_gain,
    first_shift,
    input_weight,
    query_bias,
    value_bias,
    output_weight,
    output_bias,
    second_gain,
    second_shift,
    up_weight,
    up_bias,
    down_weight,
    down_bias,
    cotangent,
):
    sequences, local_rows, model_width = hidden_in.shape
    head_size = model_width // HEADS
    tokens_here = sequences * local_rows
    first_row = lax.axis_index("blk") * local_rows
    query_places = first_row + jnp.arange(local_rows, dtype=jnp.int32)
    last_query = first_row + local_rows - 1
    row_live = (query_places[None, :] < lengths[:, None]).astype(jnp.float32)
    local_valid = key_valid(key_mask, lengths, first_row, local_rows)
    gain_one, shift_one, joint_weight, bias_query, bias_value, out_weight, bias_out = (
        fetch_attention(
            first_gain,
            first_shift,
            input_weight,
            query_bias,
            value_bias,
            output_weight,
            output_bias,
        )
    )
    inputs = hidden_in.astype(jnp.float32)
    gain_one_f = gain_one.astype(jnp.float32)
    shift_one_f = shift_one.astype(jnp.float32)
    normed_one = (
        normalize(inputs, gain_one_f, shift_one_f)
        .astype(jnp.bfloat16)
        .reshape(tokens_here, model_width)
    )
    joint = jnp.dot(normed_one, joint_weight, preferred_element_type=jnp.float32)
    joint = joint + jnp.concatenate(
        [
            bias_query.astype(jnp.float32),
            jnp.zeros((model_width,), jnp.float32),
            bias_value.astype(jnp.float32),
        ]
    )
    joint_low = joint.astype(jnp.bfloat16).reshape(sequences, local_rows, 3 * model_width)
    query_flat = joint_low[..., :model_width]
    queries = query_flat.reshape(sequences, local_rows, HEADS, head_size)
    keys_here = joint_low[..., model_width : 2 * model_width]
    values_here = joint_low[..., 2 * model_width :]
    empty_heads = jnp.zeros((sequences, HEADS, local_rows, head_size), jnp.float32)
    start_max = jnp.full((sequences, HEADS, local_rows), MASKED, jnp.float32)
    start_sum = jnp.zeros((sequences, HEADS, local_rows), jnp.float32)
    key_piece = lax.all_gather(keys_here, "blk", axis=1, tiled=True)
    value_piece = lax.all_gather(values_here, "blk", axis=1, tiled=True)
    piece_rows = key_piece.shape[1]

    def attend_visit(number, current):
        offset = number * local_rows

        def attend_work(current):
            accumulated, running_max, running_sum = current
            key_block = lax.dynamic_slice_in_dim(
                key_piece, number * local_rows, local_rows, 1
            ).reshape(sequences, local_rows, HEADS, head_size)
            value_block = lax.dynamic_slice_in_dim(
                value_piece, number * local_rows, local_rows, 1
            ).reshape(sequences, local_rows, HEADS, head_size)
            key_places = offset + jnp.arange(local_rows, dtype=jnp.int32)
            keep = allowed(
                query_places, key_places, key_valid(key_mask, lengths, offset, local_rows)
            )
            scores = (
                jnp.einsum(
                    "sqhe,skhe->shqk", queries, key_block, preferred_element_type=jnp.float32
                )
                * SCORE_SCALE
            )
            scores = jnp.where(keep, scores, MASKED)
            new_max = jnp.maximum(running_max, jnp.max(scores, axis=-1))
            fading = jnp.exp(running_max - new_max)
            weights = jnp.where(keep, jnp.exp(scores - new_max[..., None]), 0.0)
            running_sum = running_sum * fading + jnp.sum(weights, axis=-1)
            accumulated = accumulated * fading[..., None] + jnp.einsum(
                "shqk,skhe->shqe",
                weights.astype(jnp.bfloat16),
                value_block,
                preferred_element_type=jnp.float32,
            )
            return (accumulated, new_max, running_sum)

        return lax.cond(offset > last_query, lambda unchanged: unchanged, attend_work, current)

    accumulated, running_max, running_sum = lax.fori_loop(
        0, piece_rows // local_rows, attend_visit, (empty_heads, start_max, start_sum)
    )
    attended_full = accumulated / running_sum[..., None]
    log_total = running_max + jnp.log(running_sum)
    attended = (
        attended_full.transpose(0, 2, 1, 3).reshape(tokens_here, model_width).astype(jnp.bfloat16)
    )
    branch = jnp.dot(attended, out_weight, preferred_element_type=jnp.float32) + bias_out.astype(
        jnp.float32
    )
    middle = inputs + branch.reshape(sequences, local_rows, model_width)
    gain_two, shift_two, weight_up, bias_up, weight_down, bias_down = fetch_forward(
        second_gain, second_shift, up_weight, up_bias, down_weight, down_bias
    )
    gain_two_f = gain_two.astype(jnp.float32)
    shift_two_f = shift_two.astype(jnp.float32)
    normed_two = (
        normalize(middle, gain_two_f, shift_two_f)
        .astype(jnp.bfloat16)
        .reshape(tokens_here, model_width)
    )
    hidden_pre = jnp.dot(
        normed_two, weight_up, preferred_element_type=jnp.float32
    ) + bias_up.astype(jnp.float32)
    activated = jax.nn.gelu(hidden_pre, approximate=True).astype(jnp.bfloat16)
    feed_out = jnp.dot(
        activated, weight_down, preferred_element_type=jnp.float32
    ) + bias_down.astype(jnp.float32)
    layer_out = (middle + feed_out.reshape(sequences, local_rows, model_width)).astype(jnp.bfloat16)
    gain_two, shift_two, weight_up, bias_up, weight_down, bias_down = fetch_forward(
        second_gain, second_shift, up_weight, up_bias, down_weight, down_bias
    )
    gain_two_f = gain_two.astype(jnp.float32)
    shift_two_f = shift_two.astype(jnp.float32)
    gradient_out = cotangent.astype(jnp.float32) * row_live[..., None]
    gradient_down = gradient_out.reshape(tokens_here, model_width).astype(jnp.bfloat16)
    down_bias_sum = jnp.sum(gradient_down.astype(jnp.float32), axis=0)
    down_weight_sum = jnp.einsum(
        "tf,td->fd", activated, gradient_down, preferred_element_type=jnp.float32
    )
    gradient_act = jnp.einsum(
        "td,fd->tf", gradient_down, weight_down, preferred_element_type=jnp.float32
    )
    gelu_value, gelu_back = jax.vjp(lambda point: jax.nn.gelu(point, approximate=True), hidden_pre)
    gradient_pre = gelu_back(gradient_act)[0].astype(jnp.bfloat16)
    up_bias_sum = jnp.sum(gradient_pre.astype(jnp.float32), axis=0)
    up_weight_sum = jnp.einsum(
        "td,tf->df", normed_two, gradient_pre, preferred_element_type=jnp.float32
    )
    gradient_normed_two = jnp.einsum(
        "tf,df->td", gradient_pre, weight_up, preferred_element_type=jnp.float32
    )
    norm_value, norm_back = jax.vjp(normalize, middle, gain_two_f, shift_two_f)
    middle_part, gain_two_sum, shift_two_sum = norm_back(
        gradient_normed_two.reshape(sequences, local_rows, model_width)
    )
    gradient_middle = gradient_out + middle_part
    (
        second_gain_gradient,
        second_shift_gradient,
        up_weight_gradient,
        up_bias_gradient,
        down_weight_gradient,
        down_bias_gradient,
    ) = (
        lax.psum_scatter(gain_two_sum, ("blk", "batch"), scatter_dimension=0, tiled=True),
        lax.psum_scatter(shift_two_sum, ("blk", "batch"), scatter_dimension=0, tiled=True),
        lax.psum_scatter(up_weight_sum, ("blk", "batch"), scatter_dimension=0, tiled=True),
        lax.psum_scatter(up_bias_sum, ("blk", "batch"), scatter_dimension=0, tiled=True),
        lax.psum_scatter(down_weight_sum, ("blk", "batch"), scatter_dimension=0, tiled=True),
        lax.psum_scatter(down_bias_sum, ("blk", "batch"), scatter_dimension=0, tiled=True),
    )
    gain_one, shift_one, joint_weight, bias_query, bias_value, out_weight, bias_out = (
        fetch_attention(
            first_gain,
            first_shift,
            input_weight,
            query_bias,
            value_bias,
            output_weight,
            output_bias,
        )
    )
    gain_one_f = gain_one.astype(jnp.float32)
    shift_one_f = shift_one.astype(jnp.float32)
    gradient_branch = gradient_middle.reshape(tokens_here, model_width).astype(jnp.bfloat16)
    out_bias_sum = jnp.sum(gradient_branch.astype(jnp.float32), axis=0)
    out_weight_sum = jnp.einsum(
        "td,te->de", attended, gradient_branch, preferred_element_type=jnp.float32
    )
    gradient_att_flat = jnp.einsum(
        "te,de->td", gradient_branch, out_weight, preferred_element_type=jnp.float32
    ).astype(jnp.bfloat16)
    gradient_att_flat = gradient_att_flat.reshape(sequences, local_rows, model_width)
    gradient_att = gradient_att_flat.reshape(sequences, local_rows, HEADS, head_size)
    delta = jnp.einsum("sqhe,shqe->shq", gradient_att.astype(jnp.float32), attended_full)
    query_key_piece = lax.all_gather(keys_here, "blk", axis=1, tiled=True)
    query_value_piece = lax.all_gather(values_here, "blk", axis=1, tiled=True)
    piece_rows = query_key_piece.shape[1]

    def query_visit(number, current):
        offset = number * local_rows

        def query_work(current):
            key_block = lax.dynamic_slice_in_dim(
                query_key_piece, number * local_rows, local_rows, 1
            ).reshape(sequences, local_rows, HEADS, head_size)
            value_block = lax.dynamic_slice_in_dim(
                query_value_piece, number * local_rows, local_rows, 1
            ).reshape(sequences, local_rows, HEADS, head_size)
            key_places = offset + jnp.arange(local_rows, dtype=jnp.int32)
            keep = allowed(
                query_places, key_places, key_valid(key_mask, lengths, offset, local_rows)
            )
            chances_low, gradient_scores = block_terms(
                queries, gradient_att, log_total, delta, key_block, value_block, keep
            )
            return (
                current
                + jnp.einsum(
                    "shqk,skhe->shqe",
                    gradient_scores,
                    key_block,
                    preferred_element_type=jnp.float32,
                )
                * SCORE_SCALE
            )

        return lax.cond(offset > last_query, lambda unchanged: unchanged, query_work, current)

    query_total = lax.fori_loop(0, piece_rows // local_rows, query_visit, empty_heads)
    whole_top, whole_delta = (
        lax.all_gather(
            log_total.transpose(0, 2, 1).astype(jnp.bfloat16), "blk", axis=1, tiled=True
        ).astype(jnp.float32),
        lax.all_gather(
            delta.transpose(0, 2, 1).astype(jnp.bfloat16), "blk", axis=1, tiled=True
        ).astype(jnp.float32),
    )
    key_heads = keys_here.reshape(sequences, local_rows, HEADS, head_size)
    value_heads = values_here.reshape(sequences, local_rows, HEADS, head_size)
    local_zero = jnp.zeros((sequences, local_rows, HEADS, head_size), jnp.float32)
    query_piece = lax.all_gather(query_flat, "blk", axis=1, tiled=True)
    slope_piece = lax.all_gather(gradient_att_flat, "blk", axis=1, tiled=True)
    piece_rows = query_piece.shape[1]

    def collect_visit(number, current):
        offset = number * local_rows

        def collect_work(current):
            key_total, value_total = current
            query_block = lax.dynamic_slice_in_dim(
                query_piece, number * local_rows, local_rows, 1
            ).reshape(sequences, local_rows, HEADS, head_size)
            slope_block = lax.dynamic_slice_in_dim(
                slope_piece, number * local_rows, local_rows, 1
            ).reshape(sequences, local_rows, HEADS, head_size)
            top_block = lax.dynamic_slice_in_dim(whole_top, offset, local_rows, 1).transpose(
                0, 2, 1
            )
            delta_block = lax.dynamic_slice_in_dim(whole_delta, offset, local_rows, 1).transpose(
                0, 2, 1
            )
            block_places = offset + jnp.arange(local_rows, dtype=jnp.int32)
            keep = allowed(block_places, query_places, local_valid)
            chances_low, gradient_scores = block_terms(
                query_block, slope_block, top_block, delta_block, key_heads, value_heads, keep
            )
            key_total = (
                key_total
                + jnp.einsum(
                    "shqk,sqhe->skhe",
                    gradient_scores,
                    query_block,
                    preferred_element_type=jnp.float32,
                )
                * SCORE_SCALE
            )
            value_total = value_total + jnp.einsum(
                "shqk,sqhe->skhe", chances_low, slope_block, preferred_element_type=jnp.float32
            )
            return (key_total, value_total)

        return lax.cond(
            offset + local_rows - 1 < first_row, lambda unchanged: unchanged, collect_work, current
        )

    key_heads_sum, value_heads_sum = lax.fori_loop(
        0, piece_rows // local_rows, collect_visit, (local_zero, local_zero)
    )
    key_gradient = key_heads_sum.reshape(sequences, local_rows, model_width)
    value_gradient = value_heads_sum.reshape(sequences, local_rows, model_width)
    query_gradient = query_total.transpose(0, 2, 1, 3).reshape(sequences, local_rows, model_width)
    gradient_joint = jnp.concatenate([query_gradient, key_gradient, value_gradient], axis=-1)
    gradient_joint = gradient_joint.astype(jnp.bfloat16).reshape(tokens_here, 3 * model_width)
    joint_sums = jnp.sum(gradient_joint.astype(jnp.float32), axis=0)
    query_bias_sum = joint_sums[:model_width]
    value_bias_sum = joint_sums[2 * model_width :]
    joint_weight_sum = jnp.einsum(
        "td,te->de", normed_one, gradient_joint, preferred_element_type=jnp.float32
    )
    gradient_normed_one = jnp.einsum(
        "te,de->td", gradient_joint, joint_weight, preferred_element_type=jnp.float32
    )
    first_value, first_back = jax.vjp(normalize, inputs, gain_one_f, shift_one_f)
    input_part, gain_one_sum, shift_one_sum = first_back(
        gradient_normed_one.reshape(sequences, local_rows, model_width)
    )
    input_gradient = (gradient_middle + input_part).astype(jnp.bfloat16)
    (
        first_gain_gradient,
        first_shift_gradient,
        input_weight_gradient,
        query_bias_gradient,
        value_bias_gradient,
        output_weight_gradient,
        output_bias_gradient,
    ) = (
        lax.psum_scatter(gain_one_sum, ("blk", "batch"), scatter_dimension=0, tiled=True),
        lax.psum_scatter(shift_one_sum, ("blk", "batch"), scatter_dimension=0, tiled=True),
        lax.psum_scatter(joint_weight_sum, ("blk", "batch"), scatter_dimension=0, tiled=True),
        lax.psum_scatter(query_bias_sum, ("blk", "batch"), scatter_dimension=0, tiled=True),
        lax.psum_scatter(value_bias_sum, ("blk", "batch"), scatter_dimension=0, tiled=True),
        lax.psum_scatter(out_weight_sum, ("blk", "batch"), scatter_dimension=0, tiled=True),
        lax.psum_scatter(out_bias_sum, ("blk", "batch"), scatter_dimension=0, tiled=True),
    )
    return (
        layer_out,
        input_gradient,
        first_gain_gradient,
        first_shift_gradient,
        input_weight_gradient,
        query_bias_gradient,
        value_bias_gradient,
        output_weight_gradient,
        output_bias_gradient,
        second_gain_gradient,
        second_shift_gradient,
        up_weight_gradient,
        up_bias_gradient,
        down_weight_gradient,
        down_bias_gradient,
    )


def solution(mesh):
    return jax.shard_map(
        local,
        mesh=mesh,
        in_specs=(
            P("batch", "blk", None),
            P("batch", None),
            P("batch"),
            P(("blk", "batch")),
            P(("blk", "batch")),
            P(("blk", "batch"), None),
            P(("blk", "batch")),
            P(("blk", "batch")),
            P(("blk", "batch"), None),
            P(("blk", "batch")),
            P(("blk", "batch")),
            P(("blk", "batch")),
            P(("blk", "batch"), None),
            P(("blk", "batch")),
            P(("blk", "batch"), None),
            P(("blk", "batch")),
            P("batch", "blk", None),
        ),
        out_specs=(
            P("batch", "blk", None),
            P("batch", "blk", None),
            P(("blk", "batch")),
            P(("blk", "batch")),
            P(("blk", "batch"), None),
            P(("blk", "batch")),
            P(("blk", "batch")),
            P(("blk", "batch"), None),
            P(("blk", "batch")),
            P(("blk", "batch")),
            P(("blk", "batch")),
            P(("blk", "batch"), None),
            P(("blk", "batch")),
            P(("blk", "batch"), None),
            P(("blk", "batch")),
        ),
        check_vma=False,
    )
```

profile of v0, /device:TPU:0, one launch (start us, length us, event | category | flops | bytes accessed | tf_op | source)
XLA Modules:
  0.0 1171.2 jit_solution(12287033751650486327)
XLA Ops:
  14.7 42.6 %all-reduce.18 = (bf16[1024]{0:T(1024)(128)(2,1)S(1)}, bf16[1024]{0:T(1024)(128)(2,1)S(1)}, bf16[1024]{0:T(1024)(128)(2,1)S(1)}, bf16[1024]{0:T(1024)(128)(2,1)S...) all-reduce(bf16[1024]{0:T(1024)(128)(2,1)S(1)} %dynamic-update-slic, ...), channel_id=1, replica_groups=mesh['blk'=4,'batch'=8] {'blk','batch'}, use_global_device_ids=true, to_apply=%add.3 | all-reduce | flops 8192 | bytes 32768
  60.0 23.2 %all-gather.11.cloned.1.call-done = bf16[1024,3072]{1,0:T(8,128)(2,1)} async-done(((bf16[32,3072]{1,0:T(8,128)(2,1)}), bf16[1024,3072]{1,0:T(8,128)(2,1)}) %all-gather.11.cloned.1.call-update) | async-done | bytes 6291472 | tf_op jit(solution)/shard_map/all_gather | solution.py:27
  91.8 39.5 %all-gather.1 = bf16[32,1,128]{2,1,0:T(2,128)(2,1)S(1)} all-gather(bf16[1,1,128]{2,1,0:T(2,128)(2,1)S(1)} %bitcast.254), channel_id=1, replica_groups=mesh['blk'=4,'batch'=8] {'blk','batch'}, dimensions={0}, use_global_device_ids=true | all-gather | bytes 8448 | tf_op jit(solution)/shard_map/all_gather | solution.py:40
  136.8 44.0 %all-gather.15.cloned.1.call-done = bf16[1,1024,1024]{2,1,0:T(8,128)(2,1)} async-done(((bf16[1,256,1024]{2,1,0:T(8,128)(2,1)}), bf16[1,1024,1024]{2,1,0:T(8,128)(2,1)}) %all-gather.15.cloned.1.call-update) | async-done | bytes 2097168 | tf_op jit(solution)/shard_map/all_gather | solution.py:135
  193.6 45.0 %all-gather.17.cloned.1.call-done = bf16[1024,1024]{1,0:T(8,128)(2,1)} async-done(((bf16[32,1024]{1,0:T(8,128)(2,1)}), bf16[1024,1024]{1,0:T(8,128)(2,1)}) %all-gather.17.cloned.1.call-update) | async-done | bytes 2097168 | tf_op jit(solution)/shard_map/all_gather | solution.py:30
  242.4 75.3 %all-gather.19.cloned.1.call-done = bf16[1024,4096]{1,0:T(8,128)(2,1)} async-done(((bf16[32,4096]{1,0:T(8,128)(2,1)}), bf16[1024,4096]{1,0:T(8,128)(2,1)}) %all-gather.19.cloned.1.call-update) | async-done | bytes 8388624 | tf_op jit(solution)/shard_map/all_gather | solution.py:39
  326.0 70.5 %all-gather.21.cloned.1.call-done = bf16[4096,1024]{1,0:T(8,128)(2,1)} async-done(((bf16[128,1024]{1,0:T(8,128)(2,1)}), bf16[4096,1024]{1,0:T(8,128)(2,1)}) %all-gather.21.cloned.1.call-update) | async-done | bytes 8388624 | tf_op jit(solution)/shard_map/all_gather | solution.py:41
  419.7 13.5 %all_gather.81 = bf16[1,1024,16]{1,2,0:T(8,128)(2,1)S(1)} all-gather(bf16[1,256,16]{1,2,0:T(8,128)(2,1)S(1)} %get-tuple-element.1248), channel_id=1, replica_groups=mesh['blk'=4,'batch'=8] {'blk'}, dimensions={1}, use_global_device_ids=true | all-gather | bytes 40960 | tf_op jit(solution)/shard_map/all_gather | solution.py:307
  433.3 10.4 all-gather.23.cloned.1.call-done
  450.1 13.4 %all_gather.83 = bf16[1,1024,16]{1,2,0:T(8,128)(2,1)S(1)} all-gather(bf16[1,256,16]{1,2,0:T(8,128)(2,1)S(1)} %convert_bitcast_fusion), channel_id=1, replica_groups=mesh['blk'=4,'batch'=8] {'blk'}, dimensions={1}, use_global_device_ids=true | all-gather | bytes 40960 | tf_op jit(solution)/shard_map/all_gather | solution.py:310
  464.7 11.7 while.57
  465.1 11.2 conditional.11
  477.8 12.6 %all-gather.25.cloned.1.call-done = bf16[1024,1024]{1,0:T(8,128)(2,1)} async-done(((bf16[256,1024]{1,0:T(8,128)(2,1)}), bf16[1024,1024]{1,0:T(8,128)(2,1)}) %all-gather.25.cloned.1.call-update) | async-done | bytes 2097168 | tf_op jit(solution)/shard_map/all_gather | solution.py:318
  496.6 56.6 %while.58 = (s32[]{:T(128)}, f32[1,256,16,64]{1,3,2,0:T(8,128)}, f32[1,256,16,64]{1,3,2,0:T(8,128)}, s32[]{:T(128)}, bf16[1,1024,1024]{1,2,0:T(8,128)(2,1)}, /*i...) while((s32[]{:T(128)}, f32[1,256,16,64]{1,3,2,0:T(8,128)}, ...), condition=%wide.region_19.20_spmd.clone.clone, body=%wide.region_16.19_spmd.clone.clone.sunk | while | flops 550502912 | bytes 22338724 | solution.py:362
  496.7 14.2 %conditional.12 = ((f32[1,256,16,64]{1,3,2,0:T(8,128)}, f32[1,256,16,64]{1,3,2,0:T(8,128)})) conditional(s32[]{:T(128)} %convert_element_type.347, (s32[]{:T(128)}, bf16[1,1024,1024]{1,2,0:T(8,128)(2,1)}, s32[]{:T(128)}, s32[]{:T(128)}, pred[1,256]{1,0:T(4,128)(4,1)S(1)}, /*index=5*/bf16[1,256,16,64]{1,3,2,0:T(8,128)(2,1)S(1)}, ...), branch_computations={%region_17.17_spmd, %region_18.18_spmd} | conditional | flops 550502912 | bytes 22337400 | solution.py:358
  510.8 14.2 %conditional.12 = ((f32[1,256,16,64]{1,3,2,0:T(8,128)}, f32[1,256,16,64]{1,3,2,0:T(8,128)})) conditional(s32[]{:T(128)} %convert_element_type.347, (s32[]{:T(128)}, bf16[1,1024,1024]{1,2,0:T(8,128)(2,1)}, s32[]{:T(128)}, s32[]{:T(128)}, pred[1,256]{1,0:T(4,128)(4,1)S(1)}, /*index=5*/bf16[1,256,16,64]{1,3,2,0:T(8,128)(2,1)S(1)}, ...), branch_computations={%region_17.17_spmd, %region_18.18_spmd} | conditional | flops 550502912 | bytes 22337400 | solution.py:358
  525.0 14.1 %conditional.12 = ((f32[1,256,16,64]{1,3,2,0:T(8,128)}, f32[1,256,16,64]{1,3,2,0:T(8,128)})) conditional(s32[]{:T(128)} %convert_element_type.347, (s32[]{:T(128)}, bf16[1,1024,1024]{1,2,0:T(8,128)(2,1)}, s32[]{:T(128)}, s32[]{:T(128)}, pred[1,256]{1,0:T(4,128)(4,1)S(1)}, /*index=5*/bf16[1,256,16,64]{1,3,2,0:T(8,128)(2,1)S(1)}, ...), branch_computations={%region_17.17_spmd, %region_18.18_spmd} | conditional | flops 550502912 | bytes 22337400 | solution.py:358
  539.1 14.1 %conditional.12 = ((f32[1,256,16,64]{1,3,2,0:T(8,128)}, f32[1,256,16,64]{1,3,2,0:T(8,128)})) conditional(s32[]{:T(128)} %convert_element_type.347, (s32[]{:T(128)}, bf16[1,1024,1024]{1,2,0:T(8,128)(2,1)}, s32[]{:T(128)}, s32[]{:T(128)}, pred[1,256]{1,0:T(4,128)(4,1)S(1)}, /*index=5*/bf16[1,256,16,64]{1,3,2,0:T(8,128)(2,1)S(1)}, ...), branch_computations={%region_17.17_spmd, %region_18.18_spmd} | conditional | flops 550502912 | bytes 22337400 | solution.py:358
  563.8 9.9 fusion.110
  574.7 10.8 fusion.99
  602.7 38.8 %all-reduce.17 = (f32[1024]{0:T(1024)S(1)}, f32[1024]{0:T(1024)S(1)}, f32[1024]{0:T(1024)S(1)}, f32[1024]{0:T(1024)S(1)}, f32[1024]{0:T(1024)S(1)}, /*index=5*/f...) all-reduce(f32[1024]{0:T(1024)S(1)} %get-tuple-element.1155, ...), channel_id=3, replica_groups=mesh['blk'=4,'batch'=8] {'blk','batch'}, use_global_device_ids=true, to_apply=%region_23.24.clone | all-reduce | flops 12288 | bytes 98304
  648.0 143.2 %reduce-scatter.5.cloned.1.call-done = f32[32,3072]{1,0:T(8,128)} async-done(((f32[1024,3072]{1,0:T(8,128)}), f32[32,3072]{1,0:T(8,128)}) %reduce-scatter.5.cloned.1.call-update) | async-done | bytes 393232 | tf_op jit(solution)/shard_map/reduce_scatter | solution.py:395
  791.2 185.0 %reduce-scatter.9.cloned.1.call-done = f32[32,4096]{1,0:T(8,128)} async-done(((f32[1024,4096]{1,0:T(8,128)}), f32[32,4096]{1,0:T(8,128)}) %reduce-scatter.9.cloned.1.call-update) | async-done | bytes 524304 | tf_op jit(solution)/shard_map/reduce_scatter | solution.py:242
  976.2 187.9 %reduce-scatter.11.cloned.1.call-done = f32[128,1024]{1,0:T(8,128)} async-done(((f32[4096,1024]{1,0:T(8,128)}), f32[128,1024]{1,0:T(8,128)}) %reduce-scatter.11.cloned.1.call-update) | async-done | bytes 524304 | tf_op jit(solution)/shard_map/reduce_scatter | solution.py:244
  (257 shorter events, 201.6 us)
Async XLA Ops:
  7.2 76.1 %all-gather.11.cloned.1.call-start = ((), (), s32[]{:S(2)}) async-start(), calls=%async_computation.4 | async-start | bytes 6488064 | tf_op jit(solution)/shard_map/all_gather | solution.py:27
  7.9 126.0 %all-gather.13.cloned.1.call-start = ((), (), s32[]{:S(2)}) async-start(), calls=%async_computation.5 | async-start | bytes 2621440 | tf_op jit(solution)/shard_map/all_gather | solution.py:134
  60.0 28.2 %copy-start.28 = (f32[256]{0:T(256)}, f32[256]{0:T(256)S(1)}, u32[]{:S(2)}) copy-start(f32[256]{0:T(256)S(1)} %fusion.85) | copy-start | bytes 3076
  89.2 43.0 %copy-start.18 = (bf16[1,256,1024]{2,1,0:T(8,128)(2,1)}, bf16[1,256,1024]{2,1,0:T(8,128)(2,1)S(1)}, u32[]{:S(2)}) copy-start(bf16[1,256,1024]{2,1,0:T(8,128)(2,1)S(1)} %get-tuple-element.1267) | copy-start | bytes 1572868
  89.3 91.5 %all-gather.15.cloned.1.call-start = ((), (), s32[]{:S(2)}) async-start(), calls=%async_computation.6 | async-start | bytes 2621440 | tf_op jit(solution)/shard_map/all_gather | solution.py:135
  90.0 148.6 %all-gather.17.cloned.1.call-start = ((), (), s32[]{:S(2)}) async-start(), calls=%async_computation.7 | async-start | bytes 2162688 | tf_op jit(solution)/shard_map/all_gather | solution.py:30
  90.6 227.1 %all-gather.19.cloned.1.call-start = ((), (), s32[]{:S(2)}) async-start(), calls=%async_computation.8 | async-start | bytes 8650752 | tf_op jit(solution)/shard_map/all_gather | solution.py:39
  91.2 305.3 %all-gather.21.cloned.1.call-start = ((), (), s32[]{:S(2)}) async-start(), calls=%async_computation.9 | async-start | bytes 8650752 | tf_op jit(solution)/shard_map/all_gather | solution.py:41
  91.8 351.9 %all-gather.23.cloned.1.call-start = ((), (), s32[]{:S(2)}) async-start(), calls=%async_computation.10 | async-start | bytes 2621440 | tf_op jit(solution)/shard_map/all_gather | solution.py:317
  132.3 53.6 %copy-start.27 = (s32[1,1024]{1,0:T(1,128)S(1)}, s32[1,1024]{1,0:T(1,128)}, u32[]{:S(2)}) copy-start(s32[1,1024]{1,0:T(1,128)} %param.30) | copy-start | bytes 12292
  132.3 358.1 %all-gather.25.cloned.1.call-start = ((), (), s32[]{:S(2)}) async-start(), calls=%async_computation.15 | async-start | bytes 2621440 | tf_op jit(solution)/shard_map/all_gather | solution.py:318
  396.5 9.5 copy-start.3
  396.5 9.5 copy-start.32
  412.7 235.3 %reduce-scatter.7.cloned.1.call-start = ((), (), s32[]{:S(2)}) async-start(), calls=%async_computation.12 | async-start | bytes 4325376 | tf_op jit(solution)/shard_map/reduce_scatter | solution.py:398
  416.6 374.7 %reduce-scatter.5.cloned.1.call-start = ((), (), s32[]{:S(2)}) async-start(), calls=%async_computation.11 | async-start | bytes 12976128 | tf_op jit(solution)/shard_map/reduce_scatter | solution.py:395
  419.7 27.9 %copy-start.24 = (bf16[256,1024]{1,0:T(8,128)(2,1)S(1)}, bf16[256,1024]{1,0:T(8,128)(2,1)}, u32[]{:S(2)}) copy-start(bf16[256,1024]{1,0:T(8,128)(2,1)} %convolution_convert_fusion) | copy-start | bytes 1572868
  476.4 20.3 %copy-start.1 = (bf16[1,256,1024]{1,2,0:T(8,128)(2,1)S(1)}, bf16[1,256,1024]{1,2,0:T(8,128)(2,1)}, u32[]{:S(2)}) copy-start(bf16[1,256,1024]{1,2,0:T(8,128)(2,1)} %copy.64) | copy-start | bytes 1572868
  476.4 20.3 %copy-start.26 = (bf16[1,256,1024]{1,2,0:T(8,128)(2,1)S(1)}, bf16[1,256,1024]{1,2,0:T(8,128)(2,1)}, u32[]{:S(2)}) copy-start(bf16[1,256,1024]{1,2,0:T(8,128)(2,1)} %copy.65) | copy-start | bytes 1572868
  477.8 78.3 %copy-start.12 = (bf16[1,16,256,64]{2,3,1,0:T(8,128)(2,1)}, bf16[1,16,256,64]{2,3,1,0:T(8,128)(2,1)S(1)}, u32[]{:S(2)}) copy-start(bf16[1,16,256,64]{2,3,1,0:T(8,128)(2,1)S(1)} %convert.13) | copy-start | bytes 1572868
  496.6 59.4 %copy-start = (bf16[1,256,1024]{2,1,0:T(8,128)(2,1)S(1)}, bf16[1,256,1024]{2,1,0:T(8,128)(2,1)}, u32[]{:S(2)}) copy-start(bf16[1,256,1024]{2,1,0:T(8,128)(2,1)} %param.29) | copy-start | bytes 1572868
  562.6 413.6 %reduce-scatter.9.cloned.1.call-start = ((), (), s32[]{:S(2)}) async-start(), calls=%async_computation.13 | async-start | bytes 17301504 | tf_op jit(solution)/shard_map/reduce_scatter | solution.py:242
  573.7 590.5 %reduce-scatter.11.cloned.1.call-start = ((), (), s32[]{:S(2)}) async-start(), calls=%async_computation.14 | async-start | bytes 17301504 | tf_op jit(solution)/shard_map/reduce_scatter | solution.py:244
  586.9 8.4 copy-start.13
  600.1 46.7 %copy-start.7 = (f32[1,256,1024]{2,1,0:T(8,128)S(1)}, f32[1,256,1024]{2,1,0:T(8,128)}, u32[]{:S(2)}) copy-start(f32[1,256,1024]{2,1,0:T(8,128)} %copy-done.6) | copy-start | bytes 3145732
  (21 other events, 65.3 us)
Sparse Core Ops, SparseCore 0:
  10.9 72.3 all-gather.10
  89.4 44.4 all-gather.12
  136.0 44.6 all-gather.14
  183.5 55.1 all-gather.16
  241.4 76.2 all-gather.18
  320.4 76.0 all-gather.20
  398.6 44.9 all-gather.22
  445.2 45.1 all-gather.24
  493.2 140.1 reduce-scatter.6
  639.9 151.2 reduce-scatter.4
  794.2 182.0 reduce-scatter.8
  979.1 185.0 reduce-scatter.10
where the time goes:
time: 1180 us; the launch traced here: 1170 us
  waiting for transfers between devices  802 us (68%)
  blocking collectives  148 us (13%)
  matrix products  133 us (11%)
  local copies, waits for them, and re-layouts  53 us (4%)
  other arithmetic  18.1 us (2%)
  between operations  15.6 us (1%)
    reduce_scatter x1, waiting for transfers between devices, local(): lax.psum_scatter(down_weight_sum, ('blk', 'batch'), scatter_dimension=0,...  188 us
    reduce_scatter x1, waiting for transfers between devices, local(): lax.psum_scatter(up_weight_sum, ('blk', 'batch'), scatter_dimension=0, ti...  185 us
    reduce_scatter x1, waiting for transfers between devices, local(): lax.psum_scatter(joint_weight_sum, ('blk', 'batch'), scatter_dimension=0,...  143 us
    unnamed x2, blocking collectives  81.3 us
    all_gather x1, waiting for transfers between devices, fetch_forward(): lax.all_gather(up_weight, ('blk', 'batch'), axis=0, tiled=True)  75.3 us
    all_gather x1, waiting for transfers between devices, fetch_forward(): lax.all_gather(down_weight, ('blk', 'batch'), axis=0, tiled=True)  70.5 us
    all_gather x1, waiting for transfers between devices, fetch_attention(): lax.all_gather(output_weight, ('blk', 'batch'), axis=0, tiled=True)  45 us
    all_gather x1, waiting for transfers between devices, local(): value_piece = lax.all_gather(values_here, 'blk', axis=1, tiled=True)  44 us
  transfers between devices with their start and end apart: 12, of which 11 were waited for; matrix products, arithmetic and copies ran while one was open for 16% of the time, Pallas kernels for 0%

commit v1 on v0

v1 whole, which is shorter than its diff:
```python
import functools

import jax
import jax.numpy as jnp
from jax import lax
from jax.experimental import pallas as pl
from jax.experimental.pallas import tpu as pltpu
from jax.sharding import PartitionSpec as P

HEADS = 16
EPSILON = 1e-05
SCORE_SCALE = 0.125
MASKED = -1e30
LANES = 128
AXES = ("blk", "batch")
F32 = jnp.float32
BF16 = jnp.bfloat16

NT = (((1,), (1,)), ((), ()))
NN = (((1,), (0,)), ((), ()))
TN = (((0,), (0,)), ((), ()))


def dot(a, b, dims=NN):
    return lax.dot_general(a, b, dims, preferred_element_type=F32)


def bits_of(size):
    return size.bit_length() - 1


def key_mask_terms(rows):
    key = lax.broadcasted_iota(jnp.int32, (rows, rows), 0)
    query = lax.broadcasted_iota(jnp.int32, (rows, rows), 1)
    return key < query, key == query


def attend_kernel(head, rows, q_ref, k_ref, v_ref, bias_ref, att_ref, wide_ref, lse_ref):
    length, width = q_ref.shape
    earlier, same = key_mask_terms(rows)
    lane = lax.broadcasted_iota(jnp.int32, (rows, width), 1)
    value_t = v_ref[...].astype(F32).T.astype(BF16)
    for j in range(length // rows):
        here = slice(j * rows, (j + 1) * rows)
        bias_here = bias_ref[here, :]
        for h in range(width // head):
            mine = (lane >= h * head) & (lane < (h + 1) * head)
            query = jnp.where(mine, q_ref[here, :].astype(F32) * SCORE_SCALE, 0.0).astype(BF16)
            inner = dot(k_ref[here, :], query, NT)
            inner = jnp.where(same, inner, jnp.where(earlier, inner + bias_here, MASKED))
            top = jnp.max(inner, axis=0, keepdims=True)
            if j:
                outer = dot(k_ref[: j * rows, :], query, NT) + bias_ref[: j * rows, :]
                top = jnp.maximum(top, jnp.max(outer, axis=0, keepdims=True))
            inner = jnp.exp(inner - top)
            total = jnp.sum(inner, axis=0, keepdims=True)
            if j:
                outer = jnp.exp(outer - top)
                total = total + jnp.sum(outer, axis=0, keepdims=True)
            share = 1.0 / total
            value_h = value_t[h * head : (h + 1) * head]
            out = dot(value_h[:, here], (inner * share).astype(BF16))
            if j:
                out = out + dot(value_h[:, : j * rows], (outer * share).astype(BF16))
            wide_ref[h * head : (h + 1) * head, here] = out
            lse_ref[0, h : h + 1, here] = top + jnp.log(total)
    att_ref[...] = wide_ref[...].T.astype(BF16)


def attend(joint, key_bias, head, rows):
    length, width = joint.shape
    width = width // 3
    pairs = width // LANES
    column = lambda part: pl.BlockSpec((length, LANES), lambda p: (0, part * pairs + p))
    return pl.pallas_call(
        functools.partial(attend_kernel, head, rows),
        grid=(pairs,),
        in_specs=[column(0), column(1), column(2), pl.BlockSpec((length, 1), lambda p: (0, 0))],
        out_specs=[
            pl.BlockSpec((length, LANES), lambda p: (0, p)),
            pl.BlockSpec((LANES, length), lambda p: (p, 0)),
            pl.BlockSpec((1, 8, length), lambda p: (p, 0, 0)),
        ],
        out_shape=[
            jax.ShapeDtypeStruct((length, width), BF16),
            jax.ShapeDtypeStruct((width, length), F32),
            jax.ShapeDtypeStruct((pairs, 8, length), F32),
        ],
        compiler_params=pltpu.CompilerParams(vmem_limit_bytes=40 * 2**20),
        name="attend",
    )(joint, joint, joint, key_bias)


def attend_back_kernel(
    head,
    rows,
    q_ref,
    k_ref,
    v_ref,
    slope_ref,
    wide_ref,
    lse_ref,
    bias_ref,
    dq_ref,
    dk_ref,
    dv_ref,
    key_sum,
    value_sum,
    query_t,
):
    length, width = q_ref.shape
    earlier, same = key_mask_terms(rows)
    lane = lax.broadcasted_iota(jnp.int32, (rows, width), 1)
    key_t = k_ref[...].astype(F32).T.astype(BF16)
    product = slope_ref[...].astype(F32).T * wide_ref[...]
    key_sum[...] = jnp.zeros_like(key_sum)
    value_sum[...] = jnp.zeros_like(value_sum)
    for j in range(length // rows):
        here = slice(j * rows, (j + 1) * rows)
        for h in range(width // head):
            mine = (lane >= h * head) & (lane < (h + 1) * head)
            query = jnp.where(mine, q_ref[here, :].astype(F32) * SCORE_SCALE, 0.0).astype(BF16)
            slope = jnp.where(mine, slope_ref[here, :].astype(F32), 0.0).astype(BF16)
            top = lse_ref[0, h : h + 1, here]
            delta = jnp.sum(product[h * head : (h + 1) * head, here], axis=0, keepdims=True)
            key_h = key_t[h * head : (h + 1) * head]
            back = None
            for part in (slice(0, j * rows), here) if j else (here,):
                scores = dot(k_ref[part, :], query, NT)
                if part is here:
                    scores = jnp.where(
                        same, scores, jnp.where(earlier, scores + bias_ref[part, :], MASKED)
                    )
                else:
                    scores = scores + bias_ref[part, :]
                chances = jnp.exp(scores - top)
                slopes = dot(v_ref[part, :], slope, NT)
                grads = (chances * (slopes - delta)).astype(BF16)
                value_sum[part, :] += dot(chances.astype(BF16), slope)
                key_sum[part, :] += dot(grads, query)
                term = dot(key_h[:, part], grads)
                back = term if back is None else back + term
            query_t[h * head : (h + 1) * head, here] = back * SCORE_SCALE
    dq_ref[...] = query_t[...].T.astype(BF16)
    dk_ref[...] = key_sum[...].astype(BF16)
    dv_ref[...] = value_sum[...].astype(BF16)


def attend_back(joint, slope, wide, lse, key_bias, head, rows):
    length, width = slope.shape
    pairs = width // LANES
    column = lambda part: pl.BlockSpec((length, LANES), lambda p: (0, part * pairs + p))
    return pl.pallas_call(
        functools.partial(attend_back_kernel, head, rows),
        grid=(pairs,),
        in_specs=[
            column(0),
            column(1),
            column(2),
            column(0),
            pl.BlockSpec((LANES, length), lambda p: (p, 0)),
            pl.BlockSpec((1, 8, length), lambda p: (p, 0, 0)),
            pl.BlockSpec((length, 1), lambda p: (0, 0)),
        ],
        out_specs=[column(0)] * 3,
        out_shape=[jax.ShapeDtypeStruct((length, width), BF16)] * 3,
        scratch_shapes=[
            pltpu.VMEM((length, LANES), F32),
            pltpu.VMEM((length, LANES), F32),
            pltpu.VMEM((LANES, length), F32),
        ],
        compiler_params=pltpu.CompilerParams(vmem_limit_bytes=40 * 2**20),
        name="attend_back",
    )(joint, joint, joint, slope, wide, lse, key_bias)


def centre(values):
    average = jnp.mean(values, axis=-1, keepdims=True)
    centred = values - average
    variance = jnp.mean(centred * centred, axis=-1, keepdims=True)
    scale = lax.rsqrt(variance + EPSILON)
    return centred * scale, scale


def norm_back(slope, normal, scale, gain):
    weighted = slope * gain
    return scale * (
        weighted
        - jnp.mean(weighted, axis=-1, keepdims=True)
        - normal * jnp.mean(weighted * normal, axis=-1, keepdims=True)
    )


GELU_A = 0.7978845608028654
GELU_B = 0.044715


def gelu_terms(pre):
    square = pre * pre
    bend = jnp.tanh(GELU_A * pre * (1.0 + GELU_B * square))
    half = 0.5 * (1.0 + bend)
    slope = half + 0.5 * pre * (1.0 - bend * bend) * (GELU_A * (1.0 + 3.0 * GELU_B * square))
    return pre * half, slope


def solution(mesh):
    nb, nt = mesh.shape["blk"], mesh.shape["batch"]
    devices = nb * nt
    group_size = nb // 2
    total_bits = bits_of(devices)
    plane_bits = list(range(1, bits_of(nt)))
    group_bits = list(range(bits_of(nt), bits_of(nt) + bits_of(group_size)))
    top_bit = total_bits - 1
    members = 2 * group_size

    def at_home(i):
        return (i // nt) // group_size == i % 2

    def send(value, route):
        return lax.ppermute(value, AXES, route)

    def flip(value, bit, who=None):
        return send(value, [(i, i ^ (1 << bit)) for i in range(devices) if who is None or who(i)])

    def mirror(i):
        return (nb - 1 - i // nt) * nt + i % nt

    def local(
        hidden_in,
        key_mask,
        lengths,
        first_gain,
        first_shift,
        input_weight,
        query_bias,
        value_bias,
        output_weight,
        output_bias,
        second_gain,
        second_shift,
        up_weight,
        up_bias,
        down_weight,
        down_bias,
        cotangent,
    ):
        rows, width = hidden_in.shape[1:]
        length = key_mask.shape[1]
        head = width // HEADS
        blk, lane_id = lax.axis_index("blk"), lax.axis_index("batch")
        index = blk * nt + lane_id
        core = lane_id % 2
        group, place = blk // group_size, blk % group_size
        member = place * 2 + core
        home = group == core
        share = width // members
        ff = up_weight.shape[1]
        piece = ff // devices

        def bit(b):
            return (index >> b) & 1

        def ordered(mine, theirs, side, axis):
            return jnp.where(
                side == 0,
                jnp.concatenate([mine, theirs], axis),
                jnp.concatenate([theirs, mine], axis),
            )

        def side_of(value, side, axis):
            lo, hi = jnp.split(value, 2, axis)
            return jnp.where(side == 0, lo, hi)

        def spread(value):
            return value.reshape((1,) * total_bits + value.shape)

        def join(value, b):
            return ordered(value, flip(value, b), bit(b), total_bits - 1 - b)

        def trade(value, b, a):
            lead, columns = value.shape[:-1], value.shape[-1]
            view = value.reshape(lead + (a, 2, columns // (2 * a)))
            keep = side_of(view, bit(b), -2).reshape(lead + (columns // 2,))
            give = side_of(view, 1 - bit(b), -2).reshape(lead + (columns // 2,))
            return ordered(keep, flip(give, b), bit(b), total_bits - 1 - b)

        def halve(value, b):
            axis = total_bits - 1 - b
            keep = side_of(value, bit(b), axis).astype(F32)
            give = side_of(value, 1 - bit(b), axis).astype(BF16)
            return keep + flip(give, b).astype(F32)

        def untrade(value, b, a):
            axis = total_bits - 1 - b
            keep = side_of(value, bit(b), axis).astype(BF16)
            give = side_of(value, 1 - bit(b), axis).astype(BF16)
            lead, columns = keep.shape[:-1], keep.shape[-1]
            keep = keep.reshape(lead + (a, 1, columns // a))
            theirs = flip(give, b).reshape(lead + (a, 1, columns // a))
            return ordered(keep, theirs, bit(b), -2).reshape(lead + (2 * columns,))

        own = hidden_in[0]

        def first_route(i):
            return i ^ (1 << group_bits[0]) if at_home(i) else mirror(i) ^ 1

        came = send(own, [(i, first_route(i)) for i in range(devices)])
        near = ordered(own, came, bit(group_bits[0]), 0)
        for b in group_bits[1:]:
            near = ordered(near, flip(near, b, at_home), bit(b), 0)
        far = came
        away = lambda i: not at_home(i)
        for b in group_bits:
            far = ordered(far, flip(far, b, away), 1 - bit(b), 0)
        swapped = flip(jnp.where(home, near, far), 0)
        near_full = jnp.where(home, near, swapped)
        far_full = jnp.where(home, swapped, far)
        inputs = ordered(near_full, far_full, group, 0)

        small = jnp.concatenate(
            [
                first_gain,
                first_shift,
                query_bias,
                value_bias,
                output_bias,
                second_gain,
                second_shift,
                down_bias,
                up_bias,
            ]
        ).reshape(1, -1)
        small = spread(small)
        for b in range(total_bits):
            small = join(small, b)
        small = small.reshape(devices, -1).astype(F32)
        each = width // devices
        gain_one, shift_one, bias_q, bias_v, bias_out, gain_two, shift_two, bias_down = (
            small[:, v * each : (v + 1) * each].reshape(width) for v in range(8)
        )
        bias_up = small[:, 8 * each :].reshape(2, group_size, nt // 2, 2, piece)
        bias_up = lax.dynamic_index_in_dim(bias_up, place, 1, False)
        bias_up = lax.dynamic_index_in_dim(bias_up, core, 2, False).reshape(-1)
        bias_q = lax.dynamic_index_in_dim(bias_q.reshape(members, share), member, 0, False)
        bias_v = lax.dynamic_index_in_dim(bias_v.reshape(members, share), member, 0, False)

        w_in = trade(spread(input_weight), 0, 3 * group_size)
        for b in reversed(group_bits):
            w_in = trade(w_in, b, 3)
        w_in = join(w_in, top_bit)
        for b in plane_bits:
            w_in = join(w_in, b)
        w_in = w_in.reshape(width, 3 * share)

        w_up = trade(spread(up_weight), 0, 2 * group_size * (nt // 2))
        for b in reversed(group_bits):
            w_up = trade(w_up, b, 2)
        w_up = join(w_up, top_bit)
        for b in plane_bits:
            w_up = join(w_up, b)
        w_up = w_up.reshape(width, ff // members)

        w_down = join(spread(down_weight), top_bit)
        for b in reversed(plane_bits):
            w_down = join(w_down, b)
        w_down = w_down.reshape(ff // members, width)

        w_out = spread(output_weight)
        for b in group_bits + [top_bit] + plane_bits[::-1] + [0]:
            w_out = join(w_out, b)
        w_out = w_out.reshape(width, width)

        places = jnp.arange(length, dtype=jnp.int32)
        valid = ((key_mask[0] > 0) & (places < lengths[0])).astype(F32).reshape(1, length)
        valid = jnp.where(home, valid, flip(valid, 0))
        key_bias = jnp.where(valid > 0.5, 0.0, MASKED).reshape(length, 1)
        normal_one, _ = centre(inputs.astype(F32))
        normed_one = (normal_one * gain_one + shift_one).astype(BF16)
        joint = dot(normed_one, w_in)
        joint = joint + jnp.concatenate([bias_q, jnp.zeros_like(bias_q), bias_v])
        joint = joint.astype(BF16)
        att, wide, lse = attend(joint, key_bias, head, rows)

        other = own
        for b in group_bits:
            other = ordered(other, flip(other, b, away), bit(b), 0)
        other = jnp.where(home, send(other, [(i, i ^ 1) for i in range(devices) if away(i)]), other)
        base = ordered(near_full, other, group, 0).astype(F32)
        live = first_live = (
            blk * rows + jnp.arange(rows, dtype=jnp.int32) < lengths[0]
        ).astype(F32)[:, None]
        grad_out = cotangent[0].astype(F32) * live
        grad_low = grad_out.astype(BF16)
        grad_down = grad_low
        for b in group_bits:
            grad_down = ordered(grad_down, flip(grad_down, b), bit(b), 0)
        grad_down = ordered(grad_down, flip(grad_down, 0), core, 0)

        att_halves = att.reshape(2, group_size * rows, share)
        near_att = side_of(att_halves, group, 0)[0]
        far_att = side_of(att_halves, 1 - group, 0)[0]
        far_att = send(far_att, [(i, mirror(i)) for i in range(devices)])
        near_att = near_att.reshape(-1, 1, 1, share)
        far_att = far_att.reshape(-1, 1, 1, share)
        for k, b in enumerate(group_bits):
            near_att = ordered(near_att, flip(near_att, b), bit(b), 1)
            far_att = ordered(far_att, flip(far_att, b), 1 - bit(b), 1)
        att_all = ordered(near_att, far_att, group, 0)
        att_all = ordered(att_all, flip(att_all, 0), core, 2).reshape(-1, width)

        middle = base + dot(att_all, w_out) + bias_out
        normal_two, _ = centre(middle)
        normed_two = (normal_two * gain_two + shift_two).astype(BF16)
        pre = dot(normed_two, w_up) + bias_up
        act, act_slope = gelu_terms(pre)
        act = act.astype(BF16)
        out_part = dot(act, w_down).astype(BF16)
        grad_act = dot(grad_down, w_down, NT)
        grad_pre = (grad_act * act_slope).astype(BF16)
        normed_two_part = dot(grad_pre, w_up, NT).astype(BF16)
        d_down = dot(act, grad_down, TN).astype(BF16)
        d_up = dot(normed_two, grad_pre, TN).astype(BF16)
        d_bias_up = jnp.sum(grad_pre.astype(F32), axis=0)

        def own_rows(value):
            value = value.reshape(2, group_size, rows, value.shape[-1])
            value = lax.dynamic_index_in_dim(value, core, 0, False)
            return lax.dynamic_index_in_dim(value, place, 0, False)

        def reduce_rows(value):
            value = value.reshape(2, group_size * rows, width)
            total = side_of(value, core, 0)[0].astype(F32)
            total = total + flip(side_of(value, 1 - core, 0)[0], 0).astype(F32)
            for b in reversed(group_bits):
                give = side_of(total, 1 - bit(b), 0).astype(BF16)
                total = side_of(total, bit(b), 0) + flip(give, b).astype(F32)
            return total

        grad_normed_two = reduce_rows(normed_two_part)
        middle_own = own_rows(middle)
        normal_own, scale_own = centre(middle_own)
        grad_middle = grad_out + norm_back(grad_normed_two, normal_own, scale_own, gain_two)
        d_gain_two = jnp.sum(grad_normed_two * normal_own, axis=0)
        d_shift_two = jnp.sum(grad_normed_two, axis=0)
        grad_branch = grad_middle.astype(BF16)
        grad_att = dot(grad_branch, w_out, NT).astype(BF16)

        slices = grad_att.reshape(rows, members, share)
        parts = []
        for r in range(members):
            part = lax.dynamic_index_in_dim(slices, blk ^ r, 1, False)

            def route(i):
                m = (i // nt) ^ r
                return ((i % 2) * group_size + m // 2) * nt + (i % nt) - i % 2 + m % 2

            parts.append(send(part, [(i, route(i)) for i in range(devices)]))
        slope = jnp.stack(parts)
        order = [slope]
        for b in range(bits_of(members)):
            view = slope.reshape((members >> (b + 1), 2, 1 << b) + slope.shape[1:])
            flipped = view[:, ::-1].reshape(slope.shape)
            slope = jnp.where((member >> b) & 1 == 0, slope, flipped)
        slope = slope.reshape(length, share)
        dq, dk, dv = attend_back(joint, slope, wide, lse, key_bias, head, rows)
        grad_joint = jnp.concatenate([dq, dk, dv], axis=1)
        d_in = dot(normed_one, grad_joint, TN).astype(BF16)
        joint_sum = jnp.sum(grad_joint.astype(F32), axis=0)
        normed_one_part = dot(grad_joint, w_in, NT)
        d_gain_one = jnp.sum(normed_one_part * normal_one, axis=0)
        d_shift_one = jnp.sum(normed_one_part, axis=0)
        halves = normed_one_part.reshape(2, group_size * rows, width)
        keep_side = jnp.where(home, group, 1 - group)
        total = side_of(halves, keep_side, 0)[0]
        total = total + flip(side_of(halves, 1 - keep_side, 0)[0].astype(BF16), 0).astype(F32)
        for b in reversed(group_bits):
            side = jnp.where(home, bit(b), 1 - bit(b))
            give = side_of(total, 1 - side, 0).astype(BF16)
            total = side_of(total, side, 0) + flip(give, b).astype(F32)
        came = send(
            total.astype(BF16), [(i, mirror(i) ^ 1) for i in range(devices) if away(i)]
        )
        grad_normed_one = jnp.where(home, total, came.astype(F32))
        normal_in, scale_in = centre(own.astype(F32))
        input_gradient = grad_middle + norm_back(grad_normed_one, normal_in, scale_in, gain_one)

        layer_out = middle_own + reduce_rows(out_part) + bias_down

        d_up = d_up.reshape((2,) * total_bits + (each, -1))
        for b in reversed(plane_bits):
            d_up = halve(d_up, b)
        d_up = halve(d_up, top_bit)
        for b in group_bits:
            d_up = untrade(d_up, b, 2)
        d_up = untrade(d_up, 0, 2 * group_size * (nt // 2)).reshape(each, ff)

        d_down = d_down.reshape(
            tuple(2 if b in plane_bits + [top_bit] else 1 for b in reversed(range(total_bits)))
            + (piece, width)
        )
        for b in plane_bits:
            d_down = halve(d_down, b)
        d_down = halve(d_down, top_bit).reshape(piece, width)

        d_out = dot(own_rows(att_all), grad_branch, TN).astype(BF16)
        d_out = d_out.reshape((2,) * total_bits + (each, width))
        for b in [0] + plane_bits + [top_bit] + group_bits:
            d_out = halve(d_out, b)
        d_out = d_out.reshape(each, width)

        d_in = d_in.reshape((2,) * total_bits + (each, -1))
        for b in reversed(plane_bits):
            d_in = halve(d_in, b)
        d_in = halve(d_in, top_bit)
        for b in group_bits:
            d_in = untrade(d_in, b, 3)
        d_in = untrade(d_in, 0, 3 * group_size).reshape(each, 3 * width)

        def at_member(value):
            empty = jnp.zeros((members, share), F32)
            return lax.dynamic_update_slice(empty, value[None], (member, 0)).reshape(width)

        d_up_bias = jnp.zeros((2, group_size, nt // 2, 2, piece), F32)
        d_up_bias = lax.dynamic_update_slice(
            d_up_bias,
            d_bias_up.reshape(2, 1, nt // 2, 1, piece),
            (0, place, 0, core, 0),
        )
        sums = jnp.concatenate(
            [
                value.reshape(devices, -1)
                for value in (
                    d_gain_one,
                    d_shift_one,
                    at_member(joint_sum[:share]),
                    at_member(joint_sum[2 * share :]),
                    jnp.sum(grad_branch.astype(F32), axis=0),
                    d_gain_two,
                    d_shift_two,
                    jnp.sum(grad_low.astype(F32), axis=0),
                    d_up_bias,
                )
            ],
            axis=1,
        )
        sums = sums.reshape((2,) * total_bits + (1, -1))
        for b in reversed(range(total_bits)):
            axis = total_bits - 1 - b
            sums = side_of(sums, bit(b), axis) + flip(side_of(sums, 1 - bit(b), axis), b)
        sums = sums.reshape(-1)
        vectors = [sums[v * each : (v + 1) * each] for v in range(8)]
        return (
            layer_out.astype(BF16)[None],
            input_gradient.astype(BF16)[None],
            vectors[0],
            vectors[1],
            d_in.astype(F32),
            vectors[2],
            vectors[3],
            d_out.astype(F32),
            vectors[4],
            vectors[5],
            vectors[6],
            d_up.astype(F32),
            sums[8 * each :],
            d_down.astype(F32),
            vectors[7],
        )

    vector, matrix = P(AXES), P(AXES, None)
    tokens = P("batch", "blk", None)
    return jax.shard_map(
        local,
        mesh=mesh,
        in_specs=(
            tokens,
            P("batch", None),
            P("batch"),
            vector,
            vector,
            matrix,
            vector,
            vector,
            matrix,
            vector,
            vector,
            vector,
            matrix,
            vector,
            matrix,
            vector,
            tokens,
        ),
        out_specs=(
            tokens,
            tokens,
            vector,
            vector,
            matrix,
            vector,
            vector,
            matrix,
            vector,
            vector,
            vector,
            matrix,
            vector,
            matrix,
            vector,
        ),
        check_vma=False,
    )
```

time: 1180 us -> 437 us (0.37)
  waiting for transfers between devices: 802 us -> 144 us
  blocking collectives: 148 us -> 0 us
  matrix products: 133 us -> 52.4 us
  starting transfers between devices: 0.82 us -> 74.3 us
  other arithmetic: 18.1 us -> 74.2 us
  Pallas kernels: 0 us -> 17.7 us
  between operations: 15.6 us -> 3.6 us
    reduce_scatter x4 -> x0, waiting for transfers between devices: 516 us -> none  [the longest x1 188 us: local(): lax.psum_scatter(down_weight_sum, ('blk', 'batch'), scatter_dimension=0,...]
    all_gather x8 -> x0, waiting for transfers between devices: 282 us -> none  [the longest x1 75.3 us: fetch_forward(): lax.all_gather(up_weight, ('blk', 'batch'), axis=0, tiled=True)]
    ppermute x0 -> x69, waiting for transfers between devices: none -> 144 us  [send(): return lax.ppermute(value, AXES, route)]
    unnamed x2 -> x0, blocking collectives: 81.3 us -> none
    dot_general x28 -> x12, matrix products: 133 us -> 52.4 us  [dot(): return lax.dot_general(a, b, dims, preferred_element_type=F32)]
    ppermute x0 -> x69, starting transfers between devices: none -> 74.3 us  [send(): return lax.ppermute(value, AXES, route)]
    all_gather x3 -> x0, blocking collectives: 66.5 us -> none  [the longest x1 39.5 us: fetch_forward(): lax.all_gather(up_bias, ('blk', 'batch'), axis=0, tiled=True)]
    unnamed x89 -> x144, local copies, waits for them, and re-layouts: 34 us -> 7.83 us
  transfers between devices with their start and end apart: 12 -> 69, of which waited for: 11 -> 26; matrix products, arithmetic and copies ran while one was open for 16% -> 34% of each run, Pallas kernels for 0% -> 4%
where the time goes in v1:
time: 437 us; the launch traced here: 429 us
  waiting for transfers between devices  144 us (33%)
  starting transfers between devices  74.3 us (17%)
  other arithmetic  74.2 us (17%)
  local copies, waits for them, and re-layouts  62.7 us (14%)
  matrix products  52.4 us (12%)
  Pallas kernels  17.7 us (4%)
    ppermute x69, waiting for transfers between devices, send(): return lax.ppermute(value, AXES, route)  144 us
    ppermute x69, starting transfers between devices, send(): return lax.ppermute(value, AXES, route)  74.3 us
    dot_general x12, matrix products, dot(): return lax.dot_general(a, b, dims, preferred_element_type=F32)  52.4 us
    select_n x9, local copies, waits for them, and re-layouts, ordered(): jnp.where(side == 0, jnp.concatenate([mine, theirs], axis), jnp.concatena...  14.6 us
    add x12, other arithmetic, halve(): return keep + flip(give, b).astype(F32)  13.2 us
    select_n x27, other arithmetic, ordered(): jnp.where(side == 0, jnp.concatenate([mine, theirs], axis), jnp.concatena...  9.9 us
    select_n x16, other arithmetic, side_of(): return jnp.where(side == 0, lo, hi)  9.35 us
    pallas_call x1, Pallas kernels, attend_back(): pl.pallas_call(functools.partial(attend_back_kernel, head, rows), grid=(p...  9.21 us
  transfers between devices with their start and end apart: 69, of which 26 were waited for; matrix products, arithmetic and copies ran while one was open for 34% of the time, Pallas kernels for 4%

profile of v1, /device:TPU:0, one launch (start us, length us, event | category | flops | bytes accessed | tf_op | source)
XLA Modules:
  0.0 428.6 jit_solution(1728857132194914650)
XLA Ops:
  0.7 6.1 %concatenate.1298 = bf16[384]{0:T(512)(128)(2,1)S(1)} concatenate(bf16[32]{0:T(256)(128)(2,1)} %param.20, bf16[32]{0:T(256)(128)(2,1)} %param.21, bf16[32]{0:T(256)(128)(2,1)} %param.23, bf16[32]{0:T(256)(128)(2,1)} %param.24, bf16[32]{0:T(256)(128)(2,1)} %param.26, bf16[32]{0:T(256)(128)(2,1)} %param.27, bf16[32]{0:T(256)(128)(2,1)} %param.28, bf16[32]{0:T(256)(128)(2,1)} %param.32, ...), dimensions={0} | concatenate | bytes 1536 | tf_op jit(solution)/shard_map/concatenate | solution.py:320
  33.6 8.4 %collective-permute-done.9 = bf16[1,2,2,2,2,1,384]{6,4,5,3,2,1,0:T(2,128)(2,1)S(1)} collective-permute-done((bf16[1,2,2,2,2,1,384]{6,4,5,3,2,1,0:T(2,128)(2,1)S(1)}, bf16[1,2,2,2,2,1,384]{6,4,5,3,2,1,0:T(2,128)(2,1)S(1)}, u32[]{:S(2)}, u32[]{:S(2)}) %collective-permute-start.9) | collective-permute-done | bytes 12320 | tf_op jit(solution)/shard_map/ppermute | solution.py:220
  55.3 7.6 %collective-permute-done.11 = bf16[1,1,1,1,2,32,768]{6,5,4,1,3,2,0:T(8,128)(2,1)S(1)} collective-permute-done((bf16[1,1,1,1,2,32,768]{6,5,4,1,3,2,0:T(8,128)(2,1)}, bf16[1,1,1,1,2,32,768]{6,5,4,1,3,2,0:T(8,128)(2,1)S(1)}, u32[]{:S(2)}, u32[]{:S(2)}) %collective-permute-start.11) | collective-permute-done | bytes 98336 | tf_op jit(solution)/shard_map/ppermute | solution.py:220
  65.5 7.5 %collective-permute-done.12 = bf16[1,2,1,1,2,32,768]{6,5,4,1,3,2,0:T(8,128)(2,1)S(1)} collective-permute-done((bf16[1,2,1,1,2,32,768]{6,5,4,1,3,2,0:T(8,128)(2,1)S(1)}, bf16[1,2,1,1,2,32,768]{6,5,4,1,3,2,0:T(8,128)(2,1)S(1)}, u32[]{:S(2)}, u32[]{:S(2)}) %collective-permute-start.12) | collective-permute-done | bytes 196640 | tf_op jit(solution)/shard_map/ppermute | solution.py:220
  75.5 6.9 %collective-permute-done.13 = bf16[2,2,1,1,2,32,768]{6,5,4,1,3,2,0:T(8,128)(2,1)S(1)} collective-permute-done((bf16[2,2,1,1,2,32,768]{6,5,4,1,3,2,0:T(8,128)(2,1)S(1)}, bf16[2,2,1,1,2,32,768]{6,5,4,1,3,2,0:T(8,128)(2,1)S(1)}, u32[]{:S(2)}, u32[]{:S(2)}) %collective-permute-start.13) | collective-permute-done | bytes 393248 | tf_op jit(solution)/shard_map/ppermute | solution.py:220
  86.1 10.5 %collective-permute-done.27 = bf16[1,2,1,1,2,32,1024]{6,5,4,1,3,2,0:T(8,128)(2,1)S(1)} collective-permute-done((bf16[1,2,1,1,2,32,1024]{6,5,4,1,3,2,0:T(8,128)(2,1)S(1)}, bf16[1,2,1,1,2,32,1024]{6,5,4,1,3,2,0:T(8,128)(2,1)S(1)}, u32[]{:S(2)}, u32[]{:S(2)}) %collective-permute-start.27) | collective-permute-done | bytes 262176 | tf_op jit(solution)/shard_map/ppermute | solution.py:220
  98.2 12.5 %collective-permute-done.31 = bf16[2,1,1,1,1,128,1024]{6,5,4,3,2,1,0:T(8,128)(2,1)S(1)} collective-permute-done((bf16[2,1,1,1,1,128,1024]{6,5,4,3,2,1,0:T(8,128)(2,1)S(1)}, bf16[2,1,1,1,1,128,1024]{6,5,4,3,2,1,0:T(8,128)(2,1)S(1)}, u32[]{:S(2)}, u32[]{:S(2)}) %collective-permute-start.31) | collective-permute-done | bytes 524320 | tf_op jit(solution)/shard_map/ppermute | solution.py:220
  122.4 8.5 %attend.1 = (bf16[1024,256]{1,0:T(8,128)(2,1)S(1)}, f32[256,1024]{1,0:T(8,128)S(1)}, f32[2,8,1024]{2,1,0:T(8,128)S(1)}) custom-call(bf16[1024,768]{1,0:T(8,128)(2,1)S(1)} %add_convert_fusion.1.q_ref.k_ref.v_ref, bf16[1024,768]{1,0:T(8,128)(2,1)S(1)} %add_convert_fusion.1.q_ref.k_ref.v_ref, bf16[1024,768]{1,0:T(8,128)(2,1)S(1)} %add_convert_fusion.1.q_ref.k_ref.v_ref, ...), custom_call_target="tpu_custom_call" | custom-call | tf_op jit(solution)/shard_map/attend/pallas_call | solution.py:75
  130.9 5.0 %collective-permute-start.17 = (bf16[512,256]{1,0:T(8,128)(2,1)S(1)}, bf16[512,256]{1,0:T(8,128)(2,1)S(1)}, u32[]{:S(2)}, u32[]{:S(2)}) collective-permute-start(bf16[512,256]{1,0:T(8,128)(2,1)S(1)} %get-tuple-element.56), channel_id=1, source_target_pairs={{0,24},{1,25},{2,26},{3,27},{4,28},{5,29},{6,30},{7,31},{8,16},{9,... | collective-permute-start | bytes 786440 | tf_op jit(solution)/shard_map/ppermute | solution.py:220
  136.2 6.7 %collective-permute-done.17 = bf16[512,256]{1,0:T(8,128)(2,1)S(1)} collective-permute-done((bf16[512,256]{1,0:T(8,128)(2,1)S(1)}, bf16[512,256]{1,0:T(8,128)(2,1)S(1)}, u32[]{:S(2)}, u32[]{:S(2)}) %collective-permute-start.17) | collective-permute-done | bytes 262176 | tf_op jit(solution)/shard_map/ppermute | solution.py:220
  155.5 8.1 %collective-permute-done.35 = bf16[256,1024]{1,0:T(8,128)(2,1)S(1)} collective-permute-done((bf16[256,1024]{1,0:T(8,128)(2,1)S(1)}, bf16[256,1024]{1,0:T(8,128)(2,1)S(1)}, u32[]{:S(2)}, u32[]{:S(2)}) %collective-permute-start.35) | collective-permute-done | bytes 524320 | tf_op jit(solution)/shard_map/ppermute | solution.py:220
  180.6 6.5 %fusion.78 = (f32[1024]{0:T(1024)S(1)}, f32[1024,1024]{1,0:T(8,128)S(1)}) fusion(f32[1024]{0:T(1024)S(1)} %copy-done.63, bf16[512,1024]{1,0:T(8,128)(2,1)} %copy-done.20, bf16[512,1024]{1,0:T(8,128)(2,1)} %broadcast_select_fusion.6, pred[]{:T(512)S(6)} %eq.45, bf16[1024,1024]{0,1:T(8,128)(2,1)} %bitcast.286, bf16[1024,1024]{1,0:T(8,128)(2,1)} %bitcast.272), kind=kOutput, calls=%fused_computation.274 | convolution fusion | flops 2161114112 | bytes 10493953 | tf_op jit(solution)/shard_map/dot_general | solution.py:25
  200.3 7.2 %convert_reduce_fusion.1 = (f32[1024]{0:T(1024)S(1)}, bf16[1024,1024]{1,0:T(8,128)(2,1)S(1)}) fusion(f32[1024,1024]{1,0:T(8,128)S(1)} %fusion.71, f32[1024]{0:T(1024)S(1)} %bitcast.330, bf16[1024,1024]{1,0:T(8,128)(2,1)S(1)} %bitcast.283, bf16[512,1024]{1,0:T(8,128)(2,1)} %collective-permute-done.36, bf16[512,1024]{1,0:T(8,128)(2,1)} %maximum_select_fusion.10, ...), kind=kOutput, calls=%fused_computation.10 | convolution fusion | flops 2178939904 | bytes 10493953 | tf_op jit(solution)/shard_map/dot_general | solution.py:25
  219.8 7.0 %convolution_convert_fusion = bf16[1024,1024]{1,0:T(8,128)(2,1)S(1)} fusion(bf16[512,1024]{1,0:T(8,128)(2,1)} %collective-permute-done.36, bf16[512,1024]{1,0:T(8,128)(2,1)} %maximum_select_fusion.10, pred[]{:T(512)S(6)} %eq.49, f32[1024,1024]{1,0:T(8,128)} %copy-done.67, f32[1024]{0:T(1024)S(1)} %bitcast.331), kind=kOutput, calls=%fused_computation.38 | convolution fusion | flops 2168455168 | bytes 8392705 | tf_op jit(solution)/shard_map/dot_general | solution.py:25
  238.1 12.9 %collective-permute-done.66 = bf16[2,1,2,1,1,128,1024]{6,5,4,3,2,1,0:T(8,128)(2,1)} collective-permute-done((bf16[2,1,2,1,1,128,1024]{6,5,4,3,2,1,0:T(8,128)(2,1)}, bf16[2,1,2,1,1,128,1024]{6,5,4,3,2,1,0:T(8,128)(2,1)}, u32[]{:S(2)}, u32[]{:S(2)}) %collective-permute-start.66) | collective-permute-done | bytes 1048608 | tf_op jit(solution)/shard_map/ppermute | solution.py:220
  266.9 13.0 %collective-permute-done.38 = bf16[256,1024]{1,0:T(8,128)(2,1)S(1)} collective-permute-done((bf16[256,1024]{1,0:T(8,128)(2,1)S(1)}, bf16[256,1024]{1,0:T(8,128)(2,1)S(1)}, u32[]{:S(2)}, u32[]{:S(2)}) %collective-permute-start.38) | collective-permute-done | bytes 524320 | tf_op jit(solution)/shard_map/ppermute | solution.py:220
  301.9 5.4 %collective-permute-start.68 = (bf16[1,1,1,1,1,128,1024]{6,5,4,3,2,1,0:T(8,128)(2,1)S(1)}, bf16[1,1,1,1,1,128,1024]{6,5,4,3,2,1,0:T(8,128)(2,1)}, u32[]{:S(2)}, u32[]{:S(2)}) collective-permute-start(bf16[1,1,1,1,1,128,1024]{6,5,4,3,2,1,0:T(8,128)(2,1)S(1)} %select_convert_fusion.8), channel_id=1, source_target_pairs={{0,16},{1,17},{2,18},{3,19},{4,20},{5,21},{6,22},{7,23},{8,24},{9,... | collective-permute-start | bytes 786440 | tf_op jit(solution)/shard_map/ppermute | solution.py:220
  316.7 9.2 %attend_back.1 = (bf16[1024,256]{1,0:T(8,128)(2,1)S(1)}, bf16[1024,256]{1,0:T(8,128)(2,1)S(1)}, bf16[1024,256]{1,0:T(8,128)(2,1)S(1)}) custom-call(bf16[1024,768]{1,0:T(8,128)(2,1)S(1)} %add_convert_fusion.1.q_ref.k_ref.v_ref, bf16[1024,768]{1,0:T(8,128)(2,1)S(1)} %add_convert_fusion.1.q_ref.k_ref.v_ref, ...), custom_call_target="tpu_custom_call" | custom-call | tf_op jit(solution)/shard_map/attend_back/pallas_call | solution.py:153
  327.4 5.1 %fusion.74 = (f32[1024]{0:T(1024)S(1)}, f32[1024]{0:T(1024)S(1)}, f32[1024,1024]{1,0:T(8,128)}) fusion(f32[1024]{0:T(1024)S(1)} %add_rsqrt_fusion.1, f32[1024]{0:T(1024)S(1)} %broadcast_multiply_fusion.1, bf16[512,1024]{1,0:T(8,128)(2,1)S(1)} %copy-done.21, bf16[512,1024]{1,0:T(8,128)(2,1)S(1)} %copy-done.19, pred[]{:T(512)S(6)} %eq.45, ...), kind=kOutput, calls=%fused_computation.272 | convolution fusion | flops 1626339328 | bytes 9453569 | tf_op jit(solution)/shard_map/dot_general | solution.py:25
  345.0 4.6 %convolution_convert_fusion.5 = bf16[1024,768]{1,0:T(8,128)(2,1)S(1)} fusion(bf16[1024,768]{1,0:T(8,128)(2,1)} %copy-done.35, f32[1024]{0:T(1024)S(1)} %copy-done.61, f32[1024]{0:T(1024)S(1)} %copy-done.49, f32[1024]{0:T(1024)S(1)} %copy-done.66, f32[1024]{0:T(1024)S(1)} %copy-done.53, bf16[512,1024]{1,0:T(8,128)(2,1)} %copy-done.20, ...), kind=kOutput, calls=%fused_computation.43 | convolution fusion | flops 1627127808 | bytes 5259265 | tf_op jit(solution)/shard_map/dot_general | solution.py:25
  376.7 5.9 %collective-permute-done.52 = bf16[2,2,1,1,2,32,768]{6,5,4,3,2,1,0:T(8,128)(2,1)S(1)} collective-permute-done((bf16[2,2,1,1,2,32,768]{6,5,4,3,2,1,0:T(8,128)(2,1)S(1)}, bf16[2,2,1,1,2,32,768]{6,5,4,3,2,1,0:T(8,128)(2,1)S(1)}, u32[]{:S(2)}, u32[]{:S(2)}) %collective-permute-start.52) | collective-permute-done | bytes 393248 | tf_op jit(solution)/shard_map/ppermute | solution.py:220
  386.9 4.8 %collective-permute-done.53 = bf16[1,2,1,1,2,32,768]{6,5,4,3,2,1,0:T(8,128)(2,1)S(1)} collective-permute-done((bf16[1,2,1,1,2,32,768]{6,5,4,3,2,1,0:T(8,128)(2,1)S(1)}, bf16[1,2,1,1,2,32,768]{6,5,4,3,2,1,0:T(8,128)(2,1)S(1)}, u32[]{:S(2)}, u32[]{:S(2)}) %collective-permute-start.53) | collective-permute-done | bytes 196640 | tf_op jit(solution)/shard_map/ppermute | solution.py:220
  411.1 5.1 %collective-permute-done.59 = bf16[1,2,1,1,1,32,1024]{6,5,4,3,2,1,0:T(8,128)(2,1)S(1)} collective-permute-done((bf16[1,2,1,1,1,32,1024]{6,5,4,3,2,1,0:T(8,128)(2,1)S(1)}, bf16[1,2,1,1,1,32,1024]{6,5,4,3,2,1,0:T(8,128)(2,1)S(1)}, u32[]{:S(2)}, u32[]{:S(2)}) %collective-permute-start.59) | collective-permute-done | bytes 131104 | tf_op jit(solution)/shard_map/ppermute | solution.py:220
  420.1 4.8 %collective-permute-done.60 = bf16[1,1,1,1,1,32,1024]{6,5,4,3,2,1,0:T(8,128)(2,1)} collective-permute-done((bf16[1,1,1,1,1,32,1024]{6,5,4,3,2,1,0:T(8,128)(2,1)}, bf16[1,1,1,1,1,32,1024]{6,5,4,3,2,1,0:T(8,128)(2,1)}, u32[]{:S(2)}, u32[]{:S(2)}) %collective-permute-start.60) | collective-permute-done | bytes 65568 | tf_op jit(solution)/shard_map/ppermute | solution.py:220
  (492 shorter events, 245.7 us)
Async XLA Ops:
  8.6 24.4 %collective-permute-start.15 = (f32[1,1024]{1,0:T(1,128)S(1)}, f32[1,1024]{1,0:T(1,128)S(1)}, u32[]{:S(2)}, u32[]{:S(2)}) collective-permute-start(f32[1,1024]{1,0:T(1,128)S(1)} %and_convert_fusion), channel_id=1, source_target_pairs={{0,1},{1,0},{2,3},{3,2},{4,5},{5,4},{6,7},{7,6},{8,9},{9,8},{10,11... | collective-permute-start | bytes 12296 | tf_op jit(solution)/shard_map/ppermute | solution.py:220
  8.8 38.1 %collective-permute-start.20 = (bf16[1,1,1,1,1,32,1024]{6,5,4,3,2,1,0:T(8,128)(2,1)}, bf16[1,1,1,1,1,32,1024]{6,5,4,3,2,1,0:T(8,128)(2,1)S(1)}, u32[]{:S(2)}, u32[]{:S(2)}) collective-permute-start(bf16[1,1,1,1,1,32,1024]{6,5,4,3,2,1,0:T(8,128)(2,1)} %bitcast.305), channel_id=1, source_target_pairs={{0,8},{1,9},{2,10},{3,11},{4,12},{5,13},{6,14},{7,15},{8,0},{9,1},... | collective-permute-start | bytes 196616 | tf_op jit(solution)/shard_map/ppermute | solution.py:220
  13.6 34.0 %collective-permute-start.10 = (bf16[1,1,1,1,1,32,1536]{6,5,4,3,2,1,0:T(8,128)(2,1)S(1)}, bf16[1,1,1,1,1,32,1536]{6,5,4,3,2,1,0:T(8,128)(2,1)S(1)}, u32[]{:S(2)}, u32[]{:S(2)}) collective-permute-start(bf16[1,1,1,1,1,32,1536]{6,5,4,3,2,1,0:T(8,128)(2,1)S(1)} %reshape.3605), channel_id=1, source_target_pairs={{0,1},{1,0},{2,3},{3,2},{4,5},{5,4},{6,7},{7,6},{8,9},{9,8},{10,11... | collective-permute-start | bytes 294920 | tf_op jit(solution)/shard_map/ppermute | solution.py:220
  16.0 36.1 %collective-permute-start.25 = (bf16[1,1,1,1,1,32,2048]{6,5,4,3,2,1,0:T(8,128)(2,1)}, bf16[1,1,1,1,1,32,2048]{6,5,4,3,2,1,0:T(8,128)(2,1)}, u32[]{:S(2)}, u32[]{:S(2)}) collective-permute-start(bf16[1,1,1,1,1,32,2048]{6,5,4,3,2,1,0:T(8,128)(2,1)} %reshape.3611), channel_id=1, source_target_pairs={{0,1},{1,0},{2,3},{3,2},{4,5},{5,4},{6,7},{7,6},{8,9},{9,8},{10,11... | collective-permute-start | bytes 393224 | tf_op jit(solution)/shard_map/ppermute | solution.py:220
  30.3 53.9 %collective-permute-start.30 = (bf16[1,1,1,1,1,128,1024]{6,5,4,3,2,1,0:T(8,128)(2,1)S(1)}, bf16[1,1,1,1,1,128,1024]{6,5,4,3,2,1,0:T(8,128)(2,1)S(1)}, u32[]{:S(2)}, u32[]{:S(2)}) collective-permute-start(bf16[1,1,1,1,1,128,1024]{6,5,4,3,2,1,0:T(8,128)(2,1)S(1)} %bitcast.291), channel_id=1, source_target_pairs={{0,16},{1,17},{2,18},{3,19},{4,20},{5,21},{6,22},{7,23},{8,24},{9,... | collective-permute-start | bytes 786440 | tf_op jit(solution)/shard_map/ppermute | solution.py:220
  55.2 29.6 %collective-permute-start.26 = (bf16[1,1,1,1,2,32,1024]{6,5,4,1,3,2,0:T(8,128)(2,1)S(1)}, bf16[1,1,1,1,2,32,1024]{6,5,4,1,3,2,0:T(8,128)(2,1)S(1)}, u32[]{:S(2)}, u32[]{:S(2)}) collective-permute-start(bf16[1,1,1,1,2,32,1024]{6,5,4,1,3,2,0:T(8,128)(2,1)S(1)} %bitcast.317), channel_id=1, source_target_pairs={{0,8},{1,9},{2,10},{3,11},{4,12},{5,13},{6,14},{7,15},{8,0},{9,1},... | collective-permute-start | bytes 393224 | tf_op jit(solution)/shard_map/ppermute | solution.py:220
  75.4 37.9 %collective-permute-start.2 = (bf16[512,1024]{1,0:T(8,128)(2,1)S(1)}, bf16[512,1024]{1,0:T(8,128)(2,1)S(1)}, u32[]{:S(2)}, u32[]{:S(2)}) collective-permute-start(bf16[512,1024]{1,0:T(8,128)(2,1)S(1)} %broadcast_select_fusion.8), channel_id=1, source_target_pairs={{0,1},{1,0},{2,3},{3,2},{4,5},{5,4},{6,7},{7,6},{8,9},{9,8},{10,11... | collective-permute-start | bytes 3145736 | tf_op jit(solution)/shard_map/ppermute | solution.py:220
  82.6 29.9 %collective-permute-start.14 = (bf16[2,2,1,2,2,32,768]{6,5,4,1,3,2,0:T(8,128)(2,1)S(1)}, bf16[2,2,1,2,2,32,768]{6,5,4,1,3,2,0:T(8,128)(2,1)S(1)}, u32[]{:S(2)}, u32[]{:S(2)}) collective-permute-start(bf16[2,2,1,2,2,32,768]{6,5,4,1,3,2,0:T(8,128)(2,1)S(1)} %maximum_select_fusion.11), channel_id=1, source_target_pairs={{0,4},{1,5},{2,6},{3,7},{4,0},{5,1},{6,2},{7,3},{8,12},{9,13},{10,... | collective-permute-start | bytes 2359304 | tf_op jit(solution)/shard_map/ppermute | solution.py:220
  84.3 26.5 %collective-permute-start.31 = (bf16[2,1,1,1,1,128,1024]{6,5,4,3,2,1,0:T(8,128)(2,1)S(1)}, bf16[2,1,1,1,1,128,1024]{6,5,4,3,2,1,0:T(8,128)(2,1)S(1)}, u32[]{:S(2)}, u32[]{:S(2)}) collective-permute-start(bf16[2,1,1,1,1,128,1024]{6,5,4,3,2,1,0:T(8,128)(2,1)S(1)} %maximum_select_fusion.19), channel_id=1, source_target_pairs={{0,4},{1,5},{2,6},{3,7},{4,0},{5,1},{6,2},{7,3},{8,12},{9,13},{10,... | collective-permute-start | bytes 1572872 | tf_op jit(solution)/shard_map/ppermute | solution.py:220
  85.1 28.3 %collective-permute-start.3 = (bf16[256,1024]{1,0:T(8,128)(2,1)S(1)}, bf16[256,1024]{1,0:T(8,128)(2,1)S(1)}, u32[]{:S(2)}, u32[]{:S(2)}) collective-permute-start(bf16[256,1024]{1,0:T(8,128)(2,1)S(1)} %bitcast.263), channel_id=1, source_target_pairs={{1,9},{3,11},{5,13},{7,15},{9,1},{11,3},{13,5},{15,7},{16,24},{18,... | collective-permute-start | bytes 1572872 | tf_op jit(solution)/shard_map/ppermute | solution.py:220
  96.6 39.3 %collective-permute-start.23 = (bf16[2,2,2,1,1,32,1024]{6,5,4,3,2,1,0:T(8,128)(2,1)S(1)}, bf16[2,2,2,1,1,32,1024]{6,5,4,3,2,1,0:T(8,128)(2,1)S(1)}, u32[]{:S(2)}, u32[]{:S(2)}) collective-permute-start(bf16[2,2,2,1,1,32,1024]{6,5,4,3,2,1,0:T(8,128)(2,1)S(1)} %maximum_select_fusion.15), channel_id=1, source_target_pairs={{0,2},{1,3},{2,0},{3,1},{4,6},{5,7},{6,4},{7,5},{8,10},{9,11},{10,... | collective-permute-start | bytes 1572872 | tf_op jit(solution)/shard_map/ppermute | solution.py:220
  110.7 33.9 %collective-permute-start.28 = (bf16[2,2,1,1,2,32,1024]{6,5,4,1,3,2,0:T(8,128)(2,1)S(1)}, bf16[2,2,1,1,2,32,1024]{6,5,4,1,3,2,0:T(8,128)(2,1)S(1)}, u32[]{:S(2)}, u32[]{:S(2)}) collective-permute-start(bf16[2,2,1,1,2,32,1024]{6,5,4,1,3,2,0:T(8,128)(2,1)S(1)} %maximum_select_fusion.17), channel_id=1, source_target_pairs={{0,2},{1,3},{2,0},{3,1},{4,6},{5,7},{6,4},{7,5},{8,10},{9,11},{10,... | collective-permute-start | bytes 1572872 | tf_op jit(solution)/shard_map/ppermute | solution.py:220
  112.4 52.6 %collective-permute-start.32 = (bf16[2,1,2,1,1,128,1024]{6,5,4,3,2,1,0:T(8,128)(2,1)S(1)}, bf16[2,1,2,1,1,128,1024]{6,5,4,3,2,1,0:T(8,128)(2,1)S(1)}, u32[]{:S(2)}, u32[]{:S(2)}) collective-permute-start(bf16[2,1,2,1,1,128,1024]{6,5,4,3,2,1,0:T(8,128)(2,1)S(1)} %maximum_select_fusion.9), channel_id=1, source_target_pairs={{0,2},{1,3},{2,0},{3,1},{4,6},{5,7},{6,4},{7,5},{8,10},{9,11},{10,... | collective-permute-start | bytes 3145736 | tf_op jit(solution)/shard_map/ppermute | solution.py:220
  136.1 31.2 %collective-permute-start.24 = (bf16[2,2,2,2,1,32,1024]{6,5,4,3,2,1,0:T(8,128)(2,1)S(1)}, bf16[2,2,2,2,1,32,1024]{6,5,4,3,2,1,0:T(8,128)(2,1)S(1)}, u32[]{:S(2)}, u32[]{:S(2)}) collective-permute-start(bf16[2,2,2,2,1,32,1024]{6,5,4,3,2,1,0:T(8,128)(2,1)S(1)} %maximum_select_fusion.7), channel_id=1, source_target_pairs={{0,1},{1,0},{2,3},{3,2},{4,5},{5,4},{6,7},{7,6},{8,9},{9,8},{10,11... | collective-permute-start | bytes 3145736 | tf_op jit(solution)/shard_map/ppermute | solution.py:220
  148.1 23.5 %collective-permute-start.29 = (bf16[2,2,1,2,2,32,1024]{6,5,4,1,3,2,0:T(8,128)(2,1)S(1)}, bf16[2,2,1,2,2,32,1024]{6,5,4,1,3,2,0:T(8,128)(2,1)S(1)}, u32[]{:S(2)}, u32[]{:S(2)}) collective-permute-start(bf16[2,2,1,2,2,32,1024]{6,5,4,1,3,2,0:T(8,128)(2,1)S(1)} %maximum_select_fusion.8), channel_id=1, source_target_pairs={{0,4},{1,5},{2,6},{3,7},{4,0},{5,1},{6,2},{7,3},{8,12},{9,13},{10,... | collective-permute-start | bytes 3145736 | tf_op jit(solution)/shard_map/ppermute | solution.py:220
  165.1 35.3 %collective-permute-start.36 = (bf16[512,1024]{1,0:T(8,128)(2,1)}, bf16[512,1024]{1,0:T(8,128)(2,1)}, u32[]{:S(2)}, u32[]{:S(2)}) collective-permute-start(bf16[512,1024]{1,0:T(8,128)(2,1)} %maximum_select_fusion.10), channel_id=1, source_target_pairs={{0,1},{1,0},{2,3},{3,2},{4,5},{5,4},{6,7},{7,6},{8,9},{9,8},{10,11... | collective-permute-start | bytes 3145736 | tf_op jit(solution)/shard_map/ppermute | solution.py:220
  228.0 22.9 %collective-permute-start.66 = (bf16[2,1,2,1,1,128,1024]{6,5,4,3,2,1,0:T(8,128)(2,1)}, bf16[2,1,2,1,1,128,1024]{6,5,4,3,2,1,0:T(8,128)(2,1)}, u32[]{:S(2)}, u32[]{:S(2)}) collective-permute-start(bf16[2,1,2,1,1,128,1024]{6,5,4,3,2,1,0:T(8,128)(2,1)} %broadcast_select_fusion), channel_id=1, source_target_pairs={{0,2},{1,3},{2,0},{3,1},{4,6},{5,7},{6,4},{7,5},{8,10},{9,11},{10,... | collective-permute-start | bytes 3145736 | tf_op jit(solution)/shard_map/ppermute | solution.py:220
  230.7 25.4 %collective-permute-start.33 = (bf16[512,1024]{1,0:T(8,128)(2,1)}, bf16[512,1024]{1,0:T(8,128)(2,1)}, u32[]{:S(2)}, u32[]{:S(2)}) collective-permute-start(bf16[512,1024]{1,0:T(8,128)(2,1)} %broadcast_select_fusion.4), channel_id=1, source_target_pairs={{0,1},{1,0},{2,3},{3,2},{4,5},{5,4},{6,7},{7,6},{8,9},{9,8},{10,11... | collective-permute-start | bytes 3145736 | tf_op jit(solution)/shard_map/ppermute | solution.py:220
  231.8 27.2 %collective-permute-start.37 = (bf16[512,1024]{1,0:T(8,128)(2,1)}, bf16[512,1024]{1,0:T(8,128)(2,1)}, u32[]{:S(2)}, u32[]{:S(2)}) collective-permute-start(bf16[512,1024]{1,0:T(8,128)(2,1)} %broadcast_select_fusion.3), channel_id=1, source_target_pairs={{0,1},{1,0},{2,3},{3,2},{4,5},{5,4},{6,7},{7,6},{8,9},{9,8},{10,11... | collective-permute-start | bytes 3145736 | tf_op jit(solution)/shard_map/ppermute | solution.py:220
  234.8 27.7 %collective-permute-start.61 = (bf16[2,2,1,2,2,32,1024]{6,5,4,3,2,1,0:T(8,128)(2,1)}, bf16[2,2,1,2,2,32,1024]{6,5,4,3,2,1,0:T(8,128)(2,1)}, u32[]{:S(2)}, u32[]{:S(2)}) collective-permute-start(bf16[2,2,1,2,2,32,1024]{6,5,4,3,2,1,0:T(8,128)(2,1)} %broadcast_select_fusion.1), channel_id=1, source_target_pairs={{0,4},{1,5},{2,6},{3,7},{4,0},{5,1},{6,2},{7,3},{8,12},{9,13},{10,... | collective-permute-start | bytes 3145736 | tf_op jit(solution)/shard_map/ppermute | solution.py:220
  254.5 42.7 %collective-permute-start.67 = (bf16[2,1,1,1,1,128,1024]{6,5,4,3,2,1,0:T(8,128)(2,1)}, bf16[2,1,1,1,1,128,1024]{6,5,4,3,2,1,0:T(8,128)(2,1)}, u32[]{:S(2)}, u32[]{:S(2)}) collective-permute-start(bf16[2,1,1,1,1,128,1024]{6,5,4,3,2,1,0:T(8,128)(2,1)} %select_convert_fusion.1), channel_id=1, source_target_pairs={{0,4},{1,5},{2,6},{3,7},{4,0},{5,1},{6,2},{7,3},{8,12},{9,13},{10,... | collective-permute-start | bytes 1572872 | tf_op jit(solution)/shard_map/ppermute | solution.py:220
  265.4 71.5 %collective-permute-start.62 = (bf16[2,2,1,1,2,32,1024]{6,5,4,3,2,1,0:T(8,128)(2,1)}, bf16[2,2,1,1,2,32,1024]{6,5,4,3,2,1,0:T(8,128)(2,1)}, u32[]{:S(2)}, u32[]{:S(2)}) collective-permute-start(bf16[2,2,1,1,2,32,1024]{6,5,4,3,2,1,0:T(8,128)(2,1)} %select_convert_fusion.2), channel_id=1, source_target_pairs={{0,2},{1,3},{2,0},{3,1},{4,6},{5,7},{6,4},{7,5},{8,10},{9,11},{10,... | collective-permute-start | bytes 1572872 | tf_op jit(solution)/shard_map/ppermute | solution.py:220
  301.9 61.2 %collective-permute-start.68 = (bf16[1,1,1,1,1,128,1024]{6,5,4,3,2,1,0:T(8,128)(2,1)S(1)}, bf16[1,1,1,1,1,128,1024]{6,5,4,3,2,1,0:T(8,128)(2,1)}, u32[]{:S(2)}, u32[]{:S(2)}) collective-permute-start(bf16[1,1,1,1,1,128,1024]{6,5,4,3,2,1,0:T(8,128)(2,1)S(1)} %select_convert_fusion.8), channel_id=1, source_target_pairs={{0,16},{1,17},{2,18},{3,19},{4,20},{5,21},{6,22},{7,23},{8,24},{9,... | collective-permute-start | bytes 786440 | tf_op jit(solution)/shard_map/ppermute | solution.py:220
  307.3 63.7 %collective-permute-start.56 = (bf16[2,2,2,2,1,32,1024]{6,5,4,3,2,1,0:T(8,128)(2,1)}, bf16[2,2,2,2,1,32,1024]{6,5,4,3,2,1,0:T(8,128)(2,1)}, u32[]{:S(2)}, u32[]{:S(2)}) collective-permute-start(bf16[2,2,2,2,1,32,1024]{6,5,4,3,2,1,0:T(8,128)(2,1)} %broadcast_select_fusion.2), channel_id=1, source_target_pairs={{0,1},{1,0},{2,3},{3,2},{4,5},{5,4},{6,7},{7,6},{8,9},{9,8},{10,11... | collective-permute-start | bytes 3145736 | tf_op jit(solution)/shard_map/ppermute | solution.py:220
  (114 other events, 1447.1 us)

commit v2 on v1

v2 whole, which is shorter than its diff:
```python
import functools

import jax
import jax.numpy as jnp
from jax import lax
from jax.experimental import pallas as pl
from jax.experimental.pallas import tpu as pltpu
from jax.sharding import PartitionSpec as P

HEADS = 16
EPSILON = 1e-05
SCORE_SCALE = 0.125
MASKED = -1e30
LANES = 128
AXES = ("blk", "batch")
F32 = jnp.float32
BF16 = jnp.bfloat16

NT = (((1,), (1,)), ((), ()))
NN = (((1,), (0,)), ((), ()))
TN = (((0,), (0,)), ((), ()))


def dot(a, b, dims=NN):
    return lax.dot_general(a, b, dims, preferred_element_type=F32)


def bits_of(size):
    return size.bit_length() - 1


def key_mask_terms(rows):
    key = lax.broadcasted_iota(jnp.int32, (rows, rows), 0)
    query = lax.broadcasted_iota(jnp.int32, (rows, rows), 1)
    return key < query, key == query


def centre(values):
    average = jnp.mean(values, axis=-1, keepdims=True)
    centred = values - average
    variance = jnp.mean(centred * centred, axis=-1, keepdims=True)
    scale = lax.rsqrt(variance + EPSILON)
    return centred * scale, scale


def norm_back(slope, normal, scale, gain):
    weighted = slope * gain
    return scale * (
        weighted
        - jnp.mean(weighted, axis=-1, keepdims=True)
        - normal * jnp.mean(weighted * normal, axis=-1, keepdims=True)
    )


GELU_A = 0.7978845608028654
GELU_B = 0.044715


def gelu_terms(pre):
    square = pre * pre
    bend = jnp.tanh(GELU_A * pre * (1.0 + GELU_B * square))
    half = 0.5 * (1.0 + bend)
    slope = half + 0.5 * pre * (1.0 - bend * bend) * (GELU_A * (1.0 + 3.0 * GELU_B * square))
    return pre * half, slope


EXTRA = 16


def shaped(shape, kind):
    return jax.ShapeDtypeStruct(shape, kind)


def token(value):
    corner = tuple(slice(0, 1) for _ in value.shape[:-2]) + (slice(0, 8), slice(0, LANES))
    return value[corner].reshape(8, LANES)


def kernel_call(
    body, outs, *args, name, smem=(), away=(), scratch=(), vmem=8, flops=0, after=()
):
    count = len(args)
    if after:
        inner = body
        body = lambda *refs: inner(*refs[:count], *refs[count + len(after) :])
    args = args + tuple(token(v) for v in after)

    def spec(i, places):
        if i in places:
            return pl.BlockSpec(memory_space=pl.ANY)
        return pl.BlockSpec(memory_space=pltpu.VMEM)

    ins = [
        pl.BlockSpec(memory_space=pltpu.SMEM) if i in smem else spec(i, away)
        for i in range(len(args))
    ]
    moved = sum(v.size * v.dtype.itemsize for v in args + tuple(outs))
    return pl.pallas_call(
        body,
        in_specs=ins,
        out_specs=[spec(i, ()) for i in range(len(outs))],
        out_shape=list(outs),
        scratch_shapes=list(scratch),
        compiler_params=pltpu.CompilerParams(vmem_limit_bytes=vmem * 2**20),
        cost_estimate=pl.CostEstimate(flops=flops, bytes_accessed=moved if flops else 0, transcendentals=0),
        name=name,
    )(*args)


def iota(shape, dim):
    return lax.broadcasted_iota(jnp.int32, shape, dim)


class Layout:
    def __init__(self, nb, nt, rows, width, ff, length):
        self.nb, self.nt, self.rows, self.width, self.ff, self.length = nb, nt, rows, width, ff, length
        self.devices = nb * nt
        self.size = nb // 2
        self.planes = nt // 2
        self.members = 2 * self.size
        self.each = width // self.devices
        self.piece = ff // self.devices
        self.share = width // self.members
        self.ff_share = ff // self.members
        self.small = 8 * self.each + self.piece
        self.valid_at = -(-self.small // 512) * 512
        self.head = width // HEADS


def each_way(flag, write):
    pl.when(flag == 0)(lambda: write(0))
    pl.when(flag == 1)(lambda: write(1))


def write_half(lay, side, count, in_from, up_from, in_start, up_start, give, keep, n):
    hw, pc = lay.share, lay.piece
    tail = lay.planes * pc if count > 0 else pc
    spans = []
    if count == 0:
        for q in range(3 * lay.size):
            spans.append((in_from, in_start + 2 * q * hw, hw))
        for q in range(2 * lay.size * lay.planes):
            spans.append((up_from, up_start + 2 * q * pc, pc))
    else:
        for q in range(3 * count // 2):
            spans.append((in_from, in_start + 2 * q * hw, hw))
        for q in range(count):
            spans.append((up_from, up_start + 2 * q * tail, tail))
    at = 0
    for source, start, span in spans:
        mine = source[0:n, start + side * span : start + (side + 1) * span]
        other = source[0:n, start + (1 - side) * span : start + (2 - side) * span]
        keep[0:n, at : at + span] = mine
        give[0:n, at : at + span] = other
        at += span


def load_all(pairs, sems):
    copies = [pltpu.make_async_copy(a, b, sems.at[i]) for i, (a, b) in enumerate(pairs)]
    for copy in copies:
        copy.start()
    return copies


def wait_all(copies):
    for copy in copies:
        copy.wait()


def pack_kernel(lay, spot, lengths, *refs):
    sources, (give, keep), targets, sems = refs[:12], refs[12:14], refs[14:26], refs[26]
    wait_all(load_all(list(zip(sources, targets, strict=True)), sems))
    w_in, w_up, mask = targets[:3]
    smalls = targets[3:]
    n = lay.each
    base = max(n, 16)
    if base > n:
        for ref in (give, keep):
            ref[0:base, :] = jnp.zeros((base, ref.shape[1]), BF16)
    each_way(spot[2], lambda side: write_half(lay, side, 0, w_in, w_up, 0, 0, give, keep, n))
    line = jnp.zeros((1, lay.small), F32)
    at = 0
    for ref in smalls:
        span = ref.shape[1]
        where = iota((span, lay.small), 1) == iota((span, lay.small), 0) + at
        line = line + dot(ref[...], where.astype(F32).astype(BF16))
        at += span
    row = iota((EXTRA, lay.small), 0) == spot[5]
    extra = jnp.where(row, line, 0.0).astype(BF16)
    live = (mask[...] > 0) & (iota(mask.shape, 1) < lengths[0])
    valid = jnp.where(live, 1.0, 0.0) * jnp.ones((EXTRA, 1), F32)
    for ref in (give, keep):
        ref[base : base + EXTRA, :] = jnp.zeros((EXTRA, ref.shape[1]), BF16)
        ref[base : base + EXTRA, 0 : lay.small] = extra
        ref[base : base + EXTRA, lay.valid_at : lay.valid_at + lay.length] = valid.astype(BF16)


def merge_rows(keep, came, side, n, out):
    if n < 16:
        mine, theirs = keep[0:16, :].astype(F32)[0:n], came[0:16, :].astype(F32)[0:n]
        first = jnp.where(side == 0, mine, theirs)
        second = jnp.where(side == 0, theirs, mine)
        out[...] = jnp.concatenate([first, second], axis=0).astype(BF16)
        return
    out[pl.ds(pl.multiple_of(side * n, n), n), :] = keep[0:n, :]
    out[pl.ds(pl.multiple_of((1 - side) * n, n), n), :] = came[0:n, :]


def merge_extra(lay, keep, came, n):
    n = max(n, 16)
    total = keep[n : n + EXTRA, 0 : lay.small].astype(F32) + came[n : n + EXTRA, 0 : lay.small].astype(F32)
    return total.astype(BF16)


def trade_kernel(lay, step, count, spot, keep, came, give, hold, valid, both):
    n = (1 << step) * lay.each
    merge_rows(keep, came, spot[2] if step == 0 else (spot[4] >> (step - 1)) & 1, n, both)
    start = 3 * count * lay.share
    each_way(
        (spot[4] >> step) & 1,
        lambda side: write_half(lay, side, count, both, both, 0, start, give, hold, 2 * n),
    )
    extra = merge_extra(lay, keep, came, n)
    for ref in (give, hold):
        ref[2 * n : 2 * n + EXTRA, :] = jnp.zeros((EXTRA, ref.shape[1]), BF16)
        ref[2 * n : 2 * n + EXTRA, 0 : lay.small] = extra
    if step == 0:
        place = slice(lay.valid_at, lay.valid_at + lay.length)
        base = max(n, 16)
        mine, theirs = (ref[base : base + 16, place].astype(F32)[0:8] for ref in (keep, came))
        valid[...] = jnp.where(spot[6] == 1, mine, theirs)
    else:
        valid[...] = jnp.zeros_like(valid)


def settle_kernel(lay, step, spot, keep, came, far, in_block, up_block, far_out, both):
    far_out[...] = far[...]
    n = (1 << step) * lay.each
    merge_rows(keep, came, (spot[4] >> (step - 1)) & 1, n, both)
    cut = 3 * lay.share
    in_block[0 : 2 * n, :] = both[:, 0:cut]
    up_block[...] = both[:, cut:]
    in_block[2 * n : 2 * n + EXTRA, :] = jnp.zeros((EXTRA, cut), BF16)
    in_block[2 * n : 2 * n + EXTRA, 0 : lay.small] = merge_extra(lay, keep, came, n)


def split_kernel(cut, mine, came, up, down, own, left, right, up_out, down_out, own_out):
    left[0], left[1] = mine[:, 0:cut], came[:, 0:cut]
    right[0], right[1] = mine[:, cut:], came[:, cut:]
    own_out[...] = own[...]
    if up_out.shape[0] == 2:
        up_out[0], up_out[1] = up[...], down[...]
    else:
        up_out[0] = up[...]
    down_out[...] = jnp.zeros_like(down_out) if up_out.shape[0] == 2 else down[...]


def stack_kernel(one, one_came, two, two_came, one_out, two_out):
    n = one.shape[0]
    one_out[0:n], one_out[n : 2 * n] = one[...], one_came[...]
    two_out[0:n], two_out[n : 2 * n] = two[...], two_came[...]


def stack(one, one_came, two, two_came, *after):
    outs = [shaped((2 * v.shape[0],) + v.shape[1:], BF16) for v in (one, two)]
    return kernel_call(
        stack_kernel, outs, one, one_came, two, two_came, name="stack", after=after
    )


def unpair_kernel(pair, came, ups, downs):
    ups[0], ups[1] = pair[0], came[0]
    downs[0], downs[1] = pair[1], came[1]


def block_spot(lay, spot, k, flipped):
    bits = bits_of(lay.planes)
    top = (spot[3] ^ k) & 1
    order = range(bits - 1, -1, -1) if flipped else range(bits)
    plane = spot[1] >> 1
    for position, b in enumerate(order):
        plane = plane ^ (((k >> (position + 1)) & 1) << b)
    return top, plane


def vector_kernel(lay, spot, first, second, out, rows, sems):
    n, count, wide = lay.members * lay.each, 2 * lay.planes, rows.shape[1]
    copies = []
    for k in range(count):
        source = first if k < count // 2 else second
        copy = pltpu.make_async_copy(
            source.at[k % (count // 2), n : n + EXTRA, 0:wide],
            rows.at[k * EXTRA : (k + 1) * EXTRA, :],
            sems.at[k],
        )
        copy.start()
        copies.append(copy)
    for copy in copies:
        copy.wait()
    out[...] = jnp.zeros_like(out)
    tall = count * EXTRA
    line, lane = iota((tall, lay.width), 0), iota((tall, lay.width), 1)
    holder, block = jnp.zeros_like(line), jnp.zeros_like(line)
    for k in range(count):
        top, plane = block_spot(lay, spot, k, False)
        inside = line - k * EXTRA
        here = (inside >= 0) & (inside < EXTRA)
        lead = (top * lay.size + inside // 2) * lay.nt + plane * 2 + inside % 2
        holder = jnp.where(here, jnp.where(inside < lay.members, lead, -1), holder)
        block = jnp.where(here & (inside == spot[5]), top * lay.planes + plane, jnp.where(here, -1, block))
    values = rows[...]
    source, target = iota((wide, lay.width), 0), iota((wide, lay.width), 1)
    for v in range(8):
        spread = (source == v * lay.each + target % lay.each).astype(F32).astype(BF16)
        tiled = jnp.where(lane // lay.each == holder, dot(values, spread), 0.0)
        out[v : v + 1, :] = jnp.sum(tiled, axis=0, keepdims=True)
    spread = (source == 8 * lay.each + target % lay.piece).astype(F32).astype(BF16)
    tiled = jnp.where(lane // lay.piece == block, dot(values, spread), 0.0)
    out[8:9, :] = jnp.sum(tiled, axis=0, keepdims=True)
    hw = lay.share
    mine = pl.ds(pl.multiple_of(spot[5] * hw, hw), hw)
    out[9:10, 0:hw] = out[2:3, mine]
    out[9:10, 2 * hw : 3 * hw] = out[3:4, mine]


def attend_kernel(lay, spot, bias, vecs, *refs):
    g, rows, hw, length, head = lay.size, lay.rows, lay.share, lay.length, lay.head
    near, far, near_c, far_c = (refs[i * g : (i + 1) * g] for i in range(4))
    weights = refs[4 * g : 4 * g + 4]
    near_att, far_att, joint, wide, lse, normed, x, w, x_sems, w_sems = refs[4 * g + 4 :]
    group, place = spot[3], spot[4]
    pending = []
    for e in range(g):
        for side, (at_home, at_away) in enumerate(((near[e], near_c[e]), (far_c[e], far[e]))):
            spot_here = (place if side == 0 else g - 1 - place) ^ e
            spot_here = (group if side == 0 else 1 - group) * g + spot_here
            target = x.at[pl.ds(pl.multiple_of(spot_here * rows, rows), rows), :]
            sem = x_sems.at[side * g + e]
            home = pltpu.make_async_copy(at_home, target, sem)
            visit = pltpu.make_async_copy(at_away, target, sem)
            pl.when(spot[6] == 1)(home.start)
            pl.when(spot[6] == 0)(visit.start)
            pending.append(home)
    count = 2 * lay.planes
    span = 2 * lay.each
    cut = weights[0].shape[-1]
    loads = []
    for k in range(count):
        for side in range(2):
            source = weights[2 * side + (k >= count // 2)]
            top, plane = block_spot(lay, spot, k, side == 1)
            for q in range(g):
                start = ((top * g + q) * lay.planes + plane) * span
                copy = pltpu.make_async_copy(
                    source.at[k % (count // 2), q * span : (q + 1) * span, :],
                    w.at[pl.ds(pl.multiple_of(start, span), span), 0:cut]
                    if side == 0
                    else w.at[pl.ds(pl.multiple_of(start, span), span), cut:],
                    w_sems.at[(k * 2 + side) * g + q],
                )
                copy.start()
                loads.append(copy)
    for copy in pending:
        copy.wait()
    for j in range(length // rows):
        here = slice(j * rows, (j + 1) * rows)
        normal, _ = centre(x[here, :].astype(F32))
        normed[here, :] = (normal * vecs[0:1, :] + vecs[1:2, :]).astype(BF16)
    for copy in loads:
        copy.wait()
    for j in range(length // rows):
        here = slice(j * rows, (j + 1) * rows)
        joint[here, :] = (dot(normed[here, :], w[...]) + vecs[9:10, 0 : 3 * hw]).astype(BF16)
    earlier, same = key_mask_terms(rows)
    lane = iota((rows, LANES), 1)
    for p in range(hw // LANES):
        q_at, k_at, v_at = (slice(i * hw + p * LANES, i * hw + (p + 1) * LANES) for i in range(3))
        value_t = joint[:, v_at].astype(F32).T.astype(BF16)
        for j in range(length // rows):
            here, past = slice(j * rows, (j + 1) * rows), slice(0, j * rows)
            bias_here = bias[here, :]
            for h in range(LANES // head):
                mine = (lane >= h * head) & (lane < (h + 1) * head)
                query = jnp.where(mine, joint[here, q_at].astype(F32) * SCORE_SCALE, 0.0).astype(BF16)
                inner = dot(joint[here, k_at], query, NT)
                inner = jnp.where(same, inner, jnp.where(earlier, inner + bias_here, MASKED))
                top = jnp.max(inner, axis=0, keepdims=True)
                if j:
                    outer = dot(joint[past, k_at], query, NT) + bias[past, :]
                    top = jnp.maximum(top, jnp.max(outer, axis=0, keepdims=True))
                inner = jnp.exp(inner - top)
                total = jnp.sum(inner, axis=0, keepdims=True)
                if j:
                    outer = jnp.exp(outer - top)
                    total = total + jnp.sum(outer, axis=0, keepdims=True)
                share = 1.0 / total
                value_h = value_t[h * head : (h + 1) * head]
                out = dot(value_h[:, here], (inner * share).astype(BF16))
                if j:
                    out = out + dot(value_h[:, past], (outer * share).astype(BF16))
                at = p * LANES + h * head
                wide[at : at + head, here] = out
                lse[p, h : h + 1, here] = top + jnp.log(total)
    for i in range(g):
        here = slice(i * rows, (i + 1) * rows)
        for out_ref, first in ((near_att, group * g + i), (far_att, (1 - group) * g + i)):
            part = wide[:, pl.ds(pl.multiple_of(first * rows, rows), rows)]
            out_ref[here, :] = part.T.astype(BF16)


def attend(lay, spot, bias, vecs, hidden, weights, later):
    d, hw, length, g = lay.width, lay.share, lay.length, lay.size
    outs = [
        shaped((g * lay.rows, hw), BF16),
        shaped((g * lay.rows, hw), BF16),
        shaped((length, 3 * hw), BF16),
        shaped((hw, length), F32),
        shaped((hw // LANES, 8, length), F32),
        shaped((length, d), BF16),
        shaped((length, d), BF16),
        shaped((d, 3 * hw), BF16),
    ]
    copies = 2 * lay.planes * 2 * g
    args = (spot, bias, vecs) + tuple(hidden) + tuple(weights)
    return kernel_call(
        functools.partial(attend_kernel, lay),
        outs,
        *args,
        name="attend",
        smem=(0,),
        away=tuple(range(3, len(args))),
        scratch=[
            pltpu.SemaphoreType.DMA((2 * g,)),
            pltpu.SemaphoreType.DMA((copies,)),
        ],
        vmem=60,
        flops=2 * length * d * 3 * hw + 3 * length * length * d // 2,
        after=(later,),
    )


def fold_kernel(slot, shift, a, b, spot, keep, came, hold, give):
    total = keep[...].astype(F32) + came[...].astype(F32)
    side = (spot[slot] >> shift) & 1
    view = total.reshape(a, 2, b, total.shape[-1])

    def write(s):
        hold[...] = view[:, s].reshape(a * b, -1).astype(BF16)
        give[...] = view[:, 1 - s].reshape(a * b, -1).astype(BF16)

    each_way(side, write)


def fold(spot, slot, shift, a, keep, came):
    count, columns = keep.shape
    b = count // (2 * a)
    return kernel_call(
        functools.partial(fold_kernel, slot, shift, a, b),
        [shaped((a * b, columns), BF16)] * 2,
        spot,
        keep,
        came,
        name="fold",
        smem=(0,),
    )


def mask_kernel(spot, lengths, cotangent, out):
    rows = out.shape[0]
    live = spot[0] * rows + iota((rows, 1), 0) < lengths[0]
    out[...] = jnp.where(live, cotangent[...].astype(F32), 0.0).astype(BF16)


def place_rows(lay, spot, e):
    return spot[4] ^ e


def weight_loads(lay, spot, ups, ups_came, downs, downs_came, w_up, w_down):
    pairs = []
    count, span, g = 2 * lay.planes, 2 * lay.each, lay.size
    for k in range(count):
        source = ups if k < count // 2 else ups_came
        top, plane = block_spot(lay, spot, k, False)
        for q in range(g):
            start = ((top * g + q) * lay.planes + plane) * span
            pairs.append(
                (
                    source.at[k % (count // 2), q * span : (q + 1) * span, :],
                    w_up.at[pl.ds(pl.multiple_of(start, span), span), :],
                )
            )
        source = downs if k < count // 2 else downs_came
        top, plane = block_spot(lay, spot, k, True)
        start = (top * lay.planes + plane) * lay.piece
        pairs.append(
            (
                source.at[k % (count // 2)],
                w_down.at[pl.ds(pl.multiple_of(start, lay.piece), lay.piece), :],
            )
        )
    return pairs


def row_loads(lay, spot, mine, swapped, target):
    pairs = []
    g, rows = lay.size, lay.rows
    for e in range(g):
        for source, sequence in ((mine[e], spot[2]), (swapped[e], 1 - spot[2])):
            start = (sequence * g + (spot[4] ^ e)) * rows
            pairs.append((source, target.at[pl.ds(pl.multiple_of(start, rows), rows), :]))
    return pairs


def forward_kernel(lay, spot, vecs, w_out, *refs):
    g, rows, hw, d = lay.size, lay.rows, lay.share, lay.width
    lists = [refs[i * g : (i + 1) * g] for i in range(8)]
    near, far, near_c, far_c, base_m, base_c, down_m, down_c = lists
    blocks = refs[8 * g : 8 * g + 4]
    (
        dn_keep,
        dn_give,
        middle_own,
        att_own,
        normed,
        act,
        grad_pre,
        bias_sum,
        att,
        wo,
        base,
        gd,
        w_up,
        w_down,
        sems,
    ) = refs[8 * g + 4 :]
    core, group, place = spot[2], spot[3], spot[4]
    span = g * rows
    pairs = [(w_out, wo)]
    for e in range(g):
        for source, sequence, at, side in (
            (near[e], group, place ^ e, core),
            (near_c[e], group, place ^ e, 1 - core),
            (far[e], 1 - group, (g - 1 - place) ^ e, core),
            (far_c[e], 1 - group, (g - 1 - place) ^ e, 1 - core),
        ):
            row = pl.multiple_of(sequence * span, span)
            column = pl.multiple_of((at * 2 + side) * hw, hw)
            pairs.append((source, att.at[pl.ds(row, span), pl.ds(column, hw)]))
    pairs += row_loads(lay, spot, base_m, base_c, base)
    first = len(pairs)
    pairs += weight_loads(lay, spot, *blocks, w_up, w_down)
    pairs += row_loads(lay, spot, down_m, down_c, gd)
    copies = load_all(pairs, sems)
    wait_all(copies[:first])
    bias_out, gain, shift = vecs[4:5, :], vecs[5:6, :], vecs[6:7, :]
    bias_up = vecs[8:9, 0 : lay.ff_share]
    total = jnp.zeros((1, lay.ff_share), F32)
    for i in range(2 * g):
        here = slice(i * rows, (i + 1) * rows)
        middle = base[here, :].astype(F32) + (dot(att[here, :], wo[...]) + bias_out)
        normal, _ = centre(middle)
        normed[here, :] = (normal * gain + shift).astype(BF16)

        @pl.when((core == i // g) & (place == i % g))
        def _():
            middle_own[...] = middle
            att_own[...] = att[here, :]

    wait_all(copies[first:])
    for i in range(2 * g):
        here = slice(i * rows, (i + 1) * rows)
        pre = dot(normed[here, :], w_up[...]) + bias_up
        value, slope = gelu_terms(pre)
        act[here, :] = value.astype(BF16)
        grad = (dot(gd[here, :], w_down[...], NT) * slope).astype(BF16)
        grad_pre[here, :] = grad
        total = total + jnp.sum(grad.astype(F32), axis=0, keepdims=True)
        back = dot(grad, w_up[...], NT).astype(BF16)
        at = slice((i % g) * rows, (i % g + 1) * rows)

        @pl.when(core == i // g)
        def _():
            dn_keep[at, :] = back

        @pl.when(core != i // g)
        def _():
            dn_give[at, :] = back

    bias_sum[...] = total


def forward_call(lay, spot, vecs, w_out, lists, blocks):
    d, f, rows, g = lay.width, lay.ff_share, lay.rows, lay.size
    tokens = 2 * g * rows
    outs = [
        shaped((g * rows, d), BF16),
        shaped((g * rows, d), BF16),
        shaped((rows, d), F32),
        shaped((rows, d), BF16),
        shaped((tokens, d), BF16),
        shaped((tokens, f), BF16),
        shaped((tokens, f), BF16),
        shaped((1, f), F32),
    ]
    args = (spot, vecs, w_out) + tuple(lists) + tuple(blocks)
    copies = 1 + 8 * g + 2 * lay.planes * (g + 1)
    return kernel_call(
        functools.partial(forward_kernel, lay),
        outs,
        *args,
        name="feed_forward",
        smem=(0,),
        away=tuple(range(2, len(args))),
        scratch=[
            pltpu.VMEM((tokens, d), BF16),
            pltpu.VMEM((d, d), BF16),
            pltpu.VMEM((tokens, d), BF16),
            pltpu.VMEM((tokens, d), BF16),
            pltpu.VMEM((d, f), BF16),
            pltpu.VMEM((f, d), BF16),
            pltpu.SemaphoreType.DMA((copies,)),
        ],
        vmem=60,
        flops=2 * tokens * d * (d + 3 * f),
    )


def cut_rows(value, side, a, b, keep, give):
    for i in range(a):
        for ref, s in ((keep, side), (give, 1 - side)):
            start = pl.multiple_of((2 * i + s) * b, b)
            ref[i * b : (i + 1) * b, :] = value[pl.ds(start, b), :]


def gradient_kernel(lay, spot, normed, act, grad_pre, *refs):
    g, rows, d, f = lay.size, lay.rows, lay.width, lay.ff_share
    down_m, down_c, blocks = refs[:g], refs[g : 2 * g], refs[2 * g : 2 * g + 2]
    up_keep, up_give, down_keep, down_give, out_keep, out_give, gd, w_down, full, sems = refs[
        2 * g + 2 :
    ]
    pairs = row_loads(lay, spot, down_m, down_c, gd)
    count = 2 * lay.planes
    for k in range(count):
        source = blocks[k >= count // 2]
        top, plane = block_spot(lay, spot, k, True)
        start = (top * lay.planes + plane) * lay.piece
        pairs.append(
            (
                source.at[k % (count // 2)],
                w_down.at[pl.ds(pl.multiple_of(start, lay.piece), lay.piece), :],
            )
        )
    copies = load_all(pairs, sems)
    tile = 256
    for i in range(d // tile):
        here = slice(i * tile, (i + 1) * tile)
        full[here, 0:f] = dot(normed[:, here], grad_pre[...], TN).astype(BF16)
    plane_bits = bits_of(lay.planes)
    side = (spot[1] >> plane_bits) & 1
    cut_rows(full.at[0:d, 0:f], side, 2 * g, d // (4 * g), up_keep, up_give)
    wait_all(copies)
    tile = min(256, f)
    for i in range(f // tile):
        here = slice(i * tile, (i + 1) * tile)
        full[here, 0:d] = dot(act[:, here], gd[...], TN).astype(BF16)
    side = (spot[1] >> 1) & 1
    cut_rows(full.at[0:f, 0:d], side, lay.planes, lay.piece, down_keep, down_give)
    for i in range(2 * g):
        here = slice(i * rows, (i + 1) * rows)
        at = slice((i % g) * rows, (i % g + 1) * rows)
        part = dot(act[here, :], w_down[...]).astype(BF16)

        @pl.when(spot[2] == i // g)
        def _():
            out_keep[at, :] = part

        @pl.when(spot[2] != i // g)
        def _():
            out_give[at, :] = part


def gradient_call(lay, spot, normed, act, grad_pre, down_m, down_c, blocks):
    d, f, rows, g = lay.width, lay.ff_share, lay.rows, lay.size
    tokens = 2 * g * rows
    outs = [shaped((d // 2, f), BF16)] * 2 + [shaped((f // 2, d), BF16)] * 2
    outs += [shaped((g * rows, d), BF16)] * 2
    args = (spot, normed, act, grad_pre) + tuple(down_m) + tuple(down_c) + tuple(blocks)
    return kernel_call(
        functools.partial(gradient_kernel, lay),
        outs,
        *args,
        name="gradients",
        smem=(0,),
        away=tuple(range(4, len(args))),
        scratch=[
            pltpu.VMEM((tokens, d), BF16),
            pltpu.VMEM((f, d), BF16),
            pltpu.VMEM((d, d), BF16),
            pltpu.SemaphoreType.DMA((2 * g + 2 * lay.planes,)),
        ],
        vmem=60,
        flops=2 * tokens * d * 3 * f,
    )


def turn_kernel(lay, spot, vecs, keep, came, middle, grad_low, w_out, *refs):
    pieces = refs[: lay.members]
    grad_middle, grad_branch, sums, wo, att_grad, sems = refs[lay.members :]
    copies = load_all([(w_out, wo)], sems)
    normal, scale = centre(middle[...])
    slope = keep[...].astype(F32) + came[...].astype(F32)
    total = grad_low[...].astype(F32) + norm_back(slope, normal, scale, vecs[5:6, :])
    grad_middle[...] = total
    branch = total.astype(BF16)
    grad_branch[...] = branch
    sums[...] = jnp.zeros_like(sums)
    add = lambda value: jnp.sum(value, axis=0, keepdims=True)
    sums[0:1, :] = add(branch.astype(F32))
    sums[1:2, :] = add(slope * normal)
    sums[2:3, :] = add(slope)
    sums[3:4, :] = add(grad_low[...].astype(F32))
    wait_all(copies)
    att_grad[...] = dot(branch, wo[...], NT).astype(BF16)
    for r in range(lay.members):
        start = pl.multiple_of((spot[0] ^ r) * lay.share, lay.share)
        pieces[r][...] = att_grad[:, pl.ds(start, lay.share)]


def turn_call(lay, spot, vecs, keep, came, middle, grad_low, w_out, later):
    d, rows = lay.width, lay.rows
    outs = [shaped((rows, lay.share), BF16)] * lay.members
    outs += [shaped((rows, d), F32), shaped((rows, d), BF16), shaped((8, d), F32)]
    return kernel_call(
        functools.partial(turn_kernel, lay),
        outs,
        spot,
        vecs,
        keep,
        came,
        middle,
        grad_low,
        w_out,
        name="turn",
        smem=(0,),
        away=(6,),
        scratch=[
            pltpu.VMEM((d, d), BF16),
            pltpu.VMEM((rows, d), BF16),
            pltpu.SemaphoreType.DMA((1,)),
        ],
        vmem=60,
        flops=2 * rows * d * d,
        after=(later,),
    )


def attend_back_kernel(lay, spot, bias, joint, wide, lse, normed, *refs):
    m, rows, hw, length, head, d = lay.members, lay.rows, lay.share, lay.length, lay.head, lay.width
    parts = refs[:m]
    (
        grads_out,
        left_keep,
        left_give,
        right_keep,
        right_give,
        sums,
        slope_all,
        key_sum,
        value_sum,
        query_t,
        full,
    ) = refs[m:]
    for r in range(m):
        start = pl.multiple_of((spot[5] ^ r) * rows, rows)
        slope_all[pl.ds(start, rows), :] = parts[r][...]
    earlier, same = key_mask_terms(rows)
    lane = iota((rows, LANES), 1)
    for p in range(hw // LANES):
        q_at, k_at, v_at = (slice(i * hw + p * LANES, i * hw + (p + 1) * LANES) for i in range(3))
        s_at = slice(p * LANES, (p + 1) * LANES)
        key_t = joint[:, k_at].astype(F32).T.astype(BF16)
        product = slope_all[:, s_at].astype(F32).T * wide[s_at, :]
        key_sum[...] = jnp.zeros_like(key_sum)
        value_sum[...] = jnp.zeros_like(value_sum)
        for j in range(length // rows):
            here = slice(j * rows, (j + 1) * rows)
            for h in range(LANES // head):
                mine = (lane >= h * head) & (lane < (h + 1) * head)
                query = jnp.where(mine, joint[here, q_at].astype(F32) * SCORE_SCALE, 0.0).astype(BF16)
                slope = jnp.where(mine, slope_all[here, s_at].astype(F32), 0.0).astype(BF16)
                top = lse[p, h : h + 1, here]
                delta = jnp.sum(product[h * head : (h + 1) * head, here], axis=0, keepdims=True)
                key_h = key_t[h * head : (h + 1) * head]
                back = None
                for part in (slice(0, j * rows), here) if j else (here,):
                    scores = dot(joint[part, k_at], query, NT)
                    if part is here:
                        scores = jnp.where(
                            same, scores, jnp.where(earlier, scores + bias[part, :], MASKED)
                        )
                    else:
                        scores = scores + bias[part, :]
                    chances = jnp.exp(scores - top)
                    slopes = dot(joint[part, v_at], slope, NT)
                    grads = (chances * (slopes - delta)).astype(BF16)
                    value_sum[part, :] += dot(chances.astype(BF16), slope)
                    key_sum[part, :] += dot(grads, query)
                    term = dot(key_h[:, part], grads)
                    back = term if back is None else back + term
                query_t[h * head : (h + 1) * head, here] = back * SCORE_SCALE
        grads_out[:, q_at] = query_t[...].T.astype(BF16)
        grads_out[:, k_at] = key_sum[...].astype(BF16)
        grads_out[:, v_at] = value_sum[...].astype(BF16)
    sums[...] = jnp.sum(grads_out[...].astype(F32), axis=0, keepdims=True)
    tile = 256
    for i in range(d // tile):
        here = slice(i * tile, (i + 1) * tile)
        full[here, :] = dot(normed[:, here], grads_out[...], TN).astype(BF16)
    cut = left_keep.shape[1]
    g = lay.size
    side = (spot[1] >> bits_of(lay.planes)) & 1
    cut_rows(full.at[:, 0:cut], side, 2 * g, d // (4 * g), left_keep, left_give)
    side = (spot[1] >> 1) & 1
    cut_rows(full.at[:, cut:], side, g * lay.planes, 2 * lay.each, right_keep, right_give)


def attend_back(lay, spot, bias, joint, wide, lse, normed, parts, cut):
    d, hw, length = lay.width, lay.share, lay.length
    outs = [shaped((length, 3 * hw), BF16)]
    outs += [shaped((d // 2, cut), BF16)] * 2 + [shaped((d // 2, 3 * hw - cut), BF16)] * 2
    outs += [shaped((1, 3 * hw), F32)]
    return kernel_call(
        functools.partial(attend_back_kernel, lay),
        outs,
        spot,
        bias,
        joint,
        wide,
        lse,
        normed,
        *parts,
        name="attend_back",
        smem=(0,),
        scratch=[
            pltpu.VMEM((length, hw), BF16),
            pltpu.VMEM((length, LANES), F32),
            pltpu.VMEM((length, LANES), F32),
            pltpu.VMEM((LANES, length), F32),
            pltpu.VMEM((d, 3 * hw), BF16),
        ],
        vmem=60,
        flops=2 * length * d * 3 * hw + 4 * length * length * d,
    )


def input_kernel(
    lay, spot, grads, w, x, sums_two, joint_sum, bias_up_sum, keep, give, sums, sums_low, vectors
):
    rows, g, hw = lay.rows, lay.size, lay.share
    gain = jnp.zeros((1, lay.width), F32)
    shift = jnp.zeros((1, lay.width), F32)
    for i in range(2 * g):
        here = slice(i * rows, (i + 1) * rows)
        part = dot(grads[here, :], w[...], NT)
        normal, _ = centre(x[here, :].astype(F32))
        gain = gain + jnp.sum(part * normal, axis=0, keepdims=True)
        shift = shift + jnp.sum(part, axis=0, keepdims=True)
        low = part.astype(BF16)
        at = slice((i % g) * rows, (i % g + 1) * rows)

        @pl.when(spot[8] == i // g)
        def _():
            keep[at, :] = low

        @pl.when(spot[8] != i // g)
        def _():
            give[at, :] = low

    vectors[...] = jnp.zeros_like(vectors)
    vectors[0:1, :] = gain
    vectors[1:2, :] = shift
    mine = pl.ds(pl.multiple_of(spot[5] * hw, hw), hw)
    vectors[2:3, mine] = joint_sum[:, 0:hw]
    vectors[3:4, mine] = joint_sum[:, 2 * hw :]
    vectors[4:8, :] = sums_two[0:4, :]
    each, piece, small = lay.each, lay.piece, lay.small
    device, lane = iota((lay.devices, lay.width), 0), iota((lay.devices, lay.width), 1)
    total = jnp.zeros((lay.devices, small), F32)
    source, target = iota((lay.width, small), 0), iota((lay.width, small), 1)
    for v in range(8):
        value = jnp.where(lane // each == device, vectors[v : v + 1, :], 0.0)
        move = (target == v * each + source % each).astype(F32)
        total = total + jnp.dot(value, move, precision=lax.Precision.HIGHEST)
    shape = (lay.devices, lay.ff_share)
    device, lane = iota(shape, 0), iota(shape, 1)
    plane, chip = device % lay.nt // 2, device // lay.nt
    block = chip // lay.size * lay.planes + plane
    here = (lane // piece == block) & (chip % lay.size == spot[4]) & (device % 2 == spot[2])
    source, target = iota((lay.ff_share, small), 0), iota((lay.ff_share, small), 1)
    move = (target == 8 * each + source % piece).astype(F32)
    value = jnp.where(here, bias_up_sum[...], 0.0)
    total = total + jnp.dot(value, move, precision=lax.Precision.HIGHEST)
    sums[...] = total
    sums_low[...] = total.astype(BF16)


def input_call(lay, spot, grads, w, x, sums_two, joint_sum, bias_up_sum):
    d, rows, g = lay.width, lay.rows, lay.size
    small = (lay.devices, lay.small)
    return kernel_call(
        functools.partial(input_kernel, lay),
        [shaped((g * rows, d), BF16)] * 2 + [shaped(small, F32), shaped(small, BF16)],
        spot,
        grads,
        w,
        x,
        sums_two,
        joint_sum,
        bias_up_sum,
        name="input_slope",
        smem=(0,),
        scratch=[pltpu.VMEM((8, d), F32)],
        vmem=60,
        flops=2 * lay.length * d * 3 * lay.share,
    )


def fold_into(spot, cut, keep, came, hold, give, rows=None):
    slot, shift, a = cut
    count = keep.shape[0]
    b = count // (2 * a)
    side = (spot[slot] >> shift) & 1
    half = a * b

    def write(s):
        for i in range(a):
            for ref, t in ((hold, s), (give, 1 - s)):
                at = slice((2 * i + t) * b, (2 * i + t + 1) * b)
                value = keep[at, :].astype(F32) + came[at, :].astype(F32)
                ref[i * b : (i + 1) * b, :] = value.astype(BF16)

    each_way(side, write)


def two_fold_kernel(cuts, spot, one, one_came, two, two_came, one_keep, one_give, two_keep, two_give):
    fold_into(spot, cuts[0], one, one_came, one_keep, one_give)
    fold_into(spot, cuts[1], two, two_came, two_keep, two_give)


def two_fold(spot, cuts, one, one_came, two, two_came):
    outs = []
    for v in (one, two):
        outs += [shaped((v.shape[0] // 2, v.shape[1]), BF16)] * 2
    return kernel_call(
        functools.partial(two_fold_kernel, cuts),
        outs,
        spot,
        one,
        one_came,
        two,
        two_came,
        name="two_fold",
        smem=(0,),
    )


def sums_fold_kernel(
    cuts, spot, one, one_came, two, two_came, sums, sums_came, one_keep, one_give, two_keep, two_give, sums_out
):
    n, half = one.shape[0], one_keep.shape[0]
    tall, small = sums.shape
    came = one_came[n : n + tall, 0:small] if one_came.shape[0] > n else sums_came[...]
    total = sums[...] + came.astype(F32)
    sums_out[...] = total
    fold_into(spot, cuts[0], one, one_came, one_keep, one_give)
    one_give[half : half + tall, :] = jnp.zeros((tall, one_give.shape[1]), BF16)
    one_give[half : half + tall, 0:small] = total.astype(BF16)
    fold_into(spot, cuts[1], two, two_came, two_keep, two_give)


def sums_fold(spot, cuts, one, one_came, two, two_came, sums, sums_came):
    half, other = one.shape[0] // 2, two.shape[0] // 2
    outs = [
        shaped((half, one.shape[1]), BF16),
        shaped((half + sums.shape[0], one.shape[1]), BF16),
        shaped((other, two.shape[1]), BF16),
        shaped((other, two.shape[1]), BF16),
        shaped(sums.shape, F32),
    ]
    args = (spot, one, one_came, two, two_came, sums, sums_came)
    return kernel_call(
        functools.partial(sums_fold_kernel, cuts), outs, *args, name="sums_fold", smem=(0,)
    )


def top_fold_kernel(shift, spot, one, one_came, two, two_came, sums, keep, give, sums_out):
    n, cut = one.shape
    half = n // 2
    tall, small = sums.shape
    total = sums[...] + one_came[n : n + tall, 0:small].astype(F32)
    sums_out[...] = total
    give[half : half + tall, :] = jnp.zeros((tall, give.shape[1]), BF16)
    give[half : half + tall, 0:small] = total.astype(BF16)

    def write(s):
        for here, x, y in ((slice(0, cut), one, one_came), (slice(cut, None), two, two_came)):
            for ref, t in ((keep, s), (give, 1 - s)):
                at = slice(t * half, (t + 1) * half)
                value = x[at, :].astype(F32) + y[at, :].astype(F32)
                ref[0:half, here] = value.astype(BF16)

    each_way((spot[0] >> shift) & 1, write)


def top_pair_kernel(shift, spot, one, one_came, two, two_came, one_keep, two_keep, give):
    half = one_keep.shape[0]

    def write(s):
        for i, (x, y, keep) in enumerate(((one, one_came, one_keep), (two, two_came, two_keep))):
            for ref, t in ((keep, s), (give.at[i], 1 - s)):
                at = slice(t * half, (t + 1) * half)
                ref[...] = (x[at, :].astype(F32) + y[at, :].astype(F32)).astype(BF16)

    each_way((spot[0] >> shift) & 1, write)


def home_first_kernel(slot, shift, spot, w_in, w_in_came, w_up, w_up_came, sums, keep, give, sums_out):
    n, cut = w_in.shape
    half = n // 2
    tall, small = sums.shape
    total = sums[...] + w_in_came[n : n + tall, 0:small].astype(F32)
    sums_out[...] = total
    give[half : half + tall, :] = jnp.zeros((tall, give.shape[1]), BF16)
    give[half : half + tall, 0:small] = total.astype(BF16)

    def write(s):
        for here, x, y in ((slice(0, cut), w_in, w_in_came), (slice(cut, None), w_up, w_up_came)):
            for ref, t in ((keep, s), (give, 1 - s)):
                at = slice(t * half, (t + 1) * half)
                value = x[at, :].astype(F32) + y[at, :].astype(F32)
                ref[0:half, here] = value.astype(BF16)

    each_way((spot[slot] >> shift) & 1, write)


def home_next_kernel(slot, shift, spot, mine, came, sums, keep, give, sums_out):
    n, columns = mine.shape
    half = n // 2
    tall, small = sums.shape
    total = sums[...] + came[n : n + tall, 0:small].astype(F32)
    sums_out[...] = total
    base = give.shape[0] - tall
    give[base : base + tall, :] = jnp.zeros((tall, give.shape[1]), BF16)
    give[base : base + tall, 0:small] = total.astype(BF16)

    def write(s):
        for here, x in ((slice(0, columns), mine), (slice(columns, None), came)):
            for ref, t in ((keep, s), (give, 1 - s)):
                ref[0:half, here] = x[t * half : (t + 1) * half, :]

    each_way((spot[slot] >> shift) & 1, write)


def home_last_kernel(lay, spot, mine, came, sums, w_in, w_up, *vectors):
    n = lay.each
    tall = lay.devices
    base = came.shape[0] - tall
    hw, piece, cut = lay.share, lay.piece, 3 * lay.share
    span = cut + lay.ff_share
    for f, ref in enumerate((mine, came)):
        for e in range(lay.size):
            place = 0
            for k in range(bits_of(lay.size)):
                place |= ((e >> k) & 1) << (bits_of(lay.size) - 1 - k)
            member = (spot[4] ^ place) * 2 + (spot[2] ^ f)

            def write(m, ref=ref, e=e):
                for i in range(3):
                    at = i * lay.width + m * hw
                    start = e * span + i * hw
                    w_in[:, at : at + hw] = ref[0:n, start : start + hw].astype(F32)
                for b in range(2 * lay.planes):
                    top, plane = b // lay.planes, b % lay.planes
                    at = (((top * lay.size + m // 2) * lay.planes + plane) * 2 + m % 2) * piece
                    start = e * span + cut + b * piece
                    w_up[:, at : at + piece] = ref[0:n, start : start + piece].astype(F32)

            for m in range(lay.members):
                pl.when(member == m)(functools.partial(write, m))
    total = sums[...] + came[base : base + tall, 0 : lay.small].astype(F32)
    own = jnp.where(iota(total.shape, 0) == spot[7], total, 0.0)
    own = jnp.sum(own, axis=0, keepdims=True)
    at = 0
    for ref in vectors:
        ref[...] = own[:, at : at + ref.shape[1]]
        at += ref.shape[1]


def add_kernel(one, two, out):
    out[...] = (one[...].astype(F32) + two[...].astype(F32)).astype(out.dtype)


def last_kernel(spot, vecs, keep, came, sent, own, grad_middle, out):
    total = keep[...].astype(F32) + came[...].astype(F32)
    slope = jnp.where(spot[6] == 1, total, sent[...].astype(F32))
    normal, scale = centre(own[...].astype(F32))
    out[...] = (grad_middle[...] + norm_back(slope, normal, scale, vecs[0:1, :])).astype(BF16)


def out_kernel(vecs, middle, keep, came, out):
    total = keep[...].astype(F32) + came[...].astype(F32)
    out[...] = (middle[...] + (total + vecs[7:8, :])).astype(BF16)


def solution(mesh):
    nb, nt = mesh.shape["blk"], mesh.shape["batch"]
    devices = nb * nt
    group_size = nb // 2
    total_bits = bits_of(devices)
    plane_bits = list(range(1, bits_of(nt)))
    group_bits = list(range(bits_of(nt), bits_of(nt) + bits_of(group_size)))
    top_bit = total_bits - 1
    members = 2 * group_size

    def at_home(i):
        return (i // nt) // group_size == i % 2

    def send(value, route):
        return lax.ppermute(value, AXES, route)

    def flip(value, bit, who=None):
        return send(value, [(i, i ^ (1 << bit)) for i in range(devices) if who is None or who(i)])

    def mirror(i):
        return (nb - 1 - i // nt) * nt + i % nt

    def local(
        hidden_in,
        key_mask,
        lengths,
        first_gain,
        first_shift,
        input_weight,
        query_bias,
        value_bias,
        output_weight,
        output_bias,
        second_gain,
        second_shift,
        up_weight,
        up_bias,
        down_weight,
        down_bias,
        cotangent,
    ):
        rows, width = hidden_in.shape[1:]
        length = key_mask.shape[1]
        head = width // HEADS
        blk, lane_id = lax.axis_index("blk"), lax.axis_index("batch")
        index = blk * nt + lane_id
        core = lane_id % 2
        group, place = blk // group_size, blk % group_size
        member = place * 2 + core
        home = group == core
        share = width // members
        ff = up_weight.shape[1]
        piece = ff // devices

        def bit(b):
            return (index >> b) & 1

        def ordered(mine, theirs, side, axis):
            return jnp.where(
                side == 0,
                jnp.concatenate([mine, theirs], axis),
                jnp.concatenate([theirs, mine], axis),
            )

        def side_of(value, side, axis):
            lo, hi = jnp.split(value, 2, axis)
            return jnp.where(side == 0, lo, hi)

        lay = Layout(nb, nt, rows, width, ff, length)
        each = lay.each
        own = hidden_in[0]
        kept_group = jnp.where(home, group, 1 - group)
        kept_place = jnp.where(home, place, group_size - 1 - place)
        spot = jnp.stack(
            [blk, lane_id, core, group, place, member, home.astype(jnp.int32), index]
            + [kept_group, kept_place]
        )
        away = lambda i: not at_home(i)
        from_away = [(i, i ^ 1) for i in range(devices) if away(i)]
        across = [(i, mirror(i) ^ 1) for i in range(devices) if away(i)]
        mirrored = [(i, mirror(i)) for i in range(devices)]

        wide_in = 3 * group_size * share + 2 * group_size * lay.planes * piece
        row = lambda value: value.reshape(1, -1)
        vectors = [
            row(v)
            for v in (
                first_gain,
                first_shift,
                query_bias,
                value_bias,
                output_bias,
                second_gain,
                second_shift,
                down_bias,
                up_bias,
            )
        ]
        start = [input_weight, up_weight, key_mask] + vectors
        base = max(each, 16)
        give, keep = kernel_call(
            functools.partial(pack_kernel, lay),
            [shaped((base + EXTRA, wide_in), BF16)] * 2,
            spot,
            lengths,
            *start,
            name="pack",
            smem=(0, 1),
            away=tuple(range(2, 14)),
            vmem=60,
            scratch=[pltpu.VMEM(v.shape, v.dtype) for v in start] + [pltpu.SemaphoreType.DMA((12,))],
        )
        came_w = flip(give, 0)
        far = [send(own, across)]
        count = group_size
        for step, b in enumerate(group_bits):
            tall = (2 << step) * each
            columns = wide_in >> (step + 1)
            give, keep, ready = kernel_call(
                functools.partial(trade_kernel, lay, step, count),
                [shaped((tall + EXTRA, columns), BF16)] * 2 + [shaped((8, length), F32)],
                spot,
                keep,
                came_w,
                name="trade",
                smem=(0,),
                scratch=[pltpu.VMEM((tall, 2 * columns), BF16)],
            )
            valid = ready if step == 0 else valid
            came_w = flip(give, b)
            count //= 2
        tall = members * each
        in_block, up_block, far_later = kernel_call(
            functools.partial(settle_kernel, lay, len(group_bits)),
            [
                shaped((tall + EXTRA, 3 * share), BF16),
                shaped((tall, ff // members), BF16),
                shaped(own.shape, BF16),
            ],
            spot,
            keep,
            came_w,
            far[0],
            name="settle",
            smem=(0,),
            scratch=[pltpu.VMEM((tall, 3 * share + ff // members), BF16)],
        )
        cut = max(LANES, 3 * share // 2 // LANES * LANES)
        paired = up_block.shape == down_weight.shape

        def spread_group(values, who=None):
            for b in group_bits:
                values = values + [flip(v, b, who) for v in values]
            return values

        left, right, up_block, down_block, own_later = kernel_call(
            functools.partial(split_kernel, cut),
            [
                shaped((2, tall + EXTRA, cut), BF16),
                shaped((2, tall + EXTRA, 3 * share - cut), BF16),
                shaped((2 if paired else 1,) + up_block.shape, BF16),
                shaped((8, LANES) if paired else down_weight.shape, BF16),
                shaped(own.shape, BF16),
            ],
            in_block,
            flip(in_block, top_bit),
            up_block,
            down_weight,
            own,
            name="split",
        )
        far = far + spread_group([far_later], away)[1:]
        far_c = [send(v, from_away) for v in far]
        for k, (b, c) in enumerate(zip(plane_bits, reversed(plane_bits), strict=True)):
            left_came, right_came = flip(left, b), flip(right, c)
            if k + 1 < len(plane_bits):
                left, right = stack(left, left_came, right, right_came, *far[1:2])
        in_pieces = (left, left_came, right, right_came)
        vecs = kernel_call(
            functools.partial(vector_kernel, lay),
            [shaped((16, width), F32)],
            spot,
            left,
            left_came,
            name="vectors",
            smem=(0,),
            away=(1, 2),
            scratch=[
                pltpu.VMEM((2 * lay.planes * EXTRA, -(-lay.small // LANES) * LANES), BF16),
                pltpu.SemaphoreType.DMA((2 * lay.planes,)),
            ],
        )[0]

        near = [own] + spread_group([own_later])[1:]
        near_c = [flip(v, 0) for v in near]

        if paired:
            ups, downs = kernel_call(
                unpair_kernel,
                [shaped((2,) + v.shape, BF16) for v in up_block[:2]],
                up_block,
                flip(up_block, top_bit),
                name="unpair",
                after=(left, right),
            )
        else:
            ups, downs = up_block, down_block[None]
            ups, downs = stack(
                ups, flip(ups, top_bit), downs, flip(downs, top_bit), left, right
            )
        ups_first = ups
        for k, (b, c) in enumerate(zip(plane_bits, reversed(plane_bits), strict=True)):
            ups_came, downs_came = flip(ups, b), flip(downs, c)
            if k + 1 < len(plane_bits):
                ups, downs = stack(ups, ups_came, downs, downs_came)
        w_out = lax.all_gather(output_weight, AXES, axis=0, tiled=True)

        grad_low = kernel_call(
            mask_kernel,
            [shaped((rows, width), BF16)],
            spot,
            lengths,
            cotangent[0],
            name="mask",
            smem=(0, 1),
            after=(near[1],),
        )[0]
        down_m = spread_group([grad_low])
        down_c = [flip(v, 0) for v in down_m]

        key_bias = jnp.where(valid[0] > 0.5, 0.0, MASKED).astype(F32).reshape(length, 1)
        near_att, far_att, joint, wide, lse, normed_one, x_all, w_in = attend(
            lay, spot, key_bias, vecs, near + far + near_c + far_c, in_pieces, ups_first
        )
        far_att = spread_group([send(far_att, mirrored)])
        near_att = spread_group([near_att])
        att_c = [flip(v, 0) for v in near_att + far_att]

        (
            dn_keep,
            dn_give,
            middle,
            att_own,
            normed_two,
            act,
            grad_pre,
            d_bias_up,
        ) = forward_call(
            lay,
            spot,
            vecs,
            w_out,
            near_att + far_att + att_c + near + near_c + down_m + down_c,
            (ups, ups_came, downs, downs_came),
        )

        def reduce_group(keep, give, slot):
            came = flip(give, 0)
            for k in reversed(range(len(group_bits))):
                keep, give = fold(spot, slot, k, 1, keep, came)
                came = flip(give, group_bits[k])
            return keep, came

        dn_keep, dn_came = reduce_group(dn_keep, dn_give, 4)
        up_keep, up_give, down_keep, down_give, out_keep, out_give = gradient_call(
            lay, spot, normed_two, act, grad_pre, down_m, down_c, (downs, downs_came)
        )
        *slopes, grad_middle, grad_branch, sums_two = turn_call(
            lay, spot, vecs, dn_keep, dn_came, middle, grad_low, w_out, up_give
        )

        parts = []
        for r in range(members):

            def route(i):
                m = (i // nt) ^ r
                return ((i % 2) * group_size + m // 2) * nt + (i % nt) - i % 2 + m % 2

            parts.append(send(slopes[r], [(i, route(i)) for i in range(devices)]))
        grad_joint, left_keep, left_give, right_keep, right_give, joint_sum = attend_back(
            lay, spot, key_bias, joint, wide, lse, normed_one, parts, cut
        )
        in_keep, in_give, sums, sums_give = input_call(
            lay, spot, grad_joint, w_in, x_all, sums_two, joint_sum, d_bias_up
        )
        in_keep, in_came = reduce_group(in_keep, in_give, 9)
        in_sum = kernel_call(
            add_kernel, [shaped((rows, width), BF16)], in_keep, in_came, name="add"
        )[0]
        input_gradient = kernel_call(
            last_kernel,
            [shaped((rows, width), BF16)],
            spot,
            vecs,
            in_keep,
            in_came,
            send(in_sum, across),
            own,
            grad_middle,
            name="input_gradient",
            smem=(0,),
        )[0]

        planes_down = list(reversed(plane_bits))
        top_shift = bits_of(group_size)

        def cuts_of(lead, order):
            here, cuts = list(planes_down), []
            for b in order:
                cuts.append((1, b, lead << here.index(b)))
                here.remove(b)
            return cuts

        up_cuts, down_cuts = cuts_of(members, planes_down), cuts_of(2, plane_bits)
        for k, (b, c) in enumerate(zip(planes_down, plane_bits, strict=True)):
            up_came, down_came = flip(up_give, b), flip(down_give, c)
            if k + 1 < len(plane_bits):
                up_keep, up_give, down_keep, down_give = two_fold(
                    spot,
                    (up_cuts[k + 1], down_cuts[k + 1]),
                    up_keep,
                    up_came,
                    down_keep,
                    down_came,
                )
        if paired:
            half = (up_keep.shape[0] // 2, up_keep.shape[1])
            up_keep, down_keep, give = kernel_call(
                functools.partial(top_pair_kernel, top_shift),
                [shaped(half, BF16), shaped(half, BF16), shaped((2,) + half, BF16)],
                spot,
                up_keep,
                up_came,
                down_keep,
                down_came,
                name="top_pair",
                smem=(0,),
            )
            came = flip(give, top_bit)
            up_came, down_came = came[0], came[1]
        else:
            up_keep, up_give, down_keep, down_give = two_fold(
                spot, ((0, top_shift, 1),) * 2, up_keep, up_came, down_keep, down_came
            )
            up_came, down_came = flip(up_give, top_bit), flip(down_give, top_bit)
        d_down = kernel_call(
            add_kernel, [shaped((piece, width), F32)], down_keep, down_came, name="add"
        )[0]

        left_cuts, right_cuts = cuts_of(members, planes_down), cuts_of(members, plane_bits)
        sums_came = flip(sums_give, planes_down[0])
        for k, (b, c) in enumerate(zip(planes_down, plane_bits, strict=True)):
            left_came, right_came = flip(left_give, b), flip(right_give, c)
            if k + 1 < len(plane_bits):
                left_keep, left_give, right_keep, right_give, sums = sums_fold(
                    spot,
                    (left_cuts[k + 1], right_cuts[k + 1]),
                    left_keep,
                    left_came,
                    right_keep,
                    right_came,
                    sums,
                    sums_came,
                )
        tall = left_keep.shape[0] // 2
        small = (devices, lay.small)
        w_keep, w_give, sums = kernel_call(
            functools.partial(top_fold_kernel, top_shift),
            [
                shaped((tall, 3 * share), BF16),
                shaped((tall + devices, 3 * share), BF16),
                shaped(small, F32),
            ],
            spot,
            left_keep,
            left_came,
            right_keep,
            right_came,
            sums,
            name="top_fold",
            smem=(0,),
        )
        came = flip(w_give, top_bit)
        columns = 3 * share + ff // members
        steps = [(4, k, b) for k, b in reversed(list(enumerate(group_bits)))] + [(2, 0, 0)]
        for step, (slot, shift, b) in enumerate(steps):
            tall //= 2
            outs = [
                shaped((tall, columns), BF16),
                shaped((max(tall, 16) + devices, columns), BF16),
                shaped(small, F32),
            ]
            if step == 0:
                w_keep, w_give, sums = kernel_call(
                    functools.partial(home_first_kernel, slot, shift),
                    outs,
                    spot,
                    w_keep,
                    came,
                    up_keep,
                    up_came,
                    sums,
                    name="home_first",
                    smem=(0,),
                )
            else:
                w_keep, w_give, sums = kernel_call(
                    functools.partial(home_next_kernel, slot, shift),
                    outs,
                    spot,
                    w_keep,
                    came,
                    sums,
                    name="home_next",
                    smem=(0,),
                )
            came = flip(w_give, b)
            columns *= 2
        d_in, d_up, *vectors = kernel_call(
            functools.partial(home_last_kernel, lay),
            [shaped((each, 3 * width), F32), shaped((each, ff), F32)]
            + [shaped((1, each), F32)] * 8
            + [shaped((1, piece), F32)],
            spot,
            w_keep,
            came,
            sums,
            name="home_last",
            smem=(0,),
        )
        vectors = [v.reshape(-1) for v in vectors]

        d_out = dot(att_own, grad_branch, TN).astype(BF16)
        d_out = lax.psum_scatter(d_out, AXES, scatter_dimension=0, tiled=True).astype(F32)

        out_keep, out_came = reduce_group(out_keep, out_give, 4)
        layer_out = kernel_call(
            out_kernel,
            [shaped((rows, width), BF16)],
            vecs,
            middle,
            out_keep,
            out_came,
            name="layer_out",
        )[0]

        return (
            layer_out[None],
            input_gradient[None],
            vectors[0],
            vectors[1],
            d_in,
            vectors[2],
            vectors[3],
            d_out,
            vectors[4],
            vectors[5],
            vectors[6],
            d_up,
            vectors[8],
            d_down,
            vectors[7],
        )

    vector, matrix = P(AXES), P(AXES, None)
    tokens = P("batch", "blk", None)
    return jax.shard_map(
        local,
        mesh=mesh,
        in_specs=(
            tokens,
            P("batch", None),
            P("batch"),
            vector,
            vector,
            matrix,
            vector,
            vector,
            matrix,
            vector,
            vector,
            vector,
            matrix,
            vector,
            matrix,
            vector,
            tokens,
        ),
        out_specs=(
            tokens,
            tokens,
            vector,
            vector,
            matrix,
            vector,
            vector,
            matrix,
            vector,
            vector,
            vector,
            matrix,
            vector,
            matrix,
            vector,
        ),
        check_vma=False,
    )
```

time: 437 us -> 373 us (0.85); the launches traced: 429 us -> 370 us
  Pallas kernels: 17.7 us -> 110 us
  other arithmetic: 74.2 us -> 1.51 us
  matrix products: 52.4 us -> 3.28 us
  local copies, waits for them, and re-layouts: 62.7 us -> 16.8 us
  waiting for transfers between devices: 144 us -> 167 us
  starting transfers between devices: 74.3 us -> 55.2 us
  between operations: 3.6 us -> 15.8 us
    pallas_call x2 -> x29, Pallas kernels: 17.7 us -> 110 us  [kernel_call(): pl.pallas_call(body, in_specs=ins, out_specs=[spec(i, ()) for i in range(...]
    dot_general x12 -> x1, matrix products: 52.4 us -> 3.28 us  [dot(): return lax.dot_general(a, b, dims, preferred_element_type=F32)]
    select_n x48 -> x1, other arithmetic: 26.1 us -> 0.01 us  [local(): jnp.where(valid[0] > 0.5, 0.0, MASKED).astype(F32).reshape(length, 1)]
    ppermute x69 -> x53, waiting for transfers between devices: 144 us -> 166 us  [send(): return lax.ppermute(value, AXES, route)]
    ppermute x69 -> x53, starting transfers between devices: 74.3 us -> 55.1 us  [send(): return lax.ppermute(value, AXES, route)]
    add x20 -> x0, other arithmetic: 19.2 us -> none  [the longest x12 13.2 us: halve(): return keep + flip(give, b).astype(F32)]
    select_n x14 -> x1, local copies, waits for them, and re-layouts: 14.9 us -> 1.03 us  [local(): jnp.where(valid[0] > 0.5, 0.0, MASKED).astype(F32).reshape(length, 1)]
    concatenate x20 -> x0, local copies, waits for them, and re-layouts: 11.6 us -> none  [the longest x1 6.09 us: local(): jnp.concatenate([first_gain, first_shift, query_bias, value_bias, output_...]
  transfers between devices with their start and end apart: 69 -> 55, of which waited for: 26 -> 23; matrix products, arithmetic and copies ran while one was open for 34% -> 2% of each run, Pallas kernels for 4% -> 23%
where the time goes in v2:
time: 373 us; the launch traced here: 370 us
  waiting for transfers between devices  167 us (45%)
  Pallas kernels  110 us (29%)
  starting transfers between devices  55.2 us (15%)
  local copies, waits for them, and re-layouts  16.8 us (5%)
  between operations  15.8 us (4%)
    ppermute x53, waiting for transfers between devices, send(): return lax.ppermute(value, AXES, route)  166 us
    pallas_call x29, Pallas kernels, kernel_call(): pl.pallas_call(body, in_specs=ins, out_specs=[spec(i, ()) for i in range(...  110 us
    ppermute x53, starting transfers between devices, send(): return lax.ppermute(value, AXES, route)  55.1 us
    unnamed x104, local copies, waits for them, and re-layouts  11.2 us
  transfers between devices with their start and end apart: 55, of which 23 were waited for; matrix products, arithmetic and copies ran while one was open for 2% of the time, Pallas kernels for 23%

profile of v2, /device:TPU:0, one launch (start us, length us, event | category | flops | bytes accessed | tf_op | source)
XLA Modules:
  0.0 369.8 jit_solution(5387322872507330910)
XLA Ops:
  19.5 13.6 %collective-permute-done.1.came = bf16[80,1792]{1,0:T(8,128)(2,1)S(1)} collective-permute-done((bf16[80,1792]{1,0:T(8,128)(2,1)S(1)}, bf16[80,1792]{1,0:T(8,128)(2,1)S(1)}, u32[]{:S(2)}, u32[]{:S(2)}) %collective-permute-start.1) | collective-permute-done | bytes 286752 | tf_op jit(solution)/shard_map/ppermute | solution.py:1129
  35.4 5.4 %collective-permute-start.3 = (bf16[144,768]{1,0:T(8,128)(2,1)S(1)}, bf16[144,768]{1,0:T(8,128)(2,1)S(1)}, u32[]{:S(2)}, u32[]{:S(2)}) collective-permute-start(bf16[144,768]{1,0:T(8,128)(2,1)S(1)} %get-tuple-element.114.mine), channel_id=1, source_target_pairs={{0,16},{1,17},{2,18},{3,19},{4,20},{5,21},{6,22},{7,23},{8,24},{9,... | collective-permute-start | bytes 663560 | tf_op jit(solution)/shard_map/ppermute | solution.py:1129
  40.8 10.1 %collective-permute-done.3.came = bf16[144,768]{1,0:T(8,128)(2,1)S(1)} collective-permute-done((bf16[144,768]{1,0:T(8,128)(2,1)S(1)}, bf16[144,768]{1,0:T(8,128)(2,1)S(1)}, u32[]{:S(2)}, u32[]{:S(2)}) %collective-permute-start.3) | collective-permute-done | bytes 221216 | tf_op jit(solution)/shard_map/ppermute | solution.py:1129
  52.7 3.4 collective-permute-start.9
  59.2 7.8 %collective-permute-done.4.refs_1_ = bf16[2,144,384]{2,1,0:T(8,128)(2,1)S(1)} collective-permute-done((bf16[2,144,384]{2,1,0:T(8,128)(2,1)S(1)}, bf16[2,144,384]{2,1,0:T(8,128)(2,1)S(1)}, u32[]{:S(2)}, u32[]{:S(2)}) %collective-permute-start.4) | collective-permute-done | bytes 221216 | tf_op jit(solution)/shard_map/ppermute | solution.py:1129
  68.3 3.7 %collective-permute-start.8 = (bf16[256,1024]{1,0:T(8,128)(2,1)S(1)}, bf16[256,1024]{1,0:T(8,128)(2,1)}, u32[]{:S(2)}, u32[]{:S(2)}) collective-permute-start(bf16[256,1024]{1,0:T(8,128)(2,1)S(1)} %get-tuple-element.121), channel_id=1, source_target_pairs={{0,8},{1,9},{2,10},{3,11},{4,12},{5,13},{6,14},{7,15},{8,0},{9,1},... | collective-permute-start | bytes 1572872 | tf_op jit(solution)/shard_map/ppermute | solution.py:1129
  75.5 7.5 %collective-permute-done.14.refs_1_ = bf16[2,128,1024]{2,1,0:T(8,128)(2,1)S(1)} collective-permute-done((bf16[2,128,1024]{2,1,0:T(8,128)(2,1)S(1)}, bf16[2,128,1024]{2,1,0:T(8,128)(2,1)S(1)}, u32[]{:S(2)}, u32[]{:S(2)}) %collective-permute-start.14) | collective-permute-done | bytes 524320 | tf_op jit(solution)/shard_map/ppermute | solution.py:1129
  87.6 6.2 %collective-permute-done.8.refs_4_.refs_9_ = bf16[256,1024]{1,0:T(8,128)(2,1)} collective-permute-done((bf16[256,1024]{1,0:T(8,128)(2,1)S(1)}, bf16[256,1024]{1,0:T(8,128)(2,1)}, u32[]{:S(2)}, u32[]{:S(2)}) %collective-permute-start.8) | collective-permute-done | bytes 524320 | tf_op jit(solution)/shard_map/ppermute | solution.py:1129
  110.5 17.5 %attend.1 = (bf16[512,256]{1,0:T(8,128)(2,1)}, bf16[512,256]{1,0:T(8,128)(2,1)}, bf16[1024,768]{1,0:T(8,128)(2,1)}, f32[256,1024]{1,0:T(8,128)}, f32[2,8,1024]{2...) custom-call(s32[10]{0:T(128)} %stack.49.spot.refs_0_, ...), custom_call_target="tpu_custom_call" | custom-call | flops 3221225472 | bytes 15013928 | tf_op jit(solution)/shard_map/attend/pallas_call | solution.py:98
  129.2 10.1 %collective-permute-done.16.refs_2_ = bf16[512,256]{1,0:T(8,128)(2,1)S(1)} collective-permute-done((bf16[512,256]{1,0:T(8,128)(2,1)}, bf16[512,256]{1,0:T(8,128)(2,1)S(1)}, u32[]{:S(2)}, u32[]{:S(2)}) %collective-permute-start.16) | collective-permute-done | bytes 262176 | tf_op jit(solution)/shard_map/ppermute | solution.py:1129
  143.1 8.1 %collective-permute-done.17.refs_3_ = bf16[512,256]{1,0:T(8,128)(2,1)S(1)} collective-permute-done((bf16[512,256]{1,0:T(8,128)(2,1)S(1)}, bf16[512,256]{1,0:T(8,128)(2,1)S(1)}, u32[]{:S(2)}, u32[]{:S(2)}) %collective-permute-start.17) | collective-permute-done | bytes 262176 | tf_op jit(solution)/shard_map/ppermute | solution.py:1129
  154.5 20.2 %feed_forward.1 = (bf16[512,1024]{1,0:T(8,128)(2,1)}, bf16[512,1024]{1,0:T(8,128)(2,1)}, f32[256,1024]{1,0:T(8,128)}, bf16[256,1024]{1,0:T(8,128)(2,1)}, bf16[10...) custom-call(s32[10]{0:T(128)} %stack.49.spot.refs_0_, ...), custom_call_target="tpu_custom_call" | custom-call | flops 8589934592 | bytes 22614056 | tf_op jit(solution)/shard_map/feed_forward/pallas_call | solution.py:98
  181.3 15.3 %gradients.1 = (bf16[512,1024]{1,0:T(8,128)(2,1)}, bf16[512,1024]{1,0:T(8,128)(2,1)}, bf16[512,1024]{1,0:T(8,128)(2,1)}, bf16[512,1024]{1,0:T(8,128)(2,1)}, bf16...) custom-call(s32[10]{0:T(128)} %stack.49.spot.refs_0_, bf16[1024,1024]{1,0:T(8,128)(2,1)} %get-tuple-element.131.normed, ...), custom_call_target="tpu_custom_call" | custom-call | flops 6442450944 | bytes 16777256 | tf_op jit(solution)/shard_map/gradients/pallas_call | solution.py:98
  198.6 5.2 %turn.1 = (bf16[256,256]{1,0:T(8,128)(2,1)}, bf16[256,256]{1,0:T(8,128)(2,1)}, bf16[256,256]{1,0:T(8,128)(2,1)}, bf16[256,256]{1,0:T(8,128)(2,1)}, f32[256,1024]...) custom-call(s32[10]{0:T(128)} %stack.49.spot.refs_0_, f32[16,1024]{1,0:T(8,128)} %copy-done.4, ...), custom_call_target="tpu_custom_call" | custom-call | flops 536870912 | bytes 6916136 | tf_op jit(solution)/shard_map/turn/pallas_call | solution.py:98
  212.8 24.9 %collective-permute-done.47.two_came = bf16[512,1024]{1,0:T(8,128)(2,1)S(1)} collective-permute-done((bf16[512,1024]{1,0:T(8,128)(2,1)}, bf16[512,1024]{1,0:T(8,128)(2,1)S(1)}, u32[]{:S(2)}, u32[]{:S(2)}) %collective-permute-start.47) | collective-permute-done | bytes 1048608 | tf_op jit(solution)/shard_map/ppermute | solution.py:1129
  247.1 14.3 %attend_back.1 = (bf16[1024,768]{1,0:T(8,128)(2,1)}, bf16[512,384]{1,0:T(8,128)(2,1)}, bf16[512,384]{1,0:T(8,128)(2,1)}, bf16[512,384]{1,0:T(8,128)(2,1)}, bf16[512,384]{1,0:T(8,128)(2,1)}, /*index=5*/f32[1,768]{1,0:T(1,128)}) custom-call(s32[10]{0:T(128)} %stack.49.spot.refs_0_, f32[1024,1]{1,0:T(8,128)} %copy.32.refs_1_.bias, ...), custom_call_target="tpu_custom_call" | custom-call | flops 5905580032 | bytes 8461352 | tf_op jit(solution)/shard_map/attend_back/pallas_call | solution.py:98
  261.4 12.6 %input_slope.1 = (bf16[512,1024]{1,0:T(8,128)(2,1)}, bf16[512,1024]{1,0:T(8,128)(2,1)}, f32[32,384]{1,0:T(8,128)}, bf16[32,384]{1,0:T(8,128)(2,1)}) custom-call(s32[10]{0:T(128)} %stack.49.spot.refs_0_, bf16[1024,768]{1,0:T(8,128)(2,1)} %get-tuple-element.151.grads, bf16[1024,768]{1,0:T(8,128)(2,1)} %get-tuple-element.152.w, ...), custom_call_target="tpu_custom_call" | custom-call | flops 1610612736 | bytes 7453736 | tf_op jit(solution)/shard_map/input_slope/pallas_call | solution.py:98
  277.6 9.8 %collective-permute-done.42.sums_came = bf16[32,384]{1,0:T(8,128)(2,1)S(1)} collective-permute-done((bf16[32,384]{1,0:T(8,128)(2,1)}, bf16[32,384]{1,0:T(8,128)(2,1)S(1)}, u32[]{:S(2)}, u32[]{:S(2)}) %collective-permute-start.42) | collective-permute-done | bytes 24608 | tf_op jit(solution)/shard_map/ppermute | solution.py:1129
  290.8 5.6 %collective-permute-done.44.two_came = bf16[256,384]{1,0:T(8,128)(2,1)S(1)} collective-permute-done((bf16[256,384]{1,0:T(8,128)(2,1)S(1)}, bf16[256,384]{1,0:T(8,128)(2,1)S(1)}, u32[]{:S(2)}, u32[]{:S(2)}) %collective-permute-start.44) | collective-permute-done | bytes 196640 | tf_op jit(solution)/shard_map/ppermute | solution.py:1129
  300.6 18.5 %collective-permute-done.50 = bf16[2,128,1024]{2,1,0:T(8,128)(2,1)S(1)} collective-permute-done((bf16[2,128,1024]{2,1,0:T(8,128)(2,1)S(1)}, bf16[2,128,1024]{2,1,0:T(8,128)(2,1)S(1)}, u32[]{:S(2)}, u32[]{:S(2)}) %collective-permute-start.50) | collective-permute-done | bytes 524320 | tf_op jit(solution)/shard_map/ppermute | solution.py:1129
  319.1 5.4 %collective-permute-done.45.w_in_came = bf16[160,768]{1,0:T(8,128)(2,1)S(1)} collective-permute-done((bf16[160,768]{1,0:T(8,128)(2,1)S(1)}, bf16[160,768]{1,0:T(8,128)(2,1)S(1)}, u32[]{:S(2)}, u32[]{:S(2)}) %collective-permute-start.45) | collective-permute-done | bytes 245792 | tf_op jit(solution)/shard_map/ppermute | solution.py:1129
  328.4 4.4 %collective-permute-done.38.two.came = bf16[256,1024]{1,0:T(8,128)(2,1)S(1)} collective-permute-done((bf16[256,1024]{1,0:T(8,128)(2,1)S(1)}, bf16[256,1024]{1,0:T(8,128)(2,1)S(1)}, u32[]{:S(2)}, u32[]{:S(2)}) %collective-permute-start.38) | collective-permute-done | bytes 524320 | tf_op jit(solution)/shard_map/ppermute | solution.py:1129
  333.6 6.5 %collective-permute-done.51.came = bf16[96,1792]{1,0:T(8,128)(2,1)S(1)} collective-permute-done((bf16[96,1792]{1,0:T(8,128)(2,1)S(1)}, bf16[96,1792]{1,0:T(8,128)(2,1)S(1)}, u32[]{:S(2)}, u32[]{:S(2)}) %collective-permute-start.51) | collective-permute-done | bytes 344096 | tf_op jit(solution)/shard_map/ppermute | solution.py:1129
  340.8 14.5 %collective-permute-done.30.came = bf16[256,1024]{1,0:T(8,128)(2,1)S(1)} collective-permute-done((bf16[256,1024]{1,0:T(8,128)(2,1)S(1)}, bf16[256,1024]{1,0:T(8,128)(2,1)S(1)}, u32[]{:S(2)}, u32[]{:S(2)}) %collective-permute-start.30) | collective-permute-done | bytes 524320 | tf_op jit(solution)/shard_map/ppermute | solution.py:1129
  (232 shorter events, 103.2 us)
Async XLA Ops:
  7.2 146.3 %all-gather.2.cloned.1.call-start = ((), (), s32[]{:S(2)}) async-start(), calls=%async_computation.1 | async-start | bytes 2162688 | tf_op jit(solution)/shard_map/all_gather | solution.py:1330
  7.9 353.1 %reduce-scatter.2.cloned.1.call-start = ((), (), s32[]{:S(2)}) async-start(), calls=%async_computation.2 | async-start | bytes 2162688 | tf_op jit(solution)/shard_map/reduce_scatter | solution.py:1548
  33.8 34.5 %collective-permute-start.6 = (bf16[256,1024]{1,0:T(8,128)(2,1)S(1)}, bf16[256,1024]{1,0:T(8,128)(2,1)}, u32[]{:S(2)}, u32[]{:S(2)}) collective-permute-start(bf16[256,1024]{1,0:T(8,128)(2,1)S(1)} %get-tuple-element.118), channel_id=1, source_target_pairs={{1,9},{3,11},{5,13},{7,15},{9,1},{11,3},{13,5},{15,7},{16,24},{18,... | collective-permute-start | bytes 1572872 | tf_op jit(solution)/shard_map/ppermute | solution.py:1129
  52.5 30.5 %collective-permute-start.14 = (bf16[2,128,1024]{2,1,0:T(8,128)(2,1)S(1)}, bf16[2,128,1024]{2,1,0:T(8,128)(2,1)S(1)}, u32[]{:S(2)}, u32[]{:S(2)}) collective-permute-start(bf16[2,128,1024]{2,1,0:T(8,128)(2,1)S(1)} %get-tuple-element.123.refs_0_), channel_id=1, source_target_pairs={{0,16},{1,17},{2,18},{3,19},{4,20},{5,21},{6,22},{7,23},{8,24},{9,... | collective-permute-start | bytes 1572872 | tf_op jit(solution)/shard_map/ppermute | solution.py:1129
  52.7 32.1 %collective-permute-start.9 = (bf16[256,1024]{1,0:T(8,128)(2,1)S(1)}, bf16[256,1024]{1,0:T(8,128)(2,1)S(1)}, u32[]{:S(2)}, u32[]{:S(2)}) collective-permute-start(bf16[256,1024]{1,0:T(8,128)(2,1)S(1)} %bitcast.50), channel_id=1, source_target_pairs={{0,1},{1,0},{2,3},{3,2},{4,5},{5,4},{6,7},{7,6},{8,9},{9,8},{10,11... | collective-permute-start | bytes 1572872 | tf_op jit(solution)/shard_map/ppermute | solution.py:1129
  68.3 25.5 %collective-permute-start.8 = (bf16[256,1024]{1,0:T(8,128)(2,1)S(1)}, bf16[256,1024]{1,0:T(8,128)(2,1)}, u32[]{:S(2)}, u32[]{:S(2)}) collective-permute-start(bf16[256,1024]{1,0:T(8,128)(2,1)S(1)} %get-tuple-element.121), channel_id=1, source_target_pairs={{0,8},{1,9},{2,10},{3,11},{4,12},{5,13},{6,14},{7,15},{8,0},{9,1},... | collective-permute-start | bytes 1572872 | tf_op jit(solution)/shard_map/ppermute | solution.py:1129
  98.7 30.4 %collective-permute-start.23 = (bf16[256,1024]{1,0:T(8,128)(2,1)S(1)}, bf16[256,1024]{1,0:T(8,128)(2,1)}, u32[]{:S(2)}, u32[]{:S(2)}) collective-permute-start(bf16[256,1024]{1,0:T(8,128)(2,1)S(1)} %mask.1.refs_12_.refs_0_.refs_5_), channel_id=1, source_target_pairs={{0,1},{1,0},{2,3},{3,2},{4,5},{5,4},{6,7},{7,6},{8,9},{9,8},{10,11... | collective-permute-start | bytes 1572872 | tf_op jit(solution)/shard_map/ppermute | solution.py:1129
  98.9 30.2 %collective-permute-start.22 = (bf16[256,1024]{1,0:T(8,128)(2,1)S(1)}, bf16[256,1024]{1,0:T(8,128)(2,1)}, u32[]{:S(2)}, u32[]{:S(2)}) collective-permute-start(bf16[256,1024]{1,0:T(8,128)(2,1)S(1)} %mask.1.refs_12_.refs_0_.refs_5_), channel_id=1, source_target_pairs={{0,8},{1,9},{2,10},{3,11},{4,12},{5,13},{6,14},{7,15},{8,0},{9,1},... | collective-permute-start | bytes 1572872 | tf_op jit(solution)/shard_map/ppermute | solution.py:1129
  108.0 44.8 %collective-permute-start.27 = (bf16[4,128,1024]{2,1,0:T(8,128)(2,1)}, bf16[4,128,1024]{2,1,0:T(8,128)(2,1)}, u32[]{:S(2)}, u32[]{:S(2)}) collective-permute-start(bf16[4,128,1024]{2,1,0:T(8,128)(2,1)} %get-tuple-element.128.refs_16_), channel_id=1, source_target_pairs={{0,4},{1,5},{2,6},{3,7},{4,0},{5,1},{6,2},{7,3},{8,12},{9,13},{10,... | collective-permute-start | bytes 3145736 | tf_op jit(solution)/shard_map/ppermute | solution.py:1129
  109.2 44.3 %collective-permute-start.28 = (bf16[4,128,1024]{2,1,0:T(8,128)(2,1)S(1)}, bf16[4,128,1024]{2,1,0:T(8,128)(2,1)S(1)}, u32[]{:S(2)}, u32[]{:S(2)}) collective-permute-start(bf16[4,128,1024]{2,1,0:T(8,128)(2,1)S(1)} %get-tuple-element.129.refs_18_.refs_4_), channel_id=1, source_target_pairs={{0,2},{1,3},{2,0},{3,1},{4,6},{5,7},{6,4},{7,5},{8,10},{9,11},{10,... | collective-permute-start | bytes 3145736 | tf_op jit(solution)/shard_map/ppermute | solution.py:1129
  207.2 30.5 %collective-permute-start.47 = (bf16[512,1024]{1,0:T(8,128)(2,1)}, bf16[512,1024]{1,0:T(8,128)(2,1)S(1)}, u32[]{:S(2)}, u32[]{:S(2)}) collective-permute-start(bf16[512,1024]{1,0:T(8,128)(2,1)} %get-tuple-element.177), channel_id=1, source_target_pairs={{0,2},{1,3},{2,0},{3,1},{4,6},{5,7},{6,4},{7,5},{8,10},{9,11},{10,... | collective-permute-start | bytes 3145736 | tf_op jit(solution)/shard_map/ppermute | solution.py:1129
  208.0 32.4 %collective-permute-start.46 = (bf16[512,1024]{1,0:T(8,128)(2,1)}, bf16[512,1024]{1,0:T(8,128)(2,1)S(1)}, u32[]{:S(2)}, u32[]{:S(2)}) collective-permute-start(bf16[512,1024]{1,0:T(8,128)(2,1)} %get-tuple-element.146), channel_id=1, source_target_pairs={{0,4},{1,5},{2,6},{3,7},{4,0},{5,1},{6,2},{7,3},{8,12},{9,13},{10,... | collective-permute-start | bytes 3145736 | tf_op jit(solution)/shard_map/ppermute | solution.py:1129
  209.0 33.8 %collective-permute-start.33 = (bf16[256,256]{1,0:T(8,128)(2,1)}, bf16[256,256]{1,0:T(8,128)(2,1)S(1)}, u32[]{:S(2)}, u32[]{:S(2)}) collective-permute-start(bf16[256,256]{1,0:T(8,128)(2,1)} %get-tuple-element.147), channel_id=1, source_target_pairs={{0,0},{1,16},{2,2},{3,18},{4,4},{5,20},{6,6},{7,22},{8,1},{9,17},{... | collective-permute-start | bytes 393224 | tf_op jit(solution)/shard_map/ppermute | solution.py:1129
  210.5 33.5 %collective-permute-start.34 = (bf16[256,256]{1,0:T(8,128)(2,1)S(1)}, bf16[256,256]{1,0:T(8,128)(2,1)S(1)}, u32[]{:S(2)}, u32[]{:S(2)}) collective-permute-start(bf16[256,256]{1,0:T(8,128)(2,1)S(1)} %copy-done.47), channel_id=1, source_target_pairs={{0,1},{1,17},{2,3},{3,19},{4,5},{5,21},{6,7},{7,23},{8,0},{9,16},{... | collective-permute-start | bytes 393224 | tf_op jit(solution)/shard_map/ppermute | solution.py:1129
  212.1 31.9 %collective-permute-start.35 = (bf16[256,256]{1,0:T(8,128)(2,1)S(1)}, bf16[256,256]{1,0:T(8,128)(2,1)S(1)}, u32[]{:S(2)}, u32[]{:S(2)}) collective-permute-start(bf16[256,256]{1,0:T(8,128)(2,1)S(1)} %copy-done.46), channel_id=1, source_target_pairs={{0,8},{1,24},{2,10},{3,26},{4,12},{5,28},{6,14},{7,30},{8,9},{9,25... | collective-permute-start | bytes 393224 | tf_op jit(solution)/shard_map/ppermute | solution.py:1129
  242.5 33.6 %collective-permute-start.48 = (bf16[256,1024]{1,0:T(8,128)(2,1)}, bf16[256,1024]{1,0:T(8,128)(2,1)S(1)}, u32[]{:S(2)}, u32[]{:S(2)}) collective-permute-start(bf16[256,1024]{1,0:T(8,128)(2,1)} %get-tuple-element.179), channel_id=1, source_target_pairs={{0,2},{1,3},{2,0},{3,1},{4,6},{5,7},{6,4},{7,5},{8,10},{9,11},{10,... | collective-permute-start | bytes 1572872 | tf_op jit(solution)/shard_map/ppermute | solution.py:1129
  242.8 33.9 %collective-permute-start.49 = (bf16[256,1024]{1,0:T(8,128)(2,1)S(1)}, bf16[256,1024]{1,0:T(8,128)(2,1)S(1)}, u32[]{:S(2)}, u32[]{:S(2)}) collective-permute-start(bf16[256,1024]{1,0:T(8,128)(2,1)S(1)} %get-tuple-element.181), channel_id=1, source_target_pairs={{0,4},{1,5},{2,6},{3,7},{4,0},{5,1},{6,2},{7,3},{8,12},{9,13},{10,... | collective-permute-start | bytes 1572872 | tf_op jit(solution)/shard_map/ppermute | solution.py:1129
  274.0 25.3 %collective-permute-start.37 = (bf16[512,1024]{1,0:T(8,128)(2,1)}, bf16[512,1024]{1,0:T(8,128)(2,1)S(1)}, u32[]{:S(2)}, u32[]{:S(2)}) collective-permute-start(bf16[512,1024]{1,0:T(8,128)(2,1)} %get-tuple-element.158), channel_id=1, source_target_pairs={{0,1},{1,0},{2,3},{3,2},{4,5},{5,4},{6,7},{7,6},{8,9},{9,8},{10,11... | collective-permute-start | bytes 3145736 | tf_op jit(solution)/shard_map/ppermute | solution.py:1129
  276.7 49.1 %collective-permute-start.29 = (bf16[512,1024]{1,0:T(8,128)(2,1)S(1)}, bf16[512,1024]{1,0:T(8,128)(2,1)S(1)}, u32[]{:S(2)}, u32[]{:S(2)}) collective-permute-start(bf16[512,1024]{1,0:T(8,128)(2,1)S(1)} %copy-done.32), channel_id=1, source_target_pairs={{0,1},{1,0},{2,3},{3,2},{4,5},{5,4},{6,7},{7,6},{8,9},{9,8},{10,11... | collective-permute-start | bytes 3145736 | tf_op jit(solution)/shard_map/ppermute | solution.py:1129
  287.4 31.7 %collective-permute-start.50 = (bf16[2,128,1024]{2,1,0:T(8,128)(2,1)S(1)}, bf16[2,128,1024]{2,1,0:T(8,128)(2,1)S(1)}, u32[]{:S(2)}, u32[]{:S(2)}) collective-permute-start(bf16[2,128,1024]{2,1,0:T(8,128)(2,1)S(1)} %get-tuple-element.183), channel_id=1, source_target_pairs={{0,16},{1,17},{2,18},{3,19},{4,20},{5,21},{6,22},{7,23},{8,24},{9,... | collective-permute-start | bytes 1572872 | tf_op jit(solution)/shard_map/ppermute | solution.py:1129
  297.4 27.0 %collective-permute-start.45 = (bf16[160,768]{1,0:T(8,128)(2,1)S(1)}, bf16[160,768]{1,0:T(8,128)(2,1)S(1)}, u32[]{:S(2)}, u32[]{:S(2)}) collective-permute-start(bf16[160,768]{1,0:T(8,128)(2,1)S(1)} %get-tuple-element.174), channel_id=1, source_target_pairs={{0,16},{1,17},{2,18},{3,19},{4,20},{5,21},{6,22},{7,23},{8,24},{9,... | collective-permute-start | bytes 737288 | tf_op jit(solution)/shard_map/ppermute | solution.py:1129
  300.4 32.3 %collective-permute-start.38 = (bf16[256,1024]{1,0:T(8,128)(2,1)S(1)}, bf16[256,1024]{1,0:T(8,128)(2,1)S(1)}, u32[]{:S(2)}, u32[]{:S(2)}) collective-permute-start(bf16[256,1024]{1,0:T(8,128)(2,1)S(1)} %get-tuple-element.160), channel_id=1, source_target_pairs={{0,8},{1,9},{2,10},{3,11},{4,12},{5,13},{6,14},{7,15},{8,0},{9,1},... | collective-permute-start | bytes 1572872 | tf_op jit(solution)/shard_map/ppermute | solution.py:1129
  327.0 28.4 %collective-permute-start.30 = (bf16[256,1024]{1,0:T(8,128)(2,1)S(1)}, bf16[256,1024]{1,0:T(8,128)(2,1)S(1)}, u32[]{:S(2)}, u32[]{:S(2)}) collective-permute-start(bf16[256,1024]{1,0:T(8,128)(2,1)S(1)} %get-tuple-element.137), channel_id=1, source_target_pairs={{0,8},{1,9},{2,10},{3,11},{4,12},{5,13},{6,14},{7,15},{8,0},{9,1},... | collective-permute-start | bytes 1572872 | tf_op jit(solution)/shard_map/ppermute | solution.py:1129
  332.9 26.0 %collective-permute-start.39 = (bf16[256,1024]{1,0:T(8,128)(2,1)S(1)}, bf16[256,1024]{1,0:T(8,128)(2,1)S(1)}, u32[]{:S(2)}, u32[]{:S(2)}) collective-permute-start(bf16[256,1024]{1,0:T(8,128)(2,1)S(1)} %add.23), channel_id=1, source_target_pairs={{1,24},{3,26},{5,28},{7,30},{9,16},{11,18},{13,20},{15,22},{16,9},... | collective-permute-start | bytes 1572872 | tf_op jit(solution)/shard_map/ppermute | solution.py:1129
  (83 other events, 1181.2 us)
Sparse Core Ops, SparseCore 0:
  10.9 74.1 all-gather.1
  207.4 139.6 reduce-scatter.1

commit v3 on v2

--- a/solution.py
+++ b/solution.py
@@ -67,23 +67,31 @@
 EXTRA = 16
 
 
+COST = lambda flops: 10**11
+
+
 def shaped(shape, kind):
     return jax.ShapeDtypeStruct(shape, kind)
 
 
-def token(value):
-    corner = tuple(slice(0, 1) for _ in value.shape[:-2]) + (slice(0, 8), slice(0, LANES))
-    return value[corner].reshape(8, LANES)
-
-
-def kernel_call(
-    body, outs, *args, name, smem=(), away=(), scratch=(), vmem=8, flops=0, after=()
-):
-    count = len(args)
-    if after:
-        inner = body
-        body = lambda *refs: inner(*refs[:count], *refs[count + len(after) :])
-    args = args + tuple(token(v) for v in after)
+class Order:
+    def __init__(self):
+        self.ticket = jnp.zeros((8, LANES), F32)
+
+
+def kernel_call(order, body, outs, *args, name, smem=(), away=(), scratch=(), vmem=8, flops=0, after=()):
+    count, given = len(args), len(outs)
+    inner = body
+
+    def body(*refs):
+        ins, rest = refs[:count], refs[count + len(after) :]
+        before, results, ticket = rest[0], rest[1 : 1 + given], rest[1 + given]
+        ticket[...] = before[...]
+        inner(*ins, *results, *rest[2 + given :])
+
+    away = tuple(away) + tuple(range(count, count + len(after)))
+    args = args + tuple(after) + (order.ticket,)
+    outs = list(outs) + [shaped((8, LANES), F32)]
 
     def spec(i, places):
         if i in places:
@@ -95,16 +103,17 @@
         for i in range(len(args))
     ]
     moved = sum(v.size * v.dtype.itemsize for v in args + tuple(outs))
-    return pl.pallas_call(
+    *results, order.ticket = pl.pallas_call(
         body,
         in_specs=ins,
         out_specs=[spec(i, ()) for i in range(len(outs))],
         out_shape=list(outs),
         scratch_shapes=list(scratch),
         compiler_params=pltpu.CompilerParams(vmem_limit_bytes=vmem * 2**20),
-        cost_estimate=pl.CostEstimate(flops=flops, bytes_accessed=moved if flops else 0, transcendentals=0),
+        cost_estimate=pl.CostEstimate(flops=COST(flops), bytes_accessed=1, transcendentals=0),
         name=name,
     )(*args)
+    return results
 
 
 def iota(shape, dim):
@@ -125,6 +134,7 @@
         self.small = 8 * self.each + self.piece
         self.valid_at = -(-self.small // 512) * 512
         self.head = width // HEADS
+        self.order = Order()
 
 
 def each_way(flag, write):
@@ -168,16 +178,24 @@
 
 
 def pack_kernel(lay, spot, lengths, *refs):
-    sources, (give, keep), targets, sems = refs[:12], refs[12:14], refs[14:26], refs[26]
+    sources, (give, keep), targets, sems = refs[:13], refs[13:15], refs[15:28], refs[28]
     wait_all(load_all(list(zip(sources, targets, strict=True)), sems))
-    w_in, w_up, mask = targets[:3]
-    smalls = targets[3:]
+    w_in, w_up, mask, w_out = targets[:4]
+    smalls = targets[4:]
     n = lay.each
     base = max(n, 16)
     if base > n:
         for ref in (give, keep):
             ref[0:base, :] = jnp.zeros((base, ref.shape[1]), BF16)
     each_way(spot[2], lambda side: write_half(lay, side, 0, w_in, w_up, 0, 0, give, keep, n))
+    half = lay.width // 2
+    last = give.shape[1] - half
+
+    def write_out(side):
+        keep[0:n, last:] = w_out[:, side * half : (side + 1) * half]
+        give[0:n, last:] = w_out[:, (1 - side) * half : (2 - side) * half]
+
+    each_way(spot[2], write_out)
     line = jnp.zeros((1, lay.small), F32)
     at = 0
     for ref in smalls:
@@ -220,6 +238,9 @@
         (spot[4] >> step) & 1,
         lambda side: write_half(lay, side, count, both, both, 0, start, give, hold, 2 * n),
     )
+    half = lay.width // 2
+    for ref in (give, hold):
+        ref[0 : 2 * n, ref.shape[1] - half :] = both[:, both.shape[1] - half :]
     extra = merge_extra(lay, keep, came, n)
     for ref in (give, hold):
         ref[2 * n : 2 * n + EXTRA, :] = jnp.zeros((EXTRA, ref.shape[1]), BF16)
@@ -233,26 +254,35 @@
         valid[...] = jnp.zeros_like(valid)
 
 
-def settle_kernel(lay, step, spot, keep, came, far, in_block, up_block, far_out, both):
+def settle_kernel(
+    lay, step, spot, keep, came, far, down, in_block, up_block, far_out, pair, both
+):
     far_out[...] = far[...]
     n = (1 << step) * lay.each
     merge_rows(keep, came, (spot[4] >> (step - 1)) & 1, n, both)
     cut = 3 * lay.share
     in_block[0 : 2 * n, :] = both[:, 0:cut]
-    up_block[...] = both[:, cut:]
+    last = cut + lay.ff_share
+    tall, half = 2 * n, lay.width // 2
+    chunks = lay.ff_share // half
+    part = tall // chunks
+    targets = [up_block.at[0]] + ([pair] if pair.shape[0] > 8 else [])
+    for ref in targets:
+        ref[0:tall, :] = both[:, cut:last]
+        for i in range(chunks):
+            rows = both[i * part : (i + 1) * part, last:]
+            ref[tall : tall + part, i * half : (i + 1) * half] = rows
+    if pair.shape[0] > 8:
+        pair[tall + part :, :] = down[...]
     in_block[2 * n : 2 * n + EXTRA, :] = jnp.zeros((EXTRA, cut), BF16)
     in_block[2 * n : 2 * n + EXTRA, 0 : lay.small] = merge_extra(lay, keep, came, n)
 
 
-def split_kernel(cut, mine, came, up, down, own, left, right, up_out, down_out, own_out):
+def split_kernel(cut, mine, came, pair, grad, left, right, pair_out, grad_out):
+    pair_out[...] = pair[...]
+    grad_out[...] = grad[...]
     left[0], left[1] = mine[:, 0:cut], came[:, 0:cut]
     right[0], right[1] = mine[:, cut:], came[:, cut:]
-    own_out[...] = own[...]
-    if up_out.shape[0] == 2:
-        up_out[0], up_out[1] = up[...], down[...]
-    else:
-        up_out[0] = up[...]
-    down_out[...] = jnp.zeros_like(down_out) if up_out.shape[0] == 2 else down[...]
 
 
 def stack_kernel(one, one_came, two, two_came, one_out, two_out):
@@ -261,16 +291,49 @@
     two_out[0:n], two_out[n : 2 * n] = two[...], two_came[...]
 
 
-def stack(one, one_came, two, two_came, *after):
+def stack(lay, one, one_came, two, two_came, *after):
     outs = [shaped((2 * v.shape[0],) + v.shape[1:], BF16) for v in (one, two)]
     return kernel_call(
-        stack_kernel, outs, one, one_came, two, two_came, name="stack", after=after
+        lay.order, stack_kernel, outs, one, one_came, two, two_came, name="stack", after=after
     )
 
 
-def unpair_kernel(pair, came, ups, downs):
-    ups[0], ups[1] = pair[0], came[0]
-    downs[0], downs[1] = pair[1], came[1]
+def unpair_kernel(pair, up, down):
+    n = up.shape[1]
+    up[0], down[0] = pair[0:n, :], pair[n:, :]
+
+
+def bundle_kernel(g, spot, *refs):
+    near, far, out = refs[:g], refs[g : 2 * g], refs[2 * g]
+    rows = near[0].shape[0]
+
+    def write(home):
+        parts = list(near) if home else list(far) + list(near)
+        for i, ref in enumerate(parts):
+            out[i * rows : (i + 1) * rows, :] = ref[...]
+
+    each_way(spot[6], write)
+
+
+def out_kernel_rows(mine, came, out):
+    count, tall, half = out.shape
+    chunks = mine.shape[2] // half
+    part = tall // chunks
+    for k in range(count):
+        source = (mine if k < count // 2 else came).at[k % (count // 2)]
+        for i in range(chunks):
+            rows = source[tall : tall + part, i * half : (i + 1) * half]
+            out[k, i * part : (i + 1) * part, :] = rows
+
+
+def join_kernel(one, one_came, out):
+    n = one.shape[0]
+    out[0:n], out[n : 2 * n] = one[...], one_came[...]
+
+
+def join(lay, one, one_came, *after):
+    out = shaped((2 * one.shape[0],) + one.shape[1:], BF16)
+    return kernel_call(lay.order, join_kernel, [out], one, one_came, name="join", after=after)[0]
 
 
 def block_spot(lay, spot, k, flipped):
@@ -325,9 +388,10 @@
 
 def attend_kernel(lay, spot, bias, vecs, *refs):
     g, rows, hw, length, head = lay.size, lay.rows, lay.share, lay.length, lay.head
-    near, far, near_c, far_c = (refs[i * g : (i + 1) * g] for i in range(4))
-    weights = refs[4 * g : 4 * g + 4]
-    near_att, far_att, joint, wide, lse, normed, x, w, x_sems, w_sems = refs[4 * g + 4 :]
+    near, far, came = refs[:g], refs[g : 2 * g], refs[2 * g]
+    near_c = far_c = [came.at[e * rows : (e + 1) * rows, :] for e in range(g)]
+    weights = refs[2 * g + 1 : 2 * g + 5]
+    near_att, far_att, joint, wide, lse, normed, x, w, x_sems, w_sems = refs[2 * g + 5 :]
     group, place = spot[3], spot[4]
     pending = []
     for e in range(g):
@@ -408,7 +472,7 @@
             out_ref[here, :] = part.T.astype(BF16)
 
 
-def attend(lay, spot, bias, vecs, hidden, weights, later):
+def attend(lay, spot, bias, vecs, hidden, weights):
     d, hw, length, g = lay.width, lay.share, lay.length, lay.size
     outs = [
         shaped((g * lay.rows, hw), BF16),
@@ -423,6 +487,7 @@
     copies = 2 * lay.planes * 2 * g
     args = (spot, bias, vecs) + tuple(hidden) + tuple(weights)
     return kernel_call(
+        lay.order,
         functools.partial(attend_kernel, lay),
         outs,
         *args,
@@ -433,9 +498,8 @@
             pltpu.SemaphoreType.DMA((2 * g,)),
             pltpu.SemaphoreType.DMA((copies,)),
         ],
-        vmem=60,
+        vmem=24,
         flops=2 * length * d * 3 * hw + 3 * length * length * d // 2,
-        after=(later,),
     )
 
 
@@ -451,10 +515,11 @@
     each_way(side, write)
 
 
-def fold(spot, slot, shift, a, keep, came):
+def fold(lay, spot, slot, shift, a, keep, came):
     count, columns = keep.shape
     b = count // (2 * a)
     return kernel_call(
+        lay.order,
         functools.partial(fold_kernel, slot, shift, a, b),
         [shaped((a * b, columns), BF16)] * 2,
         spot,
@@ -475,29 +540,36 @@
     return spot[4] ^ e
 
 
-def weight_loads(lay, spot, ups, ups_came, downs, downs_came, w_up, w_down):
+def block_of(lay, blocks, k):
+    mine, came = blocks[2 * (k & 1)], blocks[2 * (k & 1) + 1]
+    half = lay.planes // 2
+    return (mine if k >> 1 < half else came).at[(k >> 1) % half]
+
+
+def up_loads(lay, spot, blocks, w_up):
     pairs = []
-    count, span, g = 2 * lay.planes, 2 * lay.each, lay.size
-    for k in range(count):
-        source = ups if k < count // 2 else ups_came
+    span, g = 2 * lay.each, lay.size
+    for k in range(2 * lay.planes):
+        source = block_of(lay, blocks, k)
         top, plane = block_spot(lay, spot, k, False)
         for q in range(g):
             start = ((top * g + q) * lay.planes + plane) * span
             pairs.append(
                 (
-                    source.at[k % (count // 2), q * span : (q + 1) * span, :],
+                    source.at[q * span : (q + 1) * span, :],
                     w_up.at[pl.ds(pl.multiple_of(start, span), span), :],
                 )
             )
-        source = downs if k < count // 2 else downs_came
+    return pairs
+
+
+def down_loads(lay, spot, blocks, w_down):
+    pairs = []
+    for k in range(2 * lay.planes):
         top, plane = block_spot(lay, spot, k, True)
         start = (top * lay.planes + plane) * lay.piece
-        pairs.append(
-            (
-                source.at[k % (count // 2)],
-                w_down.at[pl.ds(pl.multiple_of(start, lay.piece), lay.piece), :],
-            )
-        )
+        target = w_down.at[pl.ds(pl.multiple_of(start, lay.piece), lay.piece), :]
+        pairs.append((block_of(lay, blocks, k), target))
     return pairs
 
 
@@ -511,11 +583,27 @@
     return pairs
 
 
-def forward_kernel(lay, spot, vecs, w_out, *refs):
+def out_loads(lay, spot, blocks, target):
+    pairs = []
+    half, span, g = lay.width // 2, 2 * lay.each, lay.size
+    for i, block in enumerate(blocks):
+        column = pl.multiple_of((spot[2] ^ (i // 2)) * half, half)
+        for k in range(lay.planes):
+            top, plane = block_spot(lay, spot, 2 * k + i % 2, False)
+            for q in range(g):
+                row = pl.multiple_of(((top * g + q) * lay.planes + plane) * span, span)
+                source = block.at[k, q * span : (q + 1) * span, :]
+                pairs.append((source, target.at[pl.ds(row, span), pl.ds(column, half)]))
+    return pairs
+
+
+def forward_kernel(lay, spot, vecs, *refs):
+    outs, refs = refs[:4], refs[4:]
     g, rows, hw, d = lay.size, lay.rows, lay.share, lay.width
-    lists = [refs[i * g : (i + 1) * g] for i in range(8)]
-    near, far, near_c, far_c, base_m, base_c, down_m, down_c = lists
-    blocks = refs[8 * g : 8 * g + 4]
+    lists = [refs[i * g : (i + 1) * g] for i in range(7)]
+    near, far, near_c, far_c, base_m, down_m, down_c = lists
+    refs = refs[7 * g :]
+    bundle, ups, downs = refs[0], refs[1:5], refs[5:9]
     (
         dn_keep,
         dn_give,
@@ -525,17 +613,17 @@
         act,
         grad_pre,
         bias_sum,
+        wo,
         att,
-        wo,
         base,
         gd,
         w_up,
         w_down,
         sems,
-    ) = refs[8 * g + 4 :]
+    ) = refs[9:]
     core, group, place = spot[2], spot[3], spot[4]
     span = g * rows
-    pairs = [(w_out, wo)]
+    pairs = out_loads(lay, spot, outs, wo)
     for e in range(g):
         for source, sequence, at, side in (
             (near[e], group, place ^ e, core),
@@ -546,9 +634,13 @@
             row = pl.multiple_of(sequence * span, span)
             column = pl.multiple_of((at * 2 + side) * hw, hw)
             pairs.append((source, att.at[pl.ds(row, span), pl.ds(column, hw)]))
+    first_row = jnp.where(spot[6] == 1, span, 0)
+    base_c = [
+        bundle.at[pl.ds(pl.multiple_of(first_row + e * rows, rows), rows), :] for e in range(g)
+    ]
     pairs += row_loads(lay, spot, base_m, base_c, base)
     first = len(pairs)
-    pairs += weight_loads(lay, spot, *blocks, w_up, w_down)
+    pairs += up_loads(lay, spot, ups, w_up) + down_loads(lay, spot, downs, w_down)
     pairs += row_loads(lay, spot, down_m, down_c, gd)
     copies = load_all(pairs, sems)
     wait_all(copies[:first])
@@ -589,7 +681,7 @@
     bias_sum[...] = total
 
 
-def forward_call(lay, spot, vecs, w_out, lists, blocks):
+def forward_call(lay, spot, vecs, outs_w, lists, blocks):
     d, f, rows, g = lay.width, lay.ff_share, lay.rows, lay.size
     tokens = 2 * g * rows
     outs = [
@@ -601,10 +693,12 @@
         shaped((tokens, f), BF16),
         shaped((tokens, f), BF16),
         shaped((1, f), F32),
+        shaped((d, d), BF16),
     ]
-    args = (spot, vecs, w_out) + tuple(lists) + tuple(blocks)
-    copies = 1 + 8 * g + 2 * lay.planes * (g + 1)
+    args = (spot, vecs) + tuple(outs_w) + tuple(lists) + tuple(blocks)
+    copies = 4 * lay.planes * g + 8 * g + 2 * lay.planes * (g + 1)
     return kernel_call(
+        lay.order,
         functools.partial(forward_kernel, lay),
         outs,
         *args,
@@ -613,14 +707,13 @@
         away=tuple(range(2, len(args))),
         scratch=[
             pltpu.VMEM((tokens, d), BF16),
-            pltpu.VMEM((d, d), BF16),
             pltpu.VMEM((tokens, d), BF16),
             pltpu.VMEM((tokens, d), BF16),
             pltpu.VMEM((d, f), BF16),
             pltpu.VMEM((f, d), BF16),
             pltpu.SemaphoreType.DMA((copies,)),
         ],
-        vmem=60,
+        vmem=24,
         flops=2 * tokens * d * (d + 3 * f),
     )
 
@@ -634,22 +727,12 @@
 
 def gradient_kernel(lay, spot, normed, act, grad_pre, *refs):
     g, rows, d, f = lay.size, lay.rows, lay.width, lay.ff_share
-    down_m, down_c, blocks = refs[:g], refs[g : 2 * g], refs[2 * g : 2 * g + 2]
+    down_m, down_c, blocks = refs[:g], refs[g : 2 * g], refs[2 * g : 2 * g + 4]
     up_keep, up_give, down_keep, down_give, out_keep, out_give, gd, w_down, full, sems = refs[
-        2 * g + 2 :
+        2 * g + 4 :
     ]
     pairs = row_loads(lay, spot, down_m, down_c, gd)
-    count = 2 * lay.planes
-    for k in range(count):
-        source = blocks[k >= count // 2]
-        top, plane = block_spot(lay, spot, k, True)
-        start = (top * lay.planes + plane) * lay.piece
-        pairs.append(
-            (
-                source.at[k % (count // 2)],
-                w_down.at[pl.ds(pl.multiple_of(start, lay.piece), lay.piece), :],
-            )
-        )
+    pairs += down_loads(lay, spot, blocks, w_down)
     copies = load_all(pairs, sems)
     tile = 256
     for i in range(d // tile):
@@ -686,6 +769,7 @@
     outs += [shaped((g * rows, d), BF16)] * 2
     args = (spot, normed, act, grad_pre) + tuple(down_m) + tuple(down_c) + tuple(blocks)
     return kernel_call(
+        lay.order,
         functools.partial(gradient_kernel, lay),
         outs,
         *args,
@@ -698,14 +782,13 @@
             pltpu.VMEM((d, d), BF16),
             pltpu.SemaphoreType.DMA((2 * g + 2 * lay.planes,)),
         ],
-        vmem=60,
+        vmem=24,
         flops=2 * tokens * d * 3 * f,
     )
 
 
 def turn_kernel(lay, spot, vecs, keep, came, middle, grad_low, w_out, *refs):
-    pieces = refs[: lay.members]
-    grad_middle, grad_branch, sums, wo, att_grad, sems = refs[lay.members :]
+    keep_out, give_out, grad_middle, grad_branch, sums, wo, att_grad, sems = refs
     copies = load_all([(w_out, wo)], sems)
     normal, scale = centre(middle[...])
     slope = keep[...].astype(F32) + came[...].astype(F32)
@@ -721,16 +804,48 @@
     sums[3:4, :] = add(grad_low[...].astype(F32))
     wait_all(copies)
     att_grad[...] = dot(branch, wo[...], NT).astype(BF16)
+    hw = lay.share
+    for i in range(lay.size):
+        for ref, side in ((keep_out, spot[2]), (give_out, 1 - spot[2])):
+            start = pl.multiple_of((2 * i + side) * hw, hw)
+            ref[:, i * hw : (i + 1) * hw] = att_grad[:, pl.ds(start, hw)]
+
+
+def outer_kernel(spot, att, branch, keep, give):
+    tile, half = 256, keep.shape[1]
+
+    def write(side):
+        for i in range(keep.shape[0] // tile):
+            here = slice(i * tile, (i + 1) * tile)
+            value = dot(att[:, here], branch[...], TN).astype(BF16)
+            keep[here, :] = value[:, side * half : (side + 1) * half]
+            give[here, :] = value[:, (1 - side) * half : (2 - side) * half]
+
+    each_way(spot[2], write)
+
+
+def pick_kernel(lay, spot, mine, came, *pieces):
+    hw = lay.share
     for r in range(lay.members):
-        start = pl.multiple_of((spot[0] ^ r) * lay.share, lay.share)
-        pieces[r][...] = att_grad[:, pl.ds(start, lay.share)]
-
-
-def turn_call(lay, spot, vecs, keep, came, middle, grad_low, w_out, later):
+        chip = spot[0] ^ r
+        column = pl.ds(pl.multiple_of(chip % lay.size * hw, hw), hw)
+        own = chip // lay.size == spot[2]
+
+        @pl.when(own)
+        def _(r=r, column=column):
+            pieces[r][...] = mine[:, column]
+
+        @pl.when(jnp.logical_not(own))
+        def _(r=r, column=column):
+            pieces[r][...] = came[:, column]
+
+
+def turn_call(lay, spot, vecs, keep, came, middle, grad_low, w_out):
     d, rows = lay.width, lay.rows
-    outs = [shaped((rows, lay.share), BF16)] * lay.members
+    outs = [shaped((rows, d // 2), BF16)] * 2
     outs += [shaped((rows, d), F32), shaped((rows, d), BF16), shaped((8, d), F32)]
     return kernel_call(
+        lay.order,
         functools.partial(turn_kernel, lay),
         outs,
         spot,
@@ -748,15 +863,20 @@
             pltpu.VMEM((rows, d), BF16),
             pltpu.SemaphoreType.DMA((1,)),
         ],
-        vmem=60,
+        vmem=24,
         flops=2 * rows * d * d,
-        after=(later,),
     )
 
 
-def attend_back_kernel(lay, spot, bias, joint, wide, lse, normed, *refs):
-    m, rows, hw, length, head, d = lay.members, lay.rows, lay.share, lay.length, lay.head, lay.width
-    parts = refs[:m]
+def assemble_kernel(lay, spot, *refs):
+    out = refs[-1]
+    for r in range(lay.members):
+        start = pl.multiple_of((spot[0] ^ r) * lay.rows, lay.rows)
+        out[pl.ds(start, lay.rows), :] = refs[r][...]
+
+
+def attend_back_kernel(lay, spot, bias, joint, wide, lse, normed, slope_all, *refs):
+    rows, hw, length, head, d = lay.rows, lay.share, lay.length, lay.head, lay.width
     (
         grads_out,
         left_keep,
@@ -764,15 +884,11 @@
         right_keep,
         right_give,
         sums,
-        slope_all,
         key_sum,
         value_sum,
         query_t,
         full,
-    ) = refs[m:]
-    for r in range(m):
-        start = pl.multiple_of((spot[5] ^ r) * rows, rows)
-        slope_all[pl.ds(start, rows), :] = parts[r][...]
+    ) = refs
     earlier, same = key_mask_terms(rows)
     lane = iota((rows, LANES), 1)
     for p in range(hw // LANES):
@@ -824,12 +940,13 @@
     cut_rows(full.at[:, cut:], side, g * lay.planes, 2 * lay.each, right_keep, right_give)
 
 
-def attend_back(lay, spot, bias, joint, wide, lse, normed, parts, cut):
+def attend_back(lay, spot, bias, joint, wide, lse, normed, slope, cut):
     d, hw, length = lay.width, lay.share, lay.length
     outs = [shaped((length, 3 * hw), BF16)]
     outs += [shaped((d // 2, cut), BF16)] * 2 + [shaped((d // 2, 3 * hw - cut), BF16)] * 2
     outs += [shaped((1, 3 * hw), F32)]
     return kernel_call(
+        lay.order,
         functools.partial(attend_back_kernel, lay),
         outs,
         spot,
@@ -838,23 +955,22 @@
         wide,
         lse,
         normed,
-        *parts,
+        slope,
         name="attend_back",
         smem=(0,),
         scratch=[
-            pltpu.VMEM((length, hw), BF16),
             pltpu.VMEM((length, LANES), F32),
             pltpu.VMEM((length, LANES), F32),
             pltpu.VMEM((LANES, length), F32),
             pltpu.VMEM((d, 3 * hw), BF16),
         ],
-        vmem=60,
+        vmem=24,
         flops=2 * length * d * 3 * hw + 4 * length * length * d,
     )
 
 
 def input_kernel(
-    lay, spot, grads, w, x, sums_two, joint_sum, bias_up_sum, keep, give, sums, sums_low, vectors
+    lay, spot, grads, w, x, sums_two, joint_sum, bias_up_sum, keep, give, sums, sums_low
 ):
     rows, g, hw = lay.rows, lay.size, lay.share
     gain = jnp.zeros((1, lay.width), F32)
@@ -876,38 +992,63 @@
         def _():
             give[at, :] = low
 
-    vectors[...] = jnp.zeros_like(vectors)
-    vectors[0:1, :] = gain
-    vectors[1:2, :] = shift
+    sums[...] = jnp.zeros_like(sums)
+    sums[0:1, :] = gain
+    sums[1:2, :] = shift
     mine = pl.ds(pl.multiple_of(spot[5] * hw, hw), hw)
-    vectors[2:3, mine] = joint_sum[:, 0:hw]
-    vectors[3:4, mine] = joint_sum[:, 2 * hw :]
-    vectors[4:8, :] = sums_two[0:4, :]
-    each, piece, small = lay.each, lay.piece, lay.small
-    device, lane = iota((lay.devices, lay.width), 0), iota((lay.devices, lay.width), 1)
-    total = jnp.zeros((lay.devices, small), F32)
-    source, target = iota((lay.width, small), 0), iota((lay.width, small), 1)
-    for v in range(8):
-        value = jnp.where(lane // each == device, vectors[v : v + 1, :], 0.0)
-        move = (target == v * each + source % each).astype(F32)
-        total = total + jnp.dot(value, move, precision=lax.Precision.HIGHEST)
-    shape = (lay.devices, lay.ff_share)
-    device, lane = iota(shape, 0), iota(shape, 1)
-    plane, chip = device % lay.nt // 2, device // lay.nt
-    block = chip // lay.size * lay.planes + plane
-    here = (lane // piece == block) & (chip % lay.size == spot[4]) & (device % 2 == spot[2])
-    source, target = iota((lay.ff_share, small), 0), iota((lay.ff_share, small), 1)
-    move = (target == 8 * each + source % piece).astype(F32)
-    value = jnp.where(here, bias_up_sum[...], 0.0)
-    total = total + jnp.dot(value, move, precision=lax.Precision.HIGHEST)
-    sums[...] = total
-    sums_low[...] = total.astype(BF16)
+    sums[2:3, mine] = joint_sum[:, 0:hw]
+    sums[3:4, mine] = joint_sum[:, 2 * hw :]
+    sums[4:8, :] = sums_two[0:4, :]
+    piece = lay.piece
+
+    def write(m):
+        for b in range(2 * lay.planes):
+            at = up_column(lay, b, m)
+            line, column = 8 + at // lay.width, at % lay.width
+            sums[line : line + 1, column : column + piece] = bias_up_sum[:, b * piece : (b + 1) * piece]
+
+    for m in range(lay.members):
+        pl.when(spot[5] == m)(functools.partial(write, m))
+    sums_low[...] = sums[...].astype(BF16)
+
+
+SUM_ROWS = 16
+
+
+def up_column(lay, b, member):
+    top, plane = b // lay.planes, b % lay.planes
+    chip = top * lay.size + member // 2
+    return ((chip * lay.planes + plane) * 2 + member % 2) * lay.piece
+
+
+def sum_rows(width, columns):
+    return -(-width // columns) * SUM_ROWS
+
+
+def put_sums(ref, base, total):
+    width, columns = total.shape[1], ref.shape[1]
+    for k in range(-(-width // columns)):
+        part = total[:, k * columns : min(width, (k + 1) * columns)]
+        at = slice(base + k * SUM_ROWS, base + (k + 1) * SUM_ROWS)
+        if part.shape[1] < columns:
+            ref[at, :] = jnp.zeros((SUM_ROWS, columns), BF16)
+        ref[at, 0 : part.shape[1]] = part.astype(BF16)
+
+
+def take_sums(ref, base, width):
+    columns = ref.shape[1]
+    parts = []
+    for k in range(-(-width // columns)):
+        at = slice(base + k * SUM_ROWS, base + (k + 1) * SUM_ROWS)
+        parts.append(ref[at, 0 : min(columns, width - k * columns)].astype(F32))
+    return parts[0] if len(parts) == 1 else jnp.concatenate(parts, axis=1)
 
 
 def input_call(lay, spot, grads, w, x, sums_two, joint_sum, bias_up_sum):
     d, rows, g = lay.width, lay.rows, lay.size
-    small = (lay.devices, lay.small)
+    small = (SUM_ROWS, d)
     return kernel_call(
+        lay.order,
         functools.partial(input_kernel, lay),
         [shaped((g * rows, d), BF16)] * 2 + [shaped(small, F32), shaped(small, BF16)],
         spot,
@@ -919,8 +1060,7 @@
         bias_up_sum,
         name="input_slope",
         smem=(0,),
-        scratch=[pltpu.VMEM((8, d), F32)],
-        vmem=60,
+        vmem=24,
         flops=2 * lay.length * d * 3 * lay.share,
     )
 
@@ -947,11 +1087,12 @@
     fold_into(spot, cuts[1], two, two_came, two_keep, two_give)
 
 
-def two_fold(spot, cuts, one, one_came, two, two_came):
+def two_fold(lay, spot, cuts, one, one_came, two, two_came):
     outs = []
     for v in (one, two):
         outs += [shaped((v.shape[0] // 2, v.shape[1]), BF16)] * 2
     return kernel_call(
+        lay.order,
         functools.partial(two_fold_kernel, cuts),
         outs,
         spot,
@@ -967,40 +1108,39 @@
 def sums_fold_kernel(
     cuts, spot, one, one_came, two, two_came, sums, sums_came, one_keep, one_give, two_keep, two_give, sums_out
 ):
-    n, half = one.shape[0], one_keep.shape[0]
-    tall, small = sums.shape
-    came = one_came[n : n + tall, 0:small] if one_came.shape[0] > n else sums_came[...]
-    total = sums[...] + came.astype(F32)
+    n, half, width = one.shape[0], one_keep.shape[0], sums.shape[1]
+    if one_came.shape[0] > n:
+        came = take_sums(one_came, n, width)
+    else:
+        came = sums_came[...].astype(F32)
+    total = sums[...] + came
     sums_out[...] = total
     fold_into(spot, cuts[0], one, one_came, one_keep, one_give)
-    one_give[half : half + tall, :] = jnp.zeros((tall, one_give.shape[1]), BF16)
-    one_give[half : half + tall, 0:small] = total.astype(BF16)
+    put_sums(one_give, half, total)
     fold_into(spot, cuts[1], two, two_came, two_keep, two_give)
 
 
-def sums_fold(spot, cuts, one, one_came, two, two_came, sums, sums_came):
+def sums_fold(lay, spot, cuts, one, one_came, two, two_came, sums, sums_came):
     half, other = one.shape[0] // 2, two.shape[0] // 2
     outs = [
         shaped((half, one.shape[1]), BF16),
-        shaped((half + sums.shape[0], one.shape[1]), BF16),
+        shaped((half + sum_rows(sums.shape[1], one.shape[1]), one.shape[1]), BF16),
         shaped((other, two.shape[1]), BF16),
         shaped((other, two.shape[1]), BF16),
         shaped(sums.shape, F32),
     ]
     args = (spot, one, one_came, two, two_came, sums, sums_came)
     return kernel_call(
-        functools.partial(sums_fold_kernel, cuts), outs, *args, name="sums_fold", smem=(0,)
+        lay.order, functools.partial(sums_fold_kernel, cuts), outs, *args, name="sums_fold", smem=(0,)
     )
 
 
 def top_fold_kernel(shift, spot, one, one_came, two, two_came, sums, keep, give, sums_out):
     n, cut = one.shape
     half = n // 2
-    tall, small = sums.shape
-    total = sums[...] + one_came[n : n + tall, 0:small].astype(F32)
+    total = sums[...] + take_sums(one_came, n, sums.shape[1])
     sums_out[...] = total
-    give[half : half + tall, :] = jnp.zeros((tall, give.shape[1]), BF16)
-    give[half : half + tall, 0:small] = total.astype(BF16)
+    put_sums(give, half, total)
 
     def write(s):
         for here, x, y in ((slice(0, cut), one, one_came), (slice(cut, None), two, two_came)):
@@ -1027,11 +1167,10 @@
 def home_first_kernel(slot, shift, spot, w_in, w_in_came, w_up, w_up_came, sums, keep, give, sums_out):
     n, cut = w_in.shape
     half = n // 2
-    tall, small = sums.shape
-    total = sums[...] + w_in_came[n : n + tall, 0:small].astype(F32)
+    w_up_came = w_up_came.at[0] if len(w_up_came.shape) > len(w_up.shape) else w_up_came
+    total = sums[...] + take_sums(w_in_came, n, sums.shape[1])
     sums_out[...] = total
-    give[half : half + tall, :] = jnp.zeros((tall, give.shape[1]), BF16)
-    give[half : half + tall, 0:small] = total.astype(BF16)
+    put_sums(give, half, total)
 
     def write(s):
         for here, x, y in ((slice(0, cut), w_in, w_in_came), (slice(cut, None), w_up, w_up_came)):
@@ -1043,28 +1182,37 @@
     each_way((spot[slot] >> shift) & 1, write)
 
 
-def home_next_kernel(slot, shift, spot, mine, came, sums, keep, give, sums_out):
+def home_next_kernel(slot, shift, spot, mine, came, sums, *refs):
+    keep, give, sums_out = refs[-3:]
     n, columns = mine.shape
     half = n // 2
-    tall, small = sums.shape
-    total = sums[...] + came[n : n + tall, 0:small].astype(F32)
+    total = sums[...] + take_sums(came, max(n, 16), sums.shape[1])
     sums_out[...] = total
-    base = give.shape[0] - tall
-    give[base : base + tall, :] = jnp.zeros((tall, give.shape[1]), BF16)
-    give[base : base + tall, 0:small] = total.astype(BF16)
+    put_sums(give, max(half, 16), total)
 
     def write(s):
-        for here, x in ((slice(0, columns), mine), (slice(columns, None), came)):
+        for here, x in ((slice(0, columns), mine), (slice(columns, 2 * columns), came)):
             for ref, t in ((keep, s), (give, 1 - s)):
-                ref[0:half, here] = x[t * half : (t + 1) * half, :]
+                put_rows(ref, here, x, t * half, half)
+        if len(refs) > 3:
+            total = (refs[0][...].astype(F32) + refs[1][...].astype(F32)).astype(BF16)
+            for ref, t in ((keep, s), (give, 1 - s)):
+                put_rows(ref, slice(2 * columns, None), total, t * half, half)
 
     each_way((spot[slot] >> shift) & 1, write)
 
 
-def home_last_kernel(lay, spot, mine, came, sums, w_in, w_up, *vectors):
+def put_rows(ref, columns, source, start, count):
+    if count >= 16:
+        ref[0:count, columns] = source[start : start + count, :]
+        return
+    value = source[0:16, :].astype(F32)[start : start + count]
+    value = jnp.concatenate([value, jnp.zeros((16 - count, value.shape[1]), F32)], axis=0)
+    ref[0:16, columns] = value.astype(BF16)
+
+
+def home_last_kernel(lay, spot, mine, came, sums, w_in, w_up, w_out, *vectors):
     n = lay.each
-    tall = lay.devices
-    base = came.shape[0] - tall
     hw, piece, cut = lay.share, lay.piece, 3 * lay.share
     span = cut + lay.ff_share
     for f, ref in enumerate((mine, came)):
@@ -1078,26 +1226,42 @@
                 for i in range(3):
                     at = i * lay.width + m * hw
                     start = e * span + i * hw
-                    w_in[:, at : at + hw] = ref[0:n, start : start + hw].astype(F32)
+                    w_in[:, at : at + hw] = ref[0 : max(n, 16), start : start + hw].astype(F32)[0:n]
                 for b in range(2 * lay.planes):
-                    top, plane = b // lay.planes, b % lay.planes
-                    at = (((top * lay.size + m // 2) * lay.planes + plane) * 2 + m % 2) * piece
+                    at = up_column(lay, b, m)
                     start = e * span + cut + b * piece
-                    w_up[:, at : at + piece] = ref[0:n, start : start + piece].astype(F32)
+                    value = ref[0 : max(n, 16), start : start + piece].astype(F32)
+                    w_up[:, at : at + piece] = value[0:n]
 
             for m in range(lay.members):
                 pl.when(member == m)(functools.partial(write, m))
-    total = sums[...] + came[base : base + tall, 0 : lay.small].astype(F32)
-    own = jnp.where(iota(total.shape, 0) == spot[7], total, 0.0)
-    own = jnp.sum(own, axis=0, keepdims=True)
-    at = 0
-    for ref in vectors:
-        ref[...] = own[:, at : at + ref.shape[1]]
-        at += ref.shape[1]
+    half = lay.width // 2
+
+    def write_out(side):
+        for ref, s in ((mine, side), (came, 1 - side)):
+            at = ref.shape[1] - half
+            w_out[:, s * half : (s + 1) * half] = ref[0 : max(n, 16), at:].astype(F32)[0:n]
+
+    each_way(spot[2], write_out)
+    total = sums[...] + take_sums(came, max(n, 16), lay.width)
+
+    def part_of(start, count):
+        source, target = iota((lay.width, count), 0), iota((lay.width, count), 1)
+        move = (source == start + target).astype(F32)
+        return jnp.dot(total, move, precision=lax.Precision.HIGHEST)
+
+    own = part_of(spot[7] * n, n)
+    for v in range(8):
+        vectors[v][...] = own[v : v + 1, :]
+    first = spot[7] * piece
+    own = part_of(first % lay.width, piece)
+    line = iota(own.shape, 0) == 8 + first // lay.width
+    vectors[8][...] = jnp.sum(jnp.where(line, own, 0.0), axis=0, keepdims=True)
 
 
 def add_kernel(one, two, out):
-    out[...] = (one[...].astype(F32) + two[...].astype(F32)).astype(out.dtype)
+    other = two[1] if len(two.shape) > len(one.shape) else two[...]
+    out[...] = (one[...].astype(F32) + other.astype(F32)).astype(out.dtype)
 
 
 def last_kernel(spot, vecs, keep, came, sent, own, grad_middle, out):
@@ -1190,10 +1354,10 @@
             + [kept_group, kept_place]
         )
         away = lambda i: not at_home(i)
-        from_away = [(i, i ^ 1) for i in range(devices) if away(i)]
         across = [(i, mirror(i) ^ 1) for i in range(devices) if away(i)]
         mirrored = [(i, mirror(i)) for i in range(devices)]
 
+        call = functools.partial(kernel_call, lay.order)
         wide_in = 3 * group_size * share + 2 * group_size * lay.planes * piece
         row = lambda value: value.reshape(1, -1)
         vectors = [
@@ -1210,87 +1374,124 @@
                 up_bias,
             )
         ]
-        start = [input_weight, up_weight, key_mask] + vectors
+
+        def spread_group(values, who=None):
+            for b in group_bits:
+                values = values + [flip(v, b, who) for v in values]
+            return values
+
+        start = [input_weight, up_weight, key_mask, output_weight] + vectors
+        half = width // 2
         base = max(each, 16)
-        give, keep = kernel_call(
+        give, keep = call(
             functools.partial(pack_kernel, lay),
-            [shaped((base + EXTRA, wide_in), BF16)] * 2,
+            [shaped((base + EXTRA, wide_in + half), BF16)] * 2,
             spot,
             lengths,
             *start,
             name="pack",
             smem=(0, 1),
-            away=tuple(range(2, 14)),
+            away=tuple(range(2, 15)),
             vmem=60,
-            scratch=[pltpu.VMEM(v.shape, v.dtype) for v in start] + [pltpu.SemaphoreType.DMA((12,))],
+            scratch=[pltpu.VMEM(v.shape, v.dtype) for v in start] + [pltpu.SemaphoreType.DMA((13,))],
         )
         came_w = flip(give, 0)
         far = [send(own, across)]
+        near = spread_group([own])
+        downs = down_weight[None]
+        downs_came = flip(downs, plane_bits[-1])
+        grad_low = call(
+            mask_kernel,
+            [shaped((rows, width), BF16)],
+            spot,
+            lengths,
+            cotangent[0],
+            name="mask",
+            smem=(0, 1),
+        )[0]
         count = group_size
         for step, b in enumerate(group_bits):
             tall = (2 << step) * each
             columns = wide_in >> (step + 1)
-            give, keep, ready = kernel_call(
+            give, keep, ready = call(
                 functools.partial(trade_kernel, lay, step, count),
-                [shaped((tall + EXTRA, columns), BF16)] * 2 + [shaped((8, length), F32)],
+                [shaped((tall + EXTRA, columns + half), BF16)] * 2 + [shaped((8, length), F32)],
                 spot,
                 keep,
                 came_w,
                 name="trade",
                 smem=(0,),
-                scratch=[pltpu.VMEM((tall, 2 * columns), BF16)],
+                scratch=[pltpu.VMEM((tall, 2 * columns + half), BF16)],
+                after=(far[0], *near[1:], downs_came) if step == 0 else (),
             )
             valid = ready if step == 0 else valid
             came_w = flip(give, b)
             count //= 2
+        for b in reversed(plane_bits[:-1]):
+            downs = join(lay, downs, downs_came)
+            downs_came = flip(downs, b)
         tall = members * each
-        in_block, up_block, far_later = kernel_call(
+        paired = ff // members == width
+        up_tall = tall + tall * half // (ff // members)
+        in_block, ups, far_later, pair = call(
             functools.partial(settle_kernel, lay, len(group_bits)),
             [
                 shaped((tall + EXTRA, 3 * share), BF16),
-                shaped((tall, ff // members), BF16),
+                shaped((1, up_tall, ff // members), BF16),
                 shaped(own.shape, BF16),
+                shaped((up_tall + piece, width) if paired else (8, LANES), BF16),
             ],
             spot,
             keep,
             came_w,
             far[0],
+            down_weight,
             name="settle",
             smem=(0,),
-            scratch=[pltpu.VMEM((tall, 3 * share + ff // members), BF16)],
+            scratch=[pltpu.VMEM((tall, 3 * share + ff // members + half), BF16)],
         )
+        far = far + spread_group([far_later], away)[1:]
+        ups_first = ups
+        ups_came = flip(ups, plane_bits[0])
+        bundle = call(
+            functools.partial(bundle_kernel, group_size),
+            [shaped((2 * group_size * rows, width), BF16)],
+            spot,
+            *near,
+            *far,
+            name="bundle",
+            smem=(0,),
+            after=(downs_came,),
+        )[0]
+        rows_came = flip(bundle, 0)
         cut = max(LANES, 3 * share // 2 // LANES * LANES)
-        paired = up_block.shape == down_weight.shape
-
-        def spread_group(values, who=None):
-            for b in group_bits:
-                values = values + [flip(v, b, who) for v in values]
-            return values
-
-        left, right, up_block, down_block, own_later = kernel_call(
+        left, right, pair, grad_later = call(
             functools.partial(split_kernel, cut),
             [
                 shaped((2, tall + EXTRA, cut), BF16),
                 shaped((2, tall + EXTRA, 3 * share - cut), BF16),
-                shaped((2 if paired else 1,) + up_block.shape, BF16),
-                shaped((8, LANES) if paired else down_weight.shape, BF16),
-                shaped(own.shape, BF16),
+                shaped(pair.shape, BF16),
+                shaped(grad_low.shape, BF16),
             ],
             in_block,
             flip(in_block, top_bit),
-            up_block,
-            down_weight,
-            own,
+            pair,
+            grad_low,
             name="split",
+            after=(ups_came,),
         )
-        far = far + spread_group([far_later], away)[1:]
-        far_c = [send(v, from_away) for v in far]
-        for k, (b, c) in enumerate(zip(plane_bits, reversed(plane_bits), strict=True)):
+        left_came, right_came = flip(left, plane_bits[0]), flip(right, plane_bits[-1])
+        if paired:
+            pair_came = flip(pair, top_bit)
+        else:
+            up_far, down_far = flip(ups_first, top_bit), flip(down_weight, top_bit)[None]
+        down_m = [grad_low] + spread_group([grad_later])[1:]
+        for k, (b, c) in list(enumerate(zip(plane_bits, reversed(plane_bits), strict=True)))[1:]:
+            after = (rows_came,) if k == 1 else ()
+            left, right = stack(lay, left, left_came, right, right_came, *after)
             left_came, right_came = flip(left, b), flip(right, c)
-            if k + 1 < len(plane_bits):
-                left, right = stack(left, left_came, right, right_came, *far[1:2])
         in_pieces = (left, left_came, right, right_came)
-        vecs = kernel_call(
+        vecs = call(
             functools.partial(vector_kernel, lay),
             [shaped((16, width), F32)],
             spot,
@@ -1304,51 +1505,44 @@
                 pltpu.SemaphoreType.DMA((2 * lay.planes,)),
             ],
         )[0]
-
-        near = [own] + spread_group([own_later])[1:]
-        near_c = [flip(v, 0) for v in near]
-
-        if paired:
-            ups, downs = kernel_call(
-                unpair_kernel,
-                [shaped((2,) + v.shape, BF16) for v in up_block[:2]],
-                up_block,
-                flip(up_block, top_bit),
-                name="unpair",
-                after=(left, right),
-            )
-        else:
-            ups, downs = up_block, down_block[None]
-            ups, downs = stack(
-                ups, flip(ups, top_bit), downs, flip(downs, top_bit), left, right
-            )
-        ups_first = ups
-        for k, (b, c) in enumerate(zip(plane_bits, reversed(plane_bits), strict=True)):
-            ups_came, downs_came = flip(ups, b), flip(downs, c)
-            if k + 1 < len(plane_bits):
-                ups, downs = stack(ups, ups_came, downs, downs_came)
-        w_out = lax.all_gather(output_weight, AXES, axis=0, tiled=True)
-
-        grad_low = kernel_call(
-            mask_kernel,
-            [shaped((rows, width), BF16)],
-            spot,
-            lengths,
-            cotangent[0],
-            name="mask",
-            smem=(0, 1),
-            after=(near[1],),
-        )[0]
-        down_m = spread_group([grad_low])
-        down_c = [flip(v, 0) for v in down_m]
+        for b in plane_bits[1:]:
+            ups = join(lay, ups, ups_came)
+            ups_came = flip(ups, b)
 
         key_bias = jnp.where(valid[0] > 0.5, 0.0, MASKED).astype(F32).reshape(length, 1)
         near_att, far_att, joint, wide, lse, normed_one, x_all, w_in = attend(
-            lay, spot, key_bias, vecs, near + far + near_c + far_c, in_pieces, ups_first
+            lay, spot, key_bias, vecs, near + far + [rows_came], in_pieces
         )
-        far_att = spread_group([send(far_att, mirrored)])
+        far_att = [send(far_att, mirrored)]
         near_att = spread_group([near_att])
-        att_c = [flip(v, 0) for v in near_att + far_att]
+        att_c = [flip(near_att[0], 0)]
+
+        if paired:
+            up_far, down_far = call(
+                unpair_kernel,
+                [shaped((1, up_tall, width), BF16), shaped((1, piece, width), BF16)],
+                pair_came,
+                name="unpair",
+                after=(ups_came, *down_m[1:]),
+            )
+        out_shape = [shaped((lay.planes, tall, half), BF16)]
+        outs_w = []
+        for k, (b, c) in enumerate(zip(plane_bits, reversed(plane_bits), strict=True)):
+            if k:
+                up_far, down_far = stack(
+                    lay, up_far, up_far_came, down_far, down_far_came, att_c[0], outs_c
+                )
+            up_far_came, down_far_came = flip(up_far, b), flip(down_far, c)
+            if k == 0:
+                outs_w += call(out_kernel_rows, out_shape, ups, ups_came, name="out_rows")
+                outs_c = flip(outs_w[0], 0)
+        down_c = [flip(v, 0) for v in down_m]
+        far_att = spread_group(far_att)
+        att_c += [flip(v, 0) for v in near_att[1:] + far_att]
+        outs_w += call(out_kernel_rows, out_shape, up_far, up_far_came, name="out_rows")
+        out_blocks = (*outs_w, outs_c, flip(outs_w[1], 0))
+        up_blocks = (ups, ups_came, up_far, up_far_came)
+        down_blocks = (downs, downs_came, down_far, down_far_came)
 
         (
             dn_keep,
@@ -1359,61 +1553,21 @@
             act,
             grad_pre,
             d_bias_up,
+            w_out,
         ) = forward_call(
             lay,
             spot,
             vecs,
-            w_out,
-            near_att + far_att + att_c + near + near_c + down_m + down_c,
-            (ups, ups_came, downs, downs_came),
+            out_blocks,
+            near_att + far_att + att_c + near + down_m + down_c + [rows_came],
+            up_blocks + down_blocks,
         )
 
-        def reduce_group(keep, give, slot):
-            came = flip(give, 0)
+        def reduce_group(keep, came, slot):
             for k in reversed(range(len(group_bits))):
-                keep, give = fold(spot, slot, k, 1, keep, came)
+                keep, give = fold(lay, spot, slot, k, 1, keep, came)
                 came = flip(give, group_bits[k])
             return keep, came
-
-        dn_keep, dn_came = reduce_group(dn_keep, dn_give, 4)
-        up_keep, up_give, down_keep, down_give, out_keep, out_give = gradient_call(
-            lay, spot, normed_two, act, grad_pre, down_m, down_c, (downs, downs_came)
-        )
-        *slopes, grad_middle, grad_branch, sums_two = turn_call(
-            lay, spot, vecs, dn_keep, dn_came, middle, grad_low, w_out, up_give
-        )
-
-        parts = []
-        for r in range(members):
-
-            def route(i):
-                m = (i // nt) ^ r
-                return ((i % 2) * group_size + m // 2) * nt + (i % nt) - i % 2 + m % 2
-
-            parts.append(send(slopes[r], [(i, route(i)) for i in range(devices)]))
-        grad_joint, left_keep, left_give, right_keep, right_give, joint_sum = attend_back(
-            lay, spot, key_bias, joint, wide, lse, normed_one, parts, cut
-        )
-        in_keep, in_give, sums, sums_give = input_call(
-            lay, spot, grad_joint, w_in, x_all, sums_two, joint_sum, d_bias_up
-        )
-        in_keep, in_came = reduce_group(in_keep, in_give, 9)
-        in_sum = kernel_call(
-            add_kernel, [shaped((rows, width), BF16)], in_keep, in_came, name="add"
-        )[0]
-        input_gradient = kernel_call(
-            last_kernel,
-            [shaped((rows, width), BF16)],
-            spot,
-            vecs,
-            in_keep,
-            in_came,
-            send(in_sum, across),
-            own,
-            grad_middle,
-            name="input_gradient",
-            smem=(0,),
-        )[0]
 
         planes_down = list(reversed(plane_bits))
         top_shift = bits_of(group_size)
@@ -1425,23 +1579,81 @@
                 here.remove(b)
             return cuts
 
+        dn_keep, dn_came = reduce_group(dn_keep, flip(dn_give, 0), 4)
+        up_keep, up_give, down_keep, down_give, out_keep, out_give = gradient_call(
+            lay, spot, normed_two, act, grad_pre, down_m, down_c, down_blocks
+        )
+        up_came, down_came = flip(up_give, planes_down[0]), flip(down_give, plane_bits[0])
+        out_came = flip(out_give, 0)
+        slope_keep, slope_give, grad_middle, grad_branch, sums_two = turn_call(
+            lay, spot, vecs, dn_keep, dn_came, middle, grad_low, w_out
+        )
+        pieces = call(
+            functools.partial(pick_kernel, lay),
+            [shaped((rows, share), BF16)] * members,
+            spot,
+            slope_keep,
+            flip(slope_give, 0),
+            name="pick",
+            smem=(0,),
+        )
+        parts = [pieces[0]]
+        for r in range(1, members):
+            parts.append(send(pieces[r], [(i, i ^ (r * nt)) for i in range(devices)]))
+        o_keep, o_give = call(
+            outer_kernel,
+            [shaped((width, width // 2), BF16)] * 2,
+            spot,
+            att_own,
+            grad_branch,
+            name="output_gradient",
+            smem=(0,),
+        )
+        o_came = flip(o_give, 0)
+        out_keep, out_came = reduce_group(out_keep, out_came, 4)
+        out_cuts = [(4, k, 2) for k in reversed(range(len(group_bits)))]
+        out_cuts += cuts_of(2, planes_down) + [(0, top_shift, 1)]
+        out_bits = list(reversed(group_bits)) + planes_down + [top_bit]
+        out_steps = iter(range(len(out_bits)))
+
+        def next_out(keep, came, count=1):
+            for _ in range(count):
+                k = next(out_steps)
+                keep, give = fold(lay, spot, *out_cuts[k], keep, came)
+                came = flip(give, out_bits[k])
+            return keep, came
+
+        o_keep, o_came = next_out(o_keep, o_came)
+        slope = call(
+            functools.partial(assemble_kernel, lay),
+            [shaped((length, share), BF16)],
+            spot,
+            *parts,
+            name="assemble",
+            smem=(0,),
+        )[0]
         up_cuts, down_cuts = cuts_of(members, planes_down), cuts_of(2, plane_bits)
-        for k, (b, c) in enumerate(zip(planes_down, plane_bits, strict=True)):
-            up_came, down_came = flip(up_give, b), flip(down_give, c)
-            if k + 1 < len(plane_bits):
-                up_keep, up_give, down_keep, down_give = two_fold(
-                    spot,
-                    (up_cuts[k + 1], down_cuts[k + 1]),
-                    up_keep,
-                    up_came,
-                    down_keep,
-                    down_came,
-                )
+
+        def next_planes(k, up_keep, up_came, down_keep, down_came):
+            up_keep, up_give, down_keep, down_give = two_fold(
+                lay, spot, (up_cuts[k], down_cuts[k]), up_keep, up_came, down_keep, down_came
+            )
+            return up_keep, flip(up_give, planes_down[k]), down_keep, flip(down_give, plane_bits[k])
+
+        for k in range(1, len(plane_bits)):
+            up_keep, up_came, down_keep, down_came = next_planes(
+                k, up_keep, up_came, down_keep, down_came
+            )
+
+        grad_joint, left_keep, left_give, right_keep, right_give, joint_sum = attend_back(
+            lay, spot, key_bias, joint, wide, lse, normed_one, slope, cut
+        )
+        left_came, right_came = flip(left_give, planes_down[0]), flip(right_give, plane_bits[0])
         if paired:
-            half = (up_keep.shape[0] // 2, up_keep.shape[1])
-            up_keep, down_keep, give = kernel_call(
+            shape = (up_keep.shape[0] // 2, up_keep.shape[1])
+            up_keep, down_keep, give = call(
                 functools.partial(top_pair_kernel, top_shift),
-                [shaped(half, BF16), shaped(half, BF16), shaped((2,) + half, BF16)],
+                [shaped(shape, BF16), shaped(shape, BF16), shaped((2,) + shape, BF16)],
                 spot,
                 up_keep,
                 up_came,
@@ -1449,40 +1661,52 @@
                 down_came,
                 name="top_pair",
                 smem=(0,),
+                after=(o_came,),
             )
-            came = flip(give, top_bit)
-            up_came, down_came = came[0], came[1]
+            far_came = flip(give, top_bit)
         else:
             up_keep, up_give, down_keep, down_give = two_fold(
-                spot, ((0, top_shift, 1),) * 2, up_keep, up_came, down_keep, down_came
+                lay, spot, ((0, top_shift, 1),) * 2, up_keep, up_came, down_keep, down_came
             )
-            up_came, down_came = flip(up_give, top_bit), flip(down_give, top_bit)
-        d_down = kernel_call(
-            add_kernel, [shaped((piece, width), F32)], down_keep, down_came, name="add"
+            far_came = (flip(up_give, top_bit), flip(down_give, top_bit))
+        in_keep, in_give, sums, sums_give = input_call(
+            lay, spot, grad_joint, w_in, x_all, sums_two, joint_sum, d_bias_up
+        )
+        sums_came = flip(sums_give, planes_down[0])
+        in_came = flip(in_give, 0)
+        left_cuts, right_cuts = cuts_of(members, planes_down), cuts_of(members, plane_bits)
+        for k in range(1, len(plane_bits)):
+            left_keep, left_give, right_keep, right_give, sums = sums_fold(
+                lay,
+                spot,
+                (left_cuts[k], right_cuts[k]),
+                left_keep,
+                left_came,
+                right_keep,
+                right_came,
+                sums,
+                sums_came,
+            )
+            left_came, right_came = flip(left_give, planes_down[k]), flip(right_give, plane_bits[k])
+        in_keep, in_came = reduce_group(in_keep, in_came, 9)
+        o_keep, o_came = next_out(o_keep, o_came, len(group_bits))
+        layer_out = call(
+            out_kernel,
+            [shaped((rows, width), BF16)],
+            vecs,
+            middle,
+            out_keep,
+            out_came,
+            name="layer_out",
         )[0]
 
-        left_cuts, right_cuts = cuts_of(members, planes_down), cuts_of(members, plane_bits)
-        sums_came = flip(sums_give, planes_down[0])
-        for k, (b, c) in enumerate(zip(planes_down, plane_bits, strict=True)):
-            left_came, right_came = flip(left_give, b), flip(right_give, c)
-            if k + 1 < len(plane_bits):
-                left_keep, left_give, right_keep, right_give, sums = sums_fold(
-                    spot,
-                    (left_cuts[k + 1], right_cuts[k + 1]),
-                    left_keep,
-                    left_came,
-                    right_keep,
-                    right_came,
-                    sums,
-                    sums_came,
-                )
+        small = (SUM_ROWS, width)
         tall = left_keep.shape[0] // 2
-        small = (devices, lay.small)
-        w_keep, w_give, sums = kernel_call(
+        w_keep, w_give, sums = call(
             functools.partial(top_fold_kernel, top_shift),
             [
                 shaped((tall, 3 * share), BF16),
-                shaped((tall + devices, 3 * share), BF16),
+                shaped((tall + sum_rows(width, 3 * share), 3 * share), BF16),
                 shaped(small, F32),
             ],
             spot,
@@ -1494,18 +1718,26 @@
             name="top_fold",
             smem=(0,),
         )
-        came = flip(w_give, top_bit)
+        w_came = flip(w_give, top_bit)
+        in_sum = call(add_kernel, [shaped((rows, width), BF16)], in_keep, in_came, name="add")[0]
+        sent = send(in_sum, across)
+        o_keep, o_came = next_out(o_keep, o_came, len(plane_bits) - 1)
+        up_came, down_came = (far_came, far_came) if paired else far_came
+        d_down = call(
+            add_kernel, [shaped((piece, width), F32)], down_keep, down_came, name="add"
+        )[0]
+        came = w_came
         columns = 3 * share + ff // members
         steps = [(4, k, b) for k, b in reversed(list(enumerate(group_bits)))] + [(2, 0, 0)]
         for step, (slot, shift, b) in enumerate(steps):
             tall //= 2
             outs = [
-                shaped((tall, columns), BF16),
-                shaped((max(tall, 16) + devices, columns), BF16),
+                shaped((max(tall, 16), columns), BF16),
+                shaped((max(tall, 16) + sum_rows(width, columns), columns), BF16),
                 shaped(small, F32),
             ]
             if step == 0:
-                w_keep, w_give, sums = kernel_call(
+                w_keep, w_give, sums = call(
                     functools.partial(home_first_kernel, slot, shift),
                     outs,
                     spot,
@@ -1517,22 +1749,41 @@
                     name="home_first",
                     smem=(0,),
                 )
+                came = flip(w_give, b)
+                o_keep, o_came = next_out(o_keep, o_came)
+                input_gradient = call(
+                    last_kernel,
+                    [shaped((rows, width), BF16)],
+                    spot,
+                    vecs,
+                    in_keep,
+                    in_came,
+                    sent,
+                    own,
+                    grad_middle,
+                    name="input_gradient",
+                    smem=(0,),
+                )[0]
             else:
-                w_keep, w_give, sums = kernel_call(
+                final = (o_keep, o_came) if b == 0 else ()
+                if final:
+                    outs = [shaped((v.shape[0], columns + width // 2), BF16) for v in outs[:2]] + outs[2:]
+                w_keep, w_give, sums = call(
                     functools.partial(home_next_kernel, slot, shift),
                     outs,
                     spot,
                     w_keep,
                     came,
                     sums,
+                    *final,
                     name="home_next",
                     smem=(0,),
                 )
-            came = flip(w_give, b)
+                came = flip(w_give, b)
             columns *= 2
-        d_in, d_up, *vectors = kernel_call(
+        d_in, d_up, d_out, *vectors = call(
             functools.partial(home_last_kernel, lay),
-            [shaped((each, 3 * width), F32), shaped((each, ff), F32)]
+            [shaped((each, 3 * width), F32), shaped((each, ff), F32), shaped((each, width), F32)]
             + [shaped((1, each), F32)] * 8
             + [shaped((1, piece), F32)],
             spot,
@@ -1543,21 +1794,6 @@
             smem=(0,),
         )
         vectors = [v.reshape(-1) for v in vectors]
-
-        d_out = dot(att_own, grad_branch, TN).astype(BF16)
-        d_out = lax.psum_scatter(d_out, AXES, scatter_dimension=0, tiled=True).astype(F32)
-
-        out_keep, out_came = reduce_group(out_keep, out_give, 4)
-        layer_out = kernel_call(
-            out_kernel,
-            [shaped((rows, width), BF16)],
-            vecs,
-            middle,
-            out_keep,
-            out_came,
-            name="layer_out",
-        )[0]
-
         return (
             layer_out[None],
             input_gradient[None],

time: 373 us -> 308 us (0.83)
  waiting for transfers between devices: 167 us -> 113 us
  starting transfers between devices: 55.2 us -> 73.9 us
  between operations: 15.8 us -> 2.4 us
  local copies, waits for them, and re-layouts: 16.8 us -> 3.59 us
    ppermute x53 -> x61, waiting for transfers between devices: 166 us -> 113 us  [send(): return lax.ppermute(value, AXES, route)]
    ppermute x53 -> x61, starting transfers between devices: 55.1 us -> 73.9 us  [send(): return lax.ppermute(value, AXES, route)]
    unnamed x104 -> x66, local copies, waits for them, and re-layouts: 11.2 us -> 2.14 us
    pallas_call x29 -> x41, Pallas kernels: 110 us -> 111 us  [kernel_call(): pl.pallas_call(body, in_specs=ins, out_specs=[spec(i, ()) for i in range(...]
  transfers between devices with their start and end apart: 55 -> 61, of which waited for: 23 -> 28; matrix products, arithmetic and copies ran while one was open for 2% -> 0% of each run, Pallas kernels for 23% -> 27%
where the time goes in v3:
time: 308 us; the launch traced here: 304 us
  waiting for transfers between devices  113 us (37%)
  Pallas kernels  111 us (36%)
  starting transfers between devices  73.9 us (24%)
  local copies, waits for them, and re-layouts  3.59 us (1%)
    ppermute x61, waiting for transfers between devices, send(): return lax.ppermute(value, AXES, route)  113 us
    pallas_call x41, Pallas kernels, kernel_call(): pl.pallas_call(body, in_specs=ins, out_specs=[spec(i, ()) for i in range(...  111 us
    ppermute x61, starting transfers between devices, send(): return lax.ppermute(value, AXES, route)  73.9 us
  transfers between devices with their start and end apart: 61, of which 28 were waited for; matrix products, arithmetic and copies ran while one was open for 0% of the time, Pallas kernels for 27%

profile of v3, /device:TPU:0, one launch (start us, length us, event | category | flops | bytes accessed | tf_op | source)
XLA Modules:
  0.0 303.6 jit_solution(17791830072927296279)
XLA Ops:
  0.6 3.1 %collective-permute-start.2 = (bf16[256,1024]{1,0:T(8,128)(2,1)}, bf16[256,1024]{1,0:T(8,128)(2,1)}, u32[]{:S(2)}, u32[]{:S(2)}) collective-permute-start(bf16[256,1024]{1,0:T(8,128)(2,1)} %bitcast.36), channel_id=1, source_target_pairs={{0,8},{1,9},{2,10},{3,11},{4,12},{5,13},{6,14},{7,15},{8,0},{9,1},... | collective-permute-start | bytes 1572872 | tf_op jit(solution)/shard_map/ppermute | solution.py:1293
  8.6 3.1 %pack.1 = (bf16[48,4096]{1,0:T(8,128)(2,1)}, bf16[48,4096]{1,0:T(8,128)(2,1)}, f32[8,128]{1,0:T(8,128)}) custom-call(s32[10]{0:T(128)} %stack.49.refs_0_, s32[1]{0:T(128)S(6)} %copy.34.refs_1_, bf16[32,3072]{1,0:T(8,128)(2,1)} %refs_2_.1, bf16[32,4096]{1,0:T(8,128)(2,1)} %refs_3_.1, s32[1,1024]{1,0:T(1,128)} %refs_4_.2, bf16[32,1024]{1,0:T(8,128)(2,1)} %refs_5_.1, ...), custom_call_target="tpu_custom_call" | custom-call | flops 99999997952 | bytes 1 | tf_op jit(solution)/shard_map/pack/pallas_call | solution.py:106
  22.1 5.8 %collective-permute-done.4.refs_2_ = bf16[80,2304]{1,0:T(8,128)(2,1)S(1)} collective-permute-done((bf16[80,2304]{1,0:T(8,128)(2,1)S(1)}, bf16[80,2304]{1,0:T(8,128)(2,1)S(1)}, u32[]{:S(2)}, u32[]{:S(2)}) %collective-permute-start.4) | collective-permute-done | bytes 368672 | tf_op jit(solution)/shard_map/ppermute | solution.py:1293
  29.9 8.6 %collective-permute-start.5 = (bf16[144,768]{1,0:T(8,128)(2,1)S(1)}, bf16[144,768]{1,0:T(8,128)(2,1)S(1)}, u32[]{:S(2)}, u32[]{:S(2)}) collective-permute-start(bf16[144,768]{1,0:T(8,128)(2,1)S(1)} %get-tuple-element.185.refs_0_), channel_id=1, source_target_pairs={{0,16},{1,17},{2,18},{3,19},{4,20},{5,21},{6,22},{7,23},{8,24},{9,... | collective-permute-start | bytes 663560 | tf_op jit(solution)/shard_map/ppermute | solution.py:1293
  41.7 9.7 %collective-permute-start.11 = (bf16[1024,1024]{1,0:T(8,128)(2,1)S(1)}, bf16[1024,1024]{1,0:T(8,128)(2,1)S(1)}, u32[]{:S(2)}, u32[]{:S(2)}) collective-permute-start(bf16[1024,1024]{1,0:T(8,128)(2,1)S(1)} %get-tuple-element.195), channel_id=1, source_target_pairs={{0,1},{1,0},{2,3},{3,2},{4,5},{5,4},{6,7},{7,6},{8,9},{9,8},{10,11... | collective-permute-start | bytes 6291464 | tf_op jit(solution)/shard_map/ppermute | solution.py:1293
  55.6 4.3 %collective-permute-done.9.refs_1_ = bf16[2,144,384]{2,1,0:T(8,128)(2,1)S(1)} collective-permute-done((bf16[2,144,384]{2,1,0:T(8,128)(2,1)S(1)}, bf16[2,144,384]{2,1,0:T(8,128)(2,1)S(1)}, u32[]{:S(2)}, u32[]{:S(2)}) %collective-permute-start.9) | collective-permute-done | bytes 221216 | tf_op jit(solution)/shard_map/ppermute | solution.py:1293
  68.1 5.5 %collective-permute-done.12.refs_2_.refs_9_ = bf16[4,144,384]{2,1,0:T(8,128)(2,1)S(1)} collective-permute-done((bf16[4,144,384]{2,1,0:T(8,128)(2,1)S(1)}, bf16[4,144,384]{2,1,0:T(8,128)(2,1)S(1)}, u32[]{:S(2)}, u32[]{:S(2)}) %collective-permute-start.12) | collective-permute-done | bytes 442400 | tf_op jit(solution)/shard_map/ppermute | solution.py:1293
  78.5 13.3 %attend.1 = (bf16[512,256]{1,0:T(8,128)(2,1)S(1)}, bf16[512,256]{1,0:T(8,128)(2,1)S(1)}, bf16[1024,768]{1,0:T(8,128)(2,1)S(1)}, f32[256,1024]{1,0:T(8,128)S(1)},...) custom-call(s32[10]{0:T(128)S(1)} %copy-done.1, ...), custom_call_target="tpu_custom_call" | custom-call | flops 99999997952 | bytes 1 | tf_op jit(solution)/shard_map/attend/pallas_call | solution.py:106
  91.9 3.8 %collective-permute-done.14.refs_0_ = bf16[320,1024]{1,0:T(8,128)(2,1)} collective-permute-done((bf16[320,1024]{1,0:T(8,128)(2,1)}, bf16[320,1024]{1,0:T(8,128)(2,1)}, u32[]{:S(2)}, u32[]{:S(2)}) %collective-permute-start.14) | collective-permute-done | bytes 655392 | tf_op jit(solution)/shard_map/ppermute | solution.py:1293
  100.2 7.2 %collective-permute-done.18.refs_3_ = bf16[1,128,1024]{2,1,0:T(8,128)(2,1)S(1)} collective-permute-done((bf16[1,128,1024]{2,1,0:T(8,128)(2,1)S(1)}, bf16[1,128,1024]{2,1,0:T(8,128)(2,1)S(1)}, u32[]{:S(2)}, u32[]{:S(2)}) %collective-permute-start.18) | collective-permute-done | bytes 262176 | tf_op jit(solution)/shard_map/ppermute | solution.py:1293
  113.2 8.1 %collective-permute-done.24.refs_8_ = bf16[512,256]{1,0:T(8,128)(2,1)S(1)} collective-permute-done((bf16[512,256]{1,0:T(8,128)(2,1)S(1)}, bf16[512,256]{1,0:T(8,128)(2,1)S(1)}, u32[]{:S(2)}, u32[]{:S(2)}) %collective-permute-start.24) | collective-permute-done | bytes 262176 | tf_op jit(solution)/shard_map/ppermute | solution.py:1293
  123.2 5.8 %collective-permute-done.21.refs_1_.refs_24_ = bf16[2,192,1024]{2,1,0:T(8,128)(2,1)S(1)} collective-permute-done((bf16[2,192,1024]{2,1,0:T(8,128)(2,1)S(1)}, bf16[2,192,1024]{2,1,0:T(8,128)(2,1)S(1)}, u32[]{:S(2)}, u32[]{:S(2)}) %collective-permute-start.21) | collective-permute-done | bytes 786464 | tf_op jit(solution)/shard_map/ppermute | solution.py:1293
  132.7 8.8 %collective-permute-done.31.refs_28_.refs_11_ = bf16[2,128,1024]{2,1,0:T(8,128)(2,1)S(1)} collective-permute-done((bf16[2,128,1024]{2,1,0:T(8,128)(2,1)S(1)}, bf16[2,128,1024]{2,1,0:T(8,128)(2,1)S(1)}, u32[]{:S(2)}, u32[]{:S(2)}) %collective-permute-start.31) | collective-permute-done | bytes 524320 | tf_op jit(solution)/shard_map/ppermute | solution.py:1293
  141.6 18.9 %feed_forward.1 = (bf16[512,1024]{1,0:T(8,128)(2,1)S(1)}, bf16[512,1024]{1,0:T(8,128)(2,1)S(1)}, f32[256,1024]{1,0:T(8,128)S(1)}, bf16[256,1024]{1,0:T(8,128)(2,...) custom-call(s32[10]{0:T(128)S(1)} %copy-done.1, ...), custom_call_target="tpu_custom_call" | custom-call | flops 99999997952 | bytes 1 | tf_op jit(solution)/shard_map/feed_forward/pallas_call | solution.py:106
  164.4 10.7 %gradients.1 = (bf16[512,1024]{1,0:T(8,128)(2,1)S(1)}, bf16[512,1024]{1,0:T(8,128)(2,1)}, bf16[512,1024]{1,0:T(8,128)(2,1)S(1)}, bf16[512,1024]{1,0:T(8,128)(2,1...) custom-call(s32[10]{0:T(128)S(1)} %copy-done.1, ...), custom_call_target="tpu_custom_call" | custom-call | flops 99999997952 | bytes 1 | tf_op jit(solution)/shard_map/gradients/pallas_call | solution.py:106
  175.2 3.2 %collective-permute-done.34.refs_3_ = bf16[256,1024]{1,0:T(8,128)(2,1)S(1)} collective-permute-done((bf16[256,1024]{1,0:T(8,128)(2,1)S(1)}, bf16[256,1024]{1,0:T(8,128)(2,1)S(1)}, u32[]{:S(2)}, u32[]{:S(2)}) %collective-permute-start.34) | collective-permute-done | bytes 524320 | tf_op jit(solution)/shard_map/ppermute | solution.py:1293
  194.5 4.9 %collective-permute-done.41.refs_4_ = bf16[256,256]{1,0:T(8,128)(2,1)S(1)} collective-permute-done((bf16[256,256]{1,0:T(8,128)(2,1)S(1)}, bf16[256,256]{1,0:T(8,128)(2,1)S(1)}, u32[]{:S(2)}, u32[]{:S(2)}) %collective-permute-start.41) | collective-permute-done | bytes 131104 | tf_op jit(solution)/shard_map/ppermute | solution.py:1293
  200.4 6.6 %collective-permute-done.42.refs_2_ = bf16[512,1024]{1,0:T(8,128)(2,1)} collective-permute-done((bf16[512,1024]{1,0:T(8,128)(2,1)}, bf16[512,1024]{1,0:T(8,128)(2,1)}, u32[]{:S(2)}, u32[]{:S(2)}) %collective-permute-start.42) | collective-permute-done | bytes 1048608 | tf_op jit(solution)/shard_map/ppermute | solution.py:1293
  211.5 12.0 %attend_back.1 = (bf16[1024,768]{1,0:T(8,128)(2,1)S(1)}, bf16[512,384]{1,0:T(8,128)(2,1)S(1)}, bf16[512,384]{1,0:T(8,128)(2,1)}, bf16[512,384]{1,0:T(8,128)(2,1)...) custom-call(s32[10]{0:T(128)S(1)} %copy-done.1, f32[1024,1]{1,0:T(8,128)S(1)} %copy.32.refs_1_, ...), custom_call_target="tpu_custom_call" | custom-call | flops 99999997952 | bytes 1 | tf_op jit(solution)/shard_map/attend_back/pallas_call | solution.py:106
  227.3 3.5 %input_slope.1 = (bf16[512,1024]{1,0:T(8,128)(2,1)S(1)}, bf16[512,1024]{1,0:T(8,128)(2,1)S(1)}, f32[16,1024]{1,0:T(8,128)S(1)}, bf16[16,1024]{1,0:T(8,128)(2,1)S(1)}, f32[8,128]{1,0:T(8,128)S(1)}) custom-call(s32[10]{0:T(128)S(1)} %copy-done.1, bf16[1024,768]{1,0:T(8,128)(2,1)S(1)} %get-tuple-element.264.refs_1_, ...), custom_call_target="tpu_custom_call" | custom-call | flops 99999997952 | bytes 1 | tf_op jit(solution)/shard_map/input_slope/pallas_call | solution.py:106
  242.6 13.8 %collective-permute-done.36.refs_3_ = bf16[256,1024]{1,0:T(8,128)(2,1)} collective-permute-done((bf16[256,1024]{1,0:T(8,128)(2,1)}, bf16[256,1024]{1,0:T(8,128)(2,1)}, u32[]{:S(2)}, u32[]{:S(2)}) %collective-permute-start.36) | collective-permute-done | bytes 524320 | tf_op jit(solution)/shard_map/ppermute | solution.py:1293
  261.5 10.4 %collective-permute-done.50.refs_1_.refs_3_ = bf16[256,1024]{1,0:T(8,128)(2,1)} collective-permute-done((bf16[256,1024]{1,0:T(8,128)(2,1)}, bf16[256,1024]{1,0:T(8,128)(2,1)}, u32[]{:S(2)}, u32[]{:S(2)}) %collective-permute-start.50) | collective-permute-done | bytes 524320 | tf_op jit(solution)/shard_map/ppermute | solution.py:1293
  280.6 3.3 %collective-permute-start.59 = (bf16[64,512]{1,0:T(8,128)(2,1)S(1)}, bf16[64,512]{1,0:T(8,128)(2,1)S(1)}, u32[]{:S(2)}, u32[]{:S(2)}) collective-permute-start(bf16[64,512]{1,0:T(8,128)(2,1)S(1)} %get-tuple-element.320), channel_id=1, source_target_pairs={{0,16},{1,17},{2,18},{3,19},{4,20},{5,21},{6,22},{7,23},{8,24},{9,... | collective-permute-start | bytes 196616 | tf_op jit(solution)/shard_map/ppermute | solution.py:1293
  286.7 11.7 %collective-permute-done.59.refs_5_ = bf16[64,512]{1,0:T(8,128)(2,1)S(1)} collective-permute-done((bf16[64,512]{1,0:T(8,128)(2,1)S(1)}, bf16[64,512]{1,0:T(8,128)(2,1)S(1)}, u32[]{:S(2)}, u32[]{:S(2)}) %collective-permute-start.59) | collective-permute-done | bytes 65568 | tf_op jit(solution)/shard_map/ppermute | solution.py:1293
  (209 shorter events, 114.9 us)
Async XLA Ops:
  0.6 15.7 %collective-permute-start.2 = (bf16[256,1024]{1,0:T(8,128)(2,1)}, bf16[256,1024]{1,0:T(8,128)(2,1)}, u32[]{:S(2)}, u32[]{:S(2)}) collective-permute-start(bf16[256,1024]{1,0:T(8,128)(2,1)} %bitcast.36), channel_id=1, source_target_pairs={{0,8},{1,9},{2,10},{3,11},{4,12},{5,13},{6,14},{7,15},{8,0},{9,1},... | collective-permute-start | bytes 1572872 | tf_op jit(solution)/shard_map/ppermute | solution.py:1293
  20.6 19.4 %collective-permute-start.8 = (bf16[2,128,1024]{2,1,0:T(8,128)(2,1)S(1)}, bf16[2,128,1024]{2,1,0:T(8,128)(2,1)S(1)}, u32[]{:S(2)}, u32[]{:S(2)}) collective-permute-start(bf16[2,128,1024]{2,1,0:T(8,128)(2,1)S(1)} %get-tuple-element.190.refs_25_.refs_8_), channel_id=1, source_target_pairs={{0,2},{1,3},{2,0},{3,1},{4,6},{5,7},{6,4},{7,5},{8,10},{9,11},{10,... | collective-permute-start | bytes 1572872 | tf_op jit(solution)/shard_map/ppermute | solution.py:1293
  29.9 21.5 %collective-permute-start.5 = (bf16[144,768]{1,0:T(8,128)(2,1)S(1)}, bf16[144,768]{1,0:T(8,128)(2,1)S(1)}, u32[]{:S(2)}, u32[]{:S(2)}) collective-permute-start(bf16[144,768]{1,0:T(8,128)(2,1)S(1)} %get-tuple-element.185.refs_0_), channel_id=1, source_target_pairs={{0,16},{1,17},{2,18},{3,19},{4,20},{5,21},{6,22},{7,23},{8,24},{9,... | collective-permute-start | bytes 663560 | tf_op jit(solution)/shard_map/ppermute | solution.py:1293
  41.7 19.5 %collective-permute-start.11 = (bf16[1024,1024]{1,0:T(8,128)(2,1)S(1)}, bf16[1024,1024]{1,0:T(8,128)(2,1)S(1)}, u32[]{:S(2)}, u32[]{:S(2)}) collective-permute-start(bf16[1024,1024]{1,0:T(8,128)(2,1)S(1)} %get-tuple-element.195), channel_id=1, source_target_pairs={{0,1},{1,0},{2,3},{3,2},{4,5},{5,4},{6,7},{7,6},{8,9},{9,8},{10,11... | collective-permute-start | bytes 6291464 | tf_op jit(solution)/shard_map/ppermute | solution.py:1293
  64.5 27.4 %collective-permute-start.15 = (bf16[256,1024]{1,0:T(8,128)(2,1)}, bf16[256,1024]{1,0:T(8,128)(2,1)}, u32[]{:S(2)}, u32[]{:S(2)}) collective-permute-start(bf16[256,1024]{1,0:T(8,128)(2,1)} %get-tuple-element.203), channel_id=1, source_target_pairs={{0,8},{1,9},{2,10},{3,11},{4,12},{5,13},{6,14},{7,15},{8,0},{9,1},... | collective-permute-start | bytes 1572872 | tf_op jit(solution)/shard_map/ppermute | solution.py:1293
  64.5 31.2 %collective-permute-start.14 = (bf16[320,1024]{1,0:T(8,128)(2,1)}, bf16[320,1024]{1,0:T(8,128)(2,1)}, u32[]{:S(2)}, u32[]{:S(2)}) collective-permute-start(bf16[320,1024]{1,0:T(8,128)(2,1)} %get-tuple-element.202), channel_id=1, source_target_pairs={{0,16},{1,17},{2,18},{3,19},{4,20},{5,21},{6,22},{7,23},{8,24},{9,... | collective-permute-start | bytes 1966088 | tf_op jit(solution)/shard_map/ppermute | solution.py:1293
  75.7 20.0 %collective-permute-start.13 = (bf16[2,192,1024]{2,1,0:T(8,128)(2,1)S(1)}, bf16[2,192,1024]{2,1,0:T(8,128)(2,1)S(1)}, u32[]{:S(2)}, u32[]{:S(2)}) collective-permute-start(bf16[2,192,1024]{2,1,0:T(8,128)(2,1)S(1)} %get-tuple-element.201.refs_0_.refs_21_), channel_id=1, source_target_pairs={{0,4},{1,5},{2,6},{3,7},{4,0},{5,1},{6,2},{7,3},{8,12},{9,13},{10,... | collective-permute-start | bytes 2359304 | tf_op jit(solution)/shard_map/ppermute | solution.py:1293
  109.7 19.2 %collective-permute-start.21 = (bf16[2,192,1024]{2,1,0:T(8,128)(2,1)S(1)}, bf16[2,192,1024]{2,1,0:T(8,128)(2,1)S(1)}, u32[]{:S(2)}, u32[]{:S(2)}) collective-permute-start(bf16[2,192,1024]{2,1,0:T(8,128)(2,1)S(1)} %get-tuple-element.214.refs_0_.refs_23_), channel_id=1, source_target_pairs={{0,4},{1,5},{2,6},{3,7},{4,0},{5,1},{6,2},{7,3},{8,12},{9,13},{10,... | collective-permute-start | bytes 2359304 | tf_op jit(solution)/shard_map/ppermute | solution.py:1293
  112.7 16.9 %collective-permute-start.29 = (bf16[256,1024]{1,0:T(8,128)(2,1)S(1)}, bf16[256,1024]{1,0:T(8,128)(2,1)S(1)}, u32[]{:S(2)}, u32[]{:S(2)}) collective-permute-start(bf16[256,1024]{1,0:T(8,128)(2,1)S(1)} %copy-done.15), channel_id=1, source_target_pairs={{0,1},{1,0},{2,3},{3,2},{4,5},{5,4},{6,7},{7,6},{8,9},{9,8},{10,11... | collective-permute-start | bytes 1572872 | tf_op jit(solution)/shard_map/ppermute | solution.py:1293
  112.7 17.0 %collective-permute-start.30 = (bf16[256,1024]{1,0:T(8,128)(2,1)}, bf16[256,1024]{1,0:T(8,128)(2,1)S(1)}, u32[]{:S(2)}, u32[]{:S(2)}) collective-permute-start(bf16[256,1024]{1,0:T(8,128)(2,1)} %collective-permute-done.15.refs_2_.refs_17_.refs_5_), channel_id=1, source_target_pairs={{0,1},{1,0},{2,3},{3,2},{4,5},{5,4},{6,7},{7,6},{8,9},{9,8},{10,11... | collective-permute-start | bytes 1572872 | tf_op jit(solution)/shard_map/ppermute | solution.py:1293
  113.2 17.0 %collective-permute-start.23 = (bf16[512,256]{1,0:T(8,128)(2,1)S(1)}, bf16[512,256]{1,0:T(8,128)(2,1)S(1)}, u32[]{:S(2)}, u32[]{:S(2)}) collective-permute-start(bf16[512,256]{1,0:T(8,128)(2,1)S(1)} %get-tuple-element.212.refs_6_), channel_id=1, source_target_pairs={{0,8},{1,9},{2,10},{3,11},{4,12},{5,13},{6,14},{7,15},{8,0},{9,1},... | collective-permute-start | bytes 786440 | tf_op jit(solution)/shard_map/ppermute | solution.py:1293
  181.5 25.5 %collective-permute-start.42 = (bf16[512,1024]{1,0:T(8,128)(2,1)}, bf16[512,1024]{1,0:T(8,128)(2,1)}, u32[]{:S(2)}, u32[]{:S(2)}) collective-permute-start(bf16[512,1024]{1,0:T(8,128)(2,1)} %get-tuple-element.259), channel_id=1, source_target_pairs={{0,4},{1,5},{2,6},{3,7},{4,0},{5,1},{6,2},{7,3},{8,12},{9,13},{10,... | collective-permute-start | bytes 3145736 | tf_op jit(solution)/shard_map/ppermute | solution.py:1293
  182.1 25.2 %collective-permute-start.43 = (bf16[512,1024]{1,0:T(8,128)(2,1)}, bf16[512,1024]{1,0:T(8,128)(2,1)}, u32[]{:S(2)}, u32[]{:S(2)}) collective-permute-start(bf16[512,1024]{1,0:T(8,128)(2,1)} %get-tuple-element.261), channel_id=1, source_target_pairs={{0,2},{1,3},{2,0},{3,1},{4,6},{5,7},{6,4},{7,5},{8,10},{9,11},{10,... | collective-permute-start | bytes 3145736 | tf_op jit(solution)/shard_map/ppermute | solution.py:1293
  194.5 31.0 %collective-permute-start.38 = (bf16[512,512]{1,0:T(8,128)(2,1)}, bf16[512,512]{1,0:T(8,128)(2,1)}, u32[]{:S(2)}, u32[]{:S(2)}) collective-permute-start(bf16[512,512]{1,0:T(8,128)(2,1)} %get-tuple-element.247), channel_id=1, source_target_pairs={{0,8},{1,9},{2,10},{3,11},{4,12},{5,13},{6,14},{7,15},{8,0},{9,1},... | collective-permute-start | bytes 1572872 | tf_op jit(solution)/shard_map/ppermute | solution.py:1293
  209.3 16.2 %collective-permute-start.44 = (bf16[256,1024]{1,0:T(8,128)(2,1)S(1)}, bf16[256,1024]{1,0:T(8,128)(2,1)S(1)}, u32[]{:S(2)}, u32[]{:S(2)}) collective-permute-start(bf16[256,1024]{1,0:T(8,128)(2,1)S(1)} %get-tuple-element.271), channel_id=1, source_target_pairs={{0,2},{1,3},{2,0},{3,1},{4,6},{5,7},{6,4},{7,5},{8,10},{9,11},{10,... | collective-permute-start | bytes 1572872 | tf_op jit(solution)/shard_map/ppermute | solution.py:1293
  210.0 15.5 %collective-permute-start.45 = (bf16[256,1024]{1,0:T(8,128)(2,1)S(1)}, bf16[256,1024]{1,0:T(8,128)(2,1)S(1)}, u32[]{:S(2)}, u32[]{:S(2)}) collective-permute-start(bf16[256,1024]{1,0:T(8,128)(2,1)S(1)} %get-tuple-element.273), channel_id=1, source_target_pairs={{0,4},{1,5},{2,6},{3,7},{4,0},{5,1},{6,2},{7,3},{8,12},{9,13},{10,... | collective-permute-start | bytes 1572872 | tf_op jit(solution)/shard_map/ppermute | solution.py:1293
  232.4 24.0 %collective-permute-start.36 = (bf16[256,1024]{1,0:T(8,128)(2,1)}, bf16[256,1024]{1,0:T(8,128)(2,1)}, u32[]{:S(2)}, u32[]{:S(2)}) collective-permute-start(bf16[256,1024]{1,0:T(8,128)(2,1)} %get-tuple-element.242), channel_id=1, source_target_pairs={{0,8},{1,9},{2,10},{3,11},{4,12},{5,13},{6,14},{7,15},{8,0},{9,1},... | collective-permute-start | bytes 1572872 | tf_op jit(solution)/shard_map/ppermute | solution.py:1293
  232.7 42.2 %collective-permute-start.57 = (bf16[2,128,1024]{2,1,0:T(8,128)(2,1)}, bf16[2,128,1024]{2,1,0:T(8,128)(2,1)}, u32[]{:S(2)}, u32[]{:S(2)}) collective-permute-start(bf16[2,128,1024]{2,1,0:T(8,128)(2,1)} %get-tuple-element.308), channel_id=1, source_target_pairs={{0,16},{1,17},{2,18},{3,19},{4,20},{5,21},{6,22},{7,23},{8,24},{9,... | collective-permute-start | bytes 1572872 | tf_op jit(solution)/shard_map/ppermute | solution.py:1293
  237.6 20.9 %collective-permute-start.52 = (bf16[256,384]{1,0:T(8,128)(2,1)}, bf16[256,384]{1,0:T(8,128)(2,1)}, u32[]{:S(2)}, u32[]{:S(2)}) collective-permute-start(bf16[256,384]{1,0:T(8,128)(2,1)} %get-tuple-element.294), channel_id=1, source_target_pairs={{0,4},{1,5},{2,6},{3,7},{4,0},{5,1},{6,2},{7,3},{8,12},{9,13},{10,... | collective-permute-start | bytes 589832 | tf_op jit(solution)/shard_map/ppermute | solution.py:1293
  238.5 20.1 %collective-permute-start.51 = (bf16[304,384]{1,0:T(8,128)(2,1)}, bf16[304,384]{1,0:T(8,128)(2,1)}, u32[]{:S(2)}, u32[]{:S(2)}) collective-permute-start(bf16[304,384]{1,0:T(8,128)(2,1)} %get-tuple-element.292), channel_id=1, source_target_pairs={{0,2},{1,3},{2,0},{3,1},{4,6},{5,7},{6,4},{7,5},{8,10},{9,11},{10,... | collective-permute-start | bytes 700424 | tf_op jit(solution)/shard_map/ppermute | solution.py:1293
  240.9 30.9 %collective-permute-start.50 = (bf16[256,1024]{1,0:T(8,128)(2,1)}, bf16[256,1024]{1,0:T(8,128)(2,1)}, u32[]{:S(2)}, u32[]{:S(2)}) collective-permute-start(bf16[256,1024]{1,0:T(8,128)(2,1)} %get-tuple-element.290), channel_id=1, source_target_pairs={{0,8},{1,9},{2,10},{3,11},{4,12},{5,13},{6,14},{7,15},{8,0},{9,1},... | collective-permute-start | bytes 1572872 | tf_op jit(solution)/shard_map/ppermute | solution.py:1293
  260.4 16.4 %collective-permute-start.56 = (bf16[160,768]{1,0:T(8,128)(2,1)}, bf16[160,768]{1,0:T(8,128)(2,1)}, u32[]{:S(2)}, u32[]{:S(2)}) collective-permute-start(bf16[160,768]{1,0:T(8,128)(2,1)} %get-tuple-element.306), channel_id=1, source_target_pairs={{0,16},{1,17},{2,18},{3,19},{4,20},{5,21},{6,22},{7,23},{8,24},{9,... | collective-permute-start | bytes 737288 | tf_op jit(solution)/shard_map/ppermute | solution.py:1293
  278.8 19.6 %collective-permute-start.58 = (bf16[80,1792]{1,0:T(8,128)(2,1)}, bf16[80,1792]{1,0:T(8,128)(2,1)}, u32[]{:S(2)}, u32[]{:S(2)}) collective-permute-start(bf16[80,1792]{1,0:T(8,128)(2,1)} %get-tuple-element.317), channel_id=1, source_target_pairs={{0,8},{1,9},{2,10},{3,11},{4,12},{5,13},{6,14},{7,15},{8,0},{9,1},... | collective-permute-start | bytes 860168 | tf_op jit(solution)/shard_map/ppermute | solution.py:1293
  280.6 17.8 %collective-permute-start.59 = (bf16[64,512]{1,0:T(8,128)(2,1)S(1)}, bf16[64,512]{1,0:T(8,128)(2,1)S(1)}, u32[]{:S(2)}, u32[]{:S(2)}) collective-permute-start(bf16[64,512]{1,0:T(8,128)(2,1)S(1)} %get-tuple-element.320), channel_id=1, source_target_pairs={{0,16},{1,17},{2,18},{3,19},{4,20},{5,21},{6,22},{7,23},{8,24},{9,... | collective-permute-start | bytes 196616 | tf_op jit(solution)/shard_map/ppermute | solution.py:1293
  (70 other events, 563.0 us)

commit v4 on v3

--- a/solution.py
+++ b/solution.py
@@ -67,7 +67,55 @@
 EXTRA = 16
 
 
-COST = lambda flops: 10**11
+WEIGHTS = {'pack': 10000000000, 'unpair': 10000000000, 'trade': 1, 'join_down': 1, 'mask': 1}
+FREE = {'trade': [0]}
+WAITS = {}
+GRANTS = {'o2': 32}
+HEAVY = 10**11
+PLAN = (
+    "pack",
+    "mask",
+    "trade",
+    "join_down",
+    "settle",
+    "bundle",
+    "split",
+    "stack",
+    "vectors",
+    "join_up",
+    "attend",
+    "unpair",
+    "stack_far",
+    "relay",
+    "rows_own",
+    "rows_far",
+    "forward",
+    "fold_norm",
+    "gradients",
+    "turn",
+    "pick",
+    "outer",
+    "out_fold",
+    "o0",
+    "assemble",
+    "planes",
+    "attend_back",
+    "top_pair",
+    "input",
+    "lr",
+    "dn1",
+    "o1",
+    "top",
+    "o2",
+    "add",
+    "layer",
+    "d_down",
+    "home0",
+    "o3",
+    "last",
+    "home1",
+    "home_last",
+)
 
 
 def shaped(shape, kind):
@@ -77,9 +125,14 @@
 class Order:
     def __init__(self):
         self.ticket = jnp.zeros((8, LANES), F32)
-
-
-def kernel_call(order, body, outs, *args, name, smem=(), away=(), scratch=(), vmem=8, flops=0, after=()):
+        self.step = ""
+        self.waits = ()
+
+
+def kernel_call(order, body, outs, *args, name, smem=(), away=(), scratch=(), vmem=8, after=()):
+    weight = WEIGHTS.get(order.step, HEAVY)
+    after = tuple(v for i, v in enumerate(after) if i not in FREE.get(order.step, ()))
+    after, order.waits = after + order.waits, ()
     count, given = len(args), len(outs)
     inner = body
 
@@ -109,8 +162,8 @@
         out_specs=[spec(i, ()) for i in range(len(outs))],
         out_shape=list(outs),
         scratch_shapes=list(scratch),
-        compiler_params=pltpu.CompilerParams(vmem_limit_bytes=vmem * 2**20),
-        cost_estimate=pl.CostEstimate(flops=COST(flops), bytes_accessed=1, transcendentals=0),
+        compiler_params=pltpu.CompilerParams(vmem_limit_bytes=GRANTS.get(order.step, vmem) * 2**20),
+        cost_estimate=pl.CostEstimate(flops=weight, bytes_accessed=1, transcendentals=0),
         name=name,
     )(*args)
     return results
@@ -313,6 +366,10 @@
             out[i * rows : (i + 1) * rows, :] = ref[...]
 
     each_way(spot[6], write)
+
+
+def copy_kernel(value, out):
+    out[...] = value[...]
 
 
 def out_kernel_rows(mine, came, out):
@@ -499,7 +556,6 @@
             pltpu.SemaphoreType.DMA((copies,)),
         ],
         vmem=24,
-        flops=2 * length * d * 3 * hw + 3 * length * length * d // 2,
     )
 
 
@@ -642,8 +698,12 @@
     first = len(pairs)
     pairs += up_loads(lay, spot, ups, w_up) + down_loads(lay, spot, downs, w_down)
     pairs += row_loads(lay, spot, down_m, down_c, gd)
-    copies = load_all(pairs, sems)
+    copies = [pltpu.make_async_copy(a, b, sems.at[i]) for i, (a, b) in enumerate(pairs)]
+    for copy in copies[:first]:
+        copy.start()
     wait_all(copies[:first])
+    for copy in copies[first:]:
+        copy.start()
     bias_out, gain, shift = vecs[4:5, :], vecs[5:6, :], vecs[6:7, :]
     bias_up = vecs[8:9, 0 : lay.ff_share]
     total = jnp.zeros((1, lay.ff_share), F32)
@@ -714,7 +774,6 @@
             pltpu.SemaphoreType.DMA((copies,)),
         ],
         vmem=24,
-        flops=2 * tokens * d * (d + 3 * f),
     )
 
 
@@ -783,7 +842,6 @@
             pltpu.SemaphoreType.DMA((2 * g + 2 * lay.planes,)),
         ],
         vmem=24,
-        flops=2 * tokens * d * 3 * f,
     )
 
 
@@ -864,7 +922,6 @@
             pltpu.SemaphoreType.DMA((1,)),
         ],
         vmem=24,
-        flops=2 * rows * d * d,
     )
 
 
@@ -965,7 +1022,6 @@
             pltpu.VMEM((d, 3 * hw), BF16),
         ],
         vmem=24,
-        flops=2 * length * d * 3 * hw + 4 * length * length * d,
     )
 
 
@@ -1061,7 +1117,6 @@
         name="input_slope",
         smem=(0,),
         vmem=24,
-        flops=2 * lay.length * d * 3 * lay.share,
     )
 
 
@@ -1380,391 +1435,647 @@
                 values = values + [flip(v, b, who) for v in values]
             return values
 
-        start = [input_weight, up_weight, key_mask, output_weight] + vectors
-        half = width // 2
-        base = max(each, 16)
-        give, keep = call(
-            functools.partial(pack_kernel, lay),
-            [shaped((base + EXTRA, wide_in + half), BF16)] * 2,
-            spot,
-            lengths,
-            *start,
-            name="pack",
-            smem=(0, 1),
-            away=tuple(range(2, 15)),
-            vmem=60,
-            scratch=[pltpu.VMEM(v.shape, v.dtype) for v in start] + [pltpu.SemaphoreType.DMA((13,))],
-        )
-        came_w = flip(give, 0)
-        far = [send(own, across)]
-        near = spread_group([own])
-        downs = down_weight[None]
-        downs_came = flip(downs, plane_bits[-1])
-        grad_low = call(
-            mask_kernel,
-            [shaped((rows, width), BF16)],
-            spot,
-            lengths,
-            cotangent[0],
-            name="mask",
-            smem=(0, 1),
-        )[0]
-        count = group_size
-        for step, b in enumerate(group_bits):
-            tall = (2 << step) * each
-            columns = wide_in >> (step + 1)
-            give, keep, ready = call(
-                functools.partial(trade_kernel, lay, step, count),
-                [shaped((tall + EXTRA, columns + half), BF16)] * 2 + [shaped((8, length), F32)],
+        act = None
+        after = None
+        att_c = None
+        att_own = None
+        b = None
+        base = None
+        bundle = None
+        c = None
+        came_w = None
+        columns = None
+        count = None
+        cut = None
+        cuts_of = None
+        d_bias_up = None
+        d_down = None
+        d_in = None
+        d_out = None
+        d_up = None
+        dn_came = None
+        dn_give = None
+        dn_keep = None
+        down_blocks = None
+        down_c = None
+        down_came = None
+        down_cuts = None
+        down_far = None
+        down_far_came = None
+        down_give = None
+        down_keep = None
+        down_m = None
+        downs = None
+        downs_came = None
+        far = None
+        far_att = None
+        far_came = None
+        far_later = None
+        final = None
+        give = None
+        grad_branch = None
+        grad_joint = None
+        grad_later = None
+        grad_low = None
+        grad_middle = None
+        grad_pre = None
+        half = None
+        home_outs = None
+        home_steps = None
+        in_block = None
+        in_came = None
+        in_give = None
+        in_keep = None
+        in_pieces = None
+        in_sum = None
+        input_gradient = None
+        joint = None
+        joint_sum = None
+        k = None
+        keep = None
+        key_bias = None
+        layer_out = None
+        left = None
+        left_came = None
+        left_cuts = None
+        left_give = None
+        left_keep = None
+        lse = None
+        middle = None
+        near = None
+        near_att = None
+        next_out = None
+        next_planes = None
+        normed_one = None
+        normed_two = None
+        o_came = None
+        o_give = None
+        o_keep = None
+        out_bits = None
+        out_blocks = None
+        out_came = None
+        out_cuts = None
+        out_give = None
+        out_keep = None
+        out_shape = None
+        out_steps = None
+        outs = None
+        outs_c = None
+        outs_far = None
+        outs_w = None
+        pair = None
+        pair_came = None
+        paired = None
+        parts = None
+        pieces = None
+        planes_down = None
+        r = None
+        ready = None
+        reduce_group = None
+        right = None
+        right_came = None
+        right_cuts = None
+        right_give = None
+        right_keep = None
+        rows_came = None
+        sent = None
+        shape = None
+        shift = None
+        slope = None
+        slope_give = None
+        slope_keep = None
+        slot = None
+        small = None
+        start = None
+        step = None
+        sums = None
+        sums_came = None
+        sums_give = None
+        sums_two = None
+        tall = None
+        top_shift = None
+        up_blocks = None
+        up_came = None
+        up_cuts = None
+        up_far = None
+        up_far_came = None
+        up_give = None
+        up_keep = None
+        up_tall = None
+        ups = None
+        ups_came = None
+        ups_first = None
+        valid = None
+        vecs = None
+        w_came = None
+        w_give = None
+        w_in = None
+        w_keep = None
+        w_out = None
+        wide = None
+        x_all = None
+        def do_pack():
+            nonlocal base, came_w, downs, downs_came, far, give, half, keep, near, start
+            start = [input_weight, up_weight, key_mask, output_weight] + vectors
+            half = width // 2
+            base = max(each, 16)
+            give, keep = call(
+                functools.partial(pack_kernel, lay),
+                [shaped((base + EXTRA, wide_in + half), BF16)] * 2,
+                spot,
+                lengths,
+                *start,
+                name="pack",
+                smem=(0, 1),
+                away=tuple(range(2, 15)),
+                vmem=60,
+                scratch=[pltpu.VMEM(v.shape, v.dtype) for v in start] + [pltpu.SemaphoreType.DMA((13,))],
+            )
+            came_w = flip(give, 0)
+            far = [send(own, across)]
+            near = spread_group([own])
+            downs = down_weight[None]
+            downs_came = flip(downs, plane_bits[-1])
+
+        def do_mask():
+            nonlocal grad_low
+            grad_low = call(
+                mask_kernel,
+                [shaped((rows, width), BF16)],
+                spot,
+                lengths,
+                cotangent[0],
+                name="mask",
+                smem=(0, 1),
+            )[0]
+
+        def do_trade():
+            nonlocal b, came_w, columns, count, give, keep, ready, step, tall, valid
+            count = group_size
+            for step, b in enumerate(group_bits):
+                tall = (2 << step) * each
+                columns = wide_in >> (step + 1)
+                give, keep, ready = call(
+                    functools.partial(trade_kernel, lay, step, count),
+                    [shaped((tall + EXTRA, columns + half), BF16)] * 2 + [shaped((8, length), F32)],
+                    spot,
+                    keep,
+                    came_w,
+                    name="trade",
+                    smem=(0,),
+                    scratch=[pltpu.VMEM((tall, 2 * columns + half), BF16)],
+                    after=(far[0], *near[1:], downs_came) if step == 0 else (),
+                )
+                valid = ready if step == 0 else valid
+                came_w = flip(give, b)
+                count //= 2
+
+        def do_join_down():
+            nonlocal b, downs, downs_came
+            for b in reversed(plane_bits[:-1]):
+                downs = join(lay, downs, downs_came)
+                downs_came = flip(downs, b)
+
+        def do_settle():
+            nonlocal far, far_later, in_block, pair, paired, tall, up_tall, ups, ups_came, ups_first
+            tall = members * each
+            paired = ff // members == width
+            up_tall = tall + tall * half // (ff // members)
+            in_block, ups, far_later, pair = call(
+                functools.partial(settle_kernel, lay, len(group_bits)),
+                [
+                    shaped((tall + EXTRA, 3 * share), BF16),
+                    shaped((1, up_tall, ff // members), BF16),
+                    shaped(own.shape, BF16),
+                    shaped((up_tall + piece, width) if paired else (8, LANES), BF16),
+                ],
                 spot,
                 keep,
                 came_w,
-                name="trade",
+                far[0],
+                down_weight,
+                name="settle",
                 smem=(0,),
-                scratch=[pltpu.VMEM((tall, 2 * columns + half), BF16)],
-                after=(far[0], *near[1:], downs_came) if step == 0 else (),
+                scratch=[pltpu.VMEM((tall, 3 * share + ff // members + half), BF16)],
             )
-            valid = ready if step == 0 else valid
-            came_w = flip(give, b)
-            count //= 2
-        for b in reversed(plane_bits[:-1]):
-            downs = join(lay, downs, downs_came)
-            downs_came = flip(downs, b)
-        tall = members * each
-        paired = ff // members == width
-        up_tall = tall + tall * half // (ff // members)
-        in_block, ups, far_later, pair = call(
-            functools.partial(settle_kernel, lay, len(group_bits)),
-            [
-                shaped((tall + EXTRA, 3 * share), BF16),
-                shaped((1, up_tall, ff // members), BF16),
-                shaped(own.shape, BF16),
-                shaped((up_tall + piece, width) if paired else (8, LANES), BF16),
-            ],
-            spot,
-            keep,
-            came_w,
-            far[0],
-            down_weight,
-            name="settle",
-            smem=(0,),
-            scratch=[pltpu.VMEM((tall, 3 * share + ff // members + half), BF16)],
-        )
-        far = far + spread_group([far_later], away)[1:]
-        ups_first = ups
-        ups_came = flip(ups, plane_bits[0])
-        bundle = call(
-            functools.partial(bundle_kernel, group_size),
-            [shaped((2 * group_size * rows, width), BF16)],
-            spot,
-            *near,
-            *far,
-            name="bundle",
-            smem=(0,),
-            after=(downs_came,),
-        )[0]
-        rows_came = flip(bundle, 0)
-        cut = max(LANES, 3 * share // 2 // LANES * LANES)
-        left, right, pair, grad_later = call(
-            functools.partial(split_kernel, cut),
-            [
-                shaped((2, tall + EXTRA, cut), BF16),
-                shaped((2, tall + EXTRA, 3 * share - cut), BF16),
-                shaped(pair.shape, BF16),
-                shaped(grad_low.shape, BF16),
-            ],
-            in_block,
-            flip(in_block, top_bit),
-            pair,
-            grad_low,
-            name="split",
-            after=(ups_came,),
-        )
-        left_came, right_came = flip(left, plane_bits[0]), flip(right, plane_bits[-1])
-        if paired:
-            pair_came = flip(pair, top_bit)
-        else:
-            up_far, down_far = flip(ups_first, top_bit), flip(down_weight, top_bit)[None]
-        down_m = [grad_low] + spread_group([grad_later])[1:]
-        for k, (b, c) in list(enumerate(zip(plane_bits, reversed(plane_bits), strict=True)))[1:]:
-            after = (rows_came,) if k == 1 else ()
-            left, right = stack(lay, left, left_came, right, right_came, *after)
-            left_came, right_came = flip(left, b), flip(right, c)
-        in_pieces = (left, left_came, right, right_came)
-        vecs = call(
-            functools.partial(vector_kernel, lay),
-            [shaped((16, width), F32)],
-            spot,
-            left,
-            left_came,
-            name="vectors",
-            smem=(0,),
-            away=(1, 2),
-            scratch=[
-                pltpu.VMEM((2 * lay.planes * EXTRA, -(-lay.small // LANES) * LANES), BF16),
-                pltpu.SemaphoreType.DMA((2 * lay.planes,)),
-            ],
-        )[0]
-        for b in plane_bits[1:]:
-            ups = join(lay, ups, ups_came)
-            ups_came = flip(ups, b)
-
-        key_bias = jnp.where(valid[0] > 0.5, 0.0, MASKED).astype(F32).reshape(length, 1)
-        near_att, far_att, joint, wide, lse, normed_one, x_all, w_in = attend(
-            lay, spot, key_bias, vecs, near + far + [rows_came], in_pieces
-        )
-        far_att = [send(far_att, mirrored)]
-        near_att = spread_group([near_att])
-        att_c = [flip(near_att[0], 0)]
-
-        if paired:
-            up_far, down_far = call(
-                unpair_kernel,
-                [shaped((1, up_tall, width), BF16), shaped((1, piece, width), BF16)],
-                pair_came,
-                name="unpair",
-                after=(ups_came, *down_m[1:]),
+            far = far + spread_group([far_later], away)[1:]
+            ups_first = ups
+            ups_came = flip(ups, plane_bits[0])
+
+        def do_bundle():
+            nonlocal bundle, cut, rows_came
+            bundle = call(
+                functools.partial(bundle_kernel, group_size),
+                [shaped((2 * group_size * rows, width), BF16)],
+                spot,
+                *near,
+                *far,
+                name="bundle",
+                smem=(0,),
+                after=(downs_came,),
+            )[0]
+            rows_came = flip(bundle, 0)
+            cut = max(LANES, 3 * share // 2 // LANES * LANES)
+
+        def do_split():
+            nonlocal down_far, down_m, grad_later, left, left_came, pair, pair_came, right, right_came, up_far
+            left, right, pair, grad_later = call(
+                functools.partial(split_kernel, cut),
+                [
+                    shaped((2, tall + EXTRA, cut), BF16),
+                    shaped((2, tall + EXTRA, 3 * share - cut), BF16),
+                    shaped(pair.shape, BF16),
+                    shaped(grad_low.shape, BF16),
+                ],
+                in_block,
+                flip(in_block, top_bit),
+                pair,
+                grad_low,
+                name="split",
+                after=(ups_came,),
             )
-        out_shape = [shaped((lay.planes, tall, half), BF16)]
-        outs_w = []
-        for k, (b, c) in enumerate(zip(plane_bits, reversed(plane_bits), strict=True)):
-            if k:
-                up_far, down_far = stack(
-                    lay, up_far, up_far_came, down_far, down_far_came, att_c[0], outs_c
+            left_came, right_came = flip(left, plane_bits[0]), flip(right, plane_bits[-1])
+            if paired:
+                pair_came = flip(pair, top_bit)
+            else:
+                up_far, down_far = flip(ups_first, top_bit), flip(down_weight, top_bit)[None]
+            down_m = [grad_low] + spread_group([grad_later])[1:]
+
+        def do_stack():
+            nonlocal after, b, c, k, left, left_came, right, right_came
+            for k, (b, c) in list(enumerate(zip(plane_bits, reversed(plane_bits), strict=True)))[1:]:
+                after = (rows_came,) if k == 1 else ()
+                left, right = stack(lay, left, left_came, right, right_came, *after)
+                left_came, right_came = flip(left, b), flip(right, c)
+
+        def do_vectors():
+            nonlocal in_pieces, vecs
+            in_pieces = (left, left_came, right, right_came)
+            vecs = call(
+                functools.partial(vector_kernel, lay),
+                [shaped((16, width), F32)],
+                spot,
+                left,
+                left_came,
+                name="vectors",
+                smem=(0,),
+                away=(1, 2),
+                scratch=[
+                    pltpu.VMEM((2 * lay.planes * EXTRA, -(-lay.small // LANES) * LANES), BF16),
+                    pltpu.SemaphoreType.DMA((2 * lay.planes,)),
+                ],
+            )[0]
+
+        def do_join_up():
+            nonlocal b, ups, ups_came
+            for b in plane_bits[1:]:
+                ups = join(lay, ups, ups_came)
+                ups_came = flip(ups, b)
+
+        def do_attend():
+            nonlocal att_c, far_att, joint, key_bias, lse, near_att, normed_one, w_in, wide, x_all
+            key_bias = jnp.where(valid[0] > 0.5, 0.0, MASKED).astype(F32).reshape(length, 1)
+            near_att, far_att, joint, wide, lse, normed_one, x_all, w_in = attend(
+                lay, spot, key_bias, vecs, near + far + [rows_came], in_pieces
+            )
+            far_att = [send(far_att, mirrored)]
+            near_att = spread_group([near_att])
+            att_c = [flip(near_att[0], 0)]
+
+        def do_unpair():
+            nonlocal down_far, down_far_came, up_far, up_far_came
+            if paired:
+                up_far, down_far = call(
+                    unpair_kernel,
+                    [shaped((1, up_tall, width), BF16), shaped((1, piece, width), BF16)],
+                    pair_came,
+                    name="unpair",
+                    after=(ups_came, *down_m[1:]),
                 )
-            up_far_came, down_far_came = flip(up_far, b), flip(down_far, c)
-            if k == 0:
-                outs_w += call(out_kernel_rows, out_shape, ups, ups_came, name="out_rows")
-                outs_c = flip(outs_w[0], 0)
-        down_c = [flip(v, 0) for v in down_m]
-        far_att = spread_group(far_att)
-        att_c += [flip(v, 0) for v in near_att[1:] + far_att]
-        outs_w += call(out_kernel_rows, out_shape, up_far, up_far_came, name="out_rows")
-        out_blocks = (*outs_w, outs_c, flip(outs_w[1], 0))
-        up_blocks = (ups, ups_came, up_far, up_far_came)
-        down_blocks = (downs, downs_came, down_far, down_far_came)
-
-        (
-            dn_keep,
-            dn_give,
-            middle,
-            att_own,
-            normed_two,
-            act,
-            grad_pre,
-            d_bias_up,
-            w_out,
-        ) = forward_call(
-            lay,
-            spot,
-            vecs,
-            out_blocks,
-            near_att + far_att + att_c + near + down_m + down_c + [rows_came],
-            up_blocks + down_blocks,
-        )
-
-        def reduce_group(keep, came, slot):
-            for k in reversed(range(len(group_bits))):
-                keep, give = fold(lay, spot, slot, k, 1, keep, came)
-                came = flip(give, group_bits[k])
-            return keep, came
-
-        planes_down = list(reversed(plane_bits))
-        top_shift = bits_of(group_size)
-
-        def cuts_of(lead, order):
-            here, cuts = list(planes_down), []
-            for b in order:
-                cuts.append((1, b, lead << here.index(b)))
-                here.remove(b)
-            return cuts
-
-        dn_keep, dn_came = reduce_group(dn_keep, flip(dn_give, 0), 4)
-        up_keep, up_give, down_keep, down_give, out_keep, out_give = gradient_call(
-            lay, spot, normed_two, act, grad_pre, down_m, down_c, down_blocks
-        )
-        up_came, down_came = flip(up_give, planes_down[0]), flip(down_give, plane_bits[0])
-        out_came = flip(out_give, 0)
-        slope_keep, slope_give, grad_middle, grad_branch, sums_two = turn_call(
-            lay, spot, vecs, dn_keep, dn_came, middle, grad_low, w_out
-        )
-        pieces = call(
-            functools.partial(pick_kernel, lay),
-            [shaped((rows, share), BF16)] * members,
-            spot,
-            slope_keep,
-            flip(slope_give, 0),
-            name="pick",
-            smem=(0,),
-        )
-        parts = [pieces[0]]
-        for r in range(1, members):
-            parts.append(send(pieces[r], [(i, i ^ (r * nt)) for i in range(devices)]))
-        o_keep, o_give = call(
-            outer_kernel,
-            [shaped((width, width // 2), BF16)] * 2,
-            spot,
-            att_own,
-            grad_branch,
-            name="output_gradient",
-            smem=(0,),
-        )
-        o_came = flip(o_give, 0)
-        out_keep, out_came = reduce_group(out_keep, out_came, 4)
-        out_cuts = [(4, k, 2) for k in reversed(range(len(group_bits)))]
-        out_cuts += cuts_of(2, planes_down) + [(0, top_shift, 1)]
-        out_bits = list(reversed(group_bits)) + planes_down + [top_bit]
-        out_steps = iter(range(len(out_bits)))
-
-        def next_out(keep, came, count=1):
-            for _ in range(count):
-                k = next(out_steps)
-                keep, give = fold(lay, spot, *out_cuts[k], keep, came)
-                came = flip(give, out_bits[k])
-            return keep, came
-
-        o_keep, o_came = next_out(o_keep, o_came)
-        slope = call(
-            functools.partial(assemble_kernel, lay),
-            [shaped((length, share), BF16)],
-            spot,
-            *parts,
-            name="assemble",
-            smem=(0,),
-        )[0]
-        up_cuts, down_cuts = cuts_of(members, planes_down), cuts_of(2, plane_bits)
-
-        def next_planes(k, up_keep, up_came, down_keep, down_came):
-            up_keep, up_give, down_keep, down_give = two_fold(
-                lay, spot, (up_cuts[k], down_cuts[k]), up_keep, up_came, down_keep, down_came
-            )
-            return up_keep, flip(up_give, planes_down[k]), down_keep, flip(down_give, plane_bits[k])
-
-        for k in range(1, len(plane_bits)):
-            up_keep, up_came, down_keep, down_came = next_planes(
-                k, up_keep, up_came, down_keep, down_came
-            )
-
-        grad_joint, left_keep, left_give, right_keep, right_give, joint_sum = attend_back(
-            lay, spot, key_bias, joint, wide, lse, normed_one, slope, cut
-        )
-        left_came, right_came = flip(left_give, planes_down[0]), flip(right_give, plane_bits[0])
-        if paired:
-            shape = (up_keep.shape[0] // 2, up_keep.shape[1])
-            up_keep, down_keep, give = call(
-                functools.partial(top_pair_kernel, top_shift),
-                [shaped(shape, BF16), shaped(shape, BF16), shaped((2,) + shape, BF16)],
-                spot,
-                up_keep,
-                up_came,
-                down_keep,
-                down_came,
-                name="top_pair",
-                smem=(0,),
-                after=(o_came,),
-            )
-            far_came = flip(give, top_bit)
-        else:
-            up_keep, up_give, down_keep, down_give = two_fold(
-                lay, spot, ((0, top_shift, 1),) * 2, up_keep, up_came, down_keep, down_came
-            )
-            far_came = (flip(up_give, top_bit), flip(down_give, top_bit))
-        in_keep, in_give, sums, sums_give = input_call(
-            lay, spot, grad_joint, w_in, x_all, sums_two, joint_sum, d_bias_up
-        )
-        sums_came = flip(sums_give, planes_down[0])
-        in_came = flip(in_give, 0)
-        left_cuts, right_cuts = cuts_of(members, planes_down), cuts_of(members, plane_bits)
-        for k in range(1, len(plane_bits)):
-            left_keep, left_give, right_keep, right_give, sums = sums_fold(
+            up_far_came, down_far_came = flip(up_far, plane_bits[0]), flip(down_far, plane_bits[-1])
+
+        def do_rows_own():
+            nonlocal out_shape, outs_c, outs_w
+            out_shape = [shaped((lay.planes, tall, half), BF16)]
+            outs_w = call(out_kernel_rows, out_shape, ups, ups_came, name="out_rows")
+            outs_c = flip(outs_w[0], 0)
+
+        def do_stack_far():
+            nonlocal b, c, down_far, down_far_came, k, up_far, up_far_came
+            for k, (b, c) in list(enumerate(zip(plane_bits, reversed(plane_bits), strict=True)))[1:]:
+                up_far, down_far = stack(lay, up_far, up_far_came, down_far, down_far_came, att_c[0])
+                up_far_came, down_far_came = flip(up_far, b), flip(down_far, c)
+
+        def do_rows_far():
+            nonlocal att_c, down_blocks, down_c, far_att, out_blocks, outs_far, up_blocks
+            down_c = [flip(v, 0) for v in down_m]
+            far_att = spread_group(far_att)
+            att_c = att_c[:1] + [flip(v, 0) for v in near_att[1:] + far_att]
+            outs_far = call(out_kernel_rows, out_shape, up_far, up_far_came, name="out_rows", after=(outs_c,))[0]
+            out_blocks = (*outs_w, outs_far, outs_c, flip(outs_far, 0))
+            up_blocks = (ups, ups_came, up_far, up_far_came)
+            down_blocks = (downs, downs_came, down_far, down_far_came)
+
+        def do_forward():
+            nonlocal act, att_own, cuts_of, d_bias_up, dn_give, dn_keep, grad_pre, middle, normed_two, planes_down, reduce_group, top_shift, w_out
+            (
+                dn_keep,
+                dn_give,
+                middle,
+                att_own,
+                normed_two,
+                act,
+                grad_pre,
+                d_bias_up,
+                w_out,
+            ) = forward_call(
                 lay,
                 spot,
-                (left_cuts[k], right_cuts[k]),
+                vecs,
+                out_blocks,
+                near_att + far_att + att_c + near + down_m + down_c + [rows_came],
+                up_blocks + down_blocks,
+            )
+
+            def reduce_group(keep, came, slot):
+                for k in reversed(range(len(group_bits))):
+                    keep, give = fold(lay, spot, slot, k, 1, keep, came)
+                    came = flip(give, group_bits[k])
+                return keep, came
+
+            planes_down = list(reversed(plane_bits))
+            top_shift = bits_of(group_size)
+
+            def cuts_of(lead, order):
+                here, cuts = list(planes_down), []
+                for b in order:
+                    cuts.append((1, b, lead << here.index(b)))
+                    here.remove(b)
+                return cuts
+
+        def do_fold_norm():
+            nonlocal dn_came, dn_keep
+            dn_keep, dn_came = reduce_group(dn_keep, flip(dn_give, 0), 4)
+
+        def do_gradients():
+            nonlocal down_came, down_give, down_keep, out_came, out_give, out_keep, up_came, up_give, up_keep
+            up_keep, up_give, down_keep, down_give, out_keep, out_give = gradient_call(
+                lay, spot, normed_two, act, grad_pre, down_m, down_c, down_blocks
+            )
+            up_came, down_came = flip(up_give, planes_down[0]), flip(down_give, plane_bits[0])
+            out_came = flip(out_give, 0)
+
+        def do_turn():
+            nonlocal grad_branch, grad_middle, slope_give, slope_keep, sums_two
+            slope_keep, slope_give, grad_middle, grad_branch, sums_two = turn_call(
+                lay, spot, vecs, dn_keep, dn_came, middle, grad_low, w_out
+            )
+
+        def do_pick():
+            nonlocal parts, pieces, r
+            pieces = call(
+                functools.partial(pick_kernel, lay),
+                [shaped((rows, share), BF16)] * members,
+                spot,
+                slope_keep,
+                flip(slope_give, 0),
+                name="pick",
+                smem=(0,),
+            )
+            parts = [pieces[0]]
+            for r in range(1, members):
+                parts.append(send(pieces[r], [(i, i ^ (r * nt)) for i in range(devices)]))
+
+        def do_outer():
+            nonlocal o_came, o_give, o_keep
+            o_keep, o_give = call(
+                outer_kernel,
+                [shaped((width, width // 2), BF16)] * 2,
+                spot,
+                att_own,
+                grad_branch,
+                name="output_gradient",
+                smem=(0,),
+            )
+            o_came = flip(o_give, 0)
+
+        def do_out_fold():
+            nonlocal out_came, out_keep
+            out_keep, out_came = reduce_group(out_keep, out_came, 4)
+
+        def do_o0():
+            nonlocal next_out, o_came, o_keep, out_bits, out_cuts, out_steps
+            out_cuts = [(4, k, 2) for k in reversed(range(len(group_bits)))]
+            out_cuts += cuts_of(2, planes_down) + [(0, top_shift, 1)]
+            out_bits = list(reversed(group_bits)) + planes_down + [top_bit]
+            out_steps = iter(range(len(out_bits)))
+
+            def next_out(keep, came, count=1):
+                for _ in range(count):
+                    k = next(out_steps)
+                    keep, give = fold(lay, spot, *out_cuts[k], keep, came)
+                    came = flip(give, out_bits[k])
+                return keep, came
+
+            o_keep, o_came = next_out(o_keep, o_came)
+
+        def do_assemble():
+            nonlocal slope
+            slope = call(
+                functools.partial(assemble_kernel, lay),
+                [shaped((length, share), BF16)],
+                spot,
+                *parts,
+                name="assemble",
+                smem=(0,),
+            )[0]
+
+        def do_planes():
+            nonlocal down_came, down_cuts, down_keep, k, next_planes, up_came, up_cuts, up_keep
+            up_cuts, down_cuts = cuts_of(members, planes_down), cuts_of(2, plane_bits)
+
+            def next_planes(k, up_keep, up_came, down_keep, down_came):
+                up_keep, up_give, down_keep, down_give = two_fold(
+                    lay, spot, (up_cuts[k], down_cuts[k]), up_keep, up_came, down_keep, down_came
+                )
+                return up_keep, flip(up_give, planes_down[k]), down_keep, flip(down_give, plane_bits[k])
+
+            for k in range(1, len(plane_bits)):
+                up_keep, up_came, down_keep, down_came = next_planes(
+                    k, up_keep, up_came, down_keep, down_came
+                )
+
+        def do_attend_back():
+            nonlocal grad_joint, joint_sum, left_came, left_give, left_keep, right_came, right_give, right_keep
+            grad_joint, left_keep, left_give, right_keep, right_give, joint_sum = attend_back(
+                lay, spot, key_bias, joint, wide, lse, normed_one, slope, cut
+            )
+            left_came, right_came = flip(left_give, planes_down[0]), flip(right_give, plane_bits[0])
+
+        def do_top_pair():
+            nonlocal down_give, down_keep, far_came, give, shape, up_give, up_keep
+            if paired:
+                shape = (up_keep.shape[0] // 2, up_keep.shape[1])
+                up_keep, down_keep, give = call(
+                    functools.partial(top_pair_kernel, top_shift),
+                    [shaped(shape, BF16), shaped(shape, BF16), shaped((2,) + shape, BF16)],
+                    spot,
+                    up_keep,
+                    up_came,
+                    down_keep,
+                    down_came,
+                    name="top_pair",
+                    smem=(0,),
+                    after=(o_came,),
+                )
+                far_came = flip(give, top_bit)
+            else:
+                up_keep, up_give, down_keep, down_give = two_fold(
+                    lay, spot, ((0, top_shift, 1),) * 2, up_keep, up_came, down_keep, down_came
+                )
+                far_came = (flip(up_give, top_bit), flip(down_give, top_bit))
+
+        def do_input():
+            nonlocal in_came, in_give, in_keep, sums, sums_came, sums_give
+            in_keep, in_give, sums, sums_give = input_call(
+                lay, spot, grad_joint, w_in, x_all, sums_two, joint_sum, d_bias_up
+            )
+            sums_came = flip(sums_give, planes_down[0])
+            in_came = flip(in_give, 0)
+
+        def do_lr():
+            nonlocal k, left_came, left_cuts, left_give, left_keep, right_came, right_cuts, right_give, right_keep, sums
+            left_cuts, right_cuts = cuts_of(members, planes_down), cuts_of(members, plane_bits)
+            for k in range(1, len(plane_bits)):
+                left_keep, left_give, right_keep, right_give, sums = sums_fold(
+                    lay,
+                    spot,
+                    (left_cuts[k], right_cuts[k]),
+                    left_keep,
+                    left_came,
+                    right_keep,
+                    right_came,
+                    sums,
+                    sums_came,
+                )
+                left_came, right_came = flip(left_give, planes_down[k]), flip(right_give, plane_bits[k])
+
+        def do_dn1():
+            nonlocal in_came, in_keep
+            in_keep, in_came = reduce_group(in_keep, in_came, 9)
+
+        def do_o1():
+            nonlocal o_came, o_keep
+            o_keep, o_came = next_out(o_keep, o_came, len(group_bits))
+
+        def do_layer():
+            nonlocal layer_out
+            layer_out = call(
+                out_kernel,
+                [shaped((rows, width), BF16)],
+                vecs,
+                middle,
+                out_keep,
+                out_came,
+                name="layer_out",
+            )[0]
+
+        def do_top():
+            nonlocal small, sums, tall, w_came, w_give, w_keep
+            small = (SUM_ROWS, width)
+            tall = left_keep.shape[0] // 2
+            w_keep, w_give, sums = call(
+                functools.partial(top_fold_kernel, top_shift),
+                [
+                    shaped((tall, 3 * share), BF16),
+                    shaped((tall + sum_rows(width, 3 * share), 3 * share), BF16),
+                    shaped(small, F32),
+                ],
+                spot,
                 left_keep,
                 left_came,
                 right_keep,
                 right_came,
                 sums,
-                sums_came,
+                name="top_fold",
+                smem=(0,),
             )
-            left_came, right_came = flip(left_give, planes_down[k]), flip(right_give, plane_bits[k])
-        in_keep, in_came = reduce_group(in_keep, in_came, 9)
-        o_keep, o_came = next_out(o_keep, o_came, len(group_bits))
-        layer_out = call(
-            out_kernel,
-            [shaped((rows, width), BF16)],
-            vecs,
-            middle,
-            out_keep,
-            out_came,
-            name="layer_out",
-        )[0]
-
-        small = (SUM_ROWS, width)
-        tall = left_keep.shape[0] // 2
-        w_keep, w_give, sums = call(
-            functools.partial(top_fold_kernel, top_shift),
-            [
-                shaped((tall, 3 * share), BF16),
-                shaped((tall + sum_rows(width, 3 * share), 3 * share), BF16),
-                shaped(small, F32),
-            ],
-            spot,
-            left_keep,
-            left_came,
-            right_keep,
-            right_came,
-            sums,
-            name="top_fold",
-            smem=(0,),
-        )
-        w_came = flip(w_give, top_bit)
-        in_sum = call(add_kernel, [shaped((rows, width), BF16)], in_keep, in_came, name="add")[0]
-        sent = send(in_sum, across)
-        o_keep, o_came = next_out(o_keep, o_came, len(plane_bits) - 1)
-        up_came, down_came = (far_came, far_came) if paired else far_came
-        d_down = call(
-            add_kernel, [shaped((piece, width), F32)], down_keep, down_came, name="add"
-        )[0]
-        came = w_came
-        columns = 3 * share + ff // members
-        steps = [(4, k, b) for k, b in reversed(list(enumerate(group_bits)))] + [(2, 0, 0)]
-        for step, (slot, shift, b) in enumerate(steps):
+            w_came = flip(w_give, top_bit)
+
+        def do_add():
+            nonlocal in_sum, sent
+            in_sum = call(add_kernel, [shaped((rows, width), BF16)], in_keep, in_came, name="add")[0]
+            sent = send(in_sum, across)
+
+        def do_o2():
+            nonlocal o_came, o_keep
+            o_keep, o_came = next_out(o_keep, o_came, len(plane_bits) - 1)
+
+        def do_d_down():
+            nonlocal d_down
+            d_down = call(
+                add_kernel,
+                [shaped((piece, width), F32)],
+                down_keep,
+                far_came if paired else far_came[1],
+                name="add",
+            )[0]
+
+        def do_home0():
+            nonlocal columns, down_came, home_outs, home_steps, sums, tall, up_came, w_came, w_give, w_keep
+            up_came, down_came = (far_came, far_came) if paired else far_came
+            columns = 3 * share + ff // members
+            home_steps = [(4, k, b) for k, b in reversed(list(enumerate(group_bits)))] + [(2, 0, 0)]
+
+            def home_outs():
+                rows_here = max(tall, 16)
+                return [
+                    shaped((rows_here, columns), BF16),
+                    shaped((rows_here + sum_rows(width, columns), columns), BF16),
+                    shaped(small, F32),
+                ]
+
             tall //= 2
-            outs = [
-                shaped((max(tall, 16), columns), BF16),
-                shaped((max(tall, 16) + sum_rows(width, columns), columns), BF16),
-                shaped(small, F32),
-            ]
-            if step == 0:
-                w_keep, w_give, sums = call(
-                    functools.partial(home_first_kernel, slot, shift),
-                    outs,
-                    spot,
-                    w_keep,
-                    came,
-                    up_keep,
-                    up_came,
-                    sums,
-                    name="home_first",
-                    smem=(0,),
-                )
-                came = flip(w_give, b)
-                o_keep, o_came = next_out(o_keep, o_came)
-                input_gradient = call(
-                    last_kernel,
-                    [shaped((rows, width), BF16)],
-                    spot,
-                    vecs,
-                    in_keep,
-                    in_came,
-                    sent,
-                    own,
-                    grad_middle,
-                    name="input_gradient",
-                    smem=(0,),
-                )[0]
-            else:
+            w_keep, w_give, sums = call(
+                functools.partial(home_first_kernel, *home_steps[0][:2]),
+                home_outs(),
+                spot,
+                w_keep,
+                w_came,
+                up_keep,
+                up_came,
+                sums,
+                name="home_first",
+                smem=(0,),
+            )
+            w_came = flip(w_give, home_steps[0][2])
+
+        def do_o3():
+            nonlocal o_came, o_keep
+            o_keep, o_came = next_out(o_keep, o_came)
+
+        def do_last():
+            nonlocal input_gradient
+            input_gradient = call(
+                last_kernel,
+                [shaped((rows, width), BF16)],
+                spot,
+                vecs,
+                in_keep,
+                in_came,
+                sent,
+                own,
+                grad_middle,
+                name="input_gradient",
+                smem=(0,),
+            )[0]
+
+        def do_home1():
+            nonlocal b, columns, final, outs, shift, slot, sums, tall, w_came, w_give, w_keep
+            for slot, shift, b in home_steps[1:]:
+                tall //= 2
+                columns *= 2
+                outs = home_outs()
                 final = (o_keep, o_came) if b == 0 else ()
                 if final:
                     outs = [shaped((v.shape[0], columns + width // 2), BF16) for v in outs[:2]] + outs[2:]
@@ -1773,27 +2084,109 @@
                     outs,
                     spot,
                     w_keep,
-                    came,
+                    w_came,
                     sums,
                     *final,
                     name="home_next",
                     smem=(0,),
                 )
-                came = flip(w_give, b)
-            columns *= 2
-        d_in, d_up, d_out, *vectors = call(
-            functools.partial(home_last_kernel, lay),
-            [shaped((each, 3 * width), F32), shaped((each, ff), F32), shaped((each, width), F32)]
-            + [shaped((1, each), F32)] * 8
-            + [shaped((1, piece), F32)],
-            spot,
-            w_keep,
-            came,
-            sums,
-            name="home_last",
-            smem=(0,),
-        )
-        vectors = [v.reshape(-1) for v in vectors]
+                w_came = flip(w_give, b)
+
+        def do_home_last():
+            nonlocal d_in, d_out, d_up, vectors
+            d_in, d_up, d_out, *vectors = call(
+                functools.partial(home_last_kernel, lay),
+                [shaped((each, 3 * width), F32), shaped((each, ff), F32), shaped((each, width), F32)]
+                + [shaped((1, each), F32)] * 8
+                + [shaped((1, piece), F32)],
+                spot,
+                w_keep,
+                w_came,
+                sums,
+                name="home_last",
+                smem=(0,),
+            )
+            vectors = [v.reshape(-1) for v in vectors]
+
+        def do_relay():
+            nonlocal far_att
+            far_att = call(
+                copy_kernel, [shaped(far_att[0].shape, BF16)], far_att[0], name="relay", after=tuple(near_att[1:])
+            )
+
+        steps = {
+            "pack": do_pack,
+            "mask": do_mask,
+            "trade": do_trade,
+            "join_down": do_join_down,
+            "settle": do_settle,
+            "bundle": do_bundle,
+            "split": do_split,
+            "stack": do_stack,
+            "vectors": do_vectors,
+            "join_up": do_join_up,
+            "attend": do_attend,
+            "unpair": do_unpair,
+            "rows_own": do_rows_own,
+            "stack_far": do_stack_far,
+            "rows_far": do_rows_far,
+            "forward": do_forward,
+            "fold_norm": do_fold_norm,
+            "gradients": do_gradients,
+            "turn": do_turn,
+            "pick": do_pick,
+            "outer": do_outer,
+            "out_fold": do_out_fold,
+            "o0": do_o0,
+            "assemble": do_assemble,
+            "planes": do_planes,
+            "attend_back": do_attend_back,
+            "top_pair": do_top_pair,
+            "input": do_input,
+            "lr": do_lr,
+            "dn1": do_dn1,
+            "o1": do_o1,
+            "layer": do_layer,
+            "top": do_top,
+            "add": do_add,
+            "o2": do_o2,
+            "d_down": do_d_down,
+            "home0": do_home0,
+            "o3": do_o3,
+            "last": do_last,
+            "home1": do_home1,
+            "home_last": do_home_last,
+            "relay": do_relay,
+        }
+        for name in PLAN:
+            lay.order.step = name
+            known = {
+                "near": near,
+                "far": far,
+                "downs_came": downs_came,
+                "ups_came": ups_came,
+                "rows_came": rows_came,
+                "pair_came": pair_came,
+                "down_m": down_m,
+                "down_c": down_c,
+                "near_att": near_att,
+                "far_att": far_att,
+                "att_c": att_c,
+                "outs_c": outs_c,
+                "up_far_came": up_far_came,
+                "down_far_came": down_far_came,
+                "up_came": up_came,
+                "down_came": down_came,
+                "out_came": out_came,
+                "o_came": o_came,
+                "far_came": far_came,
+                "sums_came": sums_came,
+                "in_came": in_came,
+            }
+            lay.order.waits = tuple(
+                v for w in WAITS.get(name, ()) for v in jax.tree.leaves(known[w])
+            )
+            steps[name]()
         return (
             layer_out[None],
             input_gradient[None],

time: 308 us -> 288 us (0.935)
  waiting for transfers between devices: 113 us -> 100 us
  starting transfers between devices: 73.9 us -> 68.6 us
  Pallas kernels: 111 us -> 106 us
    ppermute x61, waiting for transfers between devices: 113 us -> 100 us  [send(): return lax.ppermute(value, AXES, route)]
    ppermute x61, starting transfers between devices: 73.9 us -> 68.6 us  [send(): return lax.ppermute(value, AXES, route)]
    pallas_call x41 -> x42, Pallas kernels: 111 us -> 106 us  [kernel_call(): pl.pallas_call(body, in_specs=ins, out_specs=[spec(i, ()) for i in range(...]
  transfers between devices with their start and end apart: 61 -> 61, of which waited for: 28 -> 25; matrix products, arithmetic and copies ran while one was open for 0% -> 1% of each run, Pallas kernels for 27% -> 28%
where the time goes in v4:
time: 288 us; the launch traced here: 283 us
  Pallas kernels  106 us (37%)
  waiting for transfers between devices  100 us (35%)
  starting transfers between devices  68.6 us (24%)
  local copies, waits for them, and re-layouts  5.69 us (2%)
    pallas_call x42, Pallas kernels, kernel_call(): pl.pallas_call(body, in_specs=ins, out_specs=[spec(i, ()) for i in range(...  106 us
    ppermute x61, waiting for transfers between devices, send(): return lax.ppermute(value, AXES, route)  100 us
    ppermute x61, starting transfers between devices, send(): return lax.ppermute(value, AXES, route)  68.6 us
  transfers between devices with their start and end apart: 61, of which 25 were waited for; matrix products, arithmetic and copies ran while one was open for 1% of the time, Pallas kernels for 28%

profile of v4, /device:TPU:0, one launch (start us, length us, event | category | flops | bytes accessed | tf_op | source)
XLA Modules:
  0.0 283.5 jit_solution(3163235343622688606)
XLA Ops:
  0.6 3.1 %collective-permute-start.1 = (bf16[256,1024]{1,0:T(8,128)(2,1)}, bf16[256,1024]{1,0:T(8,128)(2,1)S(1)}, u32[]{:S(2)}, u32[]{:S(2)}) collective-permute-start(bf16[256,1024]{1,0:T(8,128)(2,1)} %bitcast.38), channel_id=1, source_target_pairs={{0,8},{1,9},{2,10},{3,11},{4,12},{5,13},{6,14},{7,15},{8,0},{9,1},... | collective-permute-start | bytes 1572872 | tf_op jit(solution)/shard_map/ppermute | solution.py:1348
  5.6 3.1 %pack.1 = (bf16[48,4096]{1,0:T(8,128)(2,1)}, bf16[48,4096]{1,0:T(8,128)(2,1)}, f32[8,128]{1,0:T(8,128)}) custom-call(s32[10]{0:T(128)} %stack.49.refs_0_, s32[1]{0:T(128)S(6)} %copy.34.refs_1_, bf16[32,3072]{1,0:T(8,128)(2,1)} %refs_2_.1, bf16[32,4096]{1,0:T(8,128)(2,1)} %refs_3_.1, s32[1,1024]{1,0:T(1,128)} %refs_4_.2, bf16[32,1024]{1,0:T(8,128)(2,1)} %refs_5_.1, ...), custom_call_target="tpu_custom_call" | custom-call | flops 10000000000 | bytes 1 | tf_op jit(solution)/shard_map/pack/pallas_call | solution.py:159
  12.5 5.1 %collective-permute-done.2.refs_4_.refs_1_ = bf16[1,128,1024]{2,1,0:T(8,128)(2,1)S(1)} collective-permute-done((bf16[1,128,1024]{2,1,0:T(8,128)(2,1)S(1)}, bf16[1,128,1024]{2,1,0:T(8,128)(2,1)S(1)}, u32[]{:S(2)}, u32[]{:S(2)}) %collective-permute-start.2) | collective-permute-done | bytes 262176 | tf_op jit(solution)/shard_map/ppermute | solution.py:1348
  21.4 10.3 %collective-permute-done.3.refs_2_ = bf16[80,2304]{1,0:T(8,128)(2,1)S(1)} collective-permute-done((bf16[80,2304]{1,0:T(8,128)(2,1)S(1)}, bf16[80,2304]{1,0:T(8,128)(2,1)S(1)}, u32[]{:S(2)}, u32[]{:S(2)}) %collective-permute-start.3) | collective-permute-done | bytes 368672 | tf_op jit(solution)/shard_map/ppermute | solution.py:1348
  33.1 3.4 %collective-permute-start.5 = (bf16[144,768]{1,0:T(8,128)(2,1)S(1)}, bf16[144,768]{1,0:T(8,128)(2,1)S(1)}, u32[]{:S(2)}, u32[]{:S(2)}) collective-permute-start(bf16[144,768]{1,0:T(8,128)(2,1)S(1)} %get-tuple-element.187.refs_0_), channel_id=1, source_target_pairs={{0,16},{1,17},{2,18},{3,19},{4,20},{5,21},{6,22},{7,23},{8,24},{9,... | collective-permute-start | bytes 663560 | tf_op jit(solution)/shard_map/ppermute | solution.py:1348
  38.9 8.9 %collective-permute-start.11 = (bf16[1024,1024]{1,0:T(8,128)(2,1)S(1)}, bf16[1024,1024]{1,0:T(8,128)(2,1)S(1)}, u32[]{:S(2)}, u32[]{:S(2)}) collective-permute-start(bf16[1024,1024]{1,0:T(8,128)(2,1)S(1)} %get-tuple-element.197), channel_id=1, source_target_pairs={{0,1},{1,0},{2,3},{3,2},{4,5},{5,4},{6,7},{7,6},{8,9},{9,8},{10,11... | collective-permute-start | bytes 6291464 | tf_op jit(solution)/shard_map/ppermute | solution.py:1348
  52.1 4.4 %collective-permute-done.9.refs_1_ = bf16[2,144,384]{2,1,0:T(8,128)(2,1)S(1)} collective-permute-done((bf16[2,144,384]{2,1,0:T(8,128)(2,1)S(1)}, bf16[2,144,384]{2,1,0:T(8,128)(2,1)S(1)}, u32[]{:S(2)}, u32[]{:S(2)}) %collective-permute-start.9) | collective-permute-done | bytes 221216 | tf_op jit(solution)/shard_map/ppermute | solution.py:1348
  61.4 3.2 %collective-permute-start.17 = (bf16[320,1024]{1,0:T(8,128)(2,1)}, bf16[320,1024]{1,0:T(8,128)(2,1)}, u32[]{:S(2)}, u32[]{:S(2)}) collective-permute-start(bf16[320,1024]{1,0:T(8,128)(2,1)} %get-tuple-element.209), channel_id=1, source_target_pairs={{0,16},{1,17},{2,18},{3,19},{4,20},{5,21},{6,22},{7,23},{8,24},{9,... | collective-permute-start | bytes 1966088 | tf_op jit(solution)/shard_map/ppermute | solution.py:1348
  65.1 4.9 %collective-permute-done.12.refs_2_.refs_9_ = bf16[4,144,384]{2,1,0:T(8,128)(2,1)S(1)} collective-permute-done((bf16[4,144,384]{2,1,0:T(8,128)(2,1)S(1)}, bf16[4,144,384]{2,1,0:T(8,128)(2,1)S(1)}, u32[]{:S(2)}, u32[]{:S(2)}) %collective-permute-start.12) | collective-permute-done | bytes 442400 | tf_op jit(solution)/shard_map/ppermute | solution.py:1348
  75.5 12.8 %attend.1 = (bf16[512,256]{1,0:T(8,128)(2,1)S(1)}, bf16[512,256]{1,0:T(8,128)(2,1)S(1)}, bf16[1024,768]{1,0:T(8,128)(2,1)S(1)}, f32[256,1024]{1,0:T(8,128)S(1)},...) custom-call(s32[10]{0:T(128)S(1)} %copy-done.4, ...), custom_call_target="tpu_custom_call" | custom-call | flops 99999997952 | bytes 1 | tf_op jit(solution)/shard_map/attend/pallas_call | solution.py:159
  88.4 4.3 %collective-permute-done.17.refs_0_ = bf16[320,1024]{1,0:T(8,128)(2,1)} collective-permute-done((bf16[320,1024]{1,0:T(8,128)(2,1)}, bf16[320,1024]{1,0:T(8,128)(2,1)}, u32[]{:S(2)}, u32[]{:S(2)}) %collective-permute-start.17) | collective-permute-done | bytes 655392 | tf_op jit(solution)/shard_map/ppermute | solution.py:1348
  97.8 5.8 %collective-permute-done.20.refs_3_ = bf16[1,128,1024]{2,1,0:T(8,128)(2,1)S(1)} collective-permute-done((bf16[1,128,1024]{2,1,0:T(8,128)(2,1)S(1)}, bf16[1,128,1024]{2,1,0:T(8,128)(2,1)S(1)}, u32[]{:S(2)}, u32[]{:S(2)}) %collective-permute-start.20) | collective-permute-done | bytes 262176 | tf_op jit(solution)/shard_map/ppermute | solution.py:1348
  105.0 5.1 %collective-permute-done.15.refs_0_ = bf16[512,256]{1,0:T(8,128)(2,1)S(1)} collective-permute-done((bf16[512,256]{1,0:T(8,128)(2,1)S(1)}, bf16[512,256]{1,0:T(8,128)(2,1)S(1)}, u32[]{:S(2)}, u32[]{:S(2)}) %collective-permute-start.15) | collective-permute-done | bytes 262176 | tf_op jit(solution)/shard_map/ppermute | solution.py:1348
  114.8 9.2 %collective-permute-done.22.refs_1_.refs_24_ = bf16[2,192,1024]{2,1,0:T(8,128)(2,1)} collective-permute-done((bf16[2,192,1024]{2,1,0:T(8,128)(2,1)}, bf16[2,192,1024]{2,1,0:T(8,128)(2,1)}, u32[]{:S(2)}, u32[]{:S(2)}) %collective-permute-start.22) | collective-permute-done | bytes 786464 | tf_op jit(solution)/shard_map/ppermute | solution.py:1348
  128.8 17.3 %feed_forward.1 = (bf16[512,1024]{1,0:T(8,128)(2,1)S(1)}, bf16[512,1024]{1,0:T(8,128)(2,1)S(1)}, f32[256,1024]{1,0:T(8,128)S(1)}, bf16[256,1024]{1,0:T(8,128)(2,...) custom-call(s32[10]{0:T(128)S(1)} %copy-done.4, ...), custom_call_target="tpu_custom_call" | custom-call | flops 99999997952 | bytes 1 | tf_op jit(solution)/shard_map/feed_forward/pallas_call | solution.py:159
  150.0 10.7 %gradients.1 = (bf16[512,1024]{1,0:T(8,128)(2,1)S(1)}, bf16[512,1024]{1,0:T(8,128)(2,1)}, bf16[512,1024]{1,0:T(8,128)(2,1)S(1)}, bf16[512,1024]{1,0:T(8,128)(2,1...) custom-call(s32[10]{0:T(128)S(1)} %copy-done.4, ...), custom_call_target="tpu_custom_call" | custom-call | flops 99999997952 | bytes 1 | tf_op jit(solution)/shard_map/gradients/pallas_call | solution.py:159
  160.8 3.2 %collective-permute-done.34.refs_3_ = bf16[256,1024]{1,0:T(8,128)(2,1)S(1)} collective-permute-done((bf16[256,1024]{1,0:T(8,128)(2,1)S(1)}, bf16[256,1024]{1,0:T(8,128)(2,1)S(1)}, u32[]{:S(2)}, u32[]{:S(2)}) %collective-permute-start.34) | collective-permute-done | bytes 524320 | tf_op jit(solution)/shard_map/ppermute | solution.py:1348
  174.8 2.8 fold.8
  180.9 4.9 %collective-permute-done.39.refs_4_ = bf16[256,256]{1,0:T(8,128)(2,1)S(1)} collective-permute-done((bf16[256,256]{1,0:T(8,128)(2,1)S(1)}, bf16[256,256]{1,0:T(8,128)(2,1)S(1)}, u32[]{:S(2)}, u32[]{:S(2)}) %collective-permute-start.39) | collective-permute-done | bytes 131104 | tf_op jit(solution)/shard_map/ppermute | solution.py:1348
  186.8 5.8 %collective-permute-done.41.refs_2_ = bf16[512,1024]{1,0:T(8,128)(2,1)} collective-permute-done((bf16[512,1024]{1,0:T(8,128)(2,1)}, bf16[512,1024]{1,0:T(8,128)(2,1)}, u32[]{:S(2)}, u32[]{:S(2)}) %collective-permute-start.41) | collective-permute-done | bytes 1048608 | tf_op jit(solution)/shard_map/ppermute | solution.py:1348
  197.9 12.1 %attend_back.1 = (bf16[1024,768]{1,0:T(8,128)(2,1)S(1)}, bf16[512,384]{1,0:T(8,128)(2,1)S(1)}, bf16[512,384]{1,0:T(8,128)(2,1)}, bf16[512,384]{1,0:T(8,128)(2,1)...) custom-call(s32[10]{0:T(128)S(1)} %copy-done.4, f32[1024,1]{1,0:T(8,128)S(1)} %copy.32.refs_1_, ...), custom_call_target="tpu_custom_call" | custom-call | flops 99999997952 | bytes 1 | tf_op jit(solution)/shard_map/attend_back/pallas_call | solution.py:159
  212.9 3.5 %input_slope.1 = (bf16[512,1024]{1,0:T(8,128)(2,1)S(1)}, bf16[512,1024]{1,0:T(8,128)(2,1)S(1)}, f32[16,1024]{1,0:T(8,128)S(1)}, bf16[16,1024]{1,0:T(8,128)(2,1)S(1)}, f32[8,128]{1,0:T(8,128)S(1)}) custom-call(s32[10]{0:T(128)S(1)} %copy-done.4, bf16[1024,768]{1,0:T(8,128)(2,1)S(1)} %get-tuple-element.266.refs_1_, ...), custom_call_target="tpu_custom_call" | custom-call | flops 99999997952 | bytes 1 | tf_op jit(solution)/shard_map/input_slope/pallas_call | solution.py:159
  239.0 18.3 %collective-permute-done.50.refs_1_.refs_3_ = bf16[256,1024]{1,0:T(8,128)(2,1)S(1)} collective-permute-done((bf16[256,1024]{1,0:T(8,128)(2,1)S(1)}, bf16[256,1024]{1,0:T(8,128)(2,1)S(1)}, u32[]{:S(2)}, u32[]{:S(2)}) %collective-permute-start.50) | collective-permute-done | bytes 524320 | tf_op jit(solution)/shard_map/ppermute | solution.py:1348
  272.3 5.1 %collective-permute-done.59.refs_5_ = bf16[64,512]{1,0:T(8,128)(2,1)S(1)} collective-permute-done((bf16[64,512]{1,0:T(8,128)(2,1)S(1)}, bf16[64,512]{1,0:T(8,128)(2,1)S(1)}, u32[]{:S(2)}, u32[]{:S(2)}) %collective-permute-start.59) | collective-permute-done | bytes 65568 | tf_op jit(solution)/shard_map/ppermute | solution.py:1348
  (224 shorter events, 113.8 us)
Async XLA Ops:
  0.6 16.9 %collective-permute-start.1 = (bf16[256,1024]{1,0:T(8,128)(2,1)}, bf16[256,1024]{1,0:T(8,128)(2,1)S(1)}, u32[]{:S(2)}, u32[]{:S(2)}) collective-permute-start(bf16[256,1024]{1,0:T(8,128)(2,1)} %bitcast.38), channel_id=1, source_target_pairs={{0,8},{1,9},{2,10},{3,11},{4,12},{5,13},{6,14},{7,15},{8,0},{9,1},... | collective-permute-start | bytes 1572872 | tf_op jit(solution)/shard_map/ppermute | solution.py:1348
  19.6 18.4 %collective-permute-start.8 = (bf16[2,128,1024]{2,1,0:T(8,128)(2,1)S(1)}, bf16[2,128,1024]{2,1,0:T(8,128)(2,1)S(1)}, u32[]{:S(2)}, u32[]{:S(2)}) collective-permute-start(bf16[2,128,1024]{2,1,0:T(8,128)(2,1)S(1)} %get-tuple-element.192.refs_25_.refs_8_), channel_id=1, source_target_pairs={{0,2},{1,3},{2,0},{3,1},{4,6},{5,7},{6,4},{7,5},{8,10},{9,11},{10,... | collective-permute-start | bytes 1572872 | tf_op jit(solution)/shard_map/ppermute | solution.py:1348
  33.1 14.8 %collective-permute-start.5 = (bf16[144,768]{1,0:T(8,128)(2,1)S(1)}, bf16[144,768]{1,0:T(8,128)(2,1)S(1)}, u32[]{:S(2)}, u32[]{:S(2)}) collective-permute-start(bf16[144,768]{1,0:T(8,128)(2,1)S(1)} %get-tuple-element.187.refs_0_), channel_id=1, source_target_pairs={{0,16},{1,17},{2,18},{3,19},{4,20},{5,21},{6,22},{7,23},{8,24},{9,... | collective-permute-start | bytes 663560 | tf_op jit(solution)/shard_map/ppermute | solution.py:1348
  38.9 18.7 %collective-permute-start.11 = (bf16[1024,1024]{1,0:T(8,128)(2,1)S(1)}, bf16[1024,1024]{1,0:T(8,128)(2,1)S(1)}, u32[]{:S(2)}, u32[]{:S(2)}) collective-permute-start(bf16[1024,1024]{1,0:T(8,128)(2,1)S(1)} %get-tuple-element.197), channel_id=1, source_target_pairs={{0,1},{1,0},{2,3},{3,2},{4,5},{5,4},{6,7},{7,6},{8,9},{9,8},{10,11... | collective-permute-start | bytes 6291464 | tf_op jit(solution)/shard_map/ppermute | solution.py:1348
  60.8 27.6 %collective-permute-start.18 = (bf16[256,1024]{1,0:T(8,128)(2,1)}, bf16[256,1024]{1,0:T(8,128)(2,1)}, u32[]{:S(2)}, u32[]{:S(2)}) collective-permute-start(bf16[256,1024]{1,0:T(8,128)(2,1)} %get-tuple-element.210), channel_id=1, source_target_pairs={{0,8},{1,9},{2,10},{3,11},{4,12},{5,13},{6,14},{7,15},{8,0},{9,1},... | collective-permute-start | bytes 1572872 | tf_op jit(solution)/shard_map/ppermute | solution.py:1348
  61.4 31.3 %collective-permute-start.17 = (bf16[320,1024]{1,0:T(8,128)(2,1)}, bf16[320,1024]{1,0:T(8,128)(2,1)}, u32[]{:S(2)}, u32[]{:S(2)}) collective-permute-start(bf16[320,1024]{1,0:T(8,128)(2,1)} %get-tuple-element.209), channel_id=1, source_target_pairs={{0,16},{1,17},{2,18},{3,19},{4,20},{5,21},{6,22},{7,23},{8,24},{9,... | collective-permute-start | bytes 1966088 | tf_op jit(solution)/shard_map/ppermute | solution.py:1348
  72.1 20.6 %collective-permute-start.13 = (bf16[2,192,1024]{2,1,0:T(8,128)(2,1)S(1)}, bf16[2,192,1024]{2,1,0:T(8,128)(2,1)S(1)}, u32[]{:S(2)}, u32[]{:S(2)}) collective-permute-start(bf16[2,192,1024]{2,1,0:T(8,128)(2,1)S(1)} %get-tuple-element.203.refs_0_.refs_21_), channel_id=1, source_target_pairs={{0,4},{1,5},{2,6},{3,7},{4,0},{5,1},{6,2},{7,3},{8,12},{9,13},{10,... | collective-permute-start | bytes 2359304 | tf_op jit(solution)/shard_map/ppermute | solution.py:1348
  95.3 14.9 %collective-permute-start.16 = (bf16[512,256]{1,0:T(8,128)(2,1)S(1)}, bf16[512,256]{1,0:T(8,128)(2,1)S(1)}, u32[]{:S(2)}, u32[]{:S(2)}) collective-permute-start(bf16[512,256]{1,0:T(8,128)(2,1)S(1)} %get-tuple-element.208.refs_6_), channel_id=1, source_target_pairs={{0,8},{1,9},{2,10},{3,11},{4,12},{5,13},{6,14},{7,15},{8,0},{9,1},... | collective-permute-start | bytes 786440 | tf_op jit(solution)/shard_map/ppermute | solution.py:1348
  95.3 14.9 %collective-permute-start.15 = (bf16[512,256]{1,0:T(8,128)(2,1)S(1)}, bf16[512,256]{1,0:T(8,128)(2,1)S(1)}, u32[]{:S(2)}, u32[]{:S(2)}) collective-permute-start(bf16[512,256]{1,0:T(8,128)(2,1)S(1)} %get-tuple-element.207), channel_id=1, source_target_pairs={{0,24},{1,25},{2,26},{3,27},{4,28},{5,29},{6,30},{7,31},{8,16},{9,... | collective-permute-start | bytes 786440 | tf_op jit(solution)/shard_map/ppermute | solution.py:1348
  104.5 19.5 %collective-permute-start.22 = (bf16[2,192,1024]{2,1,0:T(8,128)(2,1)}, bf16[2,192,1024]{2,1,0:T(8,128)(2,1)}, u32[]{:S(2)}, u32[]{:S(2)}) collective-permute-start(bf16[2,192,1024]{2,1,0:T(8,128)(2,1)} %get-tuple-element.218.refs_0_.refs_23_), channel_id=1, source_target_pairs={{0,4},{1,5},{2,6},{3,7},{4,0},{5,1},{6,2},{7,3},{8,12},{9,13},{10,... | collective-permute-start | bytes 2359304 | tf_op jit(solution)/shard_map/ppermute | solution.py:1348
  111.9 14.3 %collective-permute-start.30 = (bf16[256,1024]{1,0:T(8,128)(2,1)}, bf16[256,1024]{1,0:T(8,128)(2,1)S(1)}, u32[]{:S(2)}, u32[]{:S(2)}) collective-permute-start(bf16[256,1024]{1,0:T(8,128)(2,1)} %collective-permute-done.18.refs_2_.refs_17_.refs_5_), channel_id=1, source_target_pairs={{0,1},{1,0},{2,3},{3,2},{4,5},{5,4},{6,7},{7,6},{8,9},{9,8},{10,11... | collective-permute-start | bytes 1572872 | tf_op jit(solution)/shard_map/ppermute | solution.py:1348
  112.4 13.9 %collective-permute-start.25 = (bf16[512,256]{1,0:T(8,128)(2,1)S(1)}, bf16[512,256]{1,0:T(8,128)(2,1)S(1)}, u32[]{:S(2)}, u32[]{:S(2)}) collective-permute-start(bf16[512,256]{1,0:T(8,128)(2,1)S(1)} %get-tuple-element.221.refs_8_), channel_id=1, source_target_pairs={{0,8},{1,9},{2,10},{3,11},{4,12},{5,13},{6,14},{7,15},{8,0},{9,1},... | collective-permute-start | bytes 786440 | tf_op jit(solution)/shard_map/ppermute | solution.py:1348
  113.4 15.0 %collective-permute-start.31 = (bf16[2,128,1024]{2,1,0:T(8,128)(2,1)S(1)}, bf16[2,128,1024]{2,1,0:T(8,128)(2,1)S(1)}, u32[]{:S(2)}, u32[]{:S(2)}) collective-permute-start(bf16[2,128,1024]{2,1,0:T(8,128)(2,1)S(1)} %get-tuple-element.222.refs_27_.refs_10_), channel_id=1, source_target_pairs={{0,2},{1,3},{2,0},{3,1},{4,6},{5,7},{6,4},{7,5},{8,10},{9,11},{10,... | collective-permute-start | bytes 1572872 | tf_op jit(solution)/shard_map/ppermute | solution.py:1348
  150.0 14.0 %collective-permute-start.34 = (bf16[256,1024]{1,0:T(8,128)(2,1)S(1)}, bf16[256,1024]{1,0:T(8,128)(2,1)S(1)}, u32[]{:S(2)}, u32[]{:S(2)}) collective-permute-start(bf16[256,1024]{1,0:T(8,128)(2,1)S(1)} %get-tuple-element.236), channel_id=1, source_target_pairs={{0,8},{1,9},{2,10},{3,11},{4,12},{5,13},{6,14},{7,15},{8,0},{9,1},... | collective-permute-start | bytes 1572872 | tf_op jit(solution)/shard_map/ppermute | solution.py:1348
  167.1 25.5 %collective-permute-start.41 = (bf16[512,1024]{1,0:T(8,128)(2,1)}, bf16[512,1024]{1,0:T(8,128)(2,1)}, u32[]{:S(2)}, u32[]{:S(2)}) collective-permute-start(bf16[512,1024]{1,0:T(8,128)(2,1)} %get-tuple-element.261), channel_id=1, source_target_pairs={{0,4},{1,5},{2,6},{3,7},{4,0},{5,1},{6,2},{7,3},{8,12},{9,13},{10,... | collective-permute-start | bytes 3145736 | tf_op jit(solution)/shard_map/ppermute | solution.py:1348
  167.7 25.2 %collective-permute-start.42 = (bf16[512,1024]{1,0:T(8,128)(2,1)}, bf16[512,1024]{1,0:T(8,128)(2,1)}, u32[]{:S(2)}, u32[]{:S(2)}) collective-permute-start(bf16[512,1024]{1,0:T(8,128)(2,1)} %get-tuple-element.263), channel_id=1, source_target_pairs={{0,2},{1,3},{2,0},{3,1},{4,6},{5,7},{6,4},{7,5},{8,10},{9,11},{10,... | collective-permute-start | bytes 3145736 | tf_op jit(solution)/shard_map/ppermute | solution.py:1348
  180.9 30.2 %collective-permute-start.45 = (bf16[512,512]{1,0:T(8,128)(2,1)}, bf16[512,512]{1,0:T(8,128)(2,1)}, u32[]{:S(2)}, u32[]{:S(2)}) collective-permute-start(bf16[512,512]{1,0:T(8,128)(2,1)} %get-tuple-element.276), channel_id=1, source_target_pairs={{0,8},{1,9},{2,10},{3,11},{4,12},{5,13},{6,14},{7,15},{8,0},{9,1},... | collective-permute-start | bytes 1572872 | tf_op jit(solution)/shard_map/ppermute | solution.py:1348
  194.9 16.2 %collective-permute-start.43 = (bf16[256,1024]{1,0:T(8,128)(2,1)S(1)}, bf16[256,1024]{1,0:T(8,128)(2,1)S(1)}, u32[]{:S(2)}, u32[]{:S(2)}) collective-permute-start(bf16[256,1024]{1,0:T(8,128)(2,1)S(1)} %get-tuple-element.273), channel_id=1, source_target_pairs={{0,2},{1,3},{2,0},{3,1},{4,6},{5,7},{6,4},{7,5},{8,10},{9,11},{10,... | collective-permute-start | bytes 1572872 | tf_op jit(solution)/shard_map/ppermute | solution.py:1348
  196.4 14.7 %collective-permute-start.44 = (bf16[256,1024]{1,0:T(8,128)(2,1)S(1)}, bf16[256,1024]{1,0:T(8,128)(2,1)S(1)}, u32[]{:S(2)}, u32[]{:S(2)}) collective-permute-start(bf16[256,1024]{1,0:T(8,128)(2,1)S(1)} %get-tuple-element.275), channel_id=1, source_target_pairs={{0,4},{1,5},{2,6},{3,7},{4,0},{5,1},{6,2},{7,3},{8,12},{9,13},{10,... | collective-permute-start | bytes 1572872 | tf_op jit(solution)/shard_map/ppermute | solution.py:1348
  218.0 41.7 %collective-permute-start.36 = (bf16[256,1024]{1,0:T(8,128)(2,1)}, bf16[256,1024]{1,0:T(8,128)(2,1)}, u32[]{:S(2)}, u32[]{:S(2)}) collective-permute-start(bf16[256,1024]{1,0:T(8,128)(2,1)} %get-tuple-element.246), channel_id=1, source_target_pairs={{0,8},{1,9},{2,10},{3,11},{4,12},{5,13},{6,14},{7,15},{8,0},{9,1},... | collective-permute-start | bytes 1572872 | tf_op jit(solution)/shard_map/ppermute | solution.py:1348
  218.3 43.4 %collective-permute-start.57 = (bf16[2,128,1024]{2,1,0:T(8,128)(2,1)}, bf16[2,128,1024]{2,1,0:T(8,128)(2,1)}, u32[]{:S(2)}, u32[]{:S(2)}) collective-permute-start(bf16[2,128,1024]{2,1,0:T(8,128)(2,1)} %get-tuple-element.312), channel_id=1, source_target_pairs={{0,16},{1,17},{2,18},{3,19},{4,20},{5,21},{6,22},{7,23},{8,24},{9,... | collective-permute-start | bytes 1572872 | tf_op jit(solution)/shard_map/ppermute | solution.py:1348
  233.6 30.0 %collective-permute-start.56 = (bf16[160,768]{1,0:T(8,128)(2,1)}, bf16[160,768]{1,0:T(8,128)(2,1)}, u32[]{:S(2)}, u32[]{:S(2)}) collective-permute-start(bf16[160,768]{1,0:T(8,128)(2,1)} %get-tuple-element.310), channel_id=1, source_target_pairs={{0,16},{1,17},{2,18},{3,19},{4,20},{5,21},{6,22},{7,23},{8,24},{9,... | collective-permute-start | bytes 737288 | tf_op jit(solution)/shard_map/ppermute | solution.py:1348
  233.9 23.4 %collective-permute-start.50 = (bf16[256,1024]{1,0:T(8,128)(2,1)S(1)}, bf16[256,1024]{1,0:T(8,128)(2,1)S(1)}, u32[]{:S(2)}, u32[]{:S(2)}) collective-permute-start(bf16[256,1024]{1,0:T(8,128)(2,1)S(1)} %get-tuple-element.290), channel_id=1, source_target_pairs={{0,8},{1,9},{2,10},{3,11},{4,12},{5,13},{6,14},{7,15},{8,0},{9,1},... | collective-permute-start | bytes 1572872 | tf_op jit(solution)/shard_map/ppermute | solution.py:1348
  237.6 27.4 %collective-permute-start.55 = (bf16[128,512]{1,0:T(8,128)(2,1)}, bf16[128,512]{1,0:T(8,128)(2,1)}, u32[]{:S(2)}, u32[]{:S(2)}) collective-permute-start(bf16[128,512]{1,0:T(8,128)(2,1)} %get-tuple-element.308), channel_id=1, source_target_pairs={{0,2},{1,3},{2,0},{3,1},{4,6},{5,7},{6,4},{7,5},{8,10},{9,11},{10,... | collective-permute-start | bytes 393224 | tf_op jit(solution)/shard_map/ppermute | solution.py:1348
  (77 other events, 542.2 us)

commit v5 on v4

--- a/solution.py
+++ b/solution.py
@@ -69,7 +69,7 @@
 
 WEIGHTS = {'pack': 10000000000, 'unpair': 10000000000, 'trade': 1, 'join_down': 1, 'mask': 1}
 FREE = {'trade': [0]}
-WAITS = {}
+WAITS = {'stack_far': ['down_c'], 'pick': ['ups_came'], 'd_down': ['down_came']}
 GRANTS = {'o2': 32}
 HEAVY = 10**11
 PLAN = (
@@ -93,10 +93,10 @@
     "fold_norm",
     "gradients",
     "turn",
+    "outer",
     "pick",
-    "outer",
+    "o0",
     "out_fold",
-    "o0",
     "assemble",
     "planes",
     "attend_back",
@@ -108,9 +108,9 @@
     "top",
     "o2",
     "add",
-    "layer",
     "d_down",
     "home0",
+    "layer",
     "o3",
     "last",
     "home1",
@@ -124,7 +124,7 @@
 
 class Order:
     def __init__(self):
-        self.ticket = jnp.zeros((8, LANES), F32)
+        self.ticket = ()
         self.step = ""
         self.waits = ()
 
@@ -133,17 +133,18 @@
     weight = WEIGHTS.get(order.step, HEAVY)
     after = tuple(v for i, v in enumerate(after) if i not in FREE.get(order.step, ()))
     after, order.waits = after + order.waits, ()
-    count, given = len(args), len(outs)
+    count, given, held = len(args), len(outs), len(order.ticket)
     inner = body
 
     def body(*refs):
         ins, rest = refs[:count], refs[count + len(after) :]
-        before, results, ticket = rest[0], rest[1 : 1 + given], rest[1 + given]
-        ticket[...] = before[...]
-        inner(*ins, *results, *rest[2 + given :])
+        before, rest = rest[:held], rest[held:]
+        results, ticket = rest[:given], rest[given]
+        ticket[...] = before[0][...] if held else jnp.zeros_like(ticket)
+        inner(*ins, *results, *rest[given + 1 :])
 
     away = tuple(away) + tuple(range(count, count + len(after)))
-    args = args + tuple(after) + (order.ticket,)
+    args = args + tuple(after) + order.ticket
     outs = list(outs) + [shaped((8, LANES), F32)]
 
     def spec(i, places):
@@ -156,7 +157,7 @@
         for i in range(len(args))
     ]
     moved = sum(v.size * v.dtype.itemsize for v in args + tuple(outs))
-    *results, order.ticket = pl.pallas_call(
+    *results, ticket = pl.pallas_call(
         body,
         in_specs=ins,
         out_specs=[spec(i, ()) for i in range(len(outs))],
@@ -166,6 +167,7 @@
         cost_estimate=pl.CostEstimate(flops=weight, bytes_accessed=1, transcendentals=0),
         name=name,
     )(*args)
+    order.ticket = (ticket,)
     return results
 
 

time: 288 us -> 283 us (0.983)
  waiting for transfers between devices: 100 us -> 95.5 us
    ppermute x61, waiting for transfers between devices: 100 us -> 95.5 us  [send(): return lax.ppermute(value, AXES, route)]
  transfers between devices with their start and end apart: 61 -> 61, of which waited for: 25 -> 26; matrix products, arithmetic and copies ran while one was open for 1% -> 0% of each run, Pallas kernels for 28% -> 30%
where the time goes in v5:
time: 283 us; the launch traced here: 279 us
  Pallas kernels  106 us (37%)
  waiting for transfers between devices  95.5 us (34%)
  starting transfers between devices  69.6 us (25%)
  local copies, waits for them, and re-layouts  5.15 us (2%)
    pallas_call x42, Pallas kernels, kernel_call(): pl.pallas_call(body, in_specs=ins, out_specs=[spec(i, ()) for i in range(...  106 us
    ppermute x61, waiting for transfers between devices, send(): return lax.ppermute(value, AXES, route)  95.5 us
    ppermute x61, starting transfers between devices, send(): return lax.ppermute(value, AXES, route)  69.6 us
  transfers between devices with their start and end apart: 61, of which 26 were waited for; matrix products, arithmetic and copies ran while one was open for 0% of the time, Pallas kernels for 30%

profile of v5, /device:TPU:0, one launch (start us, length us, event | category | flops | bytes accessed | tf_op | source)
XLA Modules:
  0.0 279.0 jit_solution(7646732380152921023)
XLA Ops:
  0.6 3.1 %collective-permute-start.1 = (bf16[256,1024]{1,0:T(8,128)(2,1)}, bf16[256,1024]{1,0:T(8,128)(2,1)S(1)}, u32[]{:S(2)}, u32[]{:S(2)}) collective-permute-start(bf16[256,1024]{1,0:T(8,128)(2,1)} %bitcast.38), channel_id=1, source_target_pairs={{0,8},{1,9},{2,10},{3,11},{4,12},{5,13},{6,14},{7,15},{8,0},{9,1},... | collective-permute-start | bytes 1572872 | tf_op jit(solution)/shard_map/ppermute | solution.py:1350
  5.0 3.1 %pack.1 = (bf16[48,4096]{1,0:T(8,128)(2,1)}, bf16[48,4096]{1,0:T(8,128)(2,1)}, f32[8,128]{1,0:T(8,128)}) custom-call(s32[10]{0:T(128)} %stack.49.refs_0_, s32[1]{0:T(128)S(6)} %copy.34.refs_1_, bf16[32,3072]{1,0:T(8,128)(2,1)} %refs_2_.1, bf16[32,4096]{1,0:T(8,128)(2,1)} %refs_3_.1, s32[1,1024]{1,0:T(1,128)} %refs_4_.2, bf16[32,1024]{1,0:T(8,128)(2,1)} %refs_5_.1, ...), custom_call_target="tpu_custom_call" | custom-call | flops 10000000000 | bytes 1 | tf_op jit(solution)/shard_map/pack/pallas_call | solution.py:160
  11.9 5.1 %collective-permute-done.2.refs_4_.refs_1_ = bf16[1,128,1024]{2,1,0:T(8,128)(2,1)S(1)} collective-permute-done((bf16[1,128,1024]{2,1,0:T(8,128)(2,1)S(1)}, bf16[1,128,1024]{2,1,0:T(8,128)(2,1)S(1)}, u32[]{:S(2)}, u32[]{:S(2)}) %collective-permute-start.2) | collective-permute-done | bytes 262176 | tf_op jit(solution)/shard_map/ppermute | solution.py:1350
  21.3 10.4 %collective-permute-done.3.refs_2_ = bf16[80,2304]{1,0:T(8,128)(2,1)S(1)} collective-permute-done((bf16[80,2304]{1,0:T(8,128)(2,1)S(1)}, bf16[80,2304]{1,0:T(8,128)(2,1)S(1)}, u32[]{:S(2)}, u32[]{:S(2)}) %collective-permute-start.3) | collective-permute-done | bytes 368672 | tf_op jit(solution)/shard_map/ppermute | solution.py:1350
  33.1 4.6 %collective-permute-start.5 = (bf16[144,768]{1,0:T(8,128)(2,1)S(1)}, bf16[144,768]{1,0:T(8,128)(2,1)S(1)}, u32[]{:S(2)}, u32[]{:S(2)}) collective-permute-start(bf16[144,768]{1,0:T(8,128)(2,1)S(1)} %get-tuple-element.187.refs_0_), channel_id=1, source_target_pairs={{0,16},{1,17},{2,18},{3,19},{4,20},{5,21},{6,22},{7,23},{8,24},{9,... | collective-permute-start | bytes 663560 | tf_op jit(solution)/shard_map/ppermute | solution.py:1350
  40.2 7.7 %collective-permute-start.11 = (bf16[1024,1024]{1,0:T(8,128)(2,1)S(1)}, bf16[1024,1024]{1,0:T(8,128)(2,1)S(1)}, u32[]{:S(2)}, u32[]{:S(2)}) collective-permute-start(bf16[1024,1024]{1,0:T(8,128)(2,1)S(1)} %get-tuple-element.197), channel_id=1, source_target_pairs={{0,1},{1,0},{2,3},{3,2},{4,5},{5,4},{6,7},{7,6},{8,9},{9,8},{10,11... | collective-permute-start | bytes 6291464 | tf_op jit(solution)/shard_map/ppermute | solution.py:1350
  52.1 4.4 %collective-permute-done.9.refs_1_ = bf16[2,144,384]{2,1,0:T(8,128)(2,1)S(1)} collective-permute-done((bf16[2,144,384]{2,1,0:T(8,128)(2,1)S(1)}, bf16[2,144,384]{2,1,0:T(8,128)(2,1)S(1)}, u32[]{:S(2)}, u32[]{:S(2)}) %collective-permute-start.9) | collective-permute-done | bytes 221216 | tf_op jit(solution)/shard_map/ppermute | solution.py:1350
  61.5 3.2 %collective-permute-start.17 = (bf16[320,1024]{1,0:T(8,128)(2,1)}, bf16[320,1024]{1,0:T(8,128)(2,1)}, u32[]{:S(2)}, u32[]{:S(2)}) collective-permute-start(bf16[320,1024]{1,0:T(8,128)(2,1)} %get-tuple-element.209), channel_id=1, source_target_pairs={{0,16},{1,17},{2,18},{3,19},{4,20},{5,21},{6,22},{7,23},{8,24},{9,... | collective-permute-start | bytes 1966088 | tf_op jit(solution)/shard_map/ppermute | solution.py:1350
  65.2 4.9 %collective-permute-done.12.refs_2_.refs_9_ = bf16[4,144,384]{2,1,0:T(8,128)(2,1)S(1)} collective-permute-done((bf16[4,144,384]{2,1,0:T(8,128)(2,1)S(1)}, bf16[4,144,384]{2,1,0:T(8,128)(2,1)S(1)}, u32[]{:S(2)}, u32[]{:S(2)}) %collective-permute-start.12) | collective-permute-done | bytes 442400 | tf_op jit(solution)/shard_map/ppermute | solution.py:1350
  75.6 12.8 %attend.1 = (bf16[512,256]{1,0:T(8,128)(2,1)S(1)}, bf16[512,256]{1,0:T(8,128)(2,1)S(1)}, bf16[1024,768]{1,0:T(8,128)(2,1)S(1)}, f32[256,1024]{1,0:T(8,128)S(1)},...) custom-call(s32[10]{0:T(128)S(1)} %copy-done.4, ...), custom_call_target="tpu_custom_call" | custom-call | flops 99999997952 | bytes 1 | tf_op jit(solution)/shard_map/attend/pallas_call | solution.py:160
  88.5 4.3 %collective-permute-done.17.refs_0_ = bf16[320,1024]{1,0:T(8,128)(2,1)} collective-permute-done((bf16[320,1024]{1,0:T(8,128)(2,1)}, bf16[320,1024]{1,0:T(8,128)(2,1)}, u32[]{:S(2)}, u32[]{:S(2)}) %collective-permute-start.17) | collective-permute-done | bytes 655392 | tf_op jit(solution)/shard_map/ppermute | solution.py:1350
  97.8 5.8 %collective-permute-done.20.refs_3_ = bf16[1,128,1024]{2,1,0:T(8,128)(2,1)S(1)} collective-permute-done((bf16[1,128,1024]{2,1,0:T(8,128)(2,1)S(1)}, bf16[1,128,1024]{2,1,0:T(8,128)(2,1)S(1)}, u32[]{:S(2)}, u32[]{:S(2)}) %collective-permute-start.20) | collective-permute-done | bytes 262176 | tf_op jit(solution)/shard_map/ppermute | solution.py:1350
  105.1 5.1 %collective-permute-done.15.refs_0_ = bf16[512,256]{1,0:T(8,128)(2,1)S(1)} collective-permute-done((bf16[512,256]{1,0:T(8,128)(2,1)S(1)}, bf16[512,256]{1,0:T(8,128)(2,1)S(1)}, u32[]{:S(2)}, u32[]{:S(2)}) %collective-permute-start.15) | collective-permute-done | bytes 262176 | tf_op jit(solution)/shard_map/ppermute | solution.py:1350
  114.9 9.2 %collective-permute-done.22.refs_1_.refs_24_ = bf16[2,192,1024]{2,1,0:T(8,128)(2,1)} collective-permute-done((bf16[2,192,1024]{2,1,0:T(8,128)(2,1)}, bf16[2,192,1024]{2,1,0:T(8,128)(2,1)}, u32[]{:S(2)}, u32[]{:S(2)}) %collective-permute-start.22) | collective-permute-done | bytes 786464 | tf_op jit(solution)/shard_map/ppermute | solution.py:1350
  128.9 17.3 %feed_forward.1 = (bf16[512,1024]{1,0:T(8,128)(2,1)S(1)}, bf16[512,1024]{1,0:T(8,128)(2,1)S(1)}, f32[256,1024]{1,0:T(8,128)S(1)}, bf16[256,1024]{1,0:T(8,128)(2,...) custom-call(s32[10]{0:T(128)S(1)} %copy-done.4, ...), custom_call_target="tpu_custom_call" | custom-call | flops 99999997952 | bytes 1 | tf_op jit(solution)/shard_map/feed_forward/pallas_call | solution.py:160
  150.1 10.7 %gradients.1 = (bf16[512,1024]{1,0:T(8,128)(2,1)S(1)}, bf16[512,1024]{1,0:T(8,128)(2,1)}, bf16[512,1024]{1,0:T(8,128)(2,1)S(1)}, bf16[512,1024]{1,0:T(8,128)(2,1...) custom-call(s32[10]{0:T(128)S(1)} %copy-done.4, ...), custom_call_target="tpu_custom_call" | custom-call | flops 99999997952 | bytes 1 | tf_op jit(solution)/shard_map/gradients/pallas_call | solution.py:160
  176.4 2.6 fold.9
  179.1 5.0 %collective-permute-done.39.refs_3_ = bf16[256,256]{1,0:T(8,128)(2,1)} collective-permute-done((bf16[256,256]{1,0:T(8,128)(2,1)}, bf16[256,256]{1,0:T(8,128)(2,1)}, u32[]{:S(2)}, u32[]{:S(2)}) %collective-permute-start.39) | collective-permute-done | bytes 131104 | tf_op jit(solution)/shard_map/ppermute | solution.py:1350
  192.1 12.0 %attend_back.1 = (bf16[1024,768]{1,0:T(8,128)(2,1)S(1)}, bf16[512,384]{1,0:T(8,128)(2,1)S(1)}, bf16[512,384]{1,0:T(8,128)(2,1)}, bf16[512,384]{1,0:T(8,128)(2,1)...) custom-call(s32[10]{0:T(128)S(1)} %copy-done.4, f32[1024,1]{1,0:T(8,128)S(1)} %copy.32.refs_1_, ...), custom_call_target="tpu_custom_call" | custom-call | flops 99999997952 | bytes 1 | tf_op jit(solution)/shard_map/attend_back/pallas_call | solution.py:160
  207.4 3.5 %input_slope.1 = (bf16[512,1024]{1,0:T(8,128)(2,1)S(1)}, bf16[512,1024]{1,0:T(8,128)(2,1)S(1)}, f32[16,1024]{1,0:T(8,128)S(1)}, bf16[16,1024]{1,0:T(8,128)(2,1)S(1)}, f32[8,128]{1,0:T(8,128)S(1)}) custom-call(s32[10]{0:T(128)S(1)} %copy-done.4, bf16[1024,768]{1,0:T(8,128)(2,1)S(1)} %get-tuple-element.270.refs_1_, ...), custom_call_target="tpu_custom_call" | custom-call | flops 99999997952 | bytes 1 | tf_op jit(solution)/shard_map/input_slope/pallas_call | solution.py:160
  233.2 18.9 %collective-permute-done.54.refs_1_.refs_3_ = bf16[256,1024]{1,0:T(8,128)(2,1)S(1)} collective-permute-done((bf16[256,1024]{1,0:T(8,128)(2,1)S(1)}, bf16[256,1024]{1,0:T(8,128)(2,1)S(1)}, u32[]{:S(2)}, u32[]{:S(2)}) %collective-permute-start.54) | collective-permute-done | bytes 524320 | tf_op jit(solution)/shard_map/ppermute | solution.py:1350
  260.9 3.3 %collective-permute-start.59 = (bf16[64,512]{1,0:T(8,128)(2,1)S(1)}, bf16[64,512]{1,0:T(8,128)(2,1)S(1)}, u32[]{:S(2)}, u32[]{:S(2)}) collective-permute-start(bf16[64,512]{1,0:T(8,128)(2,1)S(1)} %get-tuple-element.324), channel_id=1, source_target_pairs={{0,16},{1,17},{2,18},{3,19},{4,20},{5,21},{6,22},{7,23},{8,24},{9,... | collective-permute-start | bytes 196616 | tf_op jit(solution)/shard_map/ppermute | solution.py:1350
  264.4 2.7 input_gradient.1
  267.2 6.2 %collective-permute-done.59.refs_5_ = bf16[64,512]{1,0:T(8,128)(2,1)S(1)} collective-permute-done((bf16[64,512]{1,0:T(8,128)(2,1)S(1)}, bf16[64,512]{1,0:T(8,128)(2,1)S(1)}, u32[]{:S(2)}, u32[]{:S(2)}) %collective-permute-start.59) | collective-permute-done | bytes 65568 | tf_op jit(solution)/shard_map/ppermute | solution.py:1350
  (231 shorter events, 110.5 us)
Async XLA Ops:
  0.6 16.3 %collective-permute-start.1 = (bf16[256,1024]{1,0:T(8,128)(2,1)}, bf16[256,1024]{1,0:T(8,128)(2,1)S(1)}, u32[]{:S(2)}, u32[]{:S(2)}) collective-permute-start(bf16[256,1024]{1,0:T(8,128)(2,1)} %bitcast.38), channel_id=1, source_target_pairs={{0,8},{1,9},{2,10},{3,11},{4,12},{5,13},{6,14},{7,15},{8,0},{9,1},... | collective-permute-start | bytes 1572872 | tf_op jit(solution)/shard_map/ppermute | solution.py:1350
  19.7 19.5 %collective-permute-start.8 = (bf16[2,128,1024]{2,1,0:T(8,128)(2,1)S(1)}, bf16[2,128,1024]{2,1,0:T(8,128)(2,1)S(1)}, u32[]{:S(2)}, u32[]{:S(2)}) collective-permute-start(bf16[2,128,1024]{2,1,0:T(8,128)(2,1)S(1)} %get-tuple-element.192.refs_25_.refs_8_), channel_id=1, source_target_pairs={{0,2},{1,3},{2,0},{3,1},{4,6},{5,7},{6,4},{7,5},{8,10},{9,11},{10,... | collective-permute-start | bytes 1572872 | tf_op jit(solution)/shard_map/ppermute | solution.py:1350
  33.1 14.8 %collective-permute-start.5 = (bf16[144,768]{1,0:T(8,128)(2,1)S(1)}, bf16[144,768]{1,0:T(8,128)(2,1)S(1)}, u32[]{:S(2)}, u32[]{:S(2)}) collective-permute-start(bf16[144,768]{1,0:T(8,128)(2,1)S(1)} %get-tuple-element.187.refs_0_), channel_id=1, source_target_pairs={{0,16},{1,17},{2,18},{3,19},{4,20},{5,21},{6,22},{7,23},{8,24},{9,... | collective-permute-start | bytes 663560 | tf_op jit(solution)/shard_map/ppermute | solution.py:1350
  40.2 17.4 %collective-permute-start.11 = (bf16[1024,1024]{1,0:T(8,128)(2,1)S(1)}, bf16[1024,1024]{1,0:T(8,128)(2,1)S(1)}, u32[]{:S(2)}, u32[]{:S(2)}) collective-permute-start(bf16[1024,1024]{1,0:T(8,128)(2,1)S(1)} %get-tuple-element.197), channel_id=1, source_target_pairs={{0,1},{1,0},{2,3},{3,2},{4,5},{5,4},{6,7},{7,6},{8,9},{9,8},{10,11... | collective-permute-start | bytes 6291464 | tf_op jit(solution)/shard_map/ppermute | solution.py:1350
  60.9 27.6 %collective-permute-start.18 = (bf16[256,1024]{1,0:T(8,128)(2,1)}, bf16[256,1024]{1,0:T(8,128)(2,1)}, u32[]{:S(2)}, u32[]{:S(2)}) collective-permute-start(bf16[256,1024]{1,0:T(8,128)(2,1)} %get-tuple-element.210), channel_id=1, source_target_pairs={{0,8},{1,9},{2,10},{3,11},{4,12},{5,13},{6,14},{7,15},{8,0},{9,1},... | collective-permute-start | bytes 1572872 | tf_op jit(solution)/shard_map/ppermute | solution.py:1350
  61.5 31.3 %collective-permute-start.17 = (bf16[320,1024]{1,0:T(8,128)(2,1)}, bf16[320,1024]{1,0:T(8,128)(2,1)}, u32[]{:S(2)}, u32[]{:S(2)}) collective-permute-start(bf16[320,1024]{1,0:T(8,128)(2,1)} %get-tuple-element.209), channel_id=1, source_target_pairs={{0,16},{1,17},{2,18},{3,19},{4,20},{5,21},{6,22},{7,23},{8,24},{9,... | collective-permute-start | bytes 1966088 | tf_op jit(solution)/shard_map/ppermute | solution.py:1350
  72.2 20.6 %collective-permute-start.13 = (bf16[2,192,1024]{2,1,0:T(8,128)(2,1)S(1)}, bf16[2,192,1024]{2,1,0:T(8,128)(2,1)S(1)}, u32[]{:S(2)}, u32[]{:S(2)}) collective-permute-start(bf16[2,192,1024]{2,1,0:T(8,128)(2,1)S(1)} %get-tuple-element.203.refs_0_.refs_21_), channel_id=1, source_target_pairs={{0,4},{1,5},{2,6},{3,7},{4,0},{5,1},{6,2},{7,3},{8,12},{9,13},{10,... | collective-permute-start | bytes 2359304 | tf_op jit(solution)/shard_map/ppermute | solution.py:1350
  95.4 14.9 %collective-permute-start.16 = (bf16[512,256]{1,0:T(8,128)(2,1)S(1)}, bf16[512,256]{1,0:T(8,128)(2,1)S(1)}, u32[]{:S(2)}, u32[]{:S(2)}) collective-permute-start(bf16[512,256]{1,0:T(8,128)(2,1)S(1)} %get-tuple-element.208.refs_6_), channel_id=1, source_target_pairs={{0,8},{1,9},{2,10},{3,11},{4,12},{5,13},{6,14},{7,15},{8,0},{9,1},... | collective-permute-start | bytes 786440 | tf_op jit(solution)/shard_map/ppermute | solution.py:1350
  95.4 14.9 %collective-permute-start.15 = (bf16[512,256]{1,0:T(8,128)(2,1)S(1)}, bf16[512,256]{1,0:T(8,128)(2,1)S(1)}, u32[]{:S(2)}, u32[]{:S(2)}) collective-permute-start(bf16[512,256]{1,0:T(8,128)(2,1)S(1)} %get-tuple-element.207), channel_id=1, source_target_pairs={{0,24},{1,25},{2,26},{3,27},{4,28},{5,29},{6,30},{7,31},{8,16},{9,... | collective-permute-start | bytes 786440 | tf_op jit(solution)/shard_map/ppermute | solution.py:1350
  104.6 19.5 %collective-permute-start.22 = (bf16[2,192,1024]{2,1,0:T(8,128)(2,1)}, bf16[2,192,1024]{2,1,0:T(8,128)(2,1)}, u32[]{:S(2)}, u32[]{:S(2)}) collective-permute-start(bf16[2,192,1024]{2,1,0:T(8,128)(2,1)} %get-tuple-element.218.refs_0_.refs_23_), channel_id=1, source_target_pairs={{0,4},{1,5},{2,6},{3,7},{4,0},{5,1},{6,2},{7,3},{8,12},{9,13},{10,... | collective-permute-start | bytes 2359304 | tf_op jit(solution)/shard_map/ppermute | solution.py:1350
  112.0 14.3 %collective-permute-start.30 = (bf16[256,1024]{1,0:T(8,128)(2,1)}, bf16[256,1024]{1,0:T(8,128)(2,1)S(1)}, u32[]{:S(2)}, u32[]{:S(2)}) collective-permute-start(bf16[256,1024]{1,0:T(8,128)(2,1)} %collective-permute-done.18.refs_2_.refs_17_.refs_5_), channel_id=1, source_target_pairs={{0,1},{1,0},{2,3},{3,2},{4,5},{5,4},{6,7},{7,6},{8,9},{9,8},{10,11... | collective-permute-start | bytes 1572872 | tf_op jit(solution)/shard_map/ppermute | solution.py:1350
  113.5 15.0 %collective-permute-start.31 = (bf16[2,128,1024]{2,1,0:T(8,128)(2,1)S(1)}, bf16[2,128,1024]{2,1,0:T(8,128)(2,1)S(1)}, u32[]{:S(2)}, u32[]{:S(2)}) collective-permute-start(bf16[2,128,1024]{2,1,0:T(8,128)(2,1)S(1)} %get-tuple-element.222.refs_27_.refs_10_), channel_id=1, source_target_pairs={{0,2},{1,3},{2,0},{3,1},{4,6},{5,7},{6,4},{7,5},{8,10},{9,11},{10,... | collective-permute-start | bytes 1572872 | tf_op jit(solution)/shard_map/ppermute | solution.py:1350
  150.0 14.0 %collective-permute-start.34 = (bf16[256,1024]{1,0:T(8,128)(2,1)S(1)}, bf16[256,1024]{1,0:T(8,128)(2,1)S(1)}, u32[]{:S(2)}, u32[]{:S(2)}) collective-permute-start(bf16[256,1024]{1,0:T(8,128)(2,1)S(1)} %get-tuple-element.236), channel_id=1, source_target_pairs={{0,8},{1,9},{2,10},{3,11},{4,12},{5,13},{6,14},{7,15},{8,0},{9,1},... | collective-permute-start | bytes 1572872 | tf_op jit(solution)/shard_map/ppermute | solution.py:1350
  160.8 14.2 %collective-permute-start.33 = (bf16[512,1024]{1,0:T(8,128)(2,1)}, bf16[512,1024]{1,0:T(8,128)(2,1)}, u32[]{:S(2)}, u32[]{:S(2)}) collective-permute-start(bf16[512,1024]{1,0:T(8,128)(2,1)} %get-tuple-element.233), channel_id=1, source_target_pairs={{0,1},{1,0},{2,3},{3,2},{4,5},{5,4},{6,7},{7,6},{8,9},{9,8},{10,11... | collective-permute-start | bytes 3145736 | tf_op jit(solution)/shard_map/ppermute | solution.py:1350
  161.0 25.7 %collective-permute-start.41 = (bf16[512,1024]{1,0:T(8,128)(2,1)}, bf16[512,1024]{1,0:T(8,128)(2,1)}, u32[]{:S(2)}, u32[]{:S(2)}) collective-permute-start(bf16[512,1024]{1,0:T(8,128)(2,1)} %get-tuple-element.261), channel_id=1, source_target_pairs={{0,4},{1,5},{2,6},{3,7},{4,0},{5,1},{6,2},{7,3},{8,12},{9,13},{10,... | collective-permute-start | bytes 3145736 | tf_op jit(solution)/shard_map/ppermute | solution.py:1350
  161.8 25.5 %collective-permute-start.42 = (bf16[512,1024]{1,0:T(8,128)(2,1)}, bf16[512,1024]{1,0:T(8,128)(2,1)}, u32[]{:S(2)}, u32[]{:S(2)}) collective-permute-start(bf16[512,1024]{1,0:T(8,128)(2,1)} %get-tuple-element.263), channel_id=1, source_target_pairs={{0,2},{1,3},{2,0},{3,1},{4,6},{5,7},{6,4},{7,5},{8,10},{9,11},{10,... | collective-permute-start | bytes 3145736 | tf_op jit(solution)/shard_map/ppermute | solution.py:1350
  179.0 26.5 %collective-permute-start.47 = (bf16[512,512]{1,0:T(8,128)(2,1)}, bf16[512,512]{1,0:T(8,128)(2,1)}, u32[]{:S(2)}, u32[]{:S(2)}) collective-permute-start(bf16[512,512]{1,0:T(8,128)(2,1)} %get-tuple-element.280), channel_id=1, source_target_pairs={{0,8},{1,9},{2,10},{3,11},{4,12},{5,13},{6,14},{7,15},{8,0},{9,1},... | collective-permute-start | bytes 1572872 | tf_op jit(solution)/shard_map/ppermute | solution.py:1350
  189.4 16.2 %collective-permute-start.45 = (bf16[256,1024]{1,0:T(8,128)(2,1)S(1)}, bf16[256,1024]{1,0:T(8,128)(2,1)S(1)}, u32[]{:S(2)}, u32[]{:S(2)}) collective-permute-start(bf16[256,1024]{1,0:T(8,128)(2,1)S(1)} %get-tuple-element.277), channel_id=1, source_target_pairs={{0,2},{1,3},{2,0},{3,1},{4,6},{5,7},{6,4},{7,5},{8,10},{9,11},{10,... | collective-permute-start | bytes 1572872 | tf_op jit(solution)/shard_map/ppermute | solution.py:1350
  190.9 14.7 %collective-permute-start.46 = (bf16[256,1024]{1,0:T(8,128)(2,1)S(1)}, bf16[256,1024]{1,0:T(8,128)(2,1)S(1)}, u32[]{:S(2)}, u32[]{:S(2)}) collective-permute-start(bf16[256,1024]{1,0:T(8,128)(2,1)S(1)} %get-tuple-element.279), channel_id=1, source_target_pairs={{0,4},{1,5},{2,6},{3,7},{4,0},{5,1},{6,2},{7,3},{8,12},{9,13},{10,... | collective-permute-start | bytes 1572872 | tf_op jit(solution)/shard_map/ppermute | solution.py:1350
  212.2 45.5 %collective-permute-start.37 = (bf16[256,1024]{1,0:T(8,128)(2,1)}, bf16[256,1024]{1,0:T(8,128)(2,1)}, u32[]{:S(2)}, u32[]{:S(2)}) collective-permute-start(bf16[256,1024]{1,0:T(8,128)(2,1)} %get-tuple-element.249), channel_id=1, source_target_pairs={{0,8},{1,9},{2,10},{3,11},{4,12},{5,13},{6,14},{7,15},{8,0},{9,1},... | collective-permute-start | bytes 1572872 | tf_op jit(solution)/shard_map/ppermute | solution.py:1350
  214.2 40.3 %collective-permute-start.53 = (bf16[2,128,1024]{2,1,0:T(8,128)(2,1)}, bf16[2,128,1024]{2,1,0:T(8,128)(2,1)}, u32[]{:S(2)}, u32[]{:S(2)}) collective-permute-start(bf16[2,128,1024]{2,1,0:T(8,128)(2,1)} %get-tuple-element.300), channel_id=1, source_target_pairs={{0,16},{1,17},{2,18},{3,19},{4,20},{5,21},{6,22},{7,23},{8,24},{9,... | collective-permute-start | bytes 1572872 | tf_op jit(solution)/shard_map/ppermute | solution.py:1350
  227.9 28.6 %collective-permute-start.52 = (bf16[160,768]{1,0:T(8,128)(2,1)}, bf16[160,768]{1,0:T(8,128)(2,1)}, u32[]{:S(2)}, u32[]{:S(2)}) collective-permute-start(bf16[160,768]{1,0:T(8,128)(2,1)} %get-tuple-element.298), channel_id=1, source_target_pairs={{0,16},{1,17},{2,18},{3,19},{4,20},{5,21},{6,22},{7,23},{8,24},{9,... | collective-permute-start | bytes 737288 | tf_op jit(solution)/shard_map/ppermute | solution.py:1350
  230.3 21.9 %collective-permute-start.54 = (bf16[256,1024]{1,0:T(8,128)(2,1)S(1)}, bf16[256,1024]{1,0:T(8,128)(2,1)S(1)}, u32[]{:S(2)}, u32[]{:S(2)}) collective-permute-start(bf16[256,1024]{1,0:T(8,128)(2,1)S(1)} %get-tuple-element.304), channel_id=1, source_target_pairs={{0,8},{1,9},{2,10},{3,11},{4,12},{5,13},{6,14},{7,15},{8,0},{9,1},... | collective-permute-start | bytes 1572872 | tf_op jit(solution)/shard_map/ppermute | solution.py:1350
  231.8 28.0 %collective-permute-start.57 = (bf16[128,512]{1,0:T(8,128)(2,1)}, bf16[128,512]{1,0:T(8,128)(2,1)}, u32[]{:S(2)}, u32[]{:S(2)}) collective-permute-start(bf16[128,512]{1,0:T(8,128)(2,1)} %get-tuple-element.316), channel_id=1, source_target_pairs={{0,2},{1,3},{2,0},{3,1},{4,6},{5,7},{6,4},{7,5},{8,10},{9,11},{10,... | collective-permute-start | bytes 393224 | tf_op jit(solution)/shard_map/ppermute | solution.py:1350
  (81 other events, 561.6 us)

commit v6 on v5

--- a/solution.py
+++ b/solution.py
@@ -1268,7 +1268,7 @@
     ref[0:16, columns] = value.astype(BF16)
 
 
-def home_last_kernel(lay, spot, mine, came, sums, w_in, w_up, w_out, *vectors):
+def home_last_kernel(lay, spot, mine, came, sums, w_in, w_up, w_out, *refs):
     n = lay.each
     hw, piece, cut = lay.share, lay.piece, 3 * lay.share
     span = cut + lay.ff_share
@@ -1300,12 +1300,16 @@
             w_out[:, s * half : (s + 1) * half] = ref[0 : max(n, 16), at:].astype(F32)[0:n]
 
     each_way(spot[2], write_out)
-    total = sums[...] + take_sums(came, max(n, 16), lay.width)
+    vectors, held = refs[:9], refs[9]
+    held[...] = sums[...] + take_sums(came, max(n, 16), lay.width)
 
     def part_of(start, count):
-        source, target = iota((lay.width, count), 0), iota((lay.width, count), 1)
-        move = (source == start + target).astype(F32)
-        return jnp.dot(total, move, precision=lax.Precision.HIGHEST)
+        block = held[:, pl.ds(pl.multiple_of(start // LANES * LANES, LANES), LANES)]
+        part = jnp.zeros((SUM_ROWS, count), F32)
+        for i in range(LANES // count):
+            here = start % LANES == i * count
+            part = part + jnp.where(here, block[:, i * count : (i + 1) * count], 0.0)
+        return part
 
     own = part_of(spot[7] * n, n)
     for v in range(8):
@@ -2107,6 +2111,7 @@
                 sums,
                 name="home_last",
                 smem=(0,),
+                scratch=[pltpu.VMEM((SUM_ROWS, width), F32)],
             )
             vectors = [v.reshape(-1) for v in vectors]
 

time: 283 us -> 283 us (level)
  no operation moved by 1% of the time
where the time goes in v6:
time: 283 us; the launch traced here: 279 us
  Pallas kernels  106 us (37%)
  waiting for transfers between devices  95.5 us (34%)
  starting transfers between devices  69.6 us (25%)
  local copies, waits for them, and re-layouts  5.15 us (2%)
    pallas_call x42, Pallas kernels, kernel_call(): pl.pallas_call(body, in_specs=ins, out_specs=[spec(i, ()) for i in range(...  106 us
    ppermute x61, waiting for transfers between devices, send(): return lax.ppermute(value, AXES, route)  95.5 us
    ppermute x61, starting transfers between devices, send(): return lax.ppermute(value, AXES, route)  69.6 us
  transfers between devices with their start and end apart: 61, of which 26 were waited for; matrix products, arithmetic and copies ran while one was open for 0% of the time, Pallas kernels for 30%

profile of v6, /device:TPU:0, one launch (start us, length us, event | category | flops | bytes accessed | tf_op | source)
XLA Modules:
  0.0 278.7 jit_solution(10035887976396055828)
XLA Ops:
  0.6 3.1 %collective-permute-start.1 = (bf16[256,1024]{1,0:T(8,128)(2,1)}, bf16[256,1024]{1,0:T(8,128)(2,1)S(1)}, u32[]{:S(2)}, u32[]{:S(2)}) collective-permute-start(bf16[256,1024]{1,0:T(8,128)(2,1)} %bitcast.38), channel_id=1, source_target_pairs={{0,8},{1,9},{2,10},{3,11},{4,12},{5,13},{6,14},{7,15},{8,0},{9,1},... | collective-permute-start | bytes 1572872 | tf_op jit(solution)/shard_map/ppermute | solution.py:1354
  5.0 3.1 %pack.1 = (bf16[48,4096]{1,0:T(8,128)(2,1)}, bf16[48,4096]{1,0:T(8,128)(2,1)}, f32[8,128]{1,0:T(8,128)}) custom-call(s32[10]{0:T(128)} %stack.49.refs_0_, s32[1]{0:T(128)S(6)} %copy.34.refs_1_, bf16[32,3072]{1,0:T(8,128)(2,1)} %refs_2_.1, bf16[32,4096]{1,0:T(8,128)(2,1)} %refs_3_.1, s32[1,1024]{1,0:T(1,128)} %refs_4_.2, bf16[32,1024]{1,0:T(8,128)(2,1)} %refs_5_.1, ...), custom_call_target="tpu_custom_call" | custom-call | flops 10000000000 | bytes 1 | tf_op jit(solution)/shard_map/pack/pallas_call | solution.py:160
  11.9 5.1 %collective-permute-done.2.refs_4_.refs_1_ = bf16[1,128,1024]{2,1,0:T(8,128)(2,1)S(1)} collective-permute-done((bf16[1,128,1024]{2,1,0:T(8,128)(2,1)S(1)}, bf16[1,128,1024]{2,1,0:T(8,128)(2,1)S(1)}, u32[]{:S(2)}, u32[]{:S(2)}) %collective-permute-start.2) | collective-permute-done | bytes 262176 | tf_op jit(solution)/shard_map/ppermute | solution.py:1354
  21.3 10.4 %collective-permute-done.3.refs_2_ = bf16[80,2304]{1,0:T(8,128)(2,1)S(1)} collective-permute-done((bf16[80,2304]{1,0:T(8,128)(2,1)S(1)}, bf16[80,2304]{1,0:T(8,128)(2,1)S(1)}, u32[]{:S(2)}, u32[]{:S(2)}) %collective-permute-start.3) | collective-permute-done | bytes 368672 | tf_op jit(solution)/shard_map/ppermute | solution.py:1354
  33.1 4.6 %collective-permute-start.5 = (bf16[144,768]{1,0:T(8,128)(2,1)S(1)}, bf16[144,768]{1,0:T(8,128)(2,1)S(1)}, u32[]{:S(2)}, u32[]{:S(2)}) collective-permute-start(bf16[144,768]{1,0:T(8,128)(2,1)S(1)} %get-tuple-element.187.refs_0_), channel_id=1, source_target_pairs={{0,16},{1,17},{2,18},{3,19},{4,20},{5,21},{6,22},{7,23},{8,24},{9,... | collective-permute-start | bytes 663560 | tf_op jit(solution)/shard_map/ppermute | solution.py:1354
  40.2 7.7 %collective-permute-start.11 = (bf16[1024,1024]{1,0:T(8,128)(2,1)S(1)}, bf16[1024,1024]{1,0:T(8,128)(2,1)S(1)}, u32[]{:S(2)}, u32[]{:S(2)}) collective-permute-start(bf16[1024,1024]{1,0:T(8,128)(2,1)S(1)} %get-tuple-element.197), channel_id=1, source_target_pairs={{0,1},{1,0},{2,3},{3,2},{4,5},{5,4},{6,7},{7,6},{8,9},{9,8},{10,11... | collective-permute-start | bytes 6291464 | tf_op jit(solution)/shard_map/ppermute | solution.py:1354
  52.1 4.4 %collective-permute-done.9.refs_1_ = bf16[2,144,384]{2,1,0:T(8,128)(2,1)S(1)} collective-permute-done((bf16[2,144,384]{2,1,0:T(8,128)(2,1)S(1)}, bf16[2,144,384]{2,1,0:T(8,128)(2,1)S(1)}, u32[]{:S(2)}, u32[]{:S(2)}) %collective-permute-start.9) | collective-permute-done | bytes 221216 | tf_op jit(solution)/shard_map/ppermute | solution.py:1354
  61.5 3.2 %collective-permute-start.17 = (bf16[320,1024]{1,0:T(8,128)(2,1)}, bf16[320,1024]{1,0:T(8,128)(2,1)}, u32[]{:S(2)}, u32[]{:S(2)}) collective-permute-start(bf16[320,1024]{1,0:T(8,128)(2,1)} %get-tuple-element.209), channel_id=1, source_target_pairs={{0,16},{1,17},{2,18},{3,19},{4,20},{5,21},{6,22},{7,23},{8,24},{9,... | collective-permute-start | bytes 1966088 | tf_op jit(solution)/shard_map/ppermute | solution.py:1354
  65.2 4.9 %collective-permute-done.12.refs_2_.refs_9_ = bf16[4,144,384]{2,1,0:T(8,128)(2,1)S(1)} collective-permute-done((bf16[4,144,384]{2,1,0:T(8,128)(2,1)S(1)}, bf16[4,144,384]{2,1,0:T(8,128)(2,1)S(1)}, u32[]{:S(2)}, u32[]{:S(2)}) %collective-permute-start.12) | collective-permute-done | bytes 442400 | tf_op jit(solution)/shard_map/ppermute | solution.py:1354
  75.6 12.8 %attend.1 = (bf16[512,256]{1,0:T(8,128)(2,1)S(1)}, bf16[512,256]{1,0:T(8,128)(2,1)S(1)}, bf16[1024,768]{1,0:T(8,128)(2,1)S(1)}, f32[256,1024]{1,0:T(8,128)S(1)},...) custom-call(s32[10]{0:T(128)S(1)} %copy-done.4, ...), custom_call_target="tpu_custom_call" | custom-call | flops 99999997952 | bytes 1 | tf_op jit(solution)/shard_map/attend/pallas_call | solution.py:160
  88.5 4.3 %collective-permute-done.17.refs_0_ = bf16[320,1024]{1,0:T(8,128)(2,1)} collective-permute-done((bf16[320,1024]{1,0:T(8,128)(2,1)}, bf16[320,1024]{1,0:T(8,128)(2,1)}, u32[]{:S(2)}, u32[]{:S(2)}) %collective-permute-start.17) | collective-permute-done | bytes 655392 | tf_op jit(solution)/shard_map/ppermute | solution.py:1354
  97.8 5.8 %collective-permute-done.20.refs_3_ = bf16[1,128,1024]{2,1,0:T(8,128)(2,1)S(1)} collective-permute-done((bf16[1,128,1024]{2,1,0:T(8,128)(2,1)S(1)}, bf16[1,128,1024]{2,1,0:T(8,128)(2,1)S(1)}, u32[]{:S(2)}, u32[]{:S(2)}) %collective-permute-start.20) | collective-permute-done | bytes 262176 | tf_op jit(solution)/shard_map/ppermute | solution.py:1354
  105.1 5.1 %collective-permute-done.15.refs_0_ = bf16[512,256]{1,0:T(8,128)(2,1)S(1)} collective-permute-done((bf16[512,256]{1,0:T(8,128)(2,1)S(1)}, bf16[512,256]{1,0:T(8,128)(2,1)S(1)}, u32[]{:S(2)}, u32[]{:S(2)}) %collective-permute-start.15) | collective-permute-done | bytes 262176 | tf_op jit(solution)/shard_map/ppermute | solution.py:1354
  114.9 9.2 %collective-permute-done.22.refs_1_.refs_24_ = bf16[2,192,1024]{2,1,0:T(8,128)(2,1)} collective-permute-done((bf16[2,192,1024]{2,1,0:T(8,128)(2,1)}, bf16[2,192,1024]{2,1,0:T(8,128)(2,1)}, u32[]{:S(2)}, u32[]{:S(2)}) %collective-permute-start.22) | collective-permute-done | bytes 786464 | tf_op jit(solution)/shard_map/ppermute | solution.py:1354
  128.9 17.3 %feed_forward.1 = (bf16[512,1024]{1,0:T(8,128)(2,1)S(1)}, bf16[512,1024]{1,0:T(8,128)(2,1)S(1)}, f32[256,1024]{1,0:T(8,128)S(1)}, bf16[256,1024]{1,0:T(8,128)(2,...) custom-call(s32[10]{0:T(128)S(1)} %copy-done.4, ...), custom_call_target="tpu_custom_call" | custom-call | flops 99999997952 | bytes 1 | tf_op jit(solution)/shard_map/feed_forward/pallas_call | solution.py:160
  150.1 10.7 %gradients.1 = (bf16[512,1024]{1,0:T(8,128)(2,1)S(1)}, bf16[512,1024]{1,0:T(8,128)(2,1)}, bf16[512,1024]{1,0:T(8,128)(2,1)S(1)}, bf16[512,1024]{1,0:T(8,128)(2,1...) custom-call(s32[10]{0:T(128)S(1)} %copy-done.4, ...), custom_call_target="tpu_custom_call" | custom-call | flops 99999997952 | bytes 1 | tf_op jit(solution)/shard_map/gradients/pallas_call | solution.py:160
  176.4 2.6 fold.9
  179.1 5.0 %collective-permute-done.39.refs_3_ = bf16[256,256]{1,0:T(8,128)(2,1)} collective-permute-done((bf16[256,256]{1,0:T(8,128)(2,1)}, bf16[256,256]{1,0:T(8,128)(2,1)}, u32[]{:S(2)}, u32[]{:S(2)}) %collective-permute-start.39) | collective-permute-done | bytes 131104 | tf_op jit(solution)/shard_map/ppermute | solution.py:1354
  192.1 12.0 %attend_back.1 = (bf16[1024,768]{1,0:T(8,128)(2,1)S(1)}, bf16[512,384]{1,0:T(8,128)(2,1)S(1)}, bf16[512,384]{1,0:T(8,128)(2,1)}, bf16[512,384]{1,0:T(8,128)(2,1)...) custom-call(s32[10]{0:T(128)S(1)} %copy-done.4, f32[1024,1]{1,0:T(8,128)S(1)} %copy.32.refs_1_, ...), custom_call_target="tpu_custom_call" | custom-call | flops 99999997952 | bytes 1 | tf_op jit(solution)/shard_map/attend_back/pallas_call | solution.py:160
  207.4 3.5 %input_slope.1 = (bf16[512,1024]{1,0:T(8,128)(2,1)S(1)}, bf16[512,1024]{1,0:T(8,128)(2,1)S(1)}, f32[16,1024]{1,0:T(8,128)S(1)}, bf16[16,1024]{1,0:T(8,128)(2,1)S(1)}, f32[8,128]{1,0:T(8,128)S(1)}) custom-call(s32[10]{0:T(128)S(1)} %copy-done.4, bf16[1024,768]{1,0:T(8,128)(2,1)S(1)} %get-tuple-element.270.refs_1_, ...), custom_call_target="tpu_custom_call" | custom-call | flops 99999997952 | bytes 1 | tf_op jit(solution)/shard_map/input_slope/pallas_call | solution.py:160
  233.2 18.9 %collective-permute-done.54.refs_1_.refs_3_ = bf16[256,1024]{1,0:T(8,128)(2,1)S(1)} collective-permute-done((bf16[256,1024]{1,0:T(8,128)(2,1)S(1)}, bf16[256,1024]{1,0:T(8,128)(2,1)S(1)}, u32[]{:S(2)}, u32[]{:S(2)}) %collective-permute-start.54) | collective-permute-done | bytes 524320 | tf_op jit(solution)/shard_map/ppermute | solution.py:1354
  260.9 3.3 %collective-permute-start.59 = (bf16[64,512]{1,0:T(8,128)(2,1)S(1)}, bf16[64,512]{1,0:T(8,128)(2,1)S(1)}, u32[]{:S(2)}, u32[]{:S(2)}) collective-permute-start(bf16[64,512]{1,0:T(8,128)(2,1)S(1)} %get-tuple-element.324), channel_id=1, source_target_pairs={{0,16},{1,17},{2,18},{3,19},{4,20},{5,21},{6,22},{7,23},{8,24},{9,... | collective-permute-start | bytes 196616 | tf_op jit(solution)/shard_map/ppermute | solution.py:1354
  264.4 2.7 input_gradient.1
  267.2 6.2 %collective-permute-done.59.refs_5_ = bf16[64,512]{1,0:T(8,128)(2,1)S(1)} collective-permute-done((bf16[64,512]{1,0:T(8,128)(2,1)S(1)}, bf16[64,512]{1,0:T(8,128)(2,1)S(1)}, u32[]{:S(2)}, u32[]{:S(2)}) %collective-permute-start.59) | collective-permute-done | bytes 65568 | tf_op jit(solution)/shard_map/ppermute | solution.py:1354
  (231 shorter events, 110.3 us)
Async XLA Ops:
  0.6 16.3 %collective-permute-start.1 = (bf16[256,1024]{1,0:T(8,128)(2,1)}, bf16[256,1024]{1,0:T(8,128)(2,1)S(1)}, u32[]{:S(2)}, u32[]{:S(2)}) collective-permute-start(bf16[256,1024]{1,0:T(8,128)(2,1)} %bitcast.38), channel_id=1, source_target_pairs={{0,8},{1,9},{2,10},{3,11},{4,12},{5,13},{6,14},{7,15},{8,0},{9,1},... | collective-permute-start | bytes 1572872 | tf_op jit(solution)/shard_map/ppermute | solution.py:1354
  19.7 19.5 %collective-permute-start.8 = (bf16[2,128,1024]{2,1,0:T(8,128)(2,1)S(1)}, bf16[2,128,1024]{2,1,0:T(8,128)(2,1)S(1)}, u32[]{:S(2)}, u32[]{:S(2)}) collective-permute-start(bf16[2,128,1024]{2,1,0:T(8,128)(2,1)S(1)} %get-tuple-element.192.refs_25_.refs_8_), channel_id=1, source_target_pairs={{0,2},{1,3},{2,0},{3,1},{4,6},{5,7},{6,4},{7,5},{8,10},{9,11},{10,... | collective-permute-start | bytes 1572872 | tf_op jit(solution)/shard_map/ppermute | solution.py:1354
  33.1 14.8 %collective-permute-start.5 = (bf16[144,768]{1,0:T(8,128)(2,1)S(1)}, bf16[144,768]{1,0:T(8,128)(2,1)S(1)}, u32[]{:S(2)}, u32[]{:S(2)}) collective-permute-start(bf16[144,768]{1,0:T(8,128)(2,1)S(1)} %get-tuple-element.187.refs_0_), channel_id=1, source_target_pairs={{0,16},{1,17},{2,18},{3,19},{4,20},{5,21},{6,22},{7,23},{8,24},{9,... | collective-permute-start | bytes 663560 | tf_op jit(solution)/shard_map/ppermute | solution.py:1354
  40.2 17.4 %collective-permute-start.11 = (bf16[1024,1024]{1,0:T(8,128)(2,1)S(1)}, bf16[1024,1024]{1,0:T(8,128)(2,1)S(1)}, u32[]{:S(2)}, u32[]{:S(2)}) collective-permute-start(bf16[1024,1024]{1,0:T(8,128)(2,1)S(1)} %get-tuple-element.197), channel_id=1, source_target_pairs={{0,1},{1,0},{2,3},{3,2},{4,5},{5,4},{6,7},{7,6},{8,9},{9,8},{10,11... | collective-permute-start | bytes 6291464 | tf_op jit(solution)/shard_map/ppermute | solution.py:1354
  60.9 27.6 %collective-permute-start.18 = (bf16[256,1024]{1,0:T(8,128)(2,1)}, bf16[256,1024]{1,0:T(8,128)(2,1)}, u32[]{:S(2)}, u32[]{:S(2)}) collective-permute-start(bf16[256,1024]{1,0:T(8,128)(2,1)} %get-tuple-element.210), channel_id=1, source_target_pairs={{0,8},{1,9},{2,10},{3,11},{4,12},{5,13},{6,14},{7,15},{8,0},{9,1},... | collective-permute-start | bytes 1572872 | tf_op jit(solution)/shard_map/ppermute | solution.py:1354
  61.5 31.3 %collective-permute-start.17 = (bf16[320,1024]{1,0:T(8,128)(2,1)}, bf16[320,1024]{1,0:T(8,128)(2,1)}, u32[]{:S(2)}, u32[]{:S(2)}) collective-permute-start(bf16[320,1024]{1,0:T(8,128)(2,1)} %get-tuple-element.209), channel_id=1, source_target_pairs={{0,16},{1,17},{2,18},{3,19},{4,20},{5,21},{6,22},{7,23},{8,24},{9,... | collective-permute-start | bytes 1966088 | tf_op jit(solution)/shard_map/ppermute | solution.py:1354
  72.2 20.6 %collective-permute-start.13 = (bf16[2,192,1024]{2,1,0:T(8,128)(2,1)S(1)}, bf16[2,192,1024]{2,1,0:T(8,128)(2,1)S(1)}, u32[]{:S(2)}, u32[]{:S(2)}) collective-permute-start(bf16[2,192,1024]{2,1,0:T(8,128)(2,1)S(1)} %get-tuple-element.203.refs_0_.refs_21_), channel_id=1, source_target_pairs={{0,4},{1,5},{2,6},{3,7},{4,0},{5,1},{6,2},{7,3},{8,12},{9,13},{10,... | collective-permute-start | bytes 2359304 | tf_op jit(solution)/shard_map/ppermute | solution.py:1354
  95.4 14.9 %collective-permute-start.16 = (bf16[512,256]{1,0:T(8,128)(2,1)S(1)}, bf16[512,256]{1,0:T(8,128)(2,1)S(1)}, u32[]{:S(2)}, u32[]{:S(2)}) collective-permute-start(bf16[512,256]{1,0:T(8,128)(2,1)S(1)} %get-tuple-element.208.refs_6_), channel_id=1, source_target_pairs={{0,8},{1,9},{2,10},{3,11},{4,12},{5,13},{6,14},{7,15},{8,0},{9,1},... | collective-permute-start | bytes 786440 | tf_op jit(solution)/shard_map/ppermute | solution.py:1354
  95.4 14.9 %collective-permute-start.15 = (bf16[512,256]{1,0:T(8,128)(2,1)S(1)}, bf16[512,256]{1,0:T(8,128)(2,1)S(1)}, u32[]{:S(2)}, u32[]{:S(2)}) collective-permute-start(bf16[512,256]{1,0:T(8,128)(2,1)S(1)} %get-tuple-element.207), channel_id=1, source_target_pairs={{0,24},{1,25},{2,26},{3,27},{4,28},{5,29},{6,30},{7,31},{8,16},{9,... | collective-permute-start | bytes 786440 | tf_op jit(solution)/shard_map/ppermute | solution.py:1354
  104.6 19.5 %collective-permute-start.22 = (bf16[2,192,1024]{2,1,0:T(8,128)(2,1)}, bf16[2,192,1024]{2,1,0:T(8,128)(2,1)}, u32[]{:S(2)}, u32[]{:S(2)}) collective-permute-start(bf16[2,192,1024]{2,1,0:T(8,128)(2,1)} %get-tuple-element.218.refs_0_.refs_23_), channel_id=1, source_target_pairs={{0,4},{1,5},{2,6},{3,7},{4,0},{5,1},{6,2},{7,3},{8,12},{9,13},{10,... | collective-permute-start | bytes 2359304 | tf_op jit(solution)/shard_map/ppermute | solution.py:1354
  112.0 14.3 %collective-permute-start.30 = (bf16[256,1024]{1,0:T(8,128)(2,1)}, bf16[256,1024]{1,0:T(8,128)(2,1)S(1)}, u32[]{:S(2)}, u32[]{:S(2)}) collective-permute-start(bf16[256,1024]{1,0:T(8,128)(2,1)} %collective-permute-done.18.refs_2_.refs_17_.refs_5_), channel_id=1, source_target_pairs={{0,1},{1,0},{2,3},{3,2},{4,5},{5,4},{6,7},{7,6},{8,9},{9,8},{10,11... | collective-permute-start | bytes 1572872 | tf_op jit(solution)/shard_map/ppermute | solution.py:1354
  113.5 15.0 %collective-permute-start.31 = (bf16[2,128,1024]{2,1,0:T(8,128)(2,1)S(1)}, bf16[2,128,1024]{2,1,0:T(8,128)(2,1)S(1)}, u32[]{:S(2)}, u32[]{:S(2)}) collective-permute-start(bf16[2,128,1024]{2,1,0:T(8,128)(2,1)S(1)} %get-tuple-element.222.refs_27_.refs_10_), channel_id=1, source_target_pairs={{0,2},{1,3},{2,0},{3,1},{4,6},{5,7},{6,4},{7,5},{8,10},{9,11},{10,... | collective-permute-start | bytes 1572872 | tf_op jit(solution)/shard_map/ppermute | solution.py:1354
  150.0 14.0 %collective-permute-start.34 = (bf16[256,1024]{1,0:T(8,128)(2,1)S(1)}, bf16[256,1024]{1,0:T(8,128)(2,1)S(1)}, u32[]{:S(2)}, u32[]{:S(2)}) collective-permute-start(bf16[256,1024]{1,0:T(8,128)(2,1)S(1)} %get-tuple-element.236), channel_id=1, source_target_pairs={{0,8},{1,9},{2,10},{3,11},{4,12},{5,13},{6,14},{7,15},{8,0},{9,1},... | collective-permute-start | bytes 1572872 | tf_op jit(solution)/shard_map/ppermute | solution.py:1354
  160.8 14.2 %collective-permute-start.33 = (bf16[512,1024]{1,0:T(8,128)(2,1)}, bf16[512,1024]{1,0:T(8,128)(2,1)}, u32[]{:S(2)}, u32[]{:S(2)}) collective-permute-start(bf16[512,1024]{1,0:T(8,128)(2,1)} %get-tuple-element.233), channel_id=1, source_target_pairs={{0,1},{1,0},{2,3},{3,2},{4,5},{5,4},{6,7},{7,6},{8,9},{9,8},{10,11... | collective-permute-start | bytes 3145736 | tf_op jit(solution)/shard_map/ppermute | solution.py:1354
  161.0 25.7 %collective-permute-start.41 = (bf16[512,1024]{1,0:T(8,128)(2,1)}, bf16[512,1024]{1,0:T(8,128)(2,1)}, u32[]{:S(2)}, u32[]{:S(2)}) collective-permute-start(bf16[512,1024]{1,0:T(8,128)(2,1)} %get-tuple-element.261), channel_id=1, source_target_pairs={{0,4},{1,5},{2,6},{3,7},{4,0},{5,1},{6,2},{7,3},{8,12},{9,13},{10,... | collective-permute-start | bytes 3145736 | tf_op jit(solution)/shard_map/ppermute | solution.py:1354
  161.8 25.5 %collective-permute-start.42 = (bf16[512,1024]{1,0:T(8,128)(2,1)}, bf16[512,1024]{1,0:T(8,128)(2,1)}, u32[]{:S(2)}, u32[]{:S(2)}) collective-permute-start(bf16[512,1024]{1,0:T(8,128)(2,1)} %get-tuple-element.263), channel_id=1, source_target_pairs={{0,2},{1,3},{2,0},{3,1},{4,6},{5,7},{6,4},{7,5},{8,10},{9,11},{10,... | collective-permute-start | bytes 3145736 | tf_op jit(solution)/shard_map/ppermute | solution.py:1354
  179.0 26.5 %collective-permute-start.47 = (bf16[512,512]{1,0:T(8,128)(2,1)}, bf16[512,512]{1,0:T(8,128)(2,1)}, u32[]{:S(2)}, u32[]{:S(2)}) collective-permute-start(bf16[512,512]{1,0:T(8,128)(2,1)} %get-tuple-element.280), channel_id=1, source_target_pairs={{0,8},{1,9},{2,10},{3,11},{4,12},{5,13},{6,14},{7,15},{8,0},{9,1},... | collective-permute-start | bytes 1572872 | tf_op jit(solution)/shard_map/ppermute | solution.py:1354
  189.4 16.2 %collective-permute-start.45 = (bf16[256,1024]{1,0:T(8,128)(2,1)S(1)}, bf16[256,1024]{1,0:T(8,128)(2,1)S(1)}, u32[]{:S(2)}, u32[]{:S(2)}) collective-permute-start(bf16[256,1024]{1,0:T(8,128)(2,1)S(1)} %get-tuple-element.277), channel_id=1, source_target_pairs={{0,2},{1,3},{2,0},{3,1},{4,6},{5,7},{6,4},{7,5},{8,10},{9,11},{10,... | collective-permute-start | bytes 1572872 | tf_op jit(solution)/shard_map/ppermute | solution.py:1354
  190.9 14.7 %collective-permute-start.46 = (bf16[256,1024]{1,0:T(8,128)(2,1)S(1)}, bf16[256,1024]{1,0:T(8,128)(2,1)S(1)}, u32[]{:S(2)}, u32[]{:S(2)}) collective-permute-start(bf16[256,1024]{1,0:T(8,128)(2,1)S(1)} %get-tuple-element.279), channel_id=1, source_target_pairs={{0,4},{1,5},{2,6},{3,7},{4,0},{5,1},{6,2},{7,3},{8,12},{9,13},{10,... | collective-permute-start | bytes 1572872 | tf_op jit(solution)/shard_map/ppermute | solution.py:1354
  212.2 45.5 %collective-permute-start.37 = (bf16[256,1024]{1,0:T(8,128)(2,1)}, bf16[256,1024]{1,0:T(8,128)(2,1)}, u32[]{:S(2)}, u32[]{:S(2)}) collective-permute-start(bf16[256,1024]{1,0:T(8,128)(2,1)} %get-tuple-element.249), channel_id=1, source_target_pairs={{0,8},{1,9},{2,10},{3,11},{4,12},{5,13},{6,14},{7,15},{8,0},{9,1},... | collective-permute-start | bytes 1572872 | tf_op jit(solution)/shard_map/ppermute | solution.py:1354
  214.2 40.3 %collective-permute-start.53 = (bf16[2,128,1024]{2,1,0:T(8,128)(2,1)}, bf16[2,128,1024]{2,1,0:T(8,128)(2,1)}, u32[]{:S(2)}, u32[]{:S(2)}) collective-permute-start(bf16[2,128,1024]{2,1,0:T(8,128)(2,1)} %get-tuple-element.300), channel_id=1, source_target_pairs={{0,16},{1,17},{2,18},{3,19},{4,20},{5,21},{6,22},{7,23},{8,24},{9,... | collective-permute-start | bytes 1572872 | tf_op jit(solution)/shard_map/ppermute | solution.py:1354
  227.9 28.6 %collective-permute-start.52 = (bf16[160,768]{1,0:T(8,128)(2,1)}, bf16[160,768]{1,0:T(8,128)(2,1)}, u32[]{:S(2)}, u32[]{:S(2)}) collective-permute-start(bf16[160,768]{1,0:T(8,128)(2,1)} %get-tuple-element.298), channel_id=1, source_target_pairs={{0,16},{1,17},{2,18},{3,19},{4,20},{5,21},{6,22},{7,23},{8,24},{9,... | collective-permute-start | bytes 737288 | tf_op jit(solution)/shard_map/ppermute | solution.py:1354
  230.3 21.9 %collective-permute-start.54 = (bf16[256,1024]{1,0:T(8,128)(2,1)S(1)}, bf16[256,1024]{1,0:T(8,128)(2,1)S(1)}, u32[]{:S(2)}, u32[]{:S(2)}) collective-permute-start(bf16[256,1024]{1,0:T(8,128)(2,1)S(1)} %get-tuple-element.304), channel_id=1, source_target_pairs={{0,8},{1,9},{2,10},{3,11},{4,12},{5,13},{6,14},{7,15},{8,0},{9,1},... | collective-permute-start | bytes 1572872 | tf_op jit(solution)/shard_map/ppermute | solution.py:1354
  231.8 28.0 %collective-permute-start.57 = (bf16[128,512]{1,0:T(8,128)(2,1)}, bf16[128,512]{1,0:T(8,128)(2,1)}, u32[]{:S(2)}, u32[]{:S(2)}) collective-permute-start(bf16[128,512]{1,0:T(8,128)(2,1)} %get-tuple-element.316), channel_id=1, source_target_pairs={{0,2},{1,3},{2,0},{3,1},{4,6},{5,7},{6,4},{7,5},{8,10},{9,11},{10,... | collective-permute-start | bytes 393224 | tf_op jit(solution)/shard_map/ppermute | solution.py:1354
  (81 other events, 561.6 us)
